TPU v7x, 256 devices: a whole 4x4x8 slice. The times are simulated.
256 devices in a mesh: section: 2 (over y_hi), wide: 16 (over y_lo, z), narrow: 8 (over x, core).
Axes of the slice: x: 4, y: 4 (y_hi: 2, y_lo: 2; y = y_hi * 2 + y_lo), z: 8, core: 2. Of those that a mesh axis runs over, the one named last changes fastest.
Arguments:
- saved_inputs: bfloat16 [2, 512, 8192], P('section', None, 'narrow'), may hold values from -6 to 6
- upstream: bfloat16 [512, 8192], P('wide', 'narrow'), may hold values from -6 to 6
- up_weight: bfloat16 [2, 8192, 16384], P('section', 'narrow', 'wide'), may hold values from -0.0625 to 0.0625
- down_weight: bfloat16 [2, 16384, 8192], P('section', 'wide', 'narrow'), may hold values from -0.046875 to 0.046875
Outputs:
- boundary_grads: bfloat16 [2, 512, 8192], P('section', 'wide', 'narrow')
- up_grads: bfloat16 [2, 8192, 16384], P('section', 'narrow', 'wide')
- down_grads: bfloat16 [2, 16384, 8192], P('section', 'wide', 'narrow')
All inputs are finite; a program needn't handle non-finite values.
Results may differ from a plain program's by a relative error of at most 0.028.
Values may be sent and summed in bfloat16 or wider, within the bound.
No kernel may reach another device: no remote copies, remote signals or barrier semaphores. Data moves between devices by JAX's collectives and lax.ppermute only.
A program may use at most 64 MiB of HBM per device.

v0:
```python
import jax
import jax.numpy as jnp
from jax import lax
from jax.sharding import PartitionSpec as P

gelu_scale = 0.7978845608028654
cubic_term = 0.044715


def from_behind(block, axis, distance):
    devices = range(lax.axis_size(axis))
    route = [(i - distance, i) for i in devices if i - distance in devices]
    return lax.ppermute(block, axis, route)


def gelu_parts(pre_act):
    inner = jnp.tanh(gelu_scale * (pre_act + cubic_term * pre_act * pre_act * pre_act))
    act_value = 0.5 * pre_act * (1.0 + inner)
    slopes = 0.5 * (1.0 + inner) + 0.5 * pre_act * (1.0 - inner * inner) * gelu_scale * (
        1.0 + 3.0 * cubic_term * pre_act * pre_act
    )
    return (act_value, slopes)


def contract_rows(first_op, second_op):
    return lax.dot_general(
        first_op, second_op, (((0,), (0,)), ((), ())), preferred_element_type=jnp.float32
    )


def contract_cols(first_op, second_op):
    return lax.dot_general(
        first_op, second_op, (((1,), (1,)), ((), ())), preferred_element_type=jnp.float32
    )


def layer_back(whole_grad, saved_rows, w_up, w_down):
    tokens_all = whole_grad.shape[0]
    rows_wide = tokens_all // lax.axis_size("wide")
    picked = saved_rows
    pre_share = lax.psum_scatter(
        jnp.dot(picked, w_up, preferred_element_type=jnp.float32).astype(jnp.bfloat16),
        "narrow",
        scatter_dimension=0,
        tiled=True,
    ).astype(jnp.float32)
    act_share, slope_share = gelu_parts(pre_share)
    hidden = lax.all_gather(act_share.astype(jnp.bfloat16), "narrow", axis=0, tiled=True)
    grad_down = contract_rows(hidden, whole_grad).astype(jnp.bfloat16)
    picked = whole_grad
    back_share = lax.psum_scatter(
        contract_cols(picked, w_down).astype(jnp.bfloat16),
        "narrow",
        scatter_dimension=0,
        tiled=True,
    ).astype(jnp.float32)
    slope_part = (back_share * slope_share).astype(jnp.bfloat16)
    slope_grad = lax.all_gather(slope_part, "narrow", axis=0, tiled=True)
    grad_up = contract_rows(saved_rows, slope_grad).astype(jnp.bfloat16)
    picked = slope_grad
    summed = lax.psum_scatter(
        contract_cols(picked, w_up).astype(jnp.bfloat16), "wide", scatter_dimension=0, tiled=True
    ).astype(jnp.float32)
    own_rows = lax.dynamic_slice_in_dim(
        whole_grad, lax.axis_index("wide") * rows_wide, rows_wide, 0
    )
    grad_in = (own_rows.astype(jnp.float32) + summed).astype(jnp.bfloat16)
    return (grad_in, grad_up, grad_down)


def body(saved_inputs, upstream, up_weight, down_weight):
    saved_rows = saved_inputs[0]
    w_up = up_weight[0]
    w_down = down_weight[0]
    first_whole = lax.all_gather(upstream, "wide", axis=0, tiled=True)
    upper_in, upper_up, upper_down = layer_back(first_whole, saved_rows, w_up, w_down)
    assembled = lax.all_gather(upper_in, "wide", axis=0, tiled=True)
    second_whole = from_behind(assembled, "section", -1)
    lower_in, lower_up, lower_down = layer_back(second_whole, saved_rows, w_up, w_down)
    is_upper = lax.axis_index("section") == 1

    def pick_section(upper_part, lower_part):
        return jnp.where(is_upper, upper_part, lower_part)[None]

    return (
        pick_section(upper_in, lower_in),
        pick_section(upper_up, lower_up),
        pick_section(upper_down, lower_down),
    )


def solution(mesh):
    placed = (
        P("section", None, "narrow"),
        P("wide", "narrow"),
        P("section", "narrow", "wide"),
        P("section", "wide", "narrow"),
    )
    return jax.shard_map(
        body,
        mesh=mesh,
        in_specs=placed,
        out_specs=(
            P("section", "wide", "narrow"),
            P("section", "narrow", "wide"),
            P("section", "wide", "narrow"),
        ),
        check_vma=False,
    )
```

profile of v0, /device:TPU:56, one launch (start us, length us, event | category | flops | bytes accessed | tf_op | source)
XLA Modules:
  0.0 449.9 jit_solution(3568671155011216021)
XLA Ops:
  8.0 0.0 copy-start
  8.0 0.0 all-gather.6.cloned.1.call-start
  8.1 0.7 all-gather.6.cloned.1.call-update
  8.7 0.0 reduce-scatter.8.cloned.1.call-start
  8.8 0.8 copy-done
  9.6 3.4 fusion.16
  13.0 0.0 reduce-scatter.8.cloned.1.call-update
  13.1 0.0 reduce-scatter.6.cloned.1.call-start
  13.1 67.6 %all-gather.6.cloned.1.call-done = bf16[512,1024]{1,0:T(8,128)(2,1)} async-done(((bf16[32,1024]{1,0:T(8,128)(2,1)}), bf16[512,1024]{1,0:T(8,128)(2,1)}) %all-gather.6.cloned.1.call-update) | async-done | bytes 1048592 | tf_op jit(solution)/shard_map/all_gather | solution.py:75
  80.7 4.2 fusion.10
  84.9 0.0 reduce-scatter.6.cloned.1.call-update
  84.9 0.0 all-gather.8.cloned.1.call-start
  85.0 0.0 reduce-scatter.8.cloned.1.call-done
  85.0 33.2 %reduce-scatter.6.cloned.1.call-done = bf16[64,1024]{1,0:T(8,128)(2,1)} async-done(((bf16[512,1024]{1,0:T(8,128)(2,1)}), bf16[64,1024]{1,0:T(8,128)(2,1)}) %reduce-scatter.6.cloned.1.call-update) | async-done | bytes 131088 | tf_op jit(solution)/shard_map/reduce_scatter | solution.py:51
  118.3 1.8 multiply_convert_fusion.1
  120.1 0.0 all-gather.8.cloned.1.call-update
  120.1 0.0 copy-start.3
  120.1 0.0 reduce-scatter.10.cloned.1.call-start
  120.2 25.0 %all-gather.8.cloned.1.call-done = bf16[512,1024]{1,0:T(8,128)(2,1)} async-done(((bf16[64,1024]{1,0:T(8,128)(2,1)}), bf16[512,1024]{1,0:T(8,128)(2,1)}) %all-gather.8.cloned.1.call-update) | async-done | bytes 1048592 | tf_op jit(solution)/shard_map/all_gather | solution.py:58
  145.2 3.5 fusion.19
  148.6 0.0 reduce-scatter.10.cloned.1.call-update
  148.7 0.0 all-gather.10.cloned.1.call-start
  148.7 68.5 %reduce-scatter.10.cloned.1.call-done = bf16[32,1024]{1,0:T(8,128)(2,1)} async-done(((bf16[512,1024]{1,0:T(8,128)(2,1)}), bf16[32,1024]{1,0:T(8,128)(2,1)}) %reduce-scatter.10.cloned.1.call-update) | async-done | bytes 65552 | tf_op jit(solution)/shard_map/reduce_scatter | solution.py:61
  217.2 0.0 copy-done.3
  217.2 1.5 add_convert_fusion.1
  218.7 0.0 all-gather.10.cloned.1.call-update
  218.7 0.0 copy-start.2
  218.8 0.0 reduce-scatter.12.cloned.1.call-start
  218.8 67.9 %all-gather.10.cloned.1.call-done = bf16[512,1024]{1,0:T(8,128)(2,1)} async-done(((bf16[32,1024]{1,0:T(8,128)(2,1)}), bf16[512,1024]{1,0:T(8,128)(2,1)}) %all-gather.10.cloned.1.call-update) | async-done | bytes 1048592 | tf_op jit(solution)/shard_map/all_gather | solution.py:77
  286.7 3.1 collective-permute-start
  289.8 12.5 %collective-permute-done = bf16[512,1024]{1,0:T(8,128)(2,1)S(1)} collective-permute-done((bf16[512,1024]{1,0:T(8,128)(2,1)}, bf16[512,1024]{1,0:T(8,128)(2,1)S(1)}, u32[]{:S(2)}, u32[]{:S(2)}) %collective-permute-start) | collective-permute-done | bytes 1048608 | tf_op jit(solution)/shard_map/ppermute | solution.py:13
  302.4 0.0 copy-start.4
  302.4 1.0 copy-done.4
  303.3 3.8 fusion.13
  307.2 0.0 reduce-scatter.12.cloned.1.call-update
  307.2 0.0 all-gather.12.cloned.1.call-start
  307.3 34.5 %reduce-scatter.12.cloned.1.call-done = bf16[64,1024]{1,0:T(8,128)(2,1)} async-done(((bf16[512,1024]{1,0:T(8,128)(2,1)}), bf16[64,1024]{1,0:T(8,128)(2,1)}) %reduce-scatter.12.cloned.1.call-update) | async-done | bytes 131088 | tf_op jit(solution)/shard_map/reduce_scatter | solution.py:51
  341.7 0.0 copy-done.2
  341.7 1.8 fusion.34
  343.5 0.0 all-gather.12.cloned.1.call-update
  343.6 0.0 all-gather.14.cloned.1.call-start
  343.6 0.7 all-gather.14.cloned.1.call-update
  344.3 0.0 reduce-scatter.14.cloned.1.call-start
  344.4 24.7 %all-gather.12.cloned.1.call-done = bf16[512,1024]{1,0:T(8,128)(2,1)} async-done(((bf16[64,1024]{1,0:T(8,128)(2,1)}), bf16[512,1024]{1,0:T(8,128)(2,1)}) %all-gather.12.cloned.1.call-update) | async-done | bytes 1048592 | tf_op jit(solution)/shard_map/all_gather | solution.py:58
  369.0 3.5 fusion.22
  372.5 0.0 reduce-scatter.14.cloned.1.call-update
  372.5 0.0 copy-start.6
  372.5 0.0 copy-start.7
  372.5 3.0 fusion.26
  375.5 0.0 copy-done.6
  375.5 0.0 copy-done.7
  375.5 2.7 select_bitcast_fusion.1
  378.2 3.9 copy.7
  382.1 14.6 %all-gather.14.cloned.1.call-done = bf16[512,1024]{1,0:T(8,128)(2,1)} async-done(((bf16[64,1024]{1,0:T(8,128)(2,1)}), bf16[512,1024]{1,0:T(8,128)(2,1)}) %all-gather.14.cloned.1.call-update) | async-done | bytes 1048592 | tf_op jit(solution)/shard_map/all_gather | solution.py:48
  396.8 0.0 copy-start.5
  396.8 0.0 copy-start.8
  396.8 2.7 fusion.40
  399.4 0.0 copy-done.5
  399.4 0.0 copy-done.8
  399.4 0.0 copy-start.1
  399.5 2.7 select_bitcast_fusion
  402.1 39.1 %reduce-scatter.14.cloned.1.call-done = bf16[32,1024]{1,0:T(8,128)(2,1)} async-done(((bf16[512,1024]{1,0:T(8,128)(2,1)}), bf16[32,1024]{1,0:T(8,128)(2,1)}) %reduce-scatter.14.cloned.1.call-update) | async-done | bytes 65552 | tf_op jit(solution)/shard_map/reduce_scatter | solution.py:61
  441.2 0.0 copy-done.1
  441.3 1.5 fusion.39
Async XLA Ops:
  8.0 1.6 copy-start
  8.0 72.7 %all-gather.6.cloned.1.call-start = ((), (), s32[]{:S(2)}) async-start(), calls=%async_computation.5 | async-start | bytes 1114112 | tf_op jit(solution)/shard_map/all_gather | solution.py:75
  8.7 76.3 %reduce-scatter.8.cloned.1.call-start = ((), (), s32[]{:S(2)}) async-start(), calls=%async_computation.7 | async-start | bytes 1179648 | tf_op jit(solution)/shard_map/reduce_scatter | solution.py:41
  13.1 105.2 %reduce-scatter.6.cloned.1.call-start = ((), (), s32[]{:S(2)}) async-start(), calls=%async_computation.6 | async-start | bytes 1179648 | tf_op jit(solution)/shard_map/reduce_scatter | solution.py:51
  84.9 60.2 %all-gather.8.cloned.1.call-start = ((), (), s32[]{:S(2)}) async-start(), calls=%async_computation.8 | async-start | bytes 1179648 | tf_op jit(solution)/shard_map/all_gather | solution.py:58
  120.1 97.1 %copy-start.3 = (bf16[512,1024]{1,0:T(8,128)(2,1)S(1)}, bf16[512,1024]{1,0:T(8,128)(2,1)}, u32[]{:S(2)}) copy-start(bf16[512,1024]{1,0:T(8,128)(2,1)} %all-gather.6.cloned.1.call-done) | copy-start | bytes 3145732
  120.1 97.1 %reduce-scatter.10.cloned.1.call-start = ((), (), s32[]{:S(2)}) async-start(), calls=%async_computation.9 | async-start | bytes 1114112 | tf_op jit(solution)/shard_map/reduce_scatter | solution.py:61
  148.7 138.1 %all-gather.10.cloned.1.call-start = ((), (), s32[]{:S(2)}) async-start(), calls=%async_computation.10 | async-start | bytes 1114112 | tf_op jit(solution)/shard_map/all_gather | solution.py:77
  218.7 123.0 %copy-start.2 = (bf16[64,1024]{1,0:T(8,128)(2,1)S(1)}, bf16[64,1024]{1,0:T(8,128)(2,1)}, u32[]{:S(2)}) copy-start(bf16[64,1024]{1,0:T(8,128)(2,1)} %reduce-scatter.8.cloned.1.call-done) | copy-start | bytes 393220
  218.8 123.0 %reduce-scatter.12.cloned.1.call-start = ((), (), s32[]{:S(2)}) async-start(), calls=%async_computation.11 | async-start | bytes 1179648 | tf_op jit(solution)/shard_map/reduce_scatter | solution.py:51
  286.7 15.6 %collective-permute-start = (bf16[512,1024]{1,0:T(8,128)(2,1)}, bf16[512,1024]{1,0:T(8,128)(2,1)S(1)}, u32[]{:S(2)}, u32[]{:S(2)}) collective-permute-start(bf16[512,1024]{1,0:T(8,128)(2,1)} %all-gather.10.cloned.1.call-done), channel_id=1, source_target_pairs={{128,0},{129,1},{130,2},{131,3},{132,4},{133,5},{134,6},{135,7},{1... | collective-permute-start | bytes 3145736 | tf_op jit(solution)/shard_map/ppermute | solution.py:13
  302.4 1.0 copy-start.4
  307.2 61.8 %all-gather.12.cloned.1.call-start = ((), (), s32[]{:S(2)}) async-start(), calls=%async_computation.12 | async-start | bytes 1179648 | tf_op jit(solution)/shard_map/all_gather | solution.py:58
  343.6 53.2 %all-gather.14.cloned.1.call-start = ((), (), s32[]{:S(2)}) async-start(), calls=%async_computation.14 | async-start | bytes 1179648 | tf_op jit(solution)/shard_map/all_gather | solution.py:48
  344.3 96.9 %reduce-scatter.14.cloned.1.call-start = ((), (), s32[]{:S(2)}) async-start(), calls=%async_computation.13 | async-start | bytes 1114112 | tf_op jit(solution)/shard_map/reduce_scatter | solution.py:61
  372.5 3.0 copy-start.6
  372.5 3.0 copy-start.7
  396.8 2.7 copy-start.5
  396.8 2.7 copy-start.8
  399.4 41.8 %copy-start.1 = (bf16[32,1024]{1,0:T(8,128)(2,1)S(1)}, bf16[32,1024]{1,0:T(8,128)(2,1)}, u32[]{:S(2)}) copy-start(bf16[32,1024]{1,0:T(8,128)(2,1)} %add_convert_fusion.1) | copy-start | bytes 196612
Sparse Core Ops, SparseCore 0:
  10.6 70.0 all-gather.5
  148.8 68.3 reduce-scatter.9
  219.7 66.9 all-gather.9
  372.6 68.5 reduce-scatter.13
Sparse Core Ops, SparseCore 1:
  13.2 36.6 reduce-scatter.7
  85.0 33.2 reduce-scatter.5
  120.6 24.5 all-gather.7
  307.3 34.4 reduce-scatter.11
  344.4 24.6 all-gather.11
  370.9 25.8 all-gather.13
where the time goes:
time: 454 us; the launch traced here: 450 us
  waiting for transfers between devices  389 us (86%)
  matrix products  29.4 us (6%)
  between operations  15.4 us (3%)
  other arithmetic  6.62 us (1%)
  local copies, waits for them, and re-layouts  5.73 us (1%)
    reduce_scatter x2, waiting for transfers between devices, layer_back(): lax.psum_scatter(contract_cols(picked, w_up).astype(jnp.bfloat16), 'wide'...  108 us
    all_gather x1, waiting for transfers between devices, body(): assembled = lax.all_gather(upper_in, 'wide', axis=0, tiled=True)  67.9 us
    reduce_scatter x2, waiting for transfers between devices, layer_back(): lax.psum_scatter(contract_cols(picked, w_down).astype(jnp.bfloat16), 'nar...  67.7 us
    all_gather x1, waiting for transfers between devices, body(): first_whole = lax.all_gather(upstream, 'wide', axis=0, tiled=True)  67.6 us
    all_gather x2, waiting for transfers between devices, layer_back(): slope_grad = lax.all_gather(slope_part, 'narrow', axis=0, tiled=True)  49.7 us
    dot_general x4, matrix products, contract_cols(): lax.dot_general(first_op, second_op, (((1,), (1,)), ((), ())), preferred_...  15 us
    all_gather x1, waiting for transfers between devices, layer_back(): lax.all_gather(act_share.astype(jnp.bfloat16), 'narrow', axis=0, tiled=True)  14.6 us
    ppermute x1, waiting for transfers between devices, from_behind(): return lax.ppermute(block, axis, route)  12.5 us
  transfers between devices with their start and end apart: 11, of which 10 were waited for; matrix products, arithmetic and copies ran while one was open for 6% of the time, Pallas kernels for 0%

commit v1 on v0

v1 whole, which is shorter than its diff:
```python
import jax
import jax.numpy as jnp
from jax import lax
from jax.sharding import Mesh, PartitionSpec as P

gelu_scale = 0.7978845608028654
cubic_term = 0.044715

X, CORES, YLO, Z = 4, 2, 2, 8
WIDE = YLO * Z
CHUNKS = 1
AXES = ("section", "ylo", "z", "x", "core")
WIDE_AXES = ("ylo", "z")


def gelu_parts(pre_act):
    inner = jnp.tanh(gelu_scale * (pre_act + cubic_term * pre_act * pre_act * pre_act))
    act_value = 0.5 * pre_act * (1.0 + inner)
    slopes = 0.5 * (1.0 + inner) + 0.5 * pre_act * (1.0 - inner * inner) * gelu_scale * (
        1.0 + 3.0 * cubic_term * pre_act * pre_act
    )
    return (act_value, slopes)


def contract_rows(first_op, second_op):
    return lax.dot_general(
        first_op, second_op, (((0,), (0,)), ((), ())), preferred_element_type=jnp.float32
    )


def contract_cols(first_op, second_op):
    return lax.dot_general(
        first_op, second_op, (((1,), (1,)), ((), ())), preferred_element_type=jnp.float32
    )


def other_core(block):
    return lax.ppermute(block, "core", [(0, 1), (1, 0)])


def spread_narrow(partial):
    rows, cols = partial.shape
    half = rows // CORES
    core = lax.axis_index("core")
    sent = lax.dynamic_slice_in_dim(partial, (1 - core) * half, half, 0)
    kept = lax.dynamic_slice_in_dim(partial, core * half, half, 0)
    pair = kept.astype(jnp.float32) + other_core(sent).astype(jnp.float32)
    blocks = lax.all_to_all(
        pair.astype(jnp.bfloat16).reshape(X, half // X, cols), "x", 0, 0, tiled=True
    )
    return jnp.sum(blocks.astype(jnp.float32), axis=0)


def gather_narrow(block):
    rows, cols = block.shape
    mine = lax.all_to_all(
        jnp.broadcast_to(block[None], (X, rows, cols)), "x", 0, 0, tiled=True
    ).reshape(X * rows, cols)
    theirs = other_core(mine)
    first = lax.axis_index("core") == 0
    return jnp.concatenate(
        [jnp.where(first, mine, theirs), jnp.where(first, theirs, mine)], axis=0
    )


def spread_wide(partial):
    rows, cols = partial.shape
    blocks = lax.all_to_all(
        partial.reshape(WIDE, rows // WIDE, cols), WIDE_AXES, 0, 0, tiled=True
    )
    return jnp.sum(blocks.astype(jnp.float32), axis=0)


def gather_wide(block):
    rows, cols = block.shape
    return lax.all_to_all(
        jnp.broadcast_to(block[None], (WIDE, rows, cols)), WIDE_AXES, 0, 0, tiled=True
    ).reshape(WIDE * rows, cols)


def chain(own_rows, slope_share, w_up, w_down):
    whole = gather_wide(own_rows)
    back_share = spread_narrow(contract_cols(whole, w_down).astype(jnp.bfloat16))
    slope_part = (back_share * slope_share).astype(jnp.bfloat16)
    slope_grad = gather_narrow(slope_part)
    summed = spread_wide(contract_cols(slope_grad, w_up).astype(jnp.bfloat16))
    grad_in = (own_rows.astype(jnp.float32) + summed).astype(jnp.bfloat16)
    return whole, slope_grad, grad_in


def chunk_rows(block, chunks):
    rows, cols = block.shape
    split = block.reshape(WIDE, chunks, rows // (WIDE * chunks), cols)
    return [split[:, c].reshape(rows // chunks, cols) for c in range(chunks)]


def body(saved_inputs, upstream, up_weight, down_weight):
    saved = chunk_rows(saved_inputs[0], CHUNKS)
    w_up = up_weight[0]
    w_down = down_weight[0]
    step = upstream.shape[0] // CHUNKS
    upper_own = [upstream[c * step : (c + 1) * step] for c in range(CHUNKS)]

    pre = [
        spread_narrow(
            jnp.dot(rows, w_up, preferred_element_type=jnp.float32).astype(jnp.bfloat16)
        )
        for rows in saved
    ]
    parts = [gelu_parts(share) for share in pre]
    hidden = [gather_narrow(act.astype(jnp.bfloat16)) for act, _ in parts]

    upper = [chain(own, part[1], w_up, w_down) for own, part in zip(upper_own, parts)]
    lower_own = [lax.ppermute(out[2], "section", [(1, 0)]) for out in upper]
    lower = [chain(own, part[1], w_up, w_down) for own, part in zip(lower_own, parts)]

    is_upper = lax.axis_index("section") == 1

    def picked(index):
        return jnp.concatenate(
            [jnp.where(is_upper, u[index], l[index]) for u, l in zip(upper, lower)], axis=0
        )

    incoming, slope_grad, grad_in = picked(0), picked(1), picked(2)
    grad_down = contract_rows(jnp.concatenate(hidden, axis=0), incoming).astype(jnp.bfloat16)
    grad_up = contract_rows(jnp.concatenate(saved, axis=0), slope_grad).astype(jnp.bfloat16)
    return grad_in[None], grad_up[None], grad_down[None]


def solution(mesh):
    fine = Mesh(mesh.devices.reshape(2, YLO, Z, X, CORES), AXES)
    wide, narrow = WIDE_AXES, ("x", "core")
    return jax.shard_map(
        body,
        mesh=fine,
        in_specs=(
            P("section", None, narrow),
            P(wide, narrow),
            P("section", narrow, wide),
            P("section", wide, narrow),
        ),
        out_specs=(
            P("section", wide, narrow),
            P("section", narrow, wide),
            P("section", wide, narrow),
        ),
        check_vma=False,
    )
```

time: 454 us -> 237 us (0.52)
  waiting for transfers between devices: 389 us -> 69.5 us
  blocking collectives: 0 us -> 97.2 us
  starting transfers between devices: 3.49 us -> 29.1 us
  between operations: 15.4 us -> 0.88 us
  matrix products: 29.4 us -> 19.3 us
    all_gather x5 -> x0, waiting for transfers between devices: 200 us -> none  [the longest x1 67.9 us: body(): assembled = lax.all_gather(upper_in, 'wide', axis=0, tiled=True)]
    reduce_scatter x5 -> x0, waiting for transfers between devices: 175 us -> none  [the longest x2 108 us: layer_back(): lax.psum_scatter(contract_cols(picked, w_up).astype(jnp.bfloat16), 'wide'...]
    all_to_all x0 -> x5, blocking collectives: none -> 97.2 us  [the longest x1 32.1 us: spread_wide(): lax.all_to_all(partial.reshape(WIDE, rows // WIDE, cols), WIDE_AXES, 0, 0...]
    all_to_all x0 -> x5, waiting for transfers between devices: none -> 61.9 us  [the longest x1 22.5 us: gather_wide(): lax.all_to_all(jnp.broadcast_to(block[None], (WIDE, rows, cols)), WIDE_AX...]
    all_to_all x0 -> x5, starting transfers between devices: none -> 25.6 us  [the longest x1 9.49 us: gather_wide(): lax.all_to_all(jnp.broadcast_to(block[None], (WIDE, rows, cols)), WIDE_AX...]
    dot_general x4, matrix products: 15 us -> 8.09 us  [contract_cols(): lax.dot_general(first_op, second_op, (((1,), (1,)), ((), ())), preferred_...]
    ppermute x1 -> x7, waiting for transfers between devices: 12.5 us -> 7.6 us  [the longest x6 5.72 us: other_core(): return lax.ppermute(block, 'core', [(0, 1), (1, 0)])]
    dot_general x4 -> x2, matrix products: 11 us -> 8.7 us  [contract_rows(): lax.dot_general(first_op, second_op, (((0,), (0,)), ((), ())), preferred_...]
  transfers between devices with their start and end apart: 11 -> 12, of which waited for: 10 -> 9; matrix products, arithmetic and copies ran while one was open for 6% -> 10% of each run, Pallas kernels for 0% -> 0%
where the time goes in v1:
time: 237 us; the launch traced here: 234 us
  blocking collectives  97.2 us (41%)
  waiting for transfers between devices  69.5 us (29%)
  starting transfers between devices  29.1 us (12%)
  matrix products  19.3 us (8%)
  local copies, waits for them, and re-layouts  9.45 us (4%)
  other arithmetic  8.46 us (4%)
    all_to_all x1, blocking collectives, spread_wide(): lax.all_to_all(partial.reshape(WIDE, rows // WIDE, cols), WIDE_AXES, 0, 0...  32.1 us
    all_to_all x1, blocking collectives, gather_wide(): lax.all_to_all(jnp.broadcast_to(block[None], (WIDE, rows, cols)), WIDE_AX...  30.5 us
    all_to_all x1, waiting for transfers between devices, gather_wide(): lax.all_to_all(jnp.broadcast_to(block[None], (WIDE, rows, cols)), WIDE_AX...  22.5 us
    all_to_all x2, blocking collectives, gather_narrow(): lax.all_to_all(jnp.broadcast_to(block[None], (X, rows, cols)), 'x', 0, 0,...  22.1 us
    all_to_all x2, waiting for transfers between devices, spread_narrow(): lax.all_to_all(pair.astype(jnp.bfloat16).reshape(X, half // X, cols), 'x'...  17.3 us
    all_to_all x1, waiting for transfers between devices, spread_wide(): lax.all_to_all(partial.reshape(WIDE, rows // WIDE, cols), WIDE_AXES, 0, 0...  13.9 us
    all_to_all x1, blocking collectives, spread_narrow(): lax.all_to_all(pair.astype(jnp.bfloat16).reshape(X, half // X, cols), 'x'...  12.5 us
    all_to_all x1, starting transfers between devices, gather_wide(): lax.all_to_all(jnp.broadcast_to(block[None], (WIDE, rows, cols)), WIDE_AX...  9.49 us
  transfers between devices with their start and end apart: 12, of which 9 were waited for; matrix products, arithmetic and copies ran while one was open for 10% of the time, Pallas kernels for 0%

profile of v1, /device:TPU:56, one launch (start us, length us, event | category | flops | bytes accessed | tf_op | source)
XLA Modules:
  0.0 233.9 jit_solution(11775060855659784857)
XLA Ops:
  0.6 0.0 copy-start
  0.6 2.1 broadcast_in_dim.16
  2.7 9.5 %all-to-all-start = ((bf16[16,32,1024]{2,1,0:T(8,128)(2,1)}), bf16[16,32,1024]{2,1,0:T(8,128)(2,1)S(1)}, u32[]{:S(2)}, u32[]{:S(2)}) async-start(bf16[16,32,1024]{2,1,0:T(8,128)(2,1)} %broadcast_in_dim.16), calls=%async_computation | async-start | bytes 2097152 | tf_op jit(solution)/shard_map/all_to_all | solution.py:76
  12.2 2.5 %fusion.16 = bf16[512,1024]{1,0:T(8,128)(2,1)S(1)} fusion(bf16[1,1024,1024]{2,1,0:T(8,128)(2,1)S(1)} %copy-done, bf16[1,512,1024]{2,1,0:T(8,128)(2,1)} %param.4), kind=kOutput, calls=%fused_computation.16 | convolution fusion | flops 1074266112 | bytes 4194304 | tf_op jit(solution)/shard_map/dot_general | solution.py:106
  14.7 0.0 copy-start.4
  14.7 0.9 constant_dynamic-slice_fusion.1
  15.6 0.2 copy-done.4
  15.9 0.0 collective-permute-start.1
  15.9 22.5 %all-to-all-done = bf16[16,32,1024]{2,1,0:T(8,128)(2,1)S(1)} async-done(((bf16[16,32,1024]{2,1,0:T(8,128)(2,1)}), bf16[16,32,1024]{2,1,0:T(8,128)(2,1)S(1)}, u32[]{:S(2)}, u32[]{:S(2)}) %all-to-all-start) | async-done | bytes 1048608 | tf_op jit(solution)/shard_map/all_to_all | solution.py:76
  38.4 3.3 %fusion.10 = bf16[512,1024]{1,0:T(8,128)(2,1)S(1)} fusion(bf16[512,1024]{1,0:T(8,128)(2,1)S(1)} %bitcast.57, bf16[1,1024,1024]{2,1,0:T(8,128)(2,1)} %param.7), kind=kOutput, calls=%fused_computation.14 | convolution fusion | flops 1074266112 | bytes 4194304 | tf_op jit(solution)/shard_map/dot_general | solution.py:32
  41.7 0.0 copy-start.3
  41.7 0.9 constant_dynamic-slice_fusion.2
  42.6 0.2 copy-done.3
  42.8 0.0 collective-permute-start
  42.8 0.0 collective-permute-done.1
  42.8 2.2 add_convert_fusion.1
  45.0 4.3 %all-to-all-start.2 = ((bf16[4,64,1024]{2,1,0:T(8,128)(2,1)}), bf16[4,64,1024]{2,1,0:T(8,128)(2,1)S(1)}, u32[]{:S(2)}, u32[]{:S(2)}) async-start(bf16[4,64,1024]{2,1,0:T(8,128)(2,1)} %bitcast.5), calls=%async_computation.2 | async-start | bytes 1048576 | tf_op jit(solution)/shard_map/all_to_all | solution.py:48
  49.3 0.0 collective-permute-done
  49.3 2.0 add_convert_fusion.2
  51.4 8.1 %all-to-all-done.2 = bf16[4,64,1024]{2,1,0:T(8,128)(2,1)S(1)} async-done(((bf16[4,64,1024]{2,1,0:T(8,128)(2,1)}), bf16[4,64,1024]{2,1,0:T(8,128)(2,1)S(1)}, u32[]{:S(2)}, u32[]{:S(2)}) %all-to-all-start.2) | async-done | bytes 524320 | tf_op jit(solution)/shard_map/all_to_all | solution.py:48
  59.5 3.5 %all-to-all-start.1 = ((bf16[4,64,1024]{2,1,0:T(8,128)(2,1)}), bf16[4,64,1024]{2,1,0:T(8,128)(2,1)S(1)}, u32[]{:S(2)}, u32[]{:S(2)}) async-start(bf16[4,64,1024]{2,1,0:T(8,128)(2,1)} %bitcast.2), calls=%async_computation.1 | async-start | bytes 1048576 | tf_op jit(solution)/shard_map/all_to_all | solution.py:48
  63.0 0.1 convert_reduce_fusion.3
  63.0 9.2 %all-to-all-done.1 = bf16[4,64,1024]{2,1,0:T(8,128)(2,1)S(1)} async-done(((bf16[4,64,1024]{2,1,0:T(8,128)(2,1)}), bf16[4,64,1024]{2,1,0:T(8,128)(2,1)S(1)}, u32[]{:S(2)}, u32[]{:S(2)}) %all-to-all-start.1) | async-done | bytes 524320 | tf_op jit(solution)/shard_map/all_to_all | solution.py:48
  72.2 0.1 convert_reduce_fusion.4
  72.3 0.2 multiply_convert_fusion.2
  72.5 0.1 broadcast_in_dim.17
  72.6 10.5 %all_to_all.50 = bf16[4,64,1024]{2,1,0:T(8,128)(2,1)S(1)} all-to-all(bf16[4,64,1024]{2,1,0:T(8,128)(2,1)S(1)} %broadcast_in_dim.17), channel_id=1, replica_groups=mesh['section'=2,'ylo'=2,'z'=8,'x'=4,'core'=2] {'x'}, dimensions={0} | all-to-all | bytes 1048576 | tf_op jit(solution)/shard_map/all_to_all | solution.py:56
  83.1 0.0 collective-permute-start.2
  83.1 1.9 collective-permute-done.2
  85.0 0.1 broadcast_select_fusion.5
  85.1 1.3 fusion.19
  86.4 0.0 copy-start.9
  86.4 32.1 %all_to_all.51 = bf16[16,32,1024]{2,1,0:T(8,128)(2,1)S(1)} all-to-all(bf16[16,32,1024]{2,1,0:T(8,128)(2,1)S(1)} %bitcast.62), channel_id=1, replica_groups=mesh['section'=2,'ylo'=2,'z'=8,'x'=4,'core'=2] {'ylo','z'}, dimensions={0} | all-to-all | bytes 2097152 | tf_op jit(solution)/shard_map/all_to_all | solution.py:68
  118.6 0.2 convert_reduce_fusion.1
  118.7 0.0 copy-done.9
  118.8 3.3 %collective-permute-start.3 = (bf16[32,1024]{1,0:T(8,128)(2,1)S(1)}, bf16[32,1024]{1,0:T(8,128)(2,1)S(1)}, u32[]{:S(2)}, u32[]{:S(2)}) collective-permute-start(bf16[32,1024]{1,0:T(8,128)(2,1)S(1)} %add_convert_fusion.4), channel_id=1, source_target_pairs={{128,0},{129,1},{130,2},{131,3},{132,4},{133,5},{134,6},{135,7},{1... | collective-permute-start | bytes 196616 | tf_op jit(solution)/shard_map/ppermute | solution.py:114
  122.1 1.9 collective-permute-done.3
  124.0 0.1 broadcast_in_dim.18
  124.1 30.5 %all_to_all.52 = bf16[16,32,1024]{2,1,0:T(8,128)(2,1)S(1)} all-to-all(bf16[16,32,1024]{2,1,0:T(8,128)(2,1)S(1)} %broadcast_in_dim.18), channel_id=1, replica_groups=mesh['section'=2,'ylo'=2,'z'=8,'x'=4,'core'=2] {'ylo','z'}, dimensions={0} | all-to-all | bytes 2097152 | tf_op jit(solution)/shard_map/all_to_all | solution.py:76
  154.6 1.3 fusion.13
  156.0 0.1 collective-permute-start.4
  156.1 1.9 collective-permute-done.4
  158.0 0.2 add_convert_fusion
  158.2 12.5 %all_to_all.53 = bf16[4,64,1024]{2,1,0:T(8,128)(2,1)S(1)} all-to-all(bf16[4,64,1024]{2,1,0:T(8,128)(2,1)S(1)} %bitcast.56), channel_id=1, replica_groups=mesh['section'=2,'ylo'=2,'z'=8,'x'=4,'core'=2] {'x'}, dimensions={0} | all-to-all | bytes 1048576 | tf_op jit(solution)/shard_map/all_to_all | solution.py:48
  170.6 0.1 convert_reduce_fusion.2
  170.7 0.2 multiply_convert_fusion
  170.9 0.1 broadcast_in_dim.19
  171.0 11.6 %all_to_all.54 = bf16[4,64,1024]{2,1,0:T(8,128)(2,1)S(1)} all-to-all(bf16[4,64,1024]{2,1,0:T(8,128)(2,1)S(1)} %broadcast_in_dim.19), channel_id=1, replica_groups=mesh['section'=2,'ylo'=2,'z'=8,'x'=4,'core'=2] {'x'}, dimensions={0} | all-to-all | bytes 1048576 | tf_op jit(solution)/shard_map/all_to_all | solution.py:56
  182.6 0.9 broadcast_in_dim.22
  183.4 3.5 %all-to-all-start.9 = ((bf16[4,64,1024]{2,1,0:T(8,128)(2,1)}), bf16[4,64,1024]{2,1,0:T(8,128)(2,1)S(1)}, u32[]{:S(2)}, u32[]{:S(2)}) async-start(bf16[4,64,1024]{2,1,0:T(8,128)(2,1)} %broadcast_in_dim.22), calls=%async_computation.9 | async-start | bytes 1048576 | tf_op jit(solution)/shard_map/all_to_all | solution.py:56
  186.9 0.1 collective-permute-start.5
  187.0 8.2 %all-to-all-done.9 = bf16[4,64,1024]{2,1,0:T(8,128)(2,1)S(1)} async-done(((bf16[4,64,1024]{2,1,0:T(8,128)(2,1)}), bf16[4,64,1024]{2,1,0:T(8,128)(2,1)S(1)}, u32[]{:S(2)}, u32[]{:S(2)}) %all-to-all-start.9) | async-done | bytes 524320 | tf_op jit(solution)/shard_map/all_to_all | solution.py:56
  195.2 0.0 collective-permute-start.6
  195.2 0.0 collective-permute-done.5
  195.2 1.9 collective-permute-done.6
  197.1 2.3 broadcast_select_fusion.1
  199.4 2.3 fusion.22
  201.6 4.9 %all-to-all-start.8 = ((bf16[16,32,1024]{2,1,0:T(8,128)(2,1)}), bf16[16,32,1024]{2,1,0:T(8,128)(2,1)S(1)}, u32[]{:S(2)}, u32[]{:S(2)}) async-start(bf16[16,32,1024]{2,1,0:T(8,128)(2,1)} %bitcast.61), calls=%async_computation.8 | async-start | bytes 2097152 | tf_op jit(solution)/shard_map/all_to_all | solution.py:68
  206.5 4.5 %convert_bitcast_fusion.1 = bf16[1,1024,1024]{1,2,0:T(8,128)(2,1)} fusion(bf16[1,512,1024]{2,1,0:T(8,128)(2,1)} %param.4, pred[]{:T(512)S(6)} %eq.8, bf16[256,1024]{1,0:T(8,128)(2,1)} %copy-done.7, bf16[256,1024]{1,0:T(8,128)(2,1)} %copy-done.8, bf16[256,1024]{1,0:T(8,128)(2,1)} %copy-done.6, bf16[256,1024]{1,0:T(8,128)(2,1)} %copy-done.5), kind=kOutput, calls=%fused_computation.11 | convolution fusion | flops 1079508992 | bytes 5242881 | tf_op jit(solution)/shard_map/dot_general | solution.py:26
  211.0 3.9 %copy.7 = bf16[1,1024,1024]{2,1,0:T(8,128)(2,1)} copy(bf16[1,1024,1024]{1,2,0:T(8,128)(2,1)} %convert_bitcast_fusion.1) | data formatting | bytes 4194304
  215.0 4.2 %convert_bitcast_fusion = bf16[1,1024,1024]{2,1,0:T(8,128)(2,1)} fusion(bf16[256,1024]{1,0:T(8,128)(2,1)} %get-tuple-element.7, bf16[256,1024]{1,0:T(8,128)(2,1)} %get-tuple-element.6, bf16[512,1024]{1,0:T(8,128)(2,1)} %bitcast.58, bf16[512,1024]{1,0:T(8,128)(2,1)} %bitcast.60, pred[]{:T(512)S(6)} %eq.8), kind=kOutput, calls=%fused_computation.10 | convolution fusion | flops 1077411840 | bytes 5242881 | tf_op jit(solution)/shard_map/dot_general | solution.py:26
  219.1 13.9 %all-to-all-done.8 = bf16[16,32,1024]{2,1,0:T(8,128)(2,1)S(1)} async-done(((bf16[16,32,1024]{2,1,0:T(8,128)(2,1)}), bf16[16,32,1024]{2,1,0:T(8,128)(2,1)S(1)}, u32[]{:S(2)}, u32[]{:S(2)}) %all-to-all-start.8) | async-done | bytes 1048608 | tf_op jit(solution)/shard_map/all_to_all | solution.py:68
  233.0 0.2 convert_reduce_fusion
  233.2 0.7 fusion.40
  (17 shorter events, 0.1 us)
Async XLA Ops:
  0.6 11.6 %copy-start = (bf16[1,1024,1024]{2,1,0:T(8,128)(2,1)S(1)}, bf16[1,1024,1024]{2,1,0:T(8,128)(2,1)}, u32[]{:S(2)}) copy-start(bf16[1,1024,1024]{2,1,0:T(8,128)(2,1)} %param.6) | copy-start | bytes 6291460
  2.7 35.7 %all-to-all-start = ((bf16[16,32,1024]{2,1,0:T(8,128)(2,1)}), bf16[16,32,1024]{2,1,0:T(8,128)(2,1)S(1)}, u32[]{:S(2)}, u32[]{:S(2)}) async-start(bf16[16,32,1024]{2,1,0:T(8,128)(2,1)} %broadcast_in_dim.16), calls=%async_computation | async-start | bytes 2097152 | tf_op jit(solution)/shard_map/all_to_all | solution.py:76
  14.7 1.1 copy-start.4
  15.9 27.0 %collective-permute-start.1 = (bf16[256,1024]{1,0:T(8,128)(2,1)}, bf16[256,1024]{1,0:T(8,128)(2,1)}, u32[]{:S(2)}, u32[]{:S(2)}) collective-permute-start(bf16[256,1024]{1,0:T(8,128)(2,1)} %constant_dynamic-slice_fusion.1), channel_id=1, source_target_pairs={{0,1},{1,0},{2,3},{3,2},{4,5},{5,4},{6,7},{7,6},{8,9},{9,8},{10,11... | collective-permute-start | bytes 1572872 | tf_op jit(solution)/shard_map/ppermute | solution.py:38
  38.4 3.3 %copy-start.1 = (bf16[16,32,1024]{2,1,0:T(8,128)(2,1)}, bf16[16,32,1024]{2,1,0:T(8,128)(2,1)S(1)}, u32[]{:S(2)}) copy-start(bf16[16,32,1024]{2,1,0:T(8,128)(2,1)S(1)} %all-to-all-done) | copy-start | bytes 3145732
  41.7 1.1 copy-start.3
  42.8 6.5 %collective-permute-start = (bf16[256,1024]{1,0:T(8,128)(2,1)}, bf16[256,1024]{1,0:T(8,128)(2,1)S(1)}, u32[]{:S(2)}, u32[]{:S(2)}) collective-permute-start(bf16[256,1024]{1,0:T(8,128)(2,1)} %constant_dynamic-slice_fusion.2), channel_id=1, source_target_pairs={{0,1},{1,0},{2,3},{3,2},{4,5},{5,4},{6,7},{7,6},{8,9},{9,8},{10,11... | collective-permute-start | bytes 1572872 | tf_op jit(solution)/shard_map/ppermute | solution.py:38
  45.0 14.4 %all-to-all-start.2 = ((bf16[4,64,1024]{2,1,0:T(8,128)(2,1)}), bf16[4,64,1024]{2,1,0:T(8,128)(2,1)S(1)}, u32[]{:S(2)}, u32[]{:S(2)}) async-start(bf16[4,64,1024]{2,1,0:T(8,128)(2,1)} %bitcast.5), calls=%async_computation.2 | async-start | bytes 1048576 | tf_op jit(solution)/shard_map/all_to_all | solution.py:48
  59.5 12.8 %all-to-all-start.1 = ((bf16[4,64,1024]{2,1,0:T(8,128)(2,1)}), bf16[4,64,1024]{2,1,0:T(8,128)(2,1)S(1)}, u32[]{:S(2)}, u32[]{:S(2)}) async-start(bf16[4,64,1024]{2,1,0:T(8,128)(2,1)} %bitcast.2), calls=%async_computation.1 | async-start | bytes 1048576 | tf_op jit(solution)/shard_map/all_to_all | solution.py:48
  83.1 1.9 collective-permute-start.2
  85.1 1.3 copy-start.5
  85.1 1.3 copy-start.6
  86.4 32.3 %copy-start.9 = (bf16[32,1024]{1,0:T(8,128)(2,1)S(1)}, bf16[32,1024]{1,0:T(8,128)(2,1)}, u32[]{:S(2)}) copy-start(bf16[32,1024]{1,0:T(8,128)(2,1)} %param.5) | copy-start | bytes 196612
  118.6 36.0 %copy-start.10 = (bf16[1,1024,1024]{2,1,0:T(8,128)(2,1)S(1)}, bf16[1,1024,1024]{2,1,0:T(8,128)(2,1)}, u32[]{:S(2)}) copy-start(bf16[1,1024,1024]{2,1,0:T(8,128)(2,1)} %param.7) | copy-start | bytes 6291460
  118.8 5.2 %collective-permute-start.3 = (bf16[32,1024]{1,0:T(8,128)(2,1)S(1)}, bf16[32,1024]{1,0:T(8,128)(2,1)S(1)}, u32[]{:S(2)}, u32[]{:S(2)}) collective-permute-start(bf16[32,1024]{1,0:T(8,128)(2,1)S(1)} %add_convert_fusion.4), channel_id=1, source_target_pairs={{128,0},{129,1},{130,2},{131,3},{132,4},{133,5},{134,6},{135,7},{1... | collective-permute-start | bytes 196616 | tf_op jit(solution)/shard_map/ppermute | solution.py:114
  154.6 1.3 copy-start.2
  156.0 2.0 collective-permute-start.4
  183.4 11.8 %all-to-all-start.9 = ((bf16[4,64,1024]{2,1,0:T(8,128)(2,1)}), bf16[4,64,1024]{2,1,0:T(8,128)(2,1)S(1)}, u32[]{:S(2)}, u32[]{:S(2)}) async-start(bf16[4,64,1024]{2,1,0:T(8,128)(2,1)} %broadcast_in_dim.22), calls=%async_computation.9 | async-start | bytes 1048576 | tf_op jit(solution)/shard_map/all_to_all | solution.py:56
  186.9 8.3 %collective-permute-start.5 = (bf16[256,1024]{1,0:T(8,128)(2,1)S(1)}, bf16[256,1024]{1,0:T(8,128)(2,1)}, u32[]{:S(2)}, u32[]{:S(2)}) collective-permute-start(bf16[256,1024]{1,0:T(8,128)(2,1)S(1)} %bitcast.53), channel_id=1, source_target_pairs={{0,1},{1,0},{2,3},{3,2},{4,5},{5,4},{6,7},{7,6},{8,9},{9,8},{10,11... | collective-permute-start | bytes 1572872 | tf_op jit(solution)/shard_map/ppermute | solution.py:38
  195.2 1.9 collective-permute-start.6
  199.4 2.3 copy-start.7
  199.4 2.3 copy-start.8
  201.6 31.4 %all-to-all-start.8 = ((bf16[16,32,1024]{2,1,0:T(8,128)(2,1)}), bf16[16,32,1024]{2,1,0:T(8,128)(2,1)S(1)}, u32[]{:S(2)}, u32[]{:S(2)}) async-start(bf16[16,32,1024]{2,1,0:T(8,128)(2,1)} %bitcast.61), calls=%async_computation.8 | async-start | bytes 2097152 | tf_op jit(solution)/shard_map/all_to_all | solution.py:68

commit v2 on v1

v2 whole, which is shorter than its diff:
```python
import jax
import jax.numpy as jnp
from jax import lax
from jax.sharding import Mesh, PartitionSpec as P

gelu_scale = 0.7978845608028654
cubic_term = 0.044715

X, CORES, YLO, Z = 4, 2, 2, 8
WIDE = YLO * Z
CHUNKS = 2
AXES = ("section", "ylo", "z", "x", "core")
WIDE_AXES = ("ylo", "z")


def gelu_parts(pre_act):
    inner = jnp.tanh(gelu_scale * (pre_act + cubic_term * pre_act * pre_act * pre_act))
    act_value = 0.5 * pre_act * (1.0 + inner)
    slopes = 0.5 * (1.0 + inner) + 0.5 * pre_act * (1.0 - inner * inner) * gelu_scale * (
        1.0 + 3.0 * cubic_term * pre_act * pre_act
    )
    return (act_value, slopes)


def contract(first_op, second_op, first_dim, second_dim):
    return lax.dot_general(
        first_op,
        second_op,
        (((first_dim,), (second_dim,)), ((), ())),
        preferred_element_type=jnp.float32,
    )


def other_core(block):
    return lax.ppermute(block, "core", [(0, 1), (1, 0)])


def halves(weight, dim):
    size = weight.shape[dim] // CORES
    core = lax.axis_index("core")
    return (
        lax.dynamic_slice_in_dim(weight, core * size, size, dim),
        lax.dynamic_slice_in_dim(weight, (1 - core) * size, size, dim),
    )


def in_order(mine, theirs):
    first = lax.axis_index("core") == 0
    return jnp.concatenate(
        [jnp.where(first, mine, theirs), jnp.where(first, theirs, mine)], axis=1
    )


def narrow_total(mine, theirs):
    pair = mine + other_core(theirs.astype(jnp.bfloat16)).astype(jnp.float32)
    sent = pair.astype(jnp.bfloat16)
    total = pair
    for distance in (1, 3, 2):
        route = [(i, (i + distance) % X) for i in range(X)]
        total = total + lax.ppermute(sent, "x", route).astype(jnp.float32)
    return total


def spread_wide(partial):
    rows, cols = partial.shape
    blocks = lax.all_to_all(
        partial.reshape(WIDE, rows // WIDE, cols), WIDE_AXES, 0, 0, tiled=True
    )
    return jnp.sum(blocks.astype(jnp.float32), axis=0)


def gather_wide(block):
    rows, cols = block.shape
    return lax.all_to_all(
        jnp.broadcast_to(block[None], (WIDE, rows, cols)), WIDE_AXES, 0, 0, tiled=True
    ).reshape(WIDE * rows, cols)


def chain(own_rows, slopes, up_halves, down_halves):
    whole = gather_wide(own_rows)
    theirs = contract(whole, down_halves[1], 1, 1)
    mine = contract(whole, down_halves[0], 1, 1)
    slope_mine = (narrow_total(mine, theirs) * slopes).astype(jnp.bfloat16)
    slope_theirs = other_core(slope_mine)
    summed = spread_wide(
        (
            contract(slope_mine, up_halves[0], 1, 1) + contract(slope_theirs, up_halves[1], 1, 1)
        ).astype(jnp.bfloat16)
    )
    grad_in = (own_rows.astype(jnp.float32) + summed).astype(jnp.bfloat16)
    return whole, slope_mine, slope_theirs, grad_in


def chunk_rows(block):
    rows, cols = block.shape
    split = block.reshape(WIDE, CHUNKS, rows // (WIDE * CHUNKS), cols)
    return split.transpose(1, 0, 2, 3).reshape(rows, cols)


def cut(block):
    step = block.shape[0] // CHUNKS
    return [block[c * step : (c + 1) * step] for c in range(CHUNKS)]


def body(saved_inputs, upstream, up_weight, down_weight):
    saved = chunk_rows(saved_inputs[0])
    up_halves = halves(up_weight[0], 1)
    down_halves = halves(down_weight[0], 0)

    theirs = contract(saved, up_halves[1], 1, 0)
    mine = contract(saved, up_halves[0], 1, 0)
    act, slopes = gelu_parts(narrow_total(mine, theirs))
    hidden_mine = act.astype(jnp.bfloat16)
    hidden = in_order(hidden_mine, other_core(hidden_mine))

    upper_own = cut(upstream)
    upper = [chain(own, s, up_halves, down_halves) for own, s in zip(upper_own, cut(slopes))]
    lower_own = [lax.ppermute(out[3], "section", [(1, 0)]) for out in upper]
    lower = [chain(own, s, up_halves, down_halves) for own, s in zip(lower_own, cut(slopes))]

    is_upper = lax.axis_index("section") == 1

    def picked(index):
        return jnp.concatenate(
            [jnp.where(is_upper, u[index], l[index]) for u, l in zip(upper, lower)], axis=0
        )

    grad_down = contract(hidden, picked(0), 0, 0).astype(jnp.bfloat16)
    grad_up = contract(saved, in_order(picked(1), picked(2)), 0, 0).astype(jnp.bfloat16)
    return picked(3)[None], grad_up[None], grad_down[None]


def solution(mesh):
    fine = Mesh(mesh.devices.reshape(2, YLO, Z, X, CORES), AXES)
    wide, narrow = WIDE_AXES, ("x", "core")
    return jax.shard_map(
        body,
        mesh=fine,
        in_specs=(
            P("section", None, narrow),
            P(wide, narrow),
            P("section", narrow, wide),
            P("section", wide, narrow),
        ),
        out_specs=(
            P("section", wide, narrow),
            P("section", narrow, wide),
            P("section", wide, narrow),
        ),
        check_vma=False,
    )
```

time: 237 us -> 270 us (1.14)
  blocking collectives: 97.2 us -> 0 us
  starting transfers between devices: 29.1 us -> 94.6 us
  waiting for transfers between devices: 69.5 us -> 107 us
  matrix products: 19.3 us -> 34.4 us
  other arithmetic: 8.46 us -> 16 us
  local copies, waits for them, and re-layouts: 9.45 us -> 12.8 us
    all_to_all x5 -> x0, blocking collectives: 97.2 us -> none  [the longest x1 32.1 us: spread_wide(): lax.all_to_all(partial.reshape(WIDE, rows // WIDE, cols), WIDE_AXES, 0, 0...]
    ppermute x1 -> x17, starting transfers between devices: 3.27 us -> 45.8 us  [the longest x15 37 us: narrow_total(): total = total + lax.ppermute(sent, 'x', route).astype(jnp.float32)]
    ppermute x1 -> x17, waiting for transfers between devices: 1.88 us -> 31.3 us  [the longest x15 27.6 us: narrow_total(): total = total + lax.ppermute(sent, 'x', route).astype(jnp.float32)]
    all_to_all x1 -> x4, waiting for transfers between devices: 13.9 us -> 41.6 us  [spread_wide(): lax.all_to_all(partial.reshape(WIDE, rows // WIDE, cols), WIDE_AXES, 0, 0...]
    all_to_all x3 -> x0, waiting for transfers between devices: 25.5 us -> none  [the longest x2 17.3 us: spread_narrow(): lax.all_to_all(pair.astype(jnp.bfloat16).reshape(X, half // X, cols), 'x'...]
    all_to_all x1 -> x4, starting transfers between devices: 4.88 us -> 22.8 us  [spread_wide(): lax.all_to_all(partial.reshape(WIDE, rows // WIDE, cols), WIDE_AXES, 0, 0...]
    dot_general x7 -> x20, matrix products: 19.3 us -> 34.4 us  [contract(): lax.dot_general(first_op, second_op, (((first_dim,), (second_dim,)), ((),...]
    all_to_all x1 -> x4, starting transfers between devices: 9.49 us -> 24.5 us  [gather_wide(): lax.all_to_all(jnp.broadcast_to(block[None], (WIDE, rows, cols)), WIDE_AX...]
  transfers between devices with their start and end apart: 12 -> 35, of which waited for: 9 -> 20; matrix products, arithmetic and copies ran while one was open for 10% -> 18% of each run, Pallas kernels for 0% -> 0%
where the time goes in v2:
time: 270 us; the launch traced here: 266 us
  waiting for transfers between devices  107 us (40%)
  starting transfers between devices  94.6 us (35%)
  matrix products  34.4 us (13%)
  other arithmetic  16 us (6%)
  local copies, waits for them, and re-layouts  12.8 us (5%)
    all_to_all x4, waiting for transfers between devices, spread_wide(): lax.all_to_all(partial.reshape(WIDE, rows // WIDE, cols), WIDE_AXES, 0, 0...  41.6 us
    ppermute x15, starting transfers between devices, narrow_total(): total = total + lax.ppermute(sent, 'x', route).astype(jnp.float32)  37 us
    dot_general x20, matrix products, contract(): lax.dot_general(first_op, second_op, (((first_dim,), (second_dim,)), ((),...  34.4 us
    all_to_all x4, waiting for transfers between devices, gather_wide(): lax.all_to_all(jnp.broadcast_to(block[None], (WIDE, rows, cols)), WIDE_AX...  31.3 us
    ppermute x15, waiting for transfers between devices, narrow_total(): total = total + lax.ppermute(sent, 'x', route).astype(jnp.float32)  27.6 us
    all_to_all x4, starting transfers between devices, gather_wide(): lax.all_to_all(jnp.broadcast_to(block[None], (WIDE, rows, cols)), WIDE_AX...  24.5 us
    all_to_all x4, starting transfers between devices, spread_wide(): lax.all_to_all(partial.reshape(WIDE, rows // WIDE, cols), WIDE_AXES, 0, 0...  22.8 us
    ppermute x2, starting transfers between devices, body(): lower_own = [lax.ppermute(out[3], 'section', [(1, 0)]) for out in upper]  8.85 us
  transfers between devices with their start and end apart: 35, of which 20 were waited for; matrix products, arithmetic and copies ran while one was open for 18% of the time, Pallas kernels for 0%

profile of v2, /device:TPU:56, one launch (start us, length us, event | category | flops | bytes accessed | tf_op | source)
XLA Modules:
  0.0 266.0 jit_solution(5768697250067738266)
XLA Ops:
  2.4 9.5 %all-to-all-start.4 = ((bf16[16,16,1024]{2,1,0:T(8,128)(2,1)}), bf16[16,16,1024]{2,1,0:T(8,128)(2,1)S(1)}, u32[]{:S(2)}, u32[]{:S(2)}) async-start(bf16[16,16,1024]{2,1,0:T(8,128)(2,1)} %broadcast_in_dim.16), calls=%async_computation.4 | async-start | bytes 1048576 | tf_op jit(solution)/shard_map/all_to_all | solution.py:74
  11.9 2.3 copy.18
  14.2 12.8 %all-to-all-done.4 = bf16[16,16,1024]{2,1,0:T(8,128)(2,1)S(1)} async-done(((bf16[16,16,1024]{2,1,0:T(8,128)(2,1)}), bf16[16,16,1024]{2,1,0:T(8,128)(2,1)S(1)}, u32[]{:S(2)}, u32[]{:S(2)}) %all-to-all-start.4) | async-done | bytes 524320 | tf_op jit(solution)/shard_map/all_to_all | solution.py:74
  28.0 5.1 %all-to-all-start = ((bf16[16,16,1024]{2,1,0:T(8,128)(2,1)}), bf16[16,16,1024]{2,1,0:T(8,128)(2,1)S(1)}, u32[]{:S(2)}, u32[]{:S(2)}) async-start(bf16[16,16,1024]{2,1,0:T(8,128)(2,1)} %broadcast_in_dim.14), calls=%async_computation | async-start | bytes 1048576 | tf_op jit(solution)/shard_map/all_to_all | solution.py:74
  33.1 2.7 %fusion.4 = bf16[512,512]{1,0:T(8,128)(2,1)} fusion(bf16[512,1024]{1,0:T(8,128)(2,1)} %bitcast.114, bf16[1,1024,1024]{2,1,0:T(8,128)(2,1)S(1)} %copy-done, s32[]{:T(128)S(6)} %select_n.74), kind=kOutput, calls=%fused_computation.14 | convolution fusion | flops 537133056 | bytes 2621444 | tf_op jit(solution)/shard_map/dot_general | solution.py:26
  35.9 2.4 fusion.6
  38.8 3.2 %fusion.43 = (bf16[512,512]{1,0:T(8,128)(2,1)}, f32[512,512]{1,0:T(8,128)}) fusion(bf16[512,512]{1,0:T(8,128)(2,1)} %collective-permute-done.4, bf16[512,1024]{1,0:T(8,128)(2,1)} %bitcast.115, bf16[1,1024,1024]{2,1,0:T(8,128)(2,1)S(1)} %copy-done, s32[]{:T(128)S(6)} %select_n.73), kind=kOutput, calls=%fused_computation.68 | convolution fusion | flops 537657344 | bytes 4194308 | tf_op jit(solution)/shard_map/dot_general | solution.py:26
  42.0 1.5 collective-permute-start.5
  43.5 1.7 collective-permute-start.6
  45.3 1.8 collective-permute-start.7
  48.0 1.9 fusion.5
  50.1 1.9 fusion.63
  52.0 1.6 collective-permute-start.16
  53.5 1.8 collective-permute-start.17
  55.8 3.4 %collective-permute-done.5 = bf16[512,512]{1,0:T(8,128)(2,1)} collective-permute-done((bf16[512,512]{1,0:T(8,128)(2,1)}, bf16[512,512]{1,0:T(8,128)(2,1)}, u32[]{:S(2)}, u32[]{:S(2)}) %collective-permute-start.5) | collective-permute-done | bytes 524320 | tf_op jit(solution)/shard_map/ppermute | solution.py:60
  59.2 12.1 %collective-permute-start.18 = (bf16[256,512]{1,0:T(8,128)(2,1)S(1)}, bf16[256,512]{1,0:T(8,128)(2,1)S(1)}, u32[]{:S(2)}, u32[]{:S(2)}) collective-permute-start(bf16[256,512]{1,0:T(8,128)(2,1)S(1)} %get-tuple-element.34), channel_id=1, source_target_pairs={{0,4},{2,6},{4,0},{6,2},{1,5},{3,7},{5,1},{7,3},{8,12},{10,14},{12... | collective-permute-start | bytes 786440 | tf_op jit(solution)/shard_map/ppermute | solution.py:60
  71.4 3.2 %collective-permute-start.2 = (bf16[256,512]{1,0:T(8,128)(2,1)S(1)}, bf16[256,512]{1,0:T(8,128)(2,1)S(1)}, u32[]{:S(2)}, u32[]{:S(2)}) collective-permute-start(bf16[256,512]{1,0:T(8,128)(2,1)S(1)} %get-tuple-element.30), channel_id=1, source_target_pairs={{0,6},{2,0},{4,2},{6,4},{1,7},{3,1},{5,3},{7,5},{8,14},{10,8},{12,... | collective-permute-start | bytes 786440 | tf_op jit(solution)/shard_map/ppermute | solution.py:60
  74.6 1.3 collective-permute-done.16
  75.9 6.5 %collective-permute-start.3 = (bf16[256,512]{1,0:T(8,128)(2,1)S(1)}, bf16[256,512]{1,0:T(8,128)(2,1)S(1)}, u32[]{:S(2)}, u32[]{:S(2)}) collective-permute-start(bf16[256,512]{1,0:T(8,128)(2,1)S(1)} %get-tuple-element.30), channel_id=1, source_target_pairs={{0,4},{2,6},{4,0},{6,2},{1,5},{3,7},{5,1},{7,3},{8,12},{10,14},{12... | collective-permute-start | bytes 786440 | tf_op jit(solution)/shard_map/ppermute | solution.py:60
  82.5 3.3 %multiply_convert_fusion = (bf16[512,512]{1,0:T(8,128)(2,1)}, f32[512,512]{1,0:T(8,128)S(1)}) fusion(bf16[512,512]{1,0:T(8,128)(2,1)} %collective-permute-done.7, bf16[512,512]{1,0:T(8,128)(2,1)} %collective-permute-done.6, bf16[512,512]{1,0:T(8,128)(2,1)} %collective-permute-done.5, f32[512,512]{1,0:T(8,128)S(1)} %copy-done.16, ...), kind=kLoop, calls=%fused_computation.61 | loop fusion | flops 7077888 | bytes 4718592 | tf_op jit(solution)/shard_map/convert_element_type | solution.py:113
  86.7 5.3 %collective-permute-done.3 = bf16[256,512]{1,0:T(8,128)(2,1)S(1)} collective-permute-done((bf16[256,512]{1,0:T(8,128)(2,1)S(1)}, bf16[256,512]{1,0:T(8,128)(2,1)S(1)}, u32[]{:S(2)}, u32[]{:S(2)}) %collective-permute-start.3) | collective-permute-done | bytes 262176 | tf_op jit(solution)/shard_map/ppermute | solution.py:60
  92.6 1.5 collective-permute-done.19
  95.3 1.3 fusion.2
  96.6 8.1 %all-to-all-start.5 = ((bf16[16,16,1024]{2,1,0:T(8,128)(2,1)}), bf16[16,16,1024]{2,1,0:T(8,128)(2,1)}, u32[]{:S(2)}, u32[]{:S(2)}) async-start(bf16[16,16,1024]{2,1,0:T(8,128)(2,1)} %bitcast.111), calls=%async_computation.5 | async-start | bytes 1048576 | tf_op jit(solution)/shard_map/all_to_all | solution.py:66
  104.8 1.5 collective-permute-done.8
  107.5 1.3 fusion
  108.8 11.7 %all-to-all-done.5 = bf16[16,16,1024]{2,1,0:T(8,128)(2,1)} async-done(((bf16[16,16,1024]{2,1,0:T(8,128)(2,1)}), bf16[16,16,1024]{2,1,0:T(8,128)(2,1)}, u32[]{:S(2)}, u32[]{:S(2)}) %all-to-all-start.5) | async-done | bytes 524320 | tf_op jit(solution)/shard_map/all_to_all | solution.py:66
  120.5 4.9 %all-to-all-start.1 = ((bf16[16,16,1024]{2,1,0:T(8,128)(2,1)}), bf16[16,16,1024]{2,1,0:T(8,128)(2,1)}, u32[]{:S(2)}, u32[]{:S(2)}) async-start(bf16[16,16,1024]{2,1,0:T(8,128)(2,1)} %bitcast.112), calls=%async_computation.1 | async-start | bytes 1048576 | tf_op jit(solution)/shard_map/all_to_all | solution.py:66
  125.4 1.1 convert_reduce_fusion.1
  126.5 14.2 %all-to-all-done.1 = bf16[16,16,1024]{2,1,0:T(8,128)(2,1)} async-done(((bf16[16,16,1024]{2,1,0:T(8,128)(2,1)}), bf16[16,16,1024]{2,1,0:T(8,128)(2,1)}, u32[]{:S(2)}, u32[]{:S(2)}) %all-to-all-start.1) | async-done | bytes 524320 | tf_op jit(solution)/shard_map/all_to_all | solution.py:66
  140.8 1.1 convert_reduce_fusion.3
  143.2 3.1 %collective-permute-start.20 = (bf16[16,1024]{1,0:T(8,128)(2,1)S(1)}, bf16[16,1024]{1,0:T(8,128)(2,1)S(1)}, u32[]{:S(2)}, u32[]{:S(2)}) collective-permute-start(bf16[16,1024]{1,0:T(8,128)(2,1)S(1)} %get-tuple-element.27), channel_id=1, source_target_pairs={{128,0},{129,1},{130,2},{131,3},{132,4},{133,5},{134,6},{135,7},{1... | collective-permute-start | bytes 98312 | tf_op jit(solution)/shard_map/ppermute | solution.py:118
  146.3 1.6 collective-permute-done.20
  148.7 5.1 %all-to-all-start.6 = ((bf16[16,16,1024]{2,1,0:T(8,128)(2,1)}), bf16[16,16,1024]{2,1,0:T(8,128)(2,1)}, u32[]{:S(2)}, u32[]{:S(2)}) async-start(bf16[16,16,1024]{2,1,0:T(8,128)(2,1)} %broadcast_in_dim.17), calls=%async_computation.6 | async-start | bytes 1048576 | tf_op jit(solution)/shard_map/all_to_all | solution.py:74
  153.8 5.7 %collective-permute-start.9 = (bf16[16,1024]{1,0:T(8,128)(2,1)}, bf16[16,1024]{1,0:T(8,128)(2,1)S(1)}, u32[]{:S(2)}, u32[]{:S(2)}) collective-permute-start(bf16[16,1024]{1,0:T(8,128)(2,1)} %get-tuple-element.26), channel_id=1, source_target_pairs={{128,0},{129,1},{130,2},{131,3},{132,4},{133,5},{134,6},{135,7},{1... | collective-permute-start | bytes 98312 | tf_op jit(solution)/shard_map/ppermute | solution.py:118
  159.5 2.1 collective-permute-done.9
  161.6 6.4 %all-to-all-done.6 = bf16[16,16,1024]{2,1,0:T(8,128)(2,1)} async-done(((bf16[16,16,1024]{2,1,0:T(8,128)(2,1)}), bf16[16,16,1024]{2,1,0:T(8,128)(2,1)}, u32[]{:S(2)}, u32[]{:S(2)}) %all-to-all-start.6) | async-done | bytes 524320 | tf_op jit(solution)/shard_map/all_to_all | solution.py:74
  168.9 4.9 %all-to-all-start.2 = ((bf16[16,16,1024]{2,1,0:T(8,128)(2,1)}), bf16[16,16,1024]{2,1,0:T(8,128)(2,1)}, u32[]{:S(2)}, u32[]{:S(2)}) async-start(bf16[16,16,1024]{2,1,0:T(8,128)(2,1)} %broadcast_in_dim.15), calls=%async_computation.2 | async-start | bytes 1048576 | tf_op jit(solution)/shard_map/all_to_all | solution.py:74
  173.7 2.6 convolution_convert_fusion.1
  176.8 11.2 %all-to-all-done.2 = bf16[16,16,1024]{2,1,0:T(8,128)(2,1)} async-done(((bf16[16,16,1024]{2,1,0:T(8,128)(2,1)}), bf16[16,16,1024]{2,1,0:T(8,128)(2,1)}, u32[]{:S(2)}, u32[]{:S(2)}) %all-to-all-start.2) | async-done | bytes 524320 | tf_op jit(solution)/shard_map/all_to_all | solution.py:74
  188.0 2.0 convolution_convert_fusion.3
  190.2 1.9 fusion.88
  192.1 1.2 collective-permute-start.22
  193.3 2.1 collective-permute-start.23
  195.5 1.5 fusion.87
  197.0 1.5 collective-permute-start.11
  198.5 1.8 collective-permute-start.12
  200.3 7.7 %collective-permute-done.22 = bf16[256,512]{1,0:T(8,128)(2,1)S(1)} collective-permute-done((bf16[256,512]{1,0:T(8,128)(2,1)S(1)}, bf16[256,512]{1,0:T(8,128)(2,1)S(1)}, u32[]{:S(2)}, u32[]{:S(2)}) %collective-permute-start.22) | collective-permute-done | bytes 262176 | tf_op jit(solution)/shard_map/ppermute | solution.py:60
  208.0 2.1 broadcast_select_fusion.3
  210.1 3.5 %collective-permute-done.11 = bf16[256,512]{1,0:T(8,128)(2,1)S(1)} collective-permute-done((bf16[256,512]{1,0:T(8,128)(2,1)S(1)}, bf16[256,512]{1,0:T(8,128)(2,1)S(1)}, u32[]{:S(2)}, u32[]{:S(2)}) %collective-permute-start.11) | collective-permute-done | bytes 262176 | tf_op jit(solution)/shard_map/ppermute | solution.py:60
  213.6 4.6 %collective-permute-done.12 = bf16[256,512]{1,0:T(8,128)(2,1)S(1)} collective-permute-done((bf16[256,512]{1,0:T(8,128)(2,1)S(1)}, bf16[256,512]{1,0:T(8,128)(2,1)S(1)}, u32[]{:S(2)}, u32[]{:S(2)}) %collective-permute-start.12) | collective-permute-done | bytes 262176 | tf_op jit(solution)/shard_map/ppermute | solution.py:60
  219.0 1.2 broadcast_select_fusion.9
  220.3 1.9 broadcast_select_fusion
  222.7 1.3 fusion.1
  224.0 4.9 %all-to-all-start.3 = ((bf16[16,16,1024]{2,1,0:T(8,128)(2,1)}), bf16[16,16,1024]{2,1,0:T(8,128)(2,1)S(1)}, u32[]{:S(2)}, u32[]{:S(2)}) async-start(bf16[16,16,1024]{2,1,0:T(8,128)(2,1)} %bitcast.110), calls=%async_computation.3 | async-start | bytes 1048576 | tf_op jit(solution)/shard_map/all_to_all | solution.py:66
  228.9 1.1 broadcast_select_fusion.1
  230.1 4.0 %convert_bitcast_fusion = bf16[1,1024,1024]{2,1,0:T(8,128)(2,1)} fusion(bf16[512,512]{1,0:T(8,128)(2,1)} %get-tuple-element.19, bf16[512,512]{1,0:T(8,128)(2,1)} %get-tuple-element.18, bf16[256,1024]{1,0:T(8,128)(2,1)} %broadcast_select_fusion, bf16[256,1024]{1,0:T(8,128)(2,1)S(1)} %broadcast_select_fusion.1), kind=kOutput, calls=%fused_computation | convolution fusion | flops 1078984704 | bytes 4194304 | tf_op jit(solution)/shard_map/dot_general | solution.py:26
  235.3 1.3 fusion.3
  236.6 8.3 %all-to-all-done.3 = bf16[16,16,1024]{2,1,0:T(8,128)(2,1)S(1)} async-done(((bf16[16,16,1024]{2,1,0:T(8,128)(2,1)}), bf16[16,16,1024]{2,1,0:T(8,128)(2,1)S(1)}, u32[]{:S(2)}, u32[]{:S(2)}) %all-to-all-start.3) | async-done | bytes 524320 | tf_op jit(solution)/shard_map/all_to_all | solution.py:66
  244.9 4.9 %all-to-all-start.7 = ((bf16[16,16,1024]{2,1,0:T(8,128)(2,1)}), bf16[16,16,1024]{2,1,0:T(8,128)(2,1)S(1)}, u32[]{:S(2)}, u32[]{:S(2)}) async-start(bf16[16,16,1024]{2,1,0:T(8,128)(2,1)} %bitcast.109), calls=%async_computation.7 | async-start | bytes 1048576 | tf_op jit(solution)/shard_map/all_to_all | solution.py:66
  249.8 1.4 broadcast_select_fusion.5
  251.2 2.6 convert_bitcast_fusion.1
  253.9 3.9 %copy.22 = bf16[1,1024,1024]{2,1,0:T(8,128)(2,1)} copy(bf16[1,1024,1024]{1,2,0:T(8,128)(2,1)} %convert_bitcast_fusion.1) | data formatting | bytes 4194304
  257.9 7.4 %all-to-all-done.7 = bf16[16,16,1024]{2,1,0:T(8,128)(2,1)S(1)} async-done(((bf16[16,16,1024]{2,1,0:T(8,128)(2,1)}), bf16[16,16,1024]{2,1,0:T(8,128)(2,1)S(1)}, u32[]{:S(2)}, u32[]{:S(2)}) %all-to-all-start.7) | async-done | bytes 524320 | tf_op jit(solution)/shard_map/all_to_all | solution.py:66
  (98 shorter events, 15.8 us)
Async XLA Ops:
  0.6 32.5 %copy-start = (bf16[1,1024,1024]{2,1,0:T(8,128)(2,1)S(1)}, bf16[1,1024,1024]{2,1,0:T(8,128)(2,1)}, u32[]{:S(2)}) copy-start(bf16[1,1024,1024]{2,1,0:T(8,128)(2,1)} %param.6) | copy-start | bytes 6291460
  2.4 24.6 %all-to-all-start.4 = ((bf16[16,16,1024]{2,1,0:T(8,128)(2,1)}), bf16[16,16,1024]{2,1,0:T(8,128)(2,1)S(1)}, u32[]{:S(2)}, u32[]{:S(2)}) async-start(bf16[16,16,1024]{2,1,0:T(8,128)(2,1)} %broadcast_in_dim.16), calls=%async_computation.4 | async-start | bytes 1048576 | tf_op jit(solution)/shard_map/all_to_all | solution.py:74
  27.0 23.0 %copy-start.3 = (bf16[16,16,1024]{2,1,0:T(8,128)(2,1)}, bf16[16,16,1024]{2,1,0:T(8,128)(2,1)S(1)}, u32[]{:S(2)}) copy-start(bf16[16,16,1024]{2,1,0:T(8,128)(2,1)S(1)} %all-to-all-done.4) | copy-start | bytes 1572868
  28.0 20.0 %all-to-all-start = ((bf16[16,16,1024]{2,1,0:T(8,128)(2,1)}), bf16[16,16,1024]{2,1,0:T(8,128)(2,1)S(1)}, u32[]{:S(2)}, u32[]{:S(2)}) async-start(bf16[16,16,1024]{2,1,0:T(8,128)(2,1)} %broadcast_in_dim.14), calls=%async_computation | async-start | bytes 1048576 | tf_op jit(solution)/shard_map/all_to_all | solution.py:74
  35.9 2.9 %collective-permute-start.4 = (bf16[512,512]{1,0:T(8,128)(2,1)}, bf16[512,512]{1,0:T(8,128)(2,1)}, u32[]{:S(2)}, u32[]{:S(2)}) collective-permute-start(bf16[512,512]{1,0:T(8,128)(2,1)} %fusion.4), channel_id=1, source_target_pairs={{0,1},{1,0},{2,3},{3,2},{4,5},{5,4},{6,7},{7,6},{8,9},{9,8},{10,11... | collective-permute-start | bytes 1572872 | tf_op jit(solution)/shard_map/ppermute | solution.py:35
  38.3 11.7 %collective-permute-start.15 = (bf16[256,512]{1,0:T(8,128)(2,1)}, bf16[256,512]{1,0:T(8,128)(2,1)S(1)}, u32[]{:S(2)}, u32[]{:S(2)}) collective-permute-start(bf16[256,512]{1,0:T(8,128)(2,1)} %fusion.6), channel_id=1, source_target_pairs={{0,1},{1,0},{2,3},{3,2},{4,5},{5,4},{6,7},{7,6},{8,9},{9,8},{10,11... | collective-permute-start | bytes 786440 | tf_op jit(solution)/shard_map/ppermute | solution.py:35
  42.0 17.2 %collective-permute-start.5 = (bf16[512,512]{1,0:T(8,128)(2,1)}, bf16[512,512]{1,0:T(8,128)(2,1)}, u32[]{:S(2)}, u32[]{:S(2)}) collective-permute-start(bf16[512,512]{1,0:T(8,128)(2,1)} %get-tuple-element.32), channel_id=1, source_target_pairs={{0,2},{2,4},{4,6},{6,0},{1,3},{3,5},{5,7},{7,1},{8,10},{10,12},{12... | collective-permute-start | bytes 1572872 | tf_op jit(solution)/shard_map/ppermute | solution.py:60
  43.5 27.9 %collective-permute-start.6 = (bf16[512,512]{1,0:T(8,128)(2,1)}, bf16[512,512]{1,0:T(8,128)(2,1)}, u32[]{:S(2)}, u32[]{:S(2)}) collective-permute-start(bf16[512,512]{1,0:T(8,128)(2,1)} %get-tuple-element.32), channel_id=1, source_target_pairs={{0,6},{2,0},{4,2},{6,4},{1,7},{3,1},{5,3},{7,5},{8,14},{10,8},{12,... | collective-permute-start | bytes 1572872 | tf_op jit(solution)/shard_map/ppermute | solution.py:60
  45.3 26.1 %collective-permute-start.7 = (bf16[512,512]{1,0:T(8,128)(2,1)}, bf16[512,512]{1,0:T(8,128)(2,1)}, u32[]{:S(2)}, u32[]{:S(2)}) collective-permute-start(bf16[512,512]{1,0:T(8,128)(2,1)} %get-tuple-element.32), channel_id=1, source_target_pairs={{0,4},{2,6},{4,0},{6,2},{1,5},{3,7},{5,1},{7,3},{8,12},{10,14},{12... | collective-permute-start | bytes 1572872 | tf_op jit(solution)/shard_map/ppermute | solution.py:60
  48.0 7.3 %copy-start.5 = (bf16[16,16,1024]{2,1,0:T(8,128)(2,1)}, bf16[16,16,1024]{2,1,0:T(8,128)(2,1)S(1)}, u32[]{:S(2)}) copy-start(bf16[16,16,1024]{2,1,0:T(8,128)(2,1)S(1)} %all-to-all-done) | copy-start | bytes 1572868
  48.0 7.3 %copy-start.1 = (bf16[1,1024,1024]{2,1,0:T(8,128)(2,1)S(1)}, bf16[1,1024,1024]{2,1,0:T(8,128)(2,1)}, u32[]{:S(2)}) copy-start(bf16[1,1024,1024]{2,1,0:T(8,128)(2,1)} %param.7) | copy-start | bytes 6291460
  49.9 32.6 %copy-start.16 = (f32[512,512]{1,0:T(8,128)S(1)}, f32[512,512]{1,0:T(8,128)}, u32[]{:S(2)}) copy-start(f32[512,512]{1,0:T(8,128)} %get-tuple-element.33) | copy-start | bytes 3145732
  49.9 3.6 %collective-permute-start = (bf16[256,512]{1,0:T(8,128)(2,1)S(1)}, bf16[256,512]{1,0:T(8,128)(2,1)S(1)}, u32[]{:S(2)}, u32[]{:S(2)}) collective-permute-start(bf16[256,512]{1,0:T(8,128)(2,1)S(1)} %fusion.5), channel_id=1, source_target_pairs={{0,1},{1,0},{2,3},{3,2},{4,5},{5,4},{6,7},{7,6},{8,9},{9,8},{10,11... | collective-permute-start | bytes 786440 | tf_op jit(solution)/shard_map/ppermute | solution.py:35
  50.1 5.7 %copy-start.17 = (bf16[256,512]{1,0:T(8,128)(2,1)}, bf16[256,512]{1,0:T(8,128)(2,1)S(1)}, u32[]{:S(2)}) copy-start(bf16[256,512]{1,0:T(8,128)(2,1)S(1)} %collective-permute-done.15) | copy-start | bytes 786436
  52.0 24.0 %collective-permute-start.16 = (bf16[256,512]{1,0:T(8,128)(2,1)S(1)}, bf16[256,512]{1,0:T(8,128)(2,1)S(1)}, u32[]{:S(2)}, u32[]{:S(2)}) collective-permute-start(bf16[256,512]{1,0:T(8,128)(2,1)S(1)} %get-tuple-element.34), channel_id=1, source_target_pairs={{0,2},{2,4},{4,6},{6,0},{1,3},{3,5},{5,7},{7,1},{8,10},{10,12},{12... | collective-permute-start | bytes 786440 | tf_op jit(solution)/shard_map/ppermute | solution.py:60
  53.5 32.2 %collective-permute-start.17 = (bf16[256,512]{1,0:T(8,128)(2,1)S(1)}, bf16[256,512]{1,0:T(8,128)(2,1)S(1)}, u32[]{:S(2)}, u32[]{:S(2)}) collective-permute-start(bf16[256,512]{1,0:T(8,128)(2,1)S(1)} %get-tuple-element.34), channel_id=1, source_target_pairs={{0,6},{2,0},{4,2},{6,4},{1,7},{3,1},{5,3},{7,5},{8,14},{10,8},{12,... | collective-permute-start | bytes 786440 | tf_op jit(solution)/shard_map/ppermute | solution.py:60
  59.2 26.5 %collective-permute-start.18 = (bf16[256,512]{1,0:T(8,128)(2,1)S(1)}, bf16[256,512]{1,0:T(8,128)(2,1)S(1)}, u32[]{:S(2)}, u32[]{:S(2)}) collective-permute-start(bf16[256,512]{1,0:T(8,128)(2,1)S(1)} %get-tuple-element.34), channel_id=1, source_target_pairs={{0,4},{2,6},{4,0},{6,2},{1,5},{3,7},{5,1},{7,3},{8,12},{10,14},{12... | collective-permute-start | bytes 786440 | tf_op jit(solution)/shard_map/ppermute | solution.py:60
  71.4 14.4 %collective-permute-start.1 = (bf16[256,512]{1,0:T(8,128)(2,1)S(1)}, bf16[256,512]{1,0:T(8,128)(2,1)S(1)}, u32[]{:S(2)}, u32[]{:S(2)}) collective-permute-start(bf16[256,512]{1,0:T(8,128)(2,1)S(1)} %get-tuple-element.30), channel_id=1, source_target_pairs={{0,2},{2,4},{4,6},{6,0},{1,3},{3,5},{5,7},{7,1},{8,10},{10,12},{12... | collective-permute-start | bytes 786440 | tf_op jit(solution)/shard_map/ppermute | solution.py:60
  71.4 15.3 %collective-permute-start.2 = (bf16[256,512]{1,0:T(8,128)(2,1)S(1)}, bf16[256,512]{1,0:T(8,128)(2,1)S(1)}, u32[]{:S(2)}, u32[]{:S(2)}) collective-permute-start(bf16[256,512]{1,0:T(8,128)(2,1)S(1)} %get-tuple-element.30), channel_id=1, source_target_pairs={{0,6},{2,0},{4,2},{6,4},{1,7},{3,1},{5,3},{7,5},{8,14},{10,8},{12,... | collective-permute-start | bytes 786440 | tf_op jit(solution)/shard_map/ppermute | solution.py:60
  75.9 16.1 %collective-permute-start.3 = (bf16[256,512]{1,0:T(8,128)(2,1)S(1)}, bf16[256,512]{1,0:T(8,128)(2,1)S(1)}, u32[]{:S(2)}, u32[]{:S(2)}) collective-permute-start(bf16[256,512]{1,0:T(8,128)(2,1)S(1)} %get-tuple-element.30), channel_id=1, source_target_pairs={{0,4},{2,6},{4,0},{6,2},{1,5},{3,7},{5,1},{7,3},{8,12},{10,14},{12... | collective-permute-start | bytes 786440 | tf_op jit(solution)/shard_map/ppermute | solution.py:60
  82.5 9.6 %copy-start.18 = (bf16[256,512]{1,0:T(8,128)(2,1)S(1)}, bf16[256,512]{1,0:T(8,128)(2,1)}, u32[]{:S(2)}) copy-start(bf16[256,512]{1,0:T(8,128)(2,1)} %copy-done.17) | copy-start | bytes 786436
  92.5 4.1 %copy-start.7 = (bf16[256,512]{1,0:T(8,128)(2,1)}, bf16[256,512]{1,0:T(8,128)(2,1)S(1)}, u32[]{:S(2)}) copy-start(bf16[256,512]{1,0:T(8,128)(2,1)S(1)} %get-tuple-element.25) | copy-start | bytes 786436
  92.5 1.6 collective-permute-start.19
  94.1 0.7 copy-start.11
  96.6 23.9 %all-to-all-start.5 = ((bf16[16,16,1024]{2,1,0:T(8,128)(2,1)}), bf16[16,16,1024]{2,1,0:T(8,128)(2,1)}, u32[]{:S(2)}, u32[]{:S(2)}) async-start(bf16[16,16,1024]{2,1,0:T(8,128)(2,1)} %bitcast.111), calls=%async_computation.5 | async-start | bytes 1048576 | tf_op jit(solution)/shard_map/all_to_all | solution.py:66
  104.7 1.5 collective-permute-start.8
  106.3 0.7 copy-start.13
  107.5 34.4 %copy-start.20 = (bf16[32,1024]{1,0:T(8,128)(2,1)S(1)}, bf16[32,1024]{1,0:T(8,128)(2,1)}, u32[]{:S(2)}) copy-start(bf16[32,1024]{1,0:T(8,128)(2,1)} %param.5) | copy-start | bytes 196612
  120.5 20.3 %all-to-all-start.1 = ((bf16[16,16,1024]{2,1,0:T(8,128)(2,1)}), bf16[16,16,1024]{2,1,0:T(8,128)(2,1)}, u32[]{:S(2)}, u32[]{:S(2)}) async-start(bf16[16,16,1024]{2,1,0:T(8,128)(2,1)} %bitcast.112), calls=%async_computation.1 | async-start | bytes 1048576 | tf_op jit(solution)/shard_map/all_to_all | solution.py:66
  142.6 0.6 copy-start.21
  143.2 4.7 %collective-permute-start.20 = (bf16[16,1024]{1,0:T(8,128)(2,1)S(1)}, bf16[16,1024]{1,0:T(8,128)(2,1)S(1)}, u32[]{:S(2)}, u32[]{:S(2)}) collective-permute-start(bf16[16,1024]{1,0:T(8,128)(2,1)S(1)} %get-tuple-element.27), channel_id=1, source_target_pairs={{128,0},{129,1},{130,2},{131,3},{132,4},{133,5},{134,6},{135,7},{1... | collective-permute-start | bytes 98312 | tf_op jit(solution)/shard_map/ppermute | solution.py:118
  148.7 19.3 %all-to-all-start.6 = ((bf16[16,16,1024]{2,1,0:T(8,128)(2,1)}), bf16[16,16,1024]{2,1,0:T(8,128)(2,1)}, u32[]{:S(2)}, u32[]{:S(2)}) async-start(bf16[16,16,1024]{2,1,0:T(8,128)(2,1)} %broadcast_in_dim.17), calls=%async_computation.6 | async-start | bytes 1048576 | tf_op jit(solution)/shard_map/all_to_all | solution.py:74
  153.8 7.8 %collective-permute-start.9 = (bf16[16,1024]{1,0:T(8,128)(2,1)}, bf16[16,1024]{1,0:T(8,128)(2,1)S(1)}, u32[]{:S(2)}, u32[]{:S(2)}) collective-permute-start(bf16[16,1024]{1,0:T(8,128)(2,1)} %get-tuple-element.26), channel_id=1, source_target_pairs={{128,0},{129,1},{130,2},{131,3},{132,4},{133,5},{134,6},{135,7},{1... | collective-permute-start | bytes 98312 | tf_op jit(solution)/shard_map/ppermute | solution.py:118
  168.9 19.2 %all-to-all-start.2 = ((bf16[16,16,1024]{2,1,0:T(8,128)(2,1)}), bf16[16,16,1024]{2,1,0:T(8,128)(2,1)}, u32[]{:S(2)}, u32[]{:S(2)}) async-start(bf16[16,16,1024]{2,1,0:T(8,128)(2,1)} %broadcast_in_dim.15), calls=%async_computation.2 | async-start | bytes 1048576 | tf_op jit(solution)/shard_map/all_to_all | solution.py:74
  176.3 13.9 %collective-permute-start.21 = (bf16[256,512]{1,0:T(8,128)(2,1)}, bf16[256,512]{1,0:T(8,128)(2,1)}, u32[]{:S(2)}, u32[]{:S(2)}) collective-permute-start(bf16[256,512]{1,0:T(8,128)(2,1)} %convolution_convert_fusion.1), channel_id=1, source_target_pairs={{0,1},{1,0},{2,3},{3,2},{4,5},{5,4},{6,7},{7,6},{8,9},{9,8},{10,11... | collective-permute-start | bytes 786440 | tf_op jit(solution)/shard_map/ppermute | solution.py:35
  176.3 22.2 %collective-permute-start.26 = (bf16[512,512]{1,0:T(8,128)(2,1)}, bf16[512,512]{1,0:T(8,128)(2,1)}, u32[]{:S(2)}, u32[]{:S(2)}) collective-permute-start(bf16[512,512]{1,0:T(8,128)(2,1)} %get-tuple-element.16), channel_id=1, source_target_pairs={{0,1},{1,0},{2,3},{3,2},{4,5},{5,4},{6,7},{7,6},{8,9},{9,8},{10,11... | collective-permute-start | bytes 1572872 | tf_op jit(solution)/shard_map/ppermute | solution.py:35
  188.0 7.5 %copy-start.2 = (bf16[1,1024,1024]{2,1,0:T(8,128)(2,1)S(1)}, bf16[1,1024,1024]{2,1,0:T(8,128)(2,1)}, u32[]{:S(2)}) copy-start(bf16[1,1024,1024]{2,1,0:T(8,128)(2,1)} %param.7) | copy-start | bytes 6291460
  190.0 18.0 %copy-start.9 = (bf16[512,512]{1,0:T(8,128)(2,1)S(1)}, bf16[512,512]{1,0:T(8,128)(2,1)}, u32[]{:S(2)}) copy-start(bf16[512,512]{1,0:T(8,128)(2,1)} %get-tuple-element.16) | copy-start | bytes 1572868
  190.0 5.5 %collective-permute-start.10 = (bf16[256,512]{1,0:T(8,128)(2,1)S(1)}, bf16[256,512]{1,0:T(8,128)(2,1)S(1)}, u32[]{:S(2)}, u32[]{:S(2)}) collective-permute-start(bf16[256,512]{1,0:T(8,128)(2,1)S(1)} %convolution_convert_fusion.3), channel_id=1, source_target_pairs={{0,1},{1,0},{2,3},{3,2},{4,5},{5,4},{6,7},{7,6},{8,9},{9,8},{10,11... | collective-permute-start | bytes 786440 | tf_op jit(solution)/shard_map/ppermute | solution.py:35
  192.1 26.9 %copy-start.8 = (bf16[256,512]{1,0:T(8,128)(2,1)S(1)}, bf16[256,512]{1,0:T(8,128)(2,1)}, u32[]{:S(2)}) copy-start(bf16[256,512]{1,0:T(8,128)(2,1)} %copy-done.7) | copy-start | bytes 786436
  192.1 15.9 %collective-permute-start.22 = (bf16[256,512]{1,0:T(8,128)(2,1)S(1)}, bf16[256,512]{1,0:T(8,128)(2,1)S(1)}, u32[]{:S(2)}, u32[]{:S(2)}) collective-permute-start(bf16[256,512]{1,0:T(8,128)(2,1)S(1)} %get-tuple-element.38), channel_id=1, source_target_pairs={{0,2},{2,4},{4,6},{6,0},{1,3},{3,5},{5,7},{7,1},{8,10},{10,12},{12... | collective-permute-start | bytes 786440 | tf_op jit(solution)/shard_map/ppermute | solution.py:60
  193.3 16.8 %collective-permute-start.23 = (bf16[256,512]{1,0:T(8,128)(2,1)S(1)}, bf16[256,512]{1,0:T(8,128)(2,1)S(1)}, u32[]{:S(2)}, u32[]{:S(2)}) collective-permute-start(bf16[256,512]{1,0:T(8,128)(2,1)S(1)} %get-tuple-element.38), channel_id=1, source_target_pairs={{0,6},{2,0},{4,2},{6,4},{1,7},{3,1},{5,3},{7,5},{8,14},{10,8},{12,... | collective-permute-start | bytes 786440 | tf_op jit(solution)/shard_map/ppermute | solution.py:60
  195.4 14.7 %collective-permute-start.24 = (bf16[256,512]{1,0:T(8,128)(2,1)S(1)}, bf16[256,512]{1,0:T(8,128)(2,1)S(1)}, u32[]{:S(2)}, u32[]{:S(2)}) collective-permute-start(bf16[256,512]{1,0:T(8,128)(2,1)S(1)} %get-tuple-element.38), channel_id=1, source_target_pairs={{0,4},{2,6},{4,0},{6,2},{1,5},{3,7},{5,1},{7,3},{8,12},{10,14},{12... | collective-permute-start | bytes 786440 | tf_op jit(solution)/shard_map/ppermute | solution.py:60
  197.0 16.6 %collective-permute-start.11 = (bf16[256,512]{1,0:T(8,128)(2,1)S(1)}, bf16[256,512]{1,0:T(8,128)(2,1)S(1)}, u32[]{:S(2)}, u32[]{:S(2)}) collective-permute-start(bf16[256,512]{1,0:T(8,128)(2,1)S(1)} %get-tuple-element.36), channel_id=1, source_target_pairs={{0,2},{2,4},{4,6},{6,0},{1,3},{3,5},{5,7},{7,1},{8,10},{10,12},{12... | collective-permute-start | bytes 786440 | tf_op jit(solution)/shard_map/ppermute | solution.py:60
  198.5 19.7 %collective-permute-start.12 = (bf16[256,512]{1,0:T(8,128)(2,1)S(1)}, bf16[256,512]{1,0:T(8,128)(2,1)S(1)}, u32[]{:S(2)}, u32[]{:S(2)}) collective-permute-start(bf16[256,512]{1,0:T(8,128)(2,1)S(1)} %get-tuple-element.36), channel_id=1, source_target_pairs={{0,6},{2,0},{4,2},{6,4},{1,7},{3,1},{5,3},{7,5},{8,14},{10,8},{12,... | collective-permute-start | bytes 786440 | tf_op jit(solution)/shard_map/ppermute | solution.py:60
  208.0 11.0 %collective-permute-start.13 = (bf16[256,512]{1,0:T(8,128)(2,1)S(1)}, bf16[256,512]{1,0:T(8,128)(2,1)S(1)}, u32[]{:S(2)}, u32[]{:S(2)}) collective-permute-start(bf16[256,512]{1,0:T(8,128)(2,1)S(1)} %get-tuple-element.36), channel_id=1, source_target_pairs={{0,4},{2,6},{4,0},{6,2},{1,5},{3,7},{5,1},{7,3},{8,12},{10,14},{12... | collective-permute-start | bytes 786440 | tf_op jit(solution)/shard_map/ppermute | solution.py:60
  219.0 1.3 copy-start.4
  220.3 1.9 collective-permute-start.14
  222.7 6.2 %copy-start.6 = (bf16[16,16,1024]{2,1,0:T(8,128)(2,1)S(1)}, bf16[16,16,1024]{2,1,0:T(8,128)(2,1)}, u32[]{:S(2)}) copy-start(bf16[16,16,1024]{2,1,0:T(8,128)(2,1)} %copy-done.5) | copy-start | bytes 1572868
  224.0 20.9 %all-to-all-start.3 = ((bf16[16,16,1024]{2,1,0:T(8,128)(2,1)}), bf16[16,16,1024]{2,1,0:T(8,128)(2,1)S(1)}, u32[]{:S(2)}, u32[]{:S(2)}) async-start(bf16[16,16,1024]{2,1,0:T(8,128)(2,1)} %bitcast.110), calls=%async_computation.3 | async-start | bytes 1048576 | tf_op jit(solution)/shard_map/all_to_all | solution.py:66
  230.0 4.9 %collective-permute-start.25 = (bf16[256,512]{1,0:T(8,128)(2,1)}, bf16[256,512]{1,0:T(8,128)(2,1)S(1)}, u32[]{:S(2)}, u32[]{:S(2)}) collective-permute-start(bf16[256,512]{1,0:T(8,128)(2,1)} %get-tuple-element.23), channel_id=1, source_target_pairs={{0,1},{1,0},{2,3},{3,2},{4,5},{5,4},{6,7},{7,6},{8,9},{9,8},{10,11... | collective-permute-start | bytes 786440 | tf_op jit(solution)/shard_map/ppermute | solution.py:35
  230.1 4.0 %copy-start.14 = (bf16[256,512]{1,0:T(8,128)(2,1)S(1)}, bf16[256,512]{1,0:T(8,128)(2,1)}, u32[]{:S(2)}) copy-start(bf16[256,512]{1,0:T(8,128)(2,1)} %copy-done.13) | copy-start | bytes 786436
  234.1 1.2 copy-start.19
  234.8 1.8 copy-start.15
  235.3 14.4 %copy-start.12 = (bf16[256,512]{1,0:T(8,128)(2,1)S(1)}, bf16[256,512]{1,0:T(8,128)(2,1)}, u32[]{:S(2)}) copy-start(bf16[256,512]{1,0:T(8,128)(2,1)} %copy-done.11) | copy-start | bytes 786436
  244.9 20.4 %all-to-all-start.7 = ((bf16[16,16,1024]{2,1,0:T(8,128)(2,1)}), bf16[16,16,1024]{2,1,0:T(8,128)(2,1)S(1)}, u32[]{:S(2)}, u32[]{:S(2)}) async-start(bf16[16,16,1024]{2,1,0:T(8,128)(2,1)} %bitcast.109), calls=%async_computation.7 | async-start | bytes 1048576 | tf_op jit(solution)/shard_map/all_to_all | solution.py:66
  249.8 1.5 copy-start.10
  253.9 4.0 %copy-start.23 = (bf16[16,1024]{1,0:T(8,128)(2,1)S(1)}, bf16[16,1024]{1,0:T(8,128)(2,1)}, u32[]{:S(2)}) copy-start(bf16[16,1024]{1,0:T(8,128)(2,1)} %get-tuple-element.26) | copy-start | bytes 98308
  253.9 11.5 %copy-start.22 = (bf16[16,1024]{1,0:T(8,128)(2,1)S(1)}, bf16[16,1024]{1,0:T(8,128)(2,1)}, u32[]{:S(2)}) copy-start(bf16[16,1024]{1,0:T(8,128)(2,1)} %copy-done.21) | copy-start | bytes 98308

commit v3 on v2

--- a/solution.py
+++ b/solution.py
@@ -8,9 +8,9 @@
 
 X, CORES, YLO, Z = 4, 2, 2, 8
 WIDE = YLO * Z
-CHUNKS = 2
 AXES = ("section", "ylo", "z", "x", "core")
 WIDE_AXES = ("ylo", "z")
+CROSS_AXES = ("section", "ylo")
 
 
 def gelu_parts(pre_act):
@@ -31,8 +31,20 @@
     )
 
 
+def after(value, *others):
+    return lax.optimization_barrier((value, others))[0]
+
+
 def other_core(block):
     return lax.ppermute(block, "core", [(0, 1), (1, 0)])
+
+
+def to_upper(block):
+    return lax.ppermute(block, CROSS_AXES, [(0, 3), (1, 2)])
+
+
+def to_lower(block):
+    return lax.ppermute(block, CROSS_AXES, [(3, 0), (2, 1)])
 
 
 def halves(weight, dim):
@@ -76,58 +88,80 @@
     ).reshape(WIDE * rows, cols)
 
 
-def chain(own_rows, slopes, up_halves, down_halves):
-    whole = gather_wide(own_rows)
+def slope_of(whole, down_halves, slopes):
     theirs = contract(whole, down_halves[1], 1, 1)
     mine = contract(whole, down_halves[0], 1, 1)
     slope_mine = (narrow_total(mine, theirs) * slopes).astype(jnp.bfloat16)
-    slope_theirs = other_core(slope_mine)
-    summed = spread_wide(
-        (
-            contract(slope_mine, up_halves[0], 1, 1) + contract(slope_theirs, up_halves[1], 1, 1)
-        ).astype(jnp.bfloat16)
-    )
-    grad_in = (own_rows.astype(jnp.float32) + summed).astype(jnp.bfloat16)
-    return whole, slope_mine, slope_theirs, grad_in
+    return slope_mine, other_core(slope_mine)
 
 
-def chunk_rows(block):
-    rows, cols = block.shape
-    split = block.reshape(WIDE, CHUNKS, rows // (WIDE * CHUNKS), cols)
-    return split.transpose(1, 0, 2, 3).reshape(rows, cols)
-
-
-def cut(block):
-    step = block.shape[0] // CHUNKS
-    return [block[c * step : (c + 1) * step] for c in range(CHUNKS)]
+def back_through_up(slope, up_halves):
+    return (contract(slope[0], up_halves[0], 1, 1) + contract(slope[1], up_halves[1], 1, 1)).astype(
+        jnp.bfloat16
+    )
 
 
 def body(saved_inputs, upstream, up_weight, down_weight):
-    saved = chunk_rows(saved_inputs[0])
-    up_halves = halves(up_weight[0], 1)
-    down_halves = halves(down_weight[0], 0)
-
-    theirs = contract(saved, up_halves[1], 1, 0)
-    mine = contract(saved, up_halves[0], 1, 0)
-    act, slopes = gelu_parts(narrow_total(mine, theirs))
-    hidden_mine = act.astype(jnp.bfloat16)
-    hidden = in_order(hidden_mine, other_core(hidden_mine))
-
-    upper_own = cut(upstream)
-    upper = [chain(own, s, up_halves, down_halves) for own, s in zip(upper_own, cut(slopes))]
-    lower_own = [lax.ppermute(out[3], "section", [(1, 0)]) for out in upper]
-    lower = [chain(own, s, up_halves, down_halves) for own, s in zip(lower_own, cut(slopes))]
-
     is_upper = lax.axis_index("section") == 1
 
-    def picked(index):
-        return jnp.concatenate(
-            [jnp.where(is_upper, u[index], l[index]) for u, l in zip(upper, lower)], axis=0
-        )
+    def pick(upper, lower):
+        return jnp.where(is_upper, upper, lower)
 
-    grad_down = contract(hidden, picked(0), 0, 0).astype(jnp.bfloat16)
-    grad_up = contract(saved, in_order(picked(1), picked(2)), 0, 0).astype(jnp.bfloat16)
-    return picked(3)[None], grad_up[None], grad_down[None]
+    tokens = saved_inputs.shape[1]
+    part = upstream.shape[0] // 2
+    by_part = saved_inputs[0].reshape(WIDE, 2, part, -1)
+    saved = [by_part[:, c].reshape(tokens // 2, -1) for c in range(2)]
+    w_up, w_down = up_weight[0], down_weight[0]
+    up_halves, down_halves = halves(w_up, 1), halves(w_down, 0)
+
+    early, late = upstream[:part], upstream[part:]
+    gathered = gather_wide(pick(early, late))
+    sent_down = to_upper(w_down)
+    top = [gathered, to_upper(gathered)]
+
+    hidden, slopes = [], []
+    for rows in saved:
+        theirs = contract(rows, up_halves[1], 1, 0)
+        mine = contract(rows, up_halves[0], 1, 0)
+        act, slope = gelu_parts(narrow_total(mine, theirs))
+        act = act.astype(jnp.bfloat16)
+        hidden.append((act, other_core(act)))
+        slopes.append(slope)
+    lower_slopes = pick(to_upper(slopes[1].astype(jnp.bfloat16)).astype(jnp.float32), slopes[0])
+
+    top_slopes = [slope_of(top[0], down_halves, slopes[0])]
+    moved = to_lower(back_through_up(top_slopes[0], up_halves))
+    sent_up = to_upper(after(w_up, sent_down))
+    top_slopes.append(slope_of(top[1], down_halves, slopes[1]))
+    summed = spread_wide(pick(back_through_up(top_slopes[1], up_halves), moved))
+    middle = (pick(late, early).astype(jnp.float32) + summed).astype(jnp.bfloat16)
+
+    low = gather_wide(middle)
+    low_down = halves(pick(sent_down, w_down), 0)
+    low_up = halves(pick(sent_up, w_up), 1)
+    low_slope = slope_of(low, low_down, lower_slopes)
+    low_summed = spread_wide(back_through_up(low_slope, low_up))
+    bottom = (middle.astype(jnp.float32) + low_summed).astype(jnp.bfloat16)
+
+    swap = [(0, 1), (1, 0)]
+    upper_first = lax.ppermute(middle, "section", swap)
+    lower_last = lax.ppermute(bottom, "section", swap)
+    low_rest = to_lower(low)
+    low_slope_rest = [to_lower(block) for block in low_slope]
+
+    grad_in = jnp.concatenate([pick(upper_first, bottom), pick(middle, lower_last)], axis=0)
+    incoming = jnp.concatenate([pick(top[0], low), pick(top[1], low_rest)], axis=0)
+    slope_grad = jnp.concatenate(
+        [
+            in_order(*[pick(u, l) for u, l in zip(top_slopes[0], low_slope)]),
+            in_order(*[pick(u, l) for u, l in zip(top_slopes[1], low_slope_rest)]),
+        ],
+        axis=0,
+    )
+    hidden = jnp.concatenate([in_order(*block) for block in hidden], axis=0)
+    grad_down = contract(hidden, incoming, 0, 0).astype(jnp.bfloat16)
+    grad_up = contract(jnp.concatenate(saved, axis=0), slope_grad, 0, 0).astype(jnp.bfloat16)
+    return grad_in[None], grad_up[None], grad_down[None]
 
 
 def solution(mesh):

time: 270 us -> 216 us (0.80)
  waiting for transfers between devices: 107 us -> 84.8 us
  starting transfers between devices: 94.6 us -> 75.9 us
  local copies, waits for them, and re-layouts: 12.8 us -> 4.58 us
  matrix products: 34.4 us -> 27.6 us
    ppermute x2 -> x10, waiting for transfers between devices: 3.64 us -> 38.8 us  [the longest x4 29.3 us: to_upper(): return lax.ppermute(block, CROSS_AXES, [(0, 3), (1, 2)])]
    all_to_all x4 -> x2, waiting for transfers between devices: 41.6 us -> 14.3 us  [spread_wide(): lax.all_to_all(partial.reshape(WIDE, rows // WIDE, cols), WIDE_AXES, 0, 0...]
    all_to_all x4 -> x2, waiting for transfers between devices: 31.3 us -> 11.2 us  [gather_wide(): lax.all_to_all(jnp.broadcast_to(block[None], (WIDE, rows, cols)), WIDE_AX...]
    ppermute x15, starting transfers between devices: 37 us -> 26.1 us  [narrow_total(): total = total + lax.ppermute(sent, 'x', route).astype(jnp.float32)]
    ppermute x2 -> x10, starting transfers between devices: 8.85 us -> 19.3 us  [the longest x4 7.6 us: to_lower(): return lax.ppermute(block, CROSS_AXES, [(3, 0), (2, 1)])]
    all_to_all x4 -> x2, starting transfers between devices: 24.5 us -> 14.4 us  [gather_wide(): lax.all_to_all(jnp.broadcast_to(block[None], (WIDE, rows, cols)), WIDE_AX...]
    ppermute x15, waiting for transfers between devices: 27.6 us -> 17.9 us  [narrow_total(): total = total + lax.ppermute(sent, 'x', route).astype(jnp.float32)]
    all_to_all x4 -> x2, starting transfers between devices: 22.8 us -> 14 us  [spread_wide(): lax.all_to_all(partial.reshape(WIDE, rows // WIDE, cols), WIDE_AXES, 0, 0...]
  transfers between devices with their start and end apart: 35 -> 39, of which waited for: 20 -> 16; matrix products, arithmetic and copies ran while one was open for 18% -> 22% of each run, Pallas kernels for 0% -> 0%
where the time goes in v3:
time: 216 us; the launch traced here: 212 us
  waiting for transfers between devices  84.8 us (39%)
  starting transfers between devices  75.9 us (35%)
  matrix products  27.6 us (13%)
  other arithmetic  17.7 us (8%)
  local copies, waits for them, and re-layouts  4.58 us (2%)
    ppermute x4, waiting for transfers between devices, to_upper(): return lax.ppermute(block, CROSS_AXES, [(0, 3), (1, 2)])  29.3 us
    dot_general x18, matrix products, contract(): lax.dot_general(first_op, second_op, (((first_dim,), (second_dim,)), ((),...  27.6 us
    ppermute x15, starting transfers between devices, narrow_total(): total = total + lax.ppermute(sent, 'x', route).astype(jnp.float32)  26.1 us
    ppermute x15, waiting for transfers between devices, narrow_total(): total = total + lax.ppermute(sent, 'x', route).astype(jnp.float32)  17.9 us
    all_to_all x2, starting transfers between devices, gather_wide(): lax.all_to_all(jnp.broadcast_to(block[None], (WIDE, rows, cols)), WIDE_AX...  14.4 us
    all_to_all x2, waiting for transfers between devices, spread_wide(): lax.all_to_all(partial.reshape(WIDE, rows // WIDE, cols), WIDE_AXES, 0, 0...  14.3 us
    all_to_all x2, starting transfers between devices, spread_wide(): lax.all_to_all(partial.reshape(WIDE, rows // WIDE, cols), WIDE_AXES, 0, 0...  14 us
    all_to_all x2, waiting for transfers between devices, gather_wide(): lax.all_to_all(jnp.broadcast_to(block[None], (WIDE, rows, cols)), WIDE_AX...  11.2 us
  transfers between devices with their start and end apart: 39, of which 16 were waited for; matrix products, arithmetic and copies ran while one was open for 22% of the time, Pallas kernels for 0%

profile of v3, /device:TPU:56, one launch (start us, length us, event | category | flops | bytes accessed | tf_op | source)
XLA Modules:
  0.0 211.7 jit_solution(9279938307750017095)
XLA Ops:
  0.6 0.9 broadcast_select_fusion.18
  1.6 0.9 broadcast_in_dim.10
  2.4 9.5 %all-to-all-start = ((bf16[16,16,1024]{2,1,0:T(8,128)(2,1)}), bf16[16,16,1024]{2,1,0:T(8,128)(2,1)S(1)}, u32[]{:S(2)}, u32[]{:S(2)}) async-start(bf16[16,16,1024]{2,1,0:T(8,128)(2,1)} %broadcast_in_dim.10), calls=%async_computation | async-start | bytes 1048576 | tf_op jit(solution)/shard_map/all_to_all | solution.py:86
  11.9 2.1 fusion.90
  14.0 2.4 %fusion.5 = bf16[256,512]{1,0:T(8,128)(2,1)} fusion(bf16[256,1024]{1,0:T(8,128)(2,1)} %bitcast.89, bf16[1,1024,1024]{2,1,0:T(8,128)(2,1)S(1)} %copy-done, s32[]{:T(128)S(6)} %select_n.125), kind=kOutput, calls=%fused_computation.21 | convolution fusion | flops 268566528 | bytes 1835012 | tf_op jit(solution)/shard_map/dot_general | solution.py:26
  16.4 1.2 fusion.4
  18.0 1.3 collective-permute-start.21
  19.3 2.4 %fusion.70 = (bf16[256,512]{1,0:T(8,128)(2,1)}, f32[256,512]{1,0:T(8,128)}) fusion(bf16[256,512]{1,0:T(8,128)(2,1)} %collective-permute-done.14, bf16[256,1024]{1,0:T(8,128)(2,1)} %bitcast.90, bf16[1,1024,1024]{2,1,0:T(8,128)(2,1)S(1)} %copy-done, s32[]{:T(128)S(6)} %select_n.124), kind=kOutput, calls=%fused_computation.104 | convolution fusion | flops 268828672 | bytes 2621444 | tf_op jit(solution)/shard_map/dot_general | solution.py:26
  21.8 3.0 %collective-permute-start.17 = (bf16[256,512]{1,0:T(8,128)(2,1)}, bf16[256,512]{1,0:T(8,128)(2,1)}, u32[]{:S(2)}, u32[]{:S(2)}) collective-permute-start(bf16[256,512]{1,0:T(8,128)(2,1)} %get-tuple-element.25), channel_id=1, source_target_pairs={{0,4},{2,6},{4,0},{6,2},{1,5},{3,7},{5,1},{7,3},{8,12},{10,14},{12... | collective-permute-start | bytes 786440 | tf_op jit(solution)/shard_map/ppermute | solution.py:72
  24.8 1.1 collective-permute-start.16
  25.9 0.9 collective-permute-start.15
  26.8 1.3 fusion.68
  28.8 1.7 convolution_convert_fusion.3
  30.5 2.2 %collective-permute-done.17 = bf16[256,512]{1,0:T(8,128)(2,1)} collective-permute-done((bf16[256,512]{1,0:T(8,128)(2,1)}, bf16[256,512]{1,0:T(8,128)(2,1)}, u32[]{:S(2)}, u32[]{:S(2)}) %collective-permute-start.17) | collective-permute-done | bytes 262176 | tf_op jit(solution)/shard_map/ppermute | solution.py:72
  32.8 2.8 %collective-permute-start.7 = (bf16[256,512]{1,0:T(8,128)(2,1)}, bf16[256,512]{1,0:T(8,128)(2,1)S(1)}, u32[]{:S(2)}, u32[]{:S(2)}) collective-permute-start(bf16[256,512]{1,0:T(8,128)(2,1)} %get-tuple-element.27), channel_id=1, source_target_pairs={{0,6},{2,0},{4,2},{6,4},{1,7},{3,1},{5,3},{7,5},{8,14},{10,8},{12,... | collective-permute-start | bytes 786440 | tf_op jit(solution)/shard_map/ppermute | solution.py:72
  35.6 2.9 %collective-permute-done.16 = bf16[256,512]{1,0:T(8,128)(2,1)} collective-permute-done((bf16[256,512]{1,0:T(8,128)(2,1)}, bf16[256,512]{1,0:T(8,128)(2,1)}, u32[]{:S(2)}, u32[]{:S(2)}) %collective-permute-start.16) | collective-permute-done | bytes 262176 | tf_op jit(solution)/shard_map/ppermute | solution.py:72
  38.5 1.5 collective-permute-start.6
  40.0 2.5 %multiply_convert_fusion.1 = (bf16[256,512]{1,0:T(8,128)(2,1)}, f32[256,512]{1,0:T(8,128)S(1)}) fusion(bf16[256,512]{1,0:T(8,128)(2,1)} %collective-permute-done.17, bf16[256,512]{1,0:T(8,128)(2,1)} %collective-permute-done.16, bf16[256,512]{1,0:T(8,128)(2,1)} %collective-permute-done.15, f32[256,512]{1,0:T(8,128)} %get-tuple-element.26, ...), kind=kLoop, calls=%fused_computation.91 | loop fusion | flops 2228224 | bytes 2359296 | tf_op jit(solution)/shard_map/convert_element_type | solution.py:127
  42.5 1.3 collective-permute-start
  43.7 1.7 fusion.69
  45.5 2.8 %collective-permute-start.13 = (bf16[256,512]{1,0:T(8,128)(2,1)S(1)}, bf16[256,512]{1,0:T(8,128)(2,1)S(1)}, u32[]{:S(2)}, u32[]{:S(2)}) collective-permute-start(bf16[256,512]{1,0:T(8,128)(2,1)S(1)} %get-tuple-element.23), channel_id=1, source_target_pairs={{0,4},{2,6},{4,0},{6,2},{1,5},{3,7},{5,1},{7,3},{8,12},{10,14},{12... | collective-permute-start | bytes 786440 | tf_op jit(solution)/shard_map/ppermute | solution.py:72
  48.8 2.6 %collective-permute-start.12 = (bf16[256,512]{1,0:T(8,128)(2,1)S(1)}, bf16[256,512]{1,0:T(8,128)(2,1)S(1)}, u32[]{:S(2)}, u32[]{:S(2)}) collective-permute-start(bf16[256,512]{1,0:T(8,128)(2,1)S(1)} %get-tuple-element.23), channel_id=1, source_target_pairs={{0,6},{2,0},{4,2},{6,4},{1,7},{3,1},{5,3},{7,5},{8,14},{10,8},{12,... | collective-permute-start | bytes 786440 | tf_op jit(solution)/shard_map/ppermute | solution.py:72
  51.3 1.0 multiply_convert_fusion
  52.4 27.8 %collective-permute-done = bf16[256,1024]{1,0:T(8,128)(2,1)S(1)} collective-permute-done((bf16[256,1024]{1,0:T(8,128)(2,1)S(1)}, bf16[256,1024]{1,0:T(8,128)(2,1)S(1)}, u32[]{:S(2)}, u32[]{:S(2)}) %collective-permute-start) | collective-permute-done | bytes 524320 | tf_op jit(solution)/shard_map/ppermute | solution.py:43
  80.1 1.9 convolution_convert_fusion.4
  83.8 1.7 fusion.91
  85.5 3.1 %collective-permute-start.4 = (bf16[256,512]{1,0:T(8,128)(2,1)S(1)}, bf16[256,512]{1,0:T(8,128)(2,1)S(1)}, u32[]{:S(2)}, u32[]{:S(2)}) collective-permute-start(bf16[256,512]{1,0:T(8,128)(2,1)S(1)} %get-tuple-element.29), channel_id=1, source_target_pairs={{0,4},{2,6},{4,0},{6,2},{1,5},{3,7},{5,1},{7,3},{8,12},{10,14},{12... | collective-permute-start | bytes 786440 | tf_op jit(solution)/shard_map/ppermute | solution.py:72
  88.7 1.1 collective-permute-start.3
  89.8 0.9 collective-permute-start.2
  91.7 1.5 collective-permute-start.19
  93.2 3.1 %collective-permute-done.4 = bf16[256,512]{1,0:T(8,128)(2,1)S(1)} collective-permute-done((bf16[256,512]{1,0:T(8,128)(2,1)S(1)}, bf16[256,512]{1,0:T(8,128)(2,1)S(1)}, u32[]{:S(2)}, u32[]{:S(2)}) %collective-permute-start.4) | collective-permute-done | bytes 262176 | tf_op jit(solution)/shard_map/ppermute | solution.py:72
  96.3 4.9 %collective-permute-done.3 = bf16[256,512]{1,0:T(8,128)(2,1)S(1)} collective-permute-done((bf16[256,512]{1,0:T(8,128)(2,1)S(1)}, bf16[256,512]{1,0:T(8,128)(2,1)S(1)}, u32[]{:S(2)}, u32[]{:S(2)}) %collective-permute-start.3) | collective-permute-done | bytes 262176 | tf_op jit(solution)/shard_map/ppermute | solution.py:72
  101.2 1.2 fusion.89
  102.4 1.5 collective-permute-done.9
  105.1 1.3 fusion.3
  106.5 8.1 %all-to-all-start.1 = ((bf16[16,16,1024]{2,1,0:T(8,128)(2,1)}), bf16[16,16,1024]{2,1,0:T(8,128)(2,1)S(1)}, u32[]{:S(2)}, u32[]{:S(2)}) async-start(bf16[16,16,1024]{2,1,0:T(8,128)(2,1)} %bitcast.12), calls=%async_computation.1 | async-start | bytes 1048576 | tf_op jit(solution)/shard_map/all_to_all | solution.py:78
  114.6 1.3 collective-permute-start.27
  115.9 14.3 %all-to-all-done.1 = bf16[16,16,1024]{2,1,0:T(8,128)(2,1)S(1)} async-done(((bf16[16,16,1024]{2,1,0:T(8,128)(2,1)}), bf16[16,16,1024]{2,1,0:T(8,128)(2,1)S(1)}, u32[]{:S(2)}, u32[]{:S(2)}) %all-to-all-start.1) | async-done | bytes 524320 | tf_op jit(solution)/shard_map/all_to_all | solution.py:78
  130.3 0.9 broadcast_in_dim.22
  131.2 4.9 %all-to-all-start.2 = ((bf16[16,16,1024]{2,1,0:T(8,128)(2,1)}), bf16[16,16,1024]{2,1,0:T(8,128)(2,1)S(1)}, u32[]{:S(2)}, u32[]{:S(2)}) async-start(bf16[16,16,1024]{2,1,0:T(8,128)(2,1)} %broadcast_in_dim.22), calls=%async_computation.2 | async-start | bytes 1048576 | tf_op jit(solution)/shard_map/all_to_all | solution.py:86
  136.6 3.8 %broadcast_select_fusion.1 = bf16[1024,1024]{1,0:T(8,128)(2,1)} fusion(bf16[1024,1024]{1,0:T(8,128)(2,1)} %collective-permute-done.21, pred[]{:T(512)S(6)} %eq.4, bf16[1,1024,1024]{2,1,0:T(8,128)(2,1)} %param.7), kind=kLoop, calls=%fused_computation.3 | loop fusion | flops 1048576 | bytes 6291457 | tf_op jit(solution)/shard_map/jit(_where)/select_n | solution.py:108
  140.4 11.2 %all-to-all-done.2 = bf16[16,16,1024]{2,1,0:T(8,128)(2,1)S(1)} async-done(((bf16[16,16,1024]{2,1,0:T(8,128)(2,1)}), bf16[16,16,1024]{2,1,0:T(8,128)(2,1)S(1)}, u32[]{:S(2)}, u32[]{:S(2)}) %all-to-all-start.2) | async-done | bytes 524320 | tf_op jit(solution)/shard_map/all_to_all | solution.py:86
  151.6 1.9 convolution_convert_fusion.2
  153.5 1.9 broadcast_select_fusion.7
  155.4 1.8 broadcast_select_fusion.5
  157.2 1.3 collective-permute-start.26
  158.5 3.1 %collective-permute-start.20 = (bf16[16,1024]{1,0:T(8,128)(2,1)S(1)}, bf16[16,1024]{1,0:T(8,128)(2,1)S(1)}, u32[]{:S(2)}, u32[]{:S(2)}) collective-permute-start(bf16[16,1024]{1,0:T(8,128)(2,1)S(1)} %add_convert_fusion.1), channel_id=1, source_target_pairs={{0,128},{128,0},{1,129},{129,1},{2,130},{130,2},{3,131},{131,3},{4... | collective-permute-start | bytes 98312 | tf_op jit(solution)/shard_map/ppermute | solution.py:147
  162.1 3.0 %collective-permute-start.25 = (bf16[256,512]{1,0:T(8,128)(2,1)S(1)}, bf16[256,512]{1,0:T(8,128)(2,1)S(1)}, u32[]{:S(2)}, u32[]{:S(2)}) collective-permute-start(bf16[256,512]{1,0:T(8,128)(2,1)S(1)} %get-tuple-element.31), channel_id=1, source_target_pairs={{0,4},{2,6},{4,0},{6,2},{1,5},{3,7},{5,1},{7,3},{8,12},{10,14},{12... | collective-permute-start | bytes 786440 | tf_op jit(solution)/shard_map/ppermute | solution.py:72
  165.1 1.2 collective-permute-start.24
  167.1 1.4 collective-permute-start.23
  168.5 1.8 broadcast_select_fusion
  170.3 0.8 collective-permute-done.26
  171.1 2.3 %collective-permute-start.34 = (bf16[256,1024]{1,0:T(8,128)(2,1)S(1)}, bf16[256,1024]{1,0:T(8,128)(2,1)}, u32[]{:S(2)}, u32[]{:S(2)}) collective-permute-start(bf16[256,1024]{1,0:T(8,128)(2,1)S(1)} %bitcast.85), channel_id=1, source_target_pairs={{192,0},{128,64},{193,1},{129,65},{194,2},{130,66},{195,3},{131,67... | collective-permute-start | bytes 1572872 | tf_op jit(solution)/shard_map/ppermute | solution.py:47
  173.4 4.2 %collective-permute-done.24 = bf16[256,512]{1,0:T(8,128)(2,1)S(1)} collective-permute-done((bf16[256,512]{1,0:T(8,128)(2,1)S(1)}, bf16[256,512]{1,0:T(8,128)(2,1)S(1)}, u32[]{:S(2)}, u32[]{:S(2)}) %collective-permute-start.24) | collective-permute-done | bytes 262176 | tf_op jit(solution)/shard_map/ppermute | solution.py:72
  178.1 0.9 broadcast_select_fusion.3
  180.1 1.3 fusion.2
  181.4 5.8 %all-to-all-start.3 = ((bf16[16,16,1024]{2,1,0:T(8,128)(2,1)}), bf16[16,16,1024]{2,1,0:T(8,128)(2,1)S(1)}, u32[]{:S(2)}, u32[]{:S(2)}) async-start(bf16[16,16,1024]{2,1,0:T(8,128)(2,1)} %bitcast.92), calls=%async_computation.3 | async-start | bytes 1048576 | tf_op jit(solution)/shard_map/all_to_all | solution.py:78
  187.4 3.9 %convert_bitcast_fusion = bf16[1,1024,1024]{2,1,0:T(8,128)(2,1)} fusion(bf16[256,512]{1,0:T(8,128)(2,1)} %get-tuple-element.20, bf16[256,512]{1,0:T(8,128)(2,1)} %get-tuple-element.19, bf16[256,512]{1,0:T(8,128)(2,1)} %get-tuple-element.18, bf16[256,512]{1,0:T(8,128)(2,1)} %get-tuple-element.17, bf16[256,1024]{1,0:T(8,128)(2,1)S(1)} %broadcast_select_fusion.2, ...), kind=kOutput, calls=%fused_computation | convolution fusion | flops 1081081856 | bytes 4194304 | tf_op jit(solution)/shard_map/dot_general | solution.py:26
  191.3 2.6 %collective-permute-start.30 = (bf16[256,512]{1,0:T(8,128)(2,1)S(1)}, bf16[256,512]{1,0:T(8,128)(2,1)S(1)}, u32[]{:S(2)}, u32[]{:S(2)}) collective-permute-start(bf16[256,512]{1,0:T(8,128)(2,1)S(1)} %multiply_convert_fusion.2), channel_id=1, source_target_pairs={{192,0},{128,64},{193,1},{129,65},{194,2},{130,66},{195,3},{131,67... | collective-permute-start | bytes 786440 | tf_op jit(solution)/shard_map/ppermute | solution.py:47
  193.8 1.3 collective-permute-start.31
  195.2 5.3 %collective-permute-done.30 = bf16[256,512]{1,0:T(8,128)(2,1)S(1)} collective-permute-done((bf16[256,512]{1,0:T(8,128)(2,1)S(1)}, bf16[256,512]{1,0:T(8,128)(2,1)S(1)}, u32[]{:S(2)}, u32[]{:S(2)}) %collective-permute-start.30) | collective-permute-done | bytes 262176 | tf_op jit(solution)/shard_map/ppermute | solution.py:47
  200.5 4.2 %collective-permute-done.31 = bf16[256,512]{1,0:T(8,128)(2,1)S(1)} collective-permute-done((bf16[256,512]{1,0:T(8,128)(2,1)S(1)}, bf16[256,512]{1,0:T(8,128)(2,1)S(1)}, u32[]{:S(2)}, u32[]{:S(2)}) %collective-permute-start.31) | collective-permute-done | bytes 262176 | tf_op jit(solution)/shard_map/ppermute | solution.py:47
  204.9 3.5 %collective-permute-start.29 = (bf16[16,1024]{1,0:T(8,128)(2,1)S(1)}, bf16[16,1024]{1,0:T(8,128)(2,1)S(1)}, u32[]{:S(2)}, u32[]{:S(2)}) collective-permute-start(bf16[16,1024]{1,0:T(8,128)(2,1)S(1)} %get-tuple-element.10), channel_id=1, source_target_pairs={{0,128},{128,0},{1,129},{129,1},{2,130},{130,2},{3,131},{131,3},{4... | collective-permute-start | bytes 98312 | tf_op jit(solution)/shard_map/ppermute | solution.py:148
  208.4 2.6 %convert_bitcast_fusion.1 = bf16[1,1024,1024]{2,1,0:T(8,128)(2,1)} fusion(bf16[256,1024]{1,0:T(8,128)(2,1)S(1)} %bitcast.88, bf16[256,1024]{1,0:T(8,128)(2,1)S(1)} %bitcast.91, bf16[256,512]{1,0:T(8,128)(2,1)S(1)} %get-tuple-element.14, bf16[256,512]{1,0:T(8,128)(2,1)S(1)} %get-tuple-element.13, bf16[256,512]{1,0:T(8,128)(2,1)S(1)} %get-tuple-element.12, ...), kind=kOutput, calls=%fused_computation.1 | convolution fusion | flops 1081081856 | bytes 4194304 | tf_op jit(solution)/shard_map/dot_general | solution.py:26
  (99 shorter events, 10.1 us)
Async XLA Ops:
  0.6 13.4 %copy-start = (bf16[1,1024,1024]{2,1,0:T(8,128)(2,1)S(1)}, bf16[1,1024,1024]{2,1,0:T(8,128)(2,1)}, u32[]{:S(2)}) copy-start(bf16[1,1024,1024]{2,1,0:T(8,128)(2,1)} %param.6) | copy-start | bytes 6291460
  2.4 26.4 %all-to-all-start = ((bf16[16,16,1024]{2,1,0:T(8,128)(2,1)}), bf16[16,16,1024]{2,1,0:T(8,128)(2,1)S(1)}, u32[]{:S(2)}, u32[]{:S(2)}) async-start(bf16[16,16,1024]{2,1,0:T(8,128)(2,1)} %broadcast_in_dim.10), calls=%async_computation | async-start | bytes 1048576 | tf_op jit(solution)/shard_map/all_to_all | solution.py:86
  14.0 12.8 %copy-start.6 = (bf16[16,1,16,1024]{3,2,1,0:T(8,128)(2,1)}, bf16[16,1,16,1024]{3,2,1,0:T(8,128)(2,1)S(1)}, u32[]{:S(2)}) copy-start(bf16[16,1,16,1024]{3,2,1,0:T(8,128)(2,1)S(1)} %get-tuple-element.15) | copy-start | bytes 1572868
  16.4 3.0 %collective-permute-start.14 = (bf16[256,512]{1,0:T(8,128)(2,1)}, bf16[256,512]{1,0:T(8,128)(2,1)}, u32[]{:S(2)}, u32[]{:S(2)}) collective-permute-start(bf16[256,512]{1,0:T(8,128)(2,1)} %fusion.5), channel_id=1, source_target_pairs={{0,1},{1,0},{2,3},{3,2},{4,5},{5,4},{6,7},{7,6},{8,9},{9,8},{10,11... | collective-permute-start | bytes 786440 | tf_op jit(solution)/shard_map/ppermute | solution.py:39
  17.5 9.3 %collective-permute-start.5 = (bf16[256,512]{1,0:T(8,128)(2,1)}, bf16[256,512]{1,0:T(8,128)(2,1)S(1)}, u32[]{:S(2)}, u32[]{:S(2)}) collective-permute-start(bf16[256,512]{1,0:T(8,128)(2,1)} %fusion.4), channel_id=1, source_target_pairs={{0,1},{1,0},{2,3},{3,2},{4,5},{5,4},{6,7},{7,6},{8,9},{9,8},{10,11... | collective-permute-start | bytes 786440 | tf_op jit(solution)/shard_map/ppermute | solution.py:39
  18.0 96.5 %collective-permute-start.21 = (bf16[1024,1024]{1,0:T(8,128)(2,1)}, bf16[1024,1024]{1,0:T(8,128)(2,1)}, u32[]{:S(2)}, u32[]{:S(2)}) collective-permute-start(bf16[1024,1024]{1,0:T(8,128)(2,1)} %bitcast.14), channel_id=1, source_target_pairs={{0,192},{64,128},{1,193},{65,129},{2,194},{66,130},{3,195},{67,131... | collective-permute-start | bytes 6291464 | tf_op jit(solution)/shard_map/ppermute | solution.py:43
  21.8 11.0 %collective-permute-start.17 = (bf16[256,512]{1,0:T(8,128)(2,1)}, bf16[256,512]{1,0:T(8,128)(2,1)}, u32[]{:S(2)}, u32[]{:S(2)}) collective-permute-start(bf16[256,512]{1,0:T(8,128)(2,1)} %get-tuple-element.25), channel_id=1, source_target_pairs={{0,4},{2,6},{4,0},{6,2},{1,5},{3,7},{5,1},{7,3},{8,12},{10,14},{12... | collective-permute-start | bytes 786440 | tf_op jit(solution)/shard_map/ppermute | solution.py:72
  24.8 13.7 %collective-permute-start.16 = (bf16[256,512]{1,0:T(8,128)(2,1)}, bf16[256,512]{1,0:T(8,128)(2,1)}, u32[]{:S(2)}, u32[]{:S(2)}) collective-permute-start(bf16[256,512]{1,0:T(8,128)(2,1)} %get-tuple-element.25), channel_id=1, source_target_pairs={{0,6},{2,0},{4,2},{6,4},{1,7},{3,1},{5,3},{7,5},{8,14},{10,8},{12,... | collective-permute-start | bytes 786440 | tf_op jit(solution)/shard_map/ppermute | solution.py:72
  25.9 14.0 %collective-permute-start.15 = (bf16[256,512]{1,0:T(8,128)(2,1)}, bf16[256,512]{1,0:T(8,128)(2,1)}, u32[]{:S(2)}, u32[]{:S(2)}) collective-permute-start(bf16[256,512]{1,0:T(8,128)(2,1)} %get-tuple-element.25), channel_id=1, source_target_pairs={{0,2},{2,4},{4,6},{6,0},{1,3},{3,5},{5,7},{7,1},{8,10},{10,12},{12... | collective-permute-start | bytes 786440 | tf_op jit(solution)/shard_map/ppermute | solution.py:72
  28.2 17.3 %collective-permute-start.8 = (bf16[256,512]{1,0:T(8,128)(2,1)}, bf16[256,512]{1,0:T(8,128)(2,1)S(1)}, u32[]{:S(2)}, u32[]{:S(2)}) collective-permute-start(bf16[256,512]{1,0:T(8,128)(2,1)} %get-tuple-element.27), channel_id=1, source_target_pairs={{0,4},{2,6},{4,0},{6,2},{1,5},{3,7},{5,1},{7,3},{8,12},{10,14},{12... | collective-permute-start | bytes 786440 | tf_op jit(solution)/shard_map/ppermute | solution.py:72
  32.8 16.0 %collective-permute-start.7 = (bf16[256,512]{1,0:T(8,128)(2,1)}, bf16[256,512]{1,0:T(8,128)(2,1)S(1)}, u32[]{:S(2)}, u32[]{:S(2)}) collective-permute-start(bf16[256,512]{1,0:T(8,128)(2,1)} %get-tuple-element.27), channel_id=1, source_target_pairs={{0,6},{2,0},{4,2},{6,4},{1,7},{3,1},{5,3},{7,5},{8,14},{10,8},{12,... | collective-permute-start | bytes 786440 | tf_op jit(solution)/shard_map/ppermute | solution.py:72
  38.5 12.8 %collective-permute-start.6 = (bf16[256,512]{1,0:T(8,128)(2,1)}, bf16[256,512]{1,0:T(8,128)(2,1)S(1)}, u32[]{:S(2)}, u32[]{:S(2)}) collective-permute-start(bf16[256,512]{1,0:T(8,128)(2,1)} %get-tuple-element.27), channel_id=1, source_target_pairs={{0,2},{2,4},{4,6},{6,0},{1,3},{3,5},{5,7},{7,1},{8,10},{10,12},{12... | collective-permute-start | bytes 786440 | tf_op jit(solution)/shard_map/ppermute | solution.py:72
  40.0 2.5 %collective-permute-start.10 = (bf16[256,512]{1,0:T(8,128)(2,1)S(1)}, bf16[256,512]{1,0:T(8,128)(2,1)S(1)}, u32[]{:S(2)}, u32[]{:S(2)}) collective-permute-start(bf16[256,512]{1,0:T(8,128)(2,1)S(1)} %convolution_convert_fusion.3), channel_id=1, source_target_pairs={{0,1},{1,0},{2,3},{3,2},{4,5},{5,4},{6,7},{7,6},{8,9},{9,8},{10,11... | collective-permute-start | bytes 786440 | tf_op jit(solution)/shard_map/ppermute | solution.py:39
  40.0 11.4 %copy-start.11 = (f32[256,512]{1,0:T(8,128)S(1)}, f32[256,512]{1,0:T(8,128)}, u32[]{:S(2)}) copy-start(f32[256,512]{1,0:T(8,128)} %get-tuple-element.28) | copy-start | bytes 1572868
  42.5 39.9 %copy-start.2 = (f32[256,512]{1,0:T(8,128)}, f32[256,512]{1,0:T(8,128)S(1)}, u32[]{:S(2)}) copy-start(f32[256,512]{1,0:T(8,128)S(1)} %get-tuple-element.6) | copy-start | bytes 1572868
  42.5 37.7 %collective-permute-start = (bf16[256,1024]{1,0:T(8,128)(2,1)S(1)}, bf16[256,1024]{1,0:T(8,128)(2,1)S(1)}, u32[]{:S(2)}, u32[]{:S(2)}) collective-permute-start(bf16[256,1024]{1,0:T(8,128)(2,1)S(1)} %bitcast.81), channel_id=1, source_target_pairs={{0,192},{64,128},{1,193},{65,129},{2,194},{66,130},{3,195},{67,131... | collective-permute-start | bytes 1572872 | tf_op jit(solution)/shard_map/ppermute | solution.py:43
  45.5 36.8 %collective-permute-start.13 = (bf16[256,512]{1,0:T(8,128)(2,1)S(1)}, bf16[256,512]{1,0:T(8,128)(2,1)S(1)}, u32[]{:S(2)}, u32[]{:S(2)}) collective-permute-start(bf16[256,512]{1,0:T(8,128)(2,1)S(1)} %get-tuple-element.23), channel_id=1, source_target_pairs={{0,4},{2,6},{4,0},{6,2},{1,5},{3,7},{5,1},{7,3},{8,12},{10,14},{12... | collective-permute-start | bytes 786440 | tf_op jit(solution)/shard_map/ppermute | solution.py:72
  48.8 33.6 %collective-permute-start.12 = (bf16[256,512]{1,0:T(8,128)(2,1)S(1)}, bf16[256,512]{1,0:T(8,128)(2,1)S(1)}, u32[]{:S(2)}, u32[]{:S(2)}) collective-permute-start(bf16[256,512]{1,0:T(8,128)(2,1)S(1)} %get-tuple-element.23), channel_id=1, source_target_pairs={{0,6},{2,0},{4,2},{6,4},{1,7},{3,1},{5,3},{7,5},{8,14},{10,8},{12,... | collective-permute-start | bytes 786440 | tf_op jit(solution)/shard_map/ppermute | solution.py:72
  51.3 31.0 %collective-permute-start.11 = (bf16[256,512]{1,0:T(8,128)(2,1)S(1)}, bf16[256,512]{1,0:T(8,128)(2,1)S(1)}, u32[]{:S(2)}, u32[]{:S(2)}) collective-permute-start(bf16[256,512]{1,0:T(8,128)(2,1)S(1)} %get-tuple-element.23), channel_id=1, source_target_pairs={{0,2},{2,4},{4,6},{6,0},{1,3},{3,5},{5,7},{7,1},{8,10},{10,12},{12... | collective-permute-start | bytes 786440 | tf_op jit(solution)/shard_map/ppermute | solution.py:72
  80.1 3.7 %copy-start.4 = (bf16[256,1024]{1,0:T(8,128)(2,1)}, bf16[256,1024]{1,0:T(8,128)(2,1)S(1)}, u32[]{:S(2)}) copy-start(bf16[256,1024]{1,0:T(8,128)(2,1)S(1)} %collective-permute-done) | copy-start | bytes 1572868
  82.0 1.8 collective-permute-start.1
  82.8 7.9 %collective-permute-start.18 = (bf16[256,512]{1,0:T(8,128)(2,1)S(1)}, bf16[256,512]{1,0:T(8,128)(2,1)S(1)}, u32[]{:S(2)}, u32[]{:S(2)}) collective-permute-start(bf16[256,512]{1,0:T(8,128)(2,1)S(1)} %multiply_convert_fusion.3), channel_id=1, source_target_pairs={{0,1},{1,0},{2,3},{3,2},{4,5},{5,4},{6,7},{7,6},{8,9},{9,8},{10,11... | collective-permute-start | bytes 786440 | tf_op jit(solution)/shard_map/ppermute | solution.py:39
  85.5 10.8 %collective-permute-start.4 = (bf16[256,512]{1,0:T(8,128)(2,1)S(1)}, bf16[256,512]{1,0:T(8,128)(2,1)S(1)}, u32[]{:S(2)}, u32[]{:S(2)}) collective-permute-start(bf16[256,512]{1,0:T(8,128)(2,1)S(1)} %get-tuple-element.29), channel_id=1, source_target_pairs={{0,4},{2,6},{4,0},{6,2},{1,5},{3,7},{5,1},{7,3},{8,12},{10,14},{12... | collective-permute-start | bytes 786440 | tf_op jit(solution)/shard_map/ppermute | solution.py:72
  88.7 12.6 %collective-permute-start.3 = (bf16[256,512]{1,0:T(8,128)(2,1)S(1)}, bf16[256,512]{1,0:T(8,128)(2,1)S(1)}, u32[]{:S(2)}, u32[]{:S(2)}) collective-permute-start(bf16[256,512]{1,0:T(8,128)(2,1)S(1)} %get-tuple-element.29), channel_id=1, source_target_pairs={{0,6},{2,0},{4,2},{6,4},{1,7},{3,1},{5,3},{7,5},{8,14},{10,8},{12,... | collective-permute-start | bytes 786440 | tf_op jit(solution)/shard_map/ppermute | solution.py:72
  89.8 11.4 %collective-permute-start.2 = (bf16[256,512]{1,0:T(8,128)(2,1)S(1)}, bf16[256,512]{1,0:T(8,128)(2,1)S(1)}, u32[]{:S(2)}, u32[]{:S(2)}) collective-permute-start(bf16[256,512]{1,0:T(8,128)(2,1)S(1)} %get-tuple-element.29), channel_id=1, source_target_pairs={{0,2},{2,4},{4,6},{6,0},{1,3},{3,5},{5,7},{7,1},{8,10},{10,12},{12... | collective-permute-start | bytes 786440 | tf_op jit(solution)/shard_map/ppermute | solution.py:72
  90.7 1.0 copy-start.12
  91.7 13.5 %collective-permute-start.19 = (bf16[256,1024]{1,0:T(8,128)(2,1)S(1)}, bf16[256,1024]{1,0:T(8,128)(2,1)S(1)}, u32[]{:S(2)}, u32[]{:S(2)}) collective-permute-start(bf16[256,1024]{1,0:T(8,128)(2,1)S(1)} %fusion.1), channel_id=1, source_target_pairs={{192,0},{128,64},{193,1},{129,65},{194,2},{130,66},{195,3},{131,67... | collective-permute-start | bytes 1572872 | tf_op jit(solution)/shard_map/ppermute | solution.py:47
  102.4 4.0 %copy-start.9 = (bf16[256,512]{1,0:T(8,128)(2,1)}, bf16[256,512]{1,0:T(8,128)(2,1)S(1)}, u32[]{:S(2)}) copy-start(bf16[256,512]{1,0:T(8,128)(2,1)S(1)} %get-tuple-element.22) | copy-start | bytes 786436
  102.4 1.5 collective-permute-start.9
  104.0 0.7 copy-start.14
  105.1 25.2 %copy-start.21 = (bf16[32,1024]{1,0:T(8,128)(2,1)S(1)}, bf16[32,1024]{1,0:T(8,128)(2,1)}, u32[]{:S(2)}) copy-start(bf16[32,1024]{1,0:T(8,128)(2,1)} %param.5) | copy-start | bytes 196612
  106.5 23.8 %all-to-all-start.1 = ((bf16[16,16,1024]{2,1,0:T(8,128)(2,1)}), bf16[16,16,1024]{2,1,0:T(8,128)(2,1)S(1)}, u32[]{:S(2)}, u32[]{:S(2)}) async-start(bf16[16,16,1024]{2,1,0:T(8,128)(2,1)} %bitcast.12), calls=%async_computation.1 | async-start | bytes 1048576 | tf_op jit(solution)/shard_map/all_to_all | solution.py:78
  114.6 52.5 %collective-permute-start.27 = (bf16[1024,1024]{1,0:T(8,128)(2,1)S(1)}, bf16[1024,1024]{1,0:T(8,128)(2,1)}, u32[]{:S(2)}, u32[]{:S(2)}) collective-permute-start(bf16[1024,1024]{1,0:T(8,128)(2,1)S(1)} %bitcast.79), channel_id=1, source_target_pairs={{0,192},{64,128},{1,193},{65,129},{2,194},{66,130},{3,195},{67,131... | collective-permute-start | bytes 6291464 | tf_op jit(solution)/shard_map/ppermute | solution.py:43
  131.2 20.4 %all-to-all-start.2 = ((bf16[16,16,1024]{2,1,0:T(8,128)(2,1)}), bf16[16,16,1024]{2,1,0:T(8,128)(2,1)S(1)}, u32[]{:S(2)}, u32[]{:S(2)}) async-start(bf16[16,16,1024]{2,1,0:T(8,128)(2,1)} %broadcast_in_dim.22), calls=%async_computation.2 | async-start | bytes 1048576 | tf_op jit(solution)/shard_map/all_to_all | solution.py:86
  136.1 17.4 %collective-permute-start.32 = (bf16[256,512]{1,0:T(8,128)(2,1)}, bf16[256,512]{1,0:T(8,128)(2,1)}, u32[]{:S(2)}, u32[]{:S(2)}) collective-permute-start(bf16[256,512]{1,0:T(8,128)(2,1)} %get-tuple-element.5), channel_id=1, source_target_pairs={{0,1},{1,0},{2,3},{3,2},{4,5},{5,4},{6,7},{7,6},{8,9},{9,8},{10,11... | collective-permute-start | bytes 786440 | tf_op jit(solution)/shard_map/ppermute | solution.py:39
  136.1 19.3 %collective-permute-start.33 = (bf16[256,512]{1,0:T(8,128)(2,1)}, bf16[256,512]{1,0:T(8,128)(2,1)}, u32[]{:S(2)}, u32[]{:S(2)}) collective-permute-start(bf16[256,512]{1,0:T(8,128)(2,1)} %get-tuple-element.7), channel_id=1, source_target_pairs={{0,1},{1,0},{2,3},{3,2},{4,5},{5,4},{6,7},{7,6},{8,9},{9,8},{10,11... | collective-permute-start | bytes 786440 | tf_op jit(solution)/shard_map/ppermute | solution.py:39
  151.6 3.9 %copy-start.16 = (bf16[256,512]{1,0:T(8,128)(2,1)S(1)}, bf16[256,512]{1,0:T(8,128)(2,1)}, u32[]{:S(2)}) copy-start(bf16[256,512]{1,0:T(8,128)(2,1)} %get-tuple-element.7) | copy-start | bytes 786436
  151.6 5.7 %copy-start.20 = (bf16[256,512]{1,0:T(8,128)(2,1)S(1)}, bf16[256,512]{1,0:T(8,128)(2,1)}, u32[]{:S(2)}) copy-start(bf16[256,512]{1,0:T(8,128)(2,1)} %get-tuple-element.21) | copy-start | bytes 786436
  151.6 10.1 %copy-start.1 = (bf16[1024,1024]{1,0:T(8,128)(2,1)S(1)}, bf16[1024,1024]{1,0:T(8,128)(2,1)}, u32[]{:S(2)}) copy-start(bf16[1024,1024]{1,0:T(8,128)(2,1)} %broadcast_select_fusion.1) | copy-start | bytes 6291460
  153.4 8.2 %collective-permute-start.22 = (bf16[256,512]{1,0:T(8,128)(2,1)S(1)}, bf16[256,512]{1,0:T(8,128)(2,1)S(1)}, u32[]{:S(2)}, u32[]{:S(2)}) collective-permute-start(bf16[256,512]{1,0:T(8,128)(2,1)S(1)} %convolution_convert_fusion.2), channel_id=1, source_target_pairs={{0,1},{1,0},{2,3},{3,2},{4,5},{5,4},{6,7},{7,6},{8,9},{9,8},{10,11... | collective-permute-start | bytes 786440 | tf_op jit(solution)/shard_map/ppermute | solution.py:39
  157.2 13.9 %collective-permute-start.26 = (bf16[256,512]{1,0:T(8,128)(2,1)S(1)}, bf16[256,512]{1,0:T(8,128)(2,1)S(1)}, u32[]{:S(2)}, u32[]{:S(2)}) collective-permute-start(bf16[256,512]{1,0:T(8,128)(2,1)S(1)} %copy-done.20), channel_id=1, source_target_pairs={{0,192},{64,128},{1,193},{65,129},{2,194},{66,130},{3,195},{67,131... | collective-permute-start | bytes 786440 | tf_op jit(solution)/shard_map/ppermute | solution.py:43
  158.5 46.4 %collective-permute-start.20 = (bf16[16,1024]{1,0:T(8,128)(2,1)S(1)}, bf16[16,1024]{1,0:T(8,128)(2,1)S(1)}, u32[]{:S(2)}, u32[]{:S(2)}) collective-permute-start(bf16[16,1024]{1,0:T(8,128)(2,1)S(1)} %add_convert_fusion.1), channel_id=1, source_target_pairs={{0,128},{128,0},{1,129},{129,1},{2,130},{130,2},{3,131},{131,3},{4... | collective-permute-start | bytes 98312 | tf_op jit(solution)/shard_map/ppermute | solution.py:147
  162.1 15.4 %copy-start.3 = (f32[256,512]{1,0:T(8,128)S(1)}, f32[256,512]{1,0:T(8,128)}, u32[]{:S(2)}) copy-start(f32[256,512]{1,0:T(8,128)} %copy-done.2) | copy-start | bytes 1572868
  162.1 11.2 %collective-permute-start.25 = (bf16[256,512]{1,0:T(8,128)(2,1)S(1)}, bf16[256,512]{1,0:T(8,128)(2,1)S(1)}, u32[]{:S(2)}, u32[]{:S(2)}) collective-permute-start(bf16[256,512]{1,0:T(8,128)(2,1)S(1)} %get-tuple-element.31), channel_id=1, source_target_pairs={{0,4},{2,6},{4,0},{6,2},{1,5},{3,7},{5,1},{7,3},{8,12},{10,14},{12... | collective-permute-start | bytes 786440 | tf_op jit(solution)/shard_map/ppermute | solution.py:72
  165.1 12.4 %collective-permute-start.24 = (bf16[256,512]{1,0:T(8,128)(2,1)S(1)}, bf16[256,512]{1,0:T(8,128)(2,1)S(1)}, u32[]{:S(2)}, u32[]{:S(2)}) collective-permute-start(bf16[256,512]{1,0:T(8,128)(2,1)S(1)} %get-tuple-element.31), channel_id=1, source_target_pairs={{0,6},{2,0},{4,2},{6,4},{1,7},{3,1},{5,3},{7,5},{8,14},{10,8},{12,... | collective-permute-start | bytes 786440 | tf_op jit(solution)/shard_map/ppermute | solution.py:72
  167.1 10.5 %collective-permute-start.23 = (bf16[256,512]{1,0:T(8,128)(2,1)S(1)}, bf16[256,512]{1,0:T(8,128)(2,1)S(1)}, u32[]{:S(2)}, u32[]{:S(2)}) collective-permute-start(bf16[256,512]{1,0:T(8,128)(2,1)S(1)} %get-tuple-element.31), channel_id=1, source_target_pairs={{0,2},{2,4},{4,6},{6,0},{1,3},{3,5},{5,7},{7,1},{8,10},{10,12},{12... | collective-permute-start | bytes 786440 | tf_op jit(solution)/shard_map/ppermute | solution.py:72
  171.1 16.1 %collective-permute-start.34 = (bf16[256,1024]{1,0:T(8,128)(2,1)S(1)}, bf16[256,1024]{1,0:T(8,128)(2,1)}, u32[]{:S(2)}, u32[]{:S(2)}) collective-permute-start(bf16[256,1024]{1,0:T(8,128)(2,1)S(1)} %bitcast.85), channel_id=1, source_target_pairs={{192,0},{128,64},{193,1},{129,65},{194,2},{130,66},{195,3},{131,67... | collective-permute-start | bytes 1572872 | tf_op jit(solution)/shard_map/ppermute | solution.py:47
  178.0 1.6 collective-permute-start.28
  179.7 1.8 copy-start.17
  180.1 7.1 %copy-start.5 = (bf16[256,1024]{1,0:T(8,128)(2,1)S(1)}, bf16[256,1024]{1,0:T(8,128)(2,1)}, u32[]{:S(2)}) copy-start(bf16[256,1024]{1,0:T(8,128)(2,1)} %copy-done.4) | copy-start | bytes 1572868
  181.4 5.9 %copy-start.19 = (bf16[256,1024]{1,0:T(8,128)(2,1)S(1)}, bf16[256,1024]{1,0:T(8,128)(2,1)}, u32[]{:S(2)}) copy-start(bf16[256,1024]{1,0:T(8,128)(2,1)} %broadcast_select_fusion.3) | copy-start | bytes 1572868
  181.4 23.4 %all-to-all-start.3 = ((bf16[16,16,1024]{2,1,0:T(8,128)(2,1)}), bf16[16,16,1024]{2,1,0:T(8,128)(2,1)S(1)}, u32[]{:S(2)}, u32[]{:S(2)}) async-start(bf16[16,16,1024]{2,1,0:T(8,128)(2,1)} %bitcast.92), calls=%async_computation.3 | async-start | bytes 1048576 | tf_op jit(solution)/shard_map/all_to_all | solution.py:78
  187.4 6.5 %copy-start.18 = (bf16[256,512]{1,0:T(8,128)(2,1)S(1)}, bf16[256,512]{1,0:T(8,128)(2,1)}, u32[]{:S(2)}) copy-start(bf16[256,512]{1,0:T(8,128)(2,1)} %copy-done.17) | copy-start | bytes 786436
  187.4 7.8 %copy-start.13 = (bf16[256,512]{1,0:T(8,128)(2,1)S(1)}, bf16[256,512]{1,0:T(8,128)(2,1)}, u32[]{:S(2)}) copy-start(bf16[256,512]{1,0:T(8,128)(2,1)} %copy-done.12) | copy-start | bytes 786436
  187.4 17.4 %copy-start.10 = (bf16[256,512]{1,0:T(8,128)(2,1)S(1)}, bf16[256,512]{1,0:T(8,128)(2,1)}, u32[]{:S(2)}) copy-start(bf16[256,512]{1,0:T(8,128)(2,1)} %copy-done.9) | copy-start | bytes 786436
  187.4 17.4 %copy-start.15 = (bf16[256,512]{1,0:T(8,128)(2,1)S(1)}, bf16[256,512]{1,0:T(8,128)(2,1)}, u32[]{:S(2)}) copy-start(bf16[256,512]{1,0:T(8,128)(2,1)} %copy-done.14) | copy-start | bytes 786436
  191.3 17.1 %copy-start.7 = (bf16[16,1,16,1024]{3,2,1,0:T(8,128)(2,1)S(1)}, bf16[16,1,16,1024]{3,2,1,0:T(8,128)(2,1)}, u32[]{:S(2)}) copy-start(bf16[16,1,16,1024]{3,2,1,0:T(8,128)(2,1)} %copy-done.6) | copy-start | bytes 1572868
  191.3 17.1 %copy-start.8 = (bf16[16,1,16,1024]{3,2,1,0:T(8,128)(2,1)S(1)}, bf16[16,1,16,1024]{3,2,1,0:T(8,128)(2,1)}, u32[]{:S(2)}) copy-start(bf16[16,1,16,1024]{3,2,1,0:T(8,128)(2,1)} %get-tuple-element.16) | copy-start | bytes 1572868
  191.3 9.3 %collective-permute-start.30 = (bf16[256,512]{1,0:T(8,128)(2,1)S(1)}, bf16[256,512]{1,0:T(8,128)(2,1)S(1)}, u32[]{:S(2)}, u32[]{:S(2)}) collective-permute-start(bf16[256,512]{1,0:T(8,128)(2,1)S(1)} %multiply_convert_fusion.2), channel_id=1, source_target_pairs={{192,0},{128,64},{193,1},{129,65},{194,2},{130,66},{195,3},{131,67... | collective-permute-start | bytes 786440 | tf_op jit(solution)/shard_map/ppermute | solution.py:47
  193.8 10.9 %collective-permute-start.31 = (bf16[256,512]{1,0:T(8,128)(2,1)S(1)}, bf16[256,512]{1,0:T(8,128)(2,1)S(1)}, u32[]{:S(2)}, u32[]{:S(2)}) collective-permute-start(bf16[256,512]{1,0:T(8,128)(2,1)S(1)} %copy-done.18), channel_id=1, source_target_pairs={{192,0},{128,64},{193,1},{129,65},{194,2},{130,66},{195,3},{131,67... | collective-permute-start | bytes 786440 | tf_op jit(solution)/shard_map/ppermute | solution.py:47
  204.9 6.1 %collective-permute-start.29 = (bf16[16,1024]{1,0:T(8,128)(2,1)S(1)}, bf16[16,1024]{1,0:T(8,128)(2,1)S(1)}, u32[]{:S(2)}, u32[]{:S(2)}) collective-permute-start(bf16[16,1024]{1,0:T(8,128)(2,1)S(1)} %get-tuple-element.10), channel_id=1, source_target_pairs={{0,128},{128,0},{1,129},{129,1},{2,130},{130,2},{3,131},{131,3},{4... | collective-permute-start | bytes 98312 | tf_op jit(solution)/shard_map/ppermute | solution.py:148

commit v4 on v3

--- a/solution.py
+++ b/solution.py
@@ -31,8 +31,12 @@
     )
 
 
+def together(*values):
+    return lax.optimization_barrier(values)
+
+
 def after(value, *others):
-    return lax.optimization_barrier((value, others))[0]
+    return together(value, *others)[0]
 
 
 def other_core(block):
@@ -75,9 +79,12 @@
 
 def spread_wide(partial):
     rows, cols = partial.shape
-    blocks = lax.all_to_all(
+    return lax.all_to_all(
         partial.reshape(WIDE, rows // WIDE, cols), WIDE_AXES, 0, 0, tiled=True
     )
+
+
+def add_blocks(blocks):
     return jnp.sum(blocks.astype(jnp.float32), axis=0)
 
 
@@ -88,11 +95,15 @@
     ).reshape(WIDE * rows, cols)
 
 
-def slope_of(whole, down_halves, slopes):
+def back_total(whole, down_halves):
     theirs = contract(whole, down_halves[1], 1, 1)
     mine = contract(whole, down_halves[0], 1, 1)
-    slope_mine = (narrow_total(mine, theirs) * slopes).astype(jnp.bfloat16)
-    return slope_mine, other_core(slope_mine)
+    return narrow_total(mine, theirs)
+
+
+def slope_of(total, slopes):
+    mine = (total * slopes).astype(jnp.bfloat16)
+    return mine, other_core(mine)
 
 
 def back_through_up(slope, up_halves):
@@ -114,53 +125,77 @@
     w_up, w_down = up_weight[0], down_weight[0]
     up_halves, down_halves = halves(w_up, 1), halves(w_down, 0)
 
+    half = w_down.shape[0] // 2
+    down_pieces = [to_upper(w_down[:half])]
+
     early, late = upstream[:part], upstream[part:]
     gathered = gather_wide(pick(early, late))
-    sent_down = to_upper(w_down)
-    top = [gathered, to_upper(gathered)]
-
-    hidden, slopes = [], []
-    for rows in saved:
+
+    def pre_total(rows):
         theirs = contract(rows, up_halves[1], 1, 0)
         mine = contract(rows, up_halves[0], 1, 0)
-        act, slope = gelu_parts(narrow_total(mine, theirs))
+        return narrow_total(mine, theirs)
+
+    hidden, slopes = [], []
+
+    def keep(total):
+        act, slope = gelu_parts(total)
         act = act.astype(jnp.bfloat16)
         hidden.append((act, other_core(act)))
         slopes.append(slope)
-    lower_slopes = pick(to_upper(slopes[1].astype(jnp.bfloat16)).astype(jnp.float32), slopes[0])
-
-    top_slopes = [slope_of(top[0], down_halves, slopes[0])]
-    moved = to_lower(back_through_up(top_slopes[0], up_halves))
-    sent_up = to_upper(after(w_up, sent_down))
-    top_slopes.append(slope_of(top[1], down_halves, slopes[1]))
-    summed = spread_wide(pick(back_through_up(top_slopes[1], up_halves), moved))
-    middle = (pick(late, early).astype(jnp.float32) + summed).astype(jnp.bfloat16)
-
-    low = gather_wide(middle)
-    low_down = halves(pick(sent_down, w_down), 0)
-    low_up = halves(pick(sent_up, w_up), 1)
-    low_slope = slope_of(low, low_down, lower_slopes)
-    low_summed = spread_wide(back_through_up(low_slope, low_up))
-    bottom = (middle.astype(jnp.float32) + low_summed).astype(jnp.bfloat16)
+
+    keep(pre_total(saved[0]))
+    gathered, *down_pieces = together(gathered, *down_pieces)
+    top_total = back_total(gathered, down_halves)
+    top_total, top_rest = together(top_total, to_upper(gathered))
+    top_slope = slope_of(top_total, slopes[0])
+    top_slope, late_total = together(top_slope, pre_total(after(saved[1], gathered)))
+    keep(late_total)
+    moved = to_lower(back_through_up(top_slope, up_halves))
+    rest_total = back_total(top_rest, down_halves)
+    rest_total, piece = together(rest_total, to_upper(after(w_down[half:], top_rest)))
+    down_pieces.append(piece)
+    top_slope_rest = slope_of(rest_total, slopes[1])
+    partial = pick(back_through_up(top_slope_rest, up_halves), moved)
+    blocks, lower_slopes, *up_pieces = together(
+        spread_wide(partial),
+        to_upper(after(slopes[1].astype(jnp.bfloat16), rest_total)),
+        to_upper(after(w_up[:half], rest_total)),
+    )
+    lower_slopes = pick(lower_slopes.astype(jnp.float32), slopes[0])
+    middle = (pick(late, early).astype(jnp.float32) + add_blocks(blocks)).astype(jnp.bfloat16)
+    up_pieces.append(to_upper(after(w_up[half:], blocks)))
+
+    hidden = jnp.concatenate([in_order(*block) for block in hidden], axis=0)
+    low_down = pick(jnp.concatenate(down_pieces, axis=0), w_down)
+    low, hidden, low_down = together(gather_wide(middle), hidden, low_down)
+    low_rest = to_lower(low)
+    low_total = back_total(low, halves(low_down, 0))
+    incoming = jnp.concatenate([pick(gathered, low), pick(top_rest, low_rest)], axis=0)
+    grad_down = contract(hidden, incoming, 0, 0).astype(jnp.bfloat16)
+    low_up = pick(jnp.concatenate(up_pieces, axis=0), w_up)
+    low_total, grad_down, low_up = together(low_total, grad_down, low_up)
+    low_slope = slope_of(low_total, lower_slopes)
+    low_slope_rest = to_lower(low_slope[0])
+    low_blocks = spread_wide(back_through_up(low_slope, halves(low_up, 1)))
+    slope_grad = jnp.concatenate(
+        [
+            in_order(*[pick(u, l) for u, l in zip(top_slope, low_slope)]),
+            in_order(
+                pick(top_slope_rest[0], low_slope_rest),
+                pick(top_slope_rest[1], other_core(low_slope_rest)),
+            ),
+        ],
+        axis=0,
+    )
+    grad_up = contract(jnp.concatenate(saved, axis=0), slope_grad, 0, 0).astype(jnp.bfloat16)
+    low_blocks, grad_up = together(low_blocks, grad_up)
+    bottom = (middle.astype(jnp.float32) + add_blocks(low_blocks)).astype(jnp.bfloat16)
 
     swap = [(0, 1), (1, 0)]
     upper_first = lax.ppermute(middle, "section", swap)
     lower_last = lax.ppermute(bottom, "section", swap)
-    low_rest = to_lower(low)
-    low_slope_rest = [to_lower(block) for block in low_slope]
-
     grad_in = jnp.concatenate([pick(upper_first, bottom), pick(middle, lower_last)], axis=0)
-    incoming = jnp.concatenate([pick(top[0], low), pick(top[1], low_rest)], axis=0)
-    slope_grad = jnp.concatenate(
-        [
-            in_order(*[pick(u, l) for u, l in zip(top_slopes[0], low_slope)]),
-            in_order(*[pick(u, l) for u, l in zip(top_slopes[1], low_slope_rest)]),
-        ],
-        axis=0,
-    )
-    hidden = jnp.concatenate([in_order(*block) for block in hidden], axis=0)
-    grad_down = contract(hidden, incoming, 0, 0).astype(jnp.bfloat16)
-    grad_up = contract(jnp.concatenate(saved, axis=0), slope_grad, 0, 0).astype(jnp.bfloat16)
     return grad_in[None], grad_up[None], grad_down[None]
 
 

time: 216 us -> 230 us (1.065); the launches traced: 212 us -> 229 us
  waiting for transfers between devices: 84.8 us -> 105 us
  matrix products: 27.6 us -> 19.6 us
  local copies, waits for them, and re-layouts: 4.58 us -> 9.14 us
    ppermute x4 -> x6, waiting for transfers between devices: 29.3 us -> 53.7 us  [to_upper(): return lax.ppermute(block, CROSS_AXES, [(0, 3), (1, 2)])]
    ppermute x4 -> x3, waiting for transfers between devices: 9.49 us -> 0.01 us  [to_lower(): return lax.ppermute(block, CROSS_AXES, [(3, 0), (2, 1)])]
    dot_general x18, matrix products: 27.6 us -> 19.6 us  [contract(): lax.dot_general(first_op, second_op, (((first_dim,), (second_dim,)), ((),...]
    ppermute x15, waiting for transfers between devices: 17.9 us -> 24.1 us  [narrow_total(): total = total + lax.ppermute(sent, 'x', route).astype(jnp.float32)]
    ppermute x1, waiting for transfers between devices: 0.01 us -> 5.41 us  [body(): lower_last = lax.ppermute(bottom, 'section', swap)]
    slice x0 -> x2, local copies, waits for them, and re-layouts: none -> 4.51 us  [the longest x1 3.03 us: body(): w_down[half:]]
    all_to_all x2, waiting for transfers between devices: 11.2 us -> 6.74 us  [gather_wide(): lax.all_to_all(jnp.broadcast_to(block[None], (WIDE, rows, cols)), WIDE_AX...]
    ppermute x1, starting transfers between devices: 3.47 us -> 0.09 us  [body(): lower_last = lax.ppermute(bottom, 'section', swap)]
  transfers between devices with their start and end apart: 39 -> 41, of which waited for: 16 -> 16; matrix products, arithmetic and copies ran while one was open for 22% -> 18% of each run, Pallas kernels for 0% -> 0%
where the time goes in v4:
time: 230 us; the launch traced here: 229 us
  waiting for transfers between devices  105 us (46%)
  starting transfers between devices  78.2 us (34%)
  matrix products  19.6 us (9%)
  other arithmetic  16 us (7%)
  local copies, waits for them, and re-layouts  9.14 us (4%)
    ppermute x6, waiting for transfers between devices, to_upper(): return lax.ppermute(block, CROSS_AXES, [(0, 3), (1, 2)])  53.7 us
    ppermute x15, starting transfers between devices, narrow_total(): total = total + lax.ppermute(sent, 'x', route).astype(jnp.float32)  25.4 us
    ppermute x15, waiting for transfers between devices, narrow_total(): total = total + lax.ppermute(sent, 'x', route).astype(jnp.float32)  24.1 us
    dot_general x18, matrix products, contract(): lax.dot_general(first_op, second_op, (((first_dim,), (second_dim,)), ((),...  19.6 us
    all_to_all x2, starting transfers between devices, gather_wide(): lax.all_to_all(jnp.broadcast_to(block[None], (WIDE, rows, cols)), WIDE_AX...  17.6 us
    all_to_all x2, starting transfers between devices, spread_wide(): lax.all_to_all(partial.reshape(WIDE, rows // WIDE, cols), WIDE_AXES, 0, 0...  16.4 us
    all_to_all x2, waiting for transfers between devices, spread_wide(): lax.all_to_all(partial.reshape(WIDE, rows // WIDE, cols), WIDE_AXES, 0, 0...  11.5 us
    ppermute x3, starting transfers between devices, to_lower(): return lax.ppermute(block, CROSS_AXES, [(3, 0), (2, 1)])  8.6 us
  transfers between devices with their start and end apart: 41, of which 16 were waited for; matrix products, arithmetic and copies ran while one was open for 18% of the time, Pallas kernels for 0%

profile of v4, /device:TPU:56, one launch (start us, length us, event | category | flops | bytes accessed | tf_op | source)
XLA Modules:
  0.0 228.8 jit_solution(4985593665286551172)
XLA Ops:
  0.6 0.8 broadcast_select_fusion.16
  1.4 0.9 broadcast_in_dim.10
  2.3 9.5 %all-to-all-start = ((bf16[16,16,1024]{2,1,0:T(8,128)(2,1)}), bf16[16,16,1024]{2,1,0:T(8,128)(2,1)S(1)}, u32[]{:S(2)}, u32[]{:S(2)}) async-start(bf16[16,16,1024]{2,1,0:T(8,128)(2,1)} %broadcast_in_dim.10), calls=%async_computation | async-start | bytes 1048576 | tf_op jit(solution)/shard_map/all_to_all | solution.py:93
  11.8 3.0 %slice_bitcast_fusion.2 = (bf16[512,1024]{1,0:T(8,128)(2,1)}, bf16[512,1024]{1,0:T(8,128)(2,1)}) fusion(bf16[1,1024,1024]{2,1,0:T(8,128)(2,1)} %param.7), kind=kLoop, calls=%fused_computation.59 | loop fusion | bytes 4194304 | tf_op jit(solution)/shard_map/slice | solution.py:156
  14.8 1.4 collective-permute-start
  16.2 1.3 fusion.83
  17.5 0.8 copy-done.9
  18.3 1.2 fusion.4
  19.5 1.7 collective-permute-done.11
  21.3 2.4 %fusion.61 = (bf16[256,512]{1,0:T(8,128)(2,1)}, f32[256,512]{1,0:T(8,128)}) fusion(bf16[256,512]{1,0:T(8,128)(2,1)S(1)} %collective-permute-done.11, bf16[256,1024]{1,0:T(8,128)(2,1)} %bitcast.92, bf16[1,1024,1024]{2,1,0:T(8,128)(2,1)S(1)} %copy-done, s32[]{:T(128)S(6)} %select_n.124), kind=kOutput, calls=%fused_computation.102 | convolution fusion | flops 268828672 | bytes 2621444 | tf_op jit(solution)/shard_map/dot_general | solution.py:26
  23.6 3.0 %collective-permute-start.14 = (bf16[256,512]{1,0:T(8,128)(2,1)}, bf16[256,512]{1,0:T(8,128)(2,1)}, u32[]{:S(2)}, u32[]{:S(2)}) collective-permute-start(bf16[256,512]{1,0:T(8,128)(2,1)} %get-tuple-element.76), channel_id=1, source_target_pairs={{0,4},{2,6},{4,0},{6,2},{1,5},{3,7},{5,1},{7,3},{8,12},{10,14},{12... | collective-permute-start | bytes 786440 | tf_op jit(solution)/shard_map/ppermute | solution.py:76
  26.7 1.1 collective-permute-start.13
  27.8 0.9 collective-permute-start.12
  28.7 14.0 %collective-permute-done = bf16[512,1024]{1,0:T(8,128)(2,1)} collective-permute-done((bf16[512,1024]{1,0:T(8,128)(2,1)}, bf16[512,1024]{1,0:T(8,128)(2,1)}, u32[]{:S(2)}, u32[]{:S(2)}) %collective-permute-start) | collective-permute-done | bytes 1048608 | tf_op jit(solution)/shard_map/ppermute | solution.py:47
  42.7 1.7 convolution_convert_fusion.6
  44.5 2.3 multiply_convert_fusion.2
  46.8 1.3 collective-permute-start.5
  49.6 3.1 %collective-permute-start.4 = (bf16[256,512]{1,0:T(8,128)(2,1)S(1)}, bf16[256,512]{1,0:T(8,128)(2,1)S(1)}, u32[]{:S(2)}, u32[]{:S(2)}) collective-permute-start(bf16[256,512]{1,0:T(8,128)(2,1)S(1)} %get-tuple-element.74), channel_id=1, source_target_pairs={{0,4},{2,6},{4,0},{6,2},{1,5},{3,7},{5,1},{7,3},{8,12},{10,14},{12... | collective-permute-start | bytes 786440 | tf_op jit(solution)/shard_map/ppermute | solution.py:76
  52.7 1.1 collective-permute-start.3
  53.9 0.9 collective-permute-start.2
  56.0 4.4 %collective-permute-done.4 = bf16[256,512]{1,0:T(8,128)(2,1)S(1)} collective-permute-done((bf16[256,512]{1,0:T(8,128)(2,1)S(1)}, bf16[256,512]{1,0:T(8,128)(2,1)S(1)}, u32[]{:S(2)}, u32[]{:S(2)}) %collective-permute-start.4) | collective-permute-done | bytes 262176 | tf_op jit(solution)/shard_map/ppermute | solution.py:76
  60.4 2.8 %collective-permute-start.18 = (bf16[256,512]{1,0:T(8,128)(2,1)S(1)}, bf16[256,512]{1,0:T(8,128)(2,1)S(1)}, u32[]{:S(2)}, u32[]{:S(2)}) collective-permute-start(bf16[256,512]{1,0:T(8,128)(2,1)S(1)} %get-tuple-element.78), channel_id=1, source_target_pairs={{0,6},{2,0},{4,2},{6,4},{1,7},{3,1},{5,3},{7,5},{8,14},{10,8},{12,... | collective-permute-start | bytes 786440 | tf_op jit(solution)/shard_map/ppermute | solution.py:76
  63.2 2.9 %collective-permute-done.3 = bf16[256,512]{1,0:T(8,128)(2,1)S(1)} collective-permute-done((bf16[256,512]{1,0:T(8,128)(2,1)S(1)}, bf16[256,512]{1,0:T(8,128)(2,1)S(1)}, u32[]{:S(2)}, u32[]{:S(2)}) %collective-permute-start.3) | collective-permute-done | bytes 262176 | tf_op jit(solution)/shard_map/ppermute | solution.py:76
  66.1 1.5 collective-permute-start.17
  69.4 1.4 collective-permute-done.19
  70.8 1.3 collective-permute-start.10
  72.1 4.4 %collective-permute-done.18 = bf16[256,512]{1,0:T(8,128)(2,1)S(1)} collective-permute-done((bf16[256,512]{1,0:T(8,128)(2,1)S(1)}, bf16[256,512]{1,0:T(8,128)(2,1)S(1)}, u32[]{:S(2)}, u32[]{:S(2)}) %collective-permute-start.18) | collective-permute-done | bytes 262176 | tf_op jit(solution)/shard_map/ppermute | solution.py:76
  77.2 3.0 %collective-permute-start.9 = (bf16[256,512]{1,0:T(8,128)(2,1)S(1)}, bf16[256,512]{1,0:T(8,128)(2,1)S(1)}, u32[]{:S(2)}, u32[]{:S(2)}) collective-permute-start(bf16[256,512]{1,0:T(8,128)(2,1)S(1)} %get-tuple-element.80), channel_id=1, source_target_pairs={{0,4},{2,6},{4,0},{6,2},{1,5},{3,7},{5,1},{7,3},{8,12},{10,14},{12... | collective-permute-start | bytes 786440 | tf_op jit(solution)/shard_map/ppermute | solution.py:76
  80.2 1.2 collective-permute-start.8
  81.4 0.8 collective-permute-start.7
  83.2 5.8 %collective-permute-start.21 = (bf16[256,1024]{1,0:T(8,128)(2,1)S(1)}, bf16[256,1024]{1,0:T(8,128)(2,1)S(1)}, u32[]{:S(2)}, u32[]{:S(2)}) collective-permute-start(bf16[256,1024]{1,0:T(8,128)(2,1)S(1)} %fusion.1), channel_id=1, source_target_pairs={{192,0},{128,64},{193,1},{129,65},{194,2},{130,66},{195,3},{131,67... | collective-permute-start | bytes 1572872 | tf_op jit(solution)/shard_map/ppermute | solution.py:51
  89.0 3.6 %collective-permute-done.8 = bf16[256,512]{1,0:T(8,128)(2,1)S(1)} collective-permute-done((bf16[256,512]{1,0:T(8,128)(2,1)S(1)}, bf16[256,512]{1,0:T(8,128)(2,1)S(1)}, u32[]{:S(2)}, u32[]{:S(2)}) %collective-permute-start.8) | collective-permute-done | bytes 262176 | tf_op jit(solution)/shard_map/ppermute | solution.py:76
  92.7 6.1 %collective-permute-done.10 = bf16[512,1024]{1,0:T(8,128)(2,1)} collective-permute-done((bf16[512,1024]{1,0:T(8,128)(2,1)S(1)}, bf16[512,1024]{1,0:T(8,128)(2,1)}, u32[]{:S(2)}, u32[]{:S(2)}) %collective-permute-start.10) | collective-permute-done | bytes 1048608 | tf_op jit(solution)/shard_map/ppermute | solution.py:47
  98.8 1.2 multiply_convert_fusion.1
  100.0 1.5 slice_bitcast_fusion
  101.5 1.3 collective-permute-start.23
  103.4 1.3 fusion.3
  104.7 8.1 %all-to-all-start.1 = ((bf16[16,16,1024]{2,1,0:T(8,128)(2,1)}), bf16[16,16,1024]{2,1,0:T(8,128)(2,1)S(1)}, u32[]{:S(2)}, u32[]{:S(2)}) async-start(bf16[16,16,1024]{2,1,0:T(8,128)(2,1)} %bitcast.12), calls=%async_computation.1 | async-start | bytes 1048576 | tf_op jit(solution)/shard_map/all_to_all | solution.py:82
  112.8 1.3 collective-permute-start.22
  114.1 21.9 %collective-permute-done.22 = bf16[256,512]{1,0:T(8,128)(2,1)S(1)} collective-permute-done((bf16[256,512]{1,0:T(8,128)(2,1)}, bf16[256,512]{1,0:T(8,128)(2,1)S(1)}, u32[]{:S(2)}, u32[]{:S(2)}) %collective-permute-start.22) | collective-permute-done | bytes 262176 | tf_op jit(solution)/shard_map/ppermute | solution.py:47
  136.9 0.9 broadcast_in_dim.22
  137.7 8.1 %all-to-all-start.2 = ((bf16[16,16,1024]{2,1,0:T(8,128)(2,1)}), bf16[16,16,1024]{2,1,0:T(8,128)(2,1)S(1)}, u32[]{:S(2)}, u32[]{:S(2)}) async-start(bf16[16,16,1024]{2,1,0:T(8,128)(2,1)} %broadcast_in_dim.22), calls=%async_computation.2 | async-start | bytes 1048576 | tf_op jit(solution)/shard_map/all_to_all | solution.py:93
  145.8 1.1 broadcast_select_fusion.13
  147.0 1.4 collective-permute-start.32
  148.4 4.5 %maximum_select_fusion = bf16[1024,1024]{1,0:T(8,128)(2,1)} fusion(bf16[512,1024]{1,0:T(8,128)(2,1)} %collective-permute-done.10, bf16[512,1024]{1,0:T(8,128)(2,1)} %collective-permute-done, bf16[1,1024,1024]{2,1,0:T(8,128)(2,1)} %param.7, pred[]{:T(512)S(6)} %eq.4), kind=kLoop, calls=%fused_computation | loop fusion | flops 5242880 | bytes 6291457 | tf_op jit(solution)/shard_map/jit(_where)/select_n | solution.py:119
  153.0 1.1 maximum_maximum_fusion
  154.2 6.7 %all-to-all-done.2 = bf16[16,16,1024]{2,1,0:T(8,128)(2,1)S(1)} async-done(((bf16[16,16,1024]{2,1,0:T(8,128)(2,1)}), bf16[16,16,1024]{2,1,0:T(8,128)(2,1)S(1)}, u32[]{:S(2)}, u32[]{:S(2)}) %all-to-all-start.2) | async-done | bytes 524320 | tf_op jit(solution)/shard_map/all_to_all | solution.py:93
  160.9 1.3 collective-permute-start.31
  162.2 1.7 convolution_convert_fusion.3
  164.3 11.8 %collective-permute-done.32 = bf16[512,1024]{1,0:T(8,128)(2,1)} collective-permute-done((bf16[512,1024]{1,0:T(8,128)(2,1)}, bf16[512,1024]{1,0:T(8,128)(2,1)}, u32[]{:S(2)}, u32[]{:S(2)}) %collective-permute-start.32) | collective-permute-done | bytes 1048608 | tf_op jit(solution)/shard_map/ppermute | solution.py:47
  176.1 2.5 %maximum_select_fusion.1 = bf16[1024,1024]{1,0:T(8,128)(2,1)S(1)} fusion(bf16[512,1024]{1,0:T(8,128)(2,1)} %collective-permute-done.32, bf16[512,1024]{1,0:T(8,128)(2,1)} %collective-permute-done.23, bf16[1,1024,1024]{2,1,0:T(8,128)(2,1)S(1)} %copy-done, pred[]{:T(512)S(6)} %eq.4), kind=kLoop, calls=%fused_computation.1 | loop fusion | flops 5242880 | bytes 6291457 | tf_op jit(solution)/shard_map/jit(_where)/select_n | solution.py:119
  179.2 3.2 %collective-permute-start.30 = (bf16[256,512]{1,0:T(8,128)(2,1)S(1)}, bf16[256,512]{1,0:T(8,128)(2,1)S(1)}, u32[]{:S(2)}, u32[]{:S(2)}) collective-permute-start(bf16[256,512]{1,0:T(8,128)(2,1)S(1)} %get-tuple-element.82), channel_id=1, source_target_pairs={{0,4},{2,6},{4,0},{6,2},{1,5},{3,7},{5,1},{7,3},{8,12},{10,14},{12... | collective-permute-start | bytes 786440 | tf_op jit(solution)/shard_map/ppermute | solution.py:76
  182.4 1.1 collective-permute-start.29
  183.5 0.9 collective-permute-start.28
  184.5 2.6 %convolution_convert_fusion.1 = bf16[1024,1024]{1,0:T(8,128)(2,1)} fusion(bf16[512,1024]{1,0:T(8,128)(2,1)S(1)} %copy-done.14, bf16[256,1024]{1,0:T(8,128)(2,1)S(1)} %broadcast_select_fusion, bf16[256,1024]{1,0:T(8,128)(2,1)S(1)} %broadcast_select_fusion.1), kind=kOutput, calls=%fused_computation.3 | convolution fusion | flops 1076887552 | bytes 4194304 | tf_op jit(solution)/shard_map/dot_general | solution.py:26
  187.1 2.9 %collective-permute-done.30 = bf16[256,512]{1,0:T(8,128)(2,1)S(1)} collective-permute-done((bf16[256,512]{1,0:T(8,128)(2,1)S(1)}, bf16[256,512]{1,0:T(8,128)(2,1)S(1)}, u32[]{:S(2)}, u32[]{:S(2)}) %collective-permute-start.30) | collective-permute-done | bytes 262176 | tf_op jit(solution)/shard_map/ppermute | solution.py:76
  190.0 4.5 %collective-permute-done.29 = bf16[256,512]{1,0:T(8,128)(2,1)S(1)} collective-permute-done((bf16[256,512]{1,0:T(8,128)(2,1)S(1)}, bf16[256,512]{1,0:T(8,128)(2,1)S(1)}, u32[]{:S(2)}, u32[]{:S(2)}) %collective-permute-start.29) | collective-permute-done | bytes 262176 | tf_op jit(solution)/shard_map/ppermute | solution.py:76
  195.2 1.5 collective-permute-start.34
  197.2 1.3 fusion.2
  198.5 8.3 %all-to-all-start.3 = ((bf16[16,16,1024]{2,1,0:T(8,128)(2,1)}), bf16[16,16,1024]{2,1,0:T(8,128)(2,1)S(1)}, u32[]{:S(2)}, u32[]{:S(2)}) async-start(bf16[16,16,1024]{2,1,0:T(8,128)(2,1)} %bitcast.18), calls=%async_computation.3 | async-start | bytes 1048576 | tf_op jit(solution)/shard_map/all_to_all | solution.py:82
  207.0 1.4 collective-permute-done.35
  208.5 2.6 %convolution_convert_fusion = bf16[1024,1024]{1,0:T(8,128)(2,1)} fusion(bf16[256,1024]{1,0:T(8,128)(2,1)S(1)} %bitcast.90, bf16[256,1024]{1,0:T(8,128)(2,1)S(1)} %bitcast.93, bf16[256,512]{1,0:T(8,128)(2,1)S(1)} %get-tuple-element.64, bf16[256,512]{1,0:T(8,128)(2,1)S(1)} %get-tuple-element.63, bf16[256,512]{1,0:T(8,128)(2,1)S(1)} %get-tuple-element.62, ...), kind=kOutput, calls=%fused_computation.2 | convolution fusion | flops 1081081856 | bytes 4194304 | tf_op jit(solution)/shard_map/dot_general | solution.py:26
  211.1 11.5 %all-to-all-done.3 = bf16[16,16,1024]{2,1,0:T(8,128)(2,1)S(1)} async-done(((bf16[16,16,1024]{2,1,0:T(8,128)(2,1)}), bf16[16,16,1024]{2,1,0:T(8,128)(2,1)S(1)}, u32[]{:S(2)}, u32[]{:S(2)}) %all-to-all-start.3) | async-done | bytes 524320 | tf_op jit(solution)/shard_map/all_to_all | solution.py:82
  222.8 5.4 %collective-permute-done.36 = bf16[16,1024]{1,0:T(8,128)(2,1)S(1)} collective-permute-done((bf16[16,1024]{1,0:T(8,128)(2,1)S(1)}, bf16[16,1024]{1,0:T(8,128)(2,1)S(1)}, u32[]{:S(2)}, u32[]{:S(2)}) %collective-permute-start.36) | collective-permute-done | bytes 32800 | tf_op jit(solution)/shard_map/ppermute | solution.py:197
  (113 shorter events, 11.1 us)
Async XLA Ops:
  2.3 26.4 %all-to-all-start = ((bf16[16,16,1024]{2,1,0:T(8,128)(2,1)}), bf16[16,16,1024]{2,1,0:T(8,128)(2,1)S(1)}, u32[]{:S(2)}, u32[]{:S(2)}) async-start(bf16[16,16,1024]{2,1,0:T(8,128)(2,1)} %broadcast_in_dim.10), calls=%async_computation | async-start | bytes 1048576 | tf_op jit(solution)/shard_map/all_to_all | solution.py:93
  14.8 3.6 %copy-start = (bf16[1,1024,1024]{2,1,0:T(8,128)(2,1)S(1)}, bf16[1,1024,1024]{2,1,0:T(8,128)(2,1)}, u32[]{:S(2)}) copy-start(bf16[1,1024,1024]{2,1,0:T(8,128)(2,1)} %param.6) | copy-start | bytes 6291460
  14.8 27.9 %collective-permute-start = (bf16[512,1024]{1,0:T(8,128)(2,1)}, bf16[512,1024]{1,0:T(8,128)(2,1)}, u32[]{:S(2)}, u32[]{:S(2)}) collective-permute-start(bf16[512,1024]{1,0:T(8,128)(2,1)} %get-tuple-element.60), channel_id=1, source_target_pairs={{0,192},{64,128},{1,193},{65,129},{2,194},{66,130},{3,195},{67,131... | collective-permute-start | bytes 3145736 | tf_op jit(solution)/shard_map/ppermute | solution.py:47
  17.5 0.8 copy-start.9
  17.5 37.3 %copy-start.7 = (bf16[16,1,16,1024]{3,2,1,0:T(8,128)(2,1)}, bf16[16,1,16,1024]{3,2,1,0:T(8,128)(2,1)S(1)}, u32[]{:S(2)}) copy-start(bf16[16,1,16,1024]{3,2,1,0:T(8,128)(2,1)S(1)} %get-tuple-element.65) | copy-start | bytes 1572868
  19.5 1.7 collective-permute-start.11
  23.6 20.8 %collective-permute-start.14 = (bf16[256,512]{1,0:T(8,128)(2,1)}, bf16[256,512]{1,0:T(8,128)(2,1)}, u32[]{:S(2)}, u32[]{:S(2)}) collective-permute-start(bf16[256,512]{1,0:T(8,128)(2,1)} %get-tuple-element.76), channel_id=1, source_target_pairs={{0,4},{2,6},{4,0},{6,2},{1,5},{3,7},{5,1},{7,3},{8,12},{10,14},{12... | collective-permute-start | bytes 786440 | tf_op jit(solution)/shard_map/ppermute | solution.py:76
  26.7 17.8 %collective-permute-start.13 = (bf16[256,512]{1,0:T(8,128)(2,1)}, bf16[256,512]{1,0:T(8,128)(2,1)}, u32[]{:S(2)}, u32[]{:S(2)}) collective-permute-start(bf16[256,512]{1,0:T(8,128)(2,1)} %get-tuple-element.76), channel_id=1, source_target_pairs={{0,6},{2,0},{4,2},{6,4},{1,7},{3,1},{5,3},{7,5},{8,14},{10,8},{12,... | collective-permute-start | bytes 786440 | tf_op jit(solution)/shard_map/ppermute | solution.py:76
  27.8 16.7 %collective-permute-start.12 = (bf16[256,512]{1,0:T(8,128)(2,1)}, bf16[256,512]{1,0:T(8,128)(2,1)}, u32[]{:S(2)}, u32[]{:S(2)}) collective-permute-start(bf16[256,512]{1,0:T(8,128)(2,1)} %get-tuple-element.76), channel_id=1, source_target_pairs={{0,2},{2,4},{4,6},{6,0},{1,3},{3,5},{5,7},{7,1},{8,10},{10,12},{12... | collective-permute-start | bytes 786440 | tf_op jit(solution)/shard_map/ppermute | solution.py:76
  28.7 15.8 %copy-start.13 = (f32[256,512]{1,0:T(8,128)S(1)}, f32[256,512]{1,0:T(8,128)}, u32[]{:S(2)}) copy-start(f32[256,512]{1,0:T(8,128)} %get-tuple-element.77) | copy-start | bytes 1572868
  44.4 4.8 %collective-permute-start.1 = (bf16[256,512]{1,0:T(8,128)(2,1)S(1)}, bf16[256,512]{1,0:T(8,128)(2,1)S(1)}, u32[]{:S(2)}, u32[]{:S(2)}) collective-permute-start(bf16[256,512]{1,0:T(8,128)(2,1)S(1)} %convolution_convert_fusion.6), channel_id=1, source_target_pairs={{0,1},{1,0},{2,3},{3,2},{4,5},{5,4},{6,7},{7,6},{8,9},{9,8},{10,11... | collective-permute-start | bytes 786440 | tf_op jit(solution)/shard_map/ppermute | solution.py:43
  44.5 4.6 %copy-start.1 = (bf16[1,1024,1024]{2,1,0:T(8,128)(2,1)S(1)}, bf16[1,1024,1024]{2,1,0:T(8,128)(2,1)}, u32[]{:S(2)}) copy-start(bf16[1,1024,1024]{2,1,0:T(8,128)(2,1)} %param.7) | copy-start | bytes 6291460
  46.8 21.7 %copy-start.3 = (f32[256,512]{1,0:T(8,128)}, f32[256,512]{1,0:T(8,128)S(1)}, u32[]{:S(2)}) copy-start(f32[256,512]{1,0:T(8,128)S(1)} %get-tuple-element.56) | copy-start | bytes 1572868
  46.8 20.9 %collective-permute-start.5 = (bf16[256,1024]{1,0:T(8,128)(2,1)S(1)}, bf16[256,1024]{1,0:T(8,128)(2,1)S(1)}, u32[]{:S(2)}, u32[]{:S(2)}) collective-permute-start(bf16[256,1024]{1,0:T(8,128)(2,1)S(1)} %bitcast.81), channel_id=1, source_target_pairs={{0,192},{64,128},{1,193},{65,129},{2,194},{66,130},{3,195},{67,131... | collective-permute-start | bytes 1572872 | tf_op jit(solution)/shard_map/ppermute | solution.py:47
  48.6 6.2 %collective-permute-start.16 = (bf16[256,512]{1,0:T(8,128)(2,1)S(1)}, bf16[256,512]{1,0:T(8,128)(2,1)S(1)}, u32[]{:S(2)}, u32[]{:S(2)}) collective-permute-start(bf16[256,512]{1,0:T(8,128)(2,1)S(1)} %convolution_convert_fusion.4), channel_id=1, source_target_pairs={{0,1},{1,0},{2,3},{3,2},{4,5},{5,4},{6,7},{7,6},{8,9},{9,8},{10,11... | collective-permute-start | bytes 786440 | tf_op jit(solution)/shard_map/ppermute | solution.py:43
  49.6 10.8 %collective-permute-start.4 = (bf16[256,512]{1,0:T(8,128)(2,1)S(1)}, bf16[256,512]{1,0:T(8,128)(2,1)S(1)}, u32[]{:S(2)}, u32[]{:S(2)}) collective-permute-start(bf16[256,512]{1,0:T(8,128)(2,1)S(1)} %get-tuple-element.74), channel_id=1, source_target_pairs={{0,4},{2,6},{4,0},{6,2},{1,5},{3,7},{5,1},{7,3},{8,12},{10,14},{12... | collective-permute-start | bytes 786440 | tf_op jit(solution)/shard_map/ppermute | solution.py:76
  52.7 13.4 %collective-permute-start.3 = (bf16[256,512]{1,0:T(8,128)(2,1)S(1)}, bf16[256,512]{1,0:T(8,128)(2,1)S(1)}, u32[]{:S(2)}, u32[]{:S(2)}) collective-permute-start(bf16[256,512]{1,0:T(8,128)(2,1)S(1)} %get-tuple-element.74), channel_id=1, source_target_pairs={{0,6},{2,0},{4,2},{6,4},{1,7},{3,1},{5,3},{7,5},{8,14},{10,8},{12,... | collective-permute-start | bytes 786440 | tf_op jit(solution)/shard_map/ppermute | solution.py:76
  53.9 13.7 %collective-permute-start.2 = (bf16[256,512]{1,0:T(8,128)(2,1)S(1)}, bf16[256,512]{1,0:T(8,128)(2,1)S(1)}, u32[]{:S(2)}, u32[]{:S(2)}) collective-permute-start(bf16[256,512]{1,0:T(8,128)(2,1)S(1)} %get-tuple-element.74), channel_id=1, source_target_pairs={{0,2},{2,4},{4,6},{6,0},{1,3},{3,5},{5,7},{7,1},{8,10},{10,12},{12... | collective-permute-start | bytes 786440 | tf_op jit(solution)/shard_map/ppermute | solution.py:76
  55.2 15.6 %collective-permute-start.19 = (bf16[256,512]{1,0:T(8,128)(2,1)S(1)}, bf16[256,512]{1,0:T(8,128)(2,1)S(1)}, u32[]{:S(2)}, u32[]{:S(2)}) collective-permute-start(bf16[256,512]{1,0:T(8,128)(2,1)S(1)} %get-tuple-element.78), channel_id=1, source_target_pairs={{0,4},{2,6},{4,0},{6,2},{1,5},{3,7},{5,1},{7,3},{8,12},{10,14},{12... | collective-permute-start | bytes 786440 | tf_op jit(solution)/shard_map/ppermute | solution.py:76
  60.4 16.1 %collective-permute-start.18 = (bf16[256,512]{1,0:T(8,128)(2,1)S(1)}, bf16[256,512]{1,0:T(8,128)(2,1)S(1)}, u32[]{:S(2)}, u32[]{:S(2)}) collective-permute-start(bf16[256,512]{1,0:T(8,128)(2,1)S(1)} %get-tuple-element.78), channel_id=1, source_target_pairs={{0,6},{2,0},{4,2},{6,4},{1,7},{3,1},{5,3},{7,5},{8,14},{10,8},{12,... | collective-permute-start | bytes 786440 | tf_op jit(solution)/shard_map/ppermute | solution.py:76
  66.1 10.4 %collective-permute-start.17 = (bf16[256,512]{1,0:T(8,128)(2,1)S(1)}, bf16[256,512]{1,0:T(8,128)(2,1)S(1)}, u32[]{:S(2)}, u32[]{:S(2)}) collective-permute-start(bf16[256,512]{1,0:T(8,128)(2,1)S(1)} %get-tuple-element.78), channel_id=1, source_target_pairs={{0,2},{2,4},{4,6},{6,0},{1,3},{3,5},{5,7},{7,1},{8,10},{10,12},{12... | collective-permute-start | bytes 786440 | tf_op jit(solution)/shard_map/ppermute | solution.py:76
  67.6 3.2 %copy-start.20 = (bf16[512,1024]{1,0:T(8,128)(2,1)S(1)}, bf16[512,1024]{1,0:T(8,128)(2,1)}, u32[]{:S(2)}) copy-start(bf16[512,1024]{1,0:T(8,128)(2,1)} %get-tuple-element.30) | copy-start | bytes 3145732
  67.7 8.9 %copy-start.5 = (bf16[256,1024]{1,0:T(8,128)(2,1)}, bf16[256,1024]{1,0:T(8,128)(2,1)S(1)}, u32[]{:S(2)}) copy-start(bf16[256,1024]{1,0:T(8,128)(2,1)S(1)} %collective-permute-done.5) | copy-start | bytes 1572868
  68.2 8.4 %collective-permute-start.6 = (bf16[256,512]{1,0:T(8,128)(2,1)S(1)}, bf16[256,512]{1,0:T(8,128)(2,1)S(1)}, u32[]{:S(2)}, u32[]{:S(2)}) collective-permute-start(bf16[256,512]{1,0:T(8,128)(2,1)S(1)} %convolution_convert_fusion.5), channel_id=1, source_target_pairs={{0,1},{1,0},{2,3},{3,2},{4,5},{5,4},{6,7},{7,6},{8,9},{9,8},{10,11... | collective-permute-start | bytes 786440 | tf_op jit(solution)/shard_map/ppermute | solution.py:43
  68.9 13.3 %collective-permute-start.15 = (bf16[256,512]{1,0:T(8,128)(2,1)S(1)}, bf16[256,512]{1,0:T(8,128)(2,1)S(1)}, u32[]{:S(2)}, u32[]{:S(2)}) collective-permute-start(bf16[256,512]{1,0:T(8,128)(2,1)S(1)} %multiply_convert_fusion.4), channel_id=1, source_target_pairs={{0,1},{1,0},{2,3},{3,2},{4,5},{5,4},{6,7},{7,6},{8,9},{9,8},{10,11... | collective-permute-start | bytes 786440 | tf_op jit(solution)/shard_map/ppermute | solution.py:43
  70.8 28.0 %collective-permute-start.10 = (bf16[512,1024]{1,0:T(8,128)(2,1)S(1)}, bf16[512,1024]{1,0:T(8,128)(2,1)}, u32[]{:S(2)}, u32[]{:S(2)}) collective-permute-start(bf16[512,1024]{1,0:T(8,128)(2,1)S(1)} %copy-done.20), channel_id=1, source_target_pairs={{0,192},{64,128},{1,193},{65,129},{2,194},{66,130},{3,195},{67,131... | collective-permute-start | bytes 3145736 | tf_op jit(solution)/shard_map/ppermute | solution.py:47
  77.2 11.8 %collective-permute-start.9 = (bf16[256,512]{1,0:T(8,128)(2,1)S(1)}, bf16[256,512]{1,0:T(8,128)(2,1)S(1)}, u32[]{:S(2)}, u32[]{:S(2)}) collective-permute-start(bf16[256,512]{1,0:T(8,128)(2,1)S(1)} %get-tuple-element.80), channel_id=1, source_target_pairs={{0,4},{2,6},{4,0},{6,2},{1,5},{3,7},{5,1},{7,3},{8,12},{10,14},{12... | collective-permute-start | bytes 786440 | tf_op jit(solution)/shard_map/ppermute | solution.py:76
  80.2 12.4 %collective-permute-start.8 = (bf16[256,512]{1,0:T(8,128)(2,1)S(1)}, bf16[256,512]{1,0:T(8,128)(2,1)S(1)}, u32[]{:S(2)}, u32[]{:S(2)}) collective-permute-start(bf16[256,512]{1,0:T(8,128)(2,1)S(1)} %get-tuple-element.80), channel_id=1, source_target_pairs={{0,6},{2,0},{4,2},{6,4},{1,7},{3,1},{5,3},{7,5},{8,14},{10,8},{12,... | collective-permute-start | bytes 786440 | tf_op jit(solution)/shard_map/ppermute | solution.py:76
  81.4 11.2 %collective-permute-start.7 = (bf16[256,512]{1,0:T(8,128)(2,1)S(1)}, bf16[256,512]{1,0:T(8,128)(2,1)S(1)}, u32[]{:S(2)}, u32[]{:S(2)}) collective-permute-start(bf16[256,512]{1,0:T(8,128)(2,1)S(1)} %get-tuple-element.80), channel_id=1, source_target_pairs={{0,2},{2,4},{4,6},{6,0},{1,3},{3,5},{5,7},{7,1},{8,10},{10,12},{12... | collective-permute-start | bytes 786440 | tf_op jit(solution)/shard_map/ppermute | solution.py:76
  82.2 1.0 copy-start.15
  83.2 20.2 %collective-permute-start.21 = (bf16[256,1024]{1,0:T(8,128)(2,1)S(1)}, bf16[256,1024]{1,0:T(8,128)(2,1)S(1)}, u32[]{:S(2)}, u32[]{:S(2)}) collective-permute-start(bf16[256,1024]{1,0:T(8,128)(2,1)S(1)} %fusion.1), channel_id=1, source_target_pairs={{192,0},{128,64},{193,1},{129,65},{194,2},{130,66},{195,3},{131,67... | collective-permute-start | bytes 1572872 | tf_op jit(solution)/shard_map/ppermute | solution.py:51
  100.0 2.8 %copy-start.11 = (bf16[256,512]{1,0:T(8,128)(2,1)}, bf16[256,512]{1,0:T(8,128)(2,1)S(1)}, u32[]{:S(2)}) copy-start(bf16[256,512]{1,0:T(8,128)(2,1)S(1)} %get-tuple-element.73) | copy-start | bytes 786436
  100.0 3.3 %collective-permute-start.20 = (bf16[256,512]{1,0:T(8,128)(2,1)S(1)}, bf16[256,512]{1,0:T(8,128)(2,1)S(1)}, u32[]{:S(2)}, u32[]{:S(2)}) collective-permute-start(bf16[256,512]{1,0:T(8,128)(2,1)S(1)} %get-tuple-element.73), channel_id=1, source_target_pairs={{0,1},{1,0},{2,3},{3,2},{4,5},{5,4},{6,7},{7,6},{8,9},{9,8},{10,11... | collective-permute-start | bytes 786440 | tf_op jit(solution)/shard_map/ppermute | solution.py:43
  101.5 35.2 %collective-permute-start.23 = (bf16[512,1024]{1,0:T(8,128)(2,1)}, bf16[512,1024]{1,0:T(8,128)(2,1)}, u32[]{:S(2)}, u32[]{:S(2)}) collective-permute-start(bf16[512,1024]{1,0:T(8,128)(2,1)} %get-tuple-element.38), channel_id=1, source_target_pairs={{0,192},{64,128},{1,193},{65,129},{2,194},{66,130},{3,195},{67,131... | collective-permute-start | bytes 3145736 | tf_op jit(solution)/shard_map/ppermute | solution.py:47
  103.3 33.5 %copy-start.21 = (bf16[32,1024]{1,0:T(8,128)(2,1)S(1)}, bf16[32,1024]{1,0:T(8,128)(2,1)}, u32[]{:S(2)}) copy-start(bf16[32,1024]{1,0:T(8,128)(2,1)} %param.5) | copy-start | bytes 196612
  103.4 1.3 copy-start.17
  104.7 32.1 %all-to-all-start.1 = ((bf16[16,16,1024]{2,1,0:T(8,128)(2,1)}), bf16[16,16,1024]{2,1,0:T(8,128)(2,1)S(1)}, u32[]{:S(2)}, u32[]{:S(2)}) async-start(bf16[16,16,1024]{2,1,0:T(8,128)(2,1)} %bitcast.12), calls=%async_computation.1 | async-start | bytes 1048576 | tf_op jit(solution)/shard_map/all_to_all | solution.py:82
  112.8 23.3 %collective-permute-start.22 = (bf16[256,512]{1,0:T(8,128)(2,1)}, bf16[256,512]{1,0:T(8,128)(2,1)S(1)}, u32[]{:S(2)}, u32[]{:S(2)}) collective-permute-start(bf16[256,512]{1,0:T(8,128)(2,1)} %get-tuple-element.37), channel_id=1, source_target_pairs={{0,192},{64,128},{1,193},{65,129},{2,194},{66,130},{3,195},{67,131... | collective-permute-start | bytes 786440 | tf_op jit(solution)/shard_map/ppermute | solution.py:47
  114.0 31.8 %collective-permute-start.25 = (bf16[256,512]{1,0:T(8,128)(2,1)}, bf16[256,512]{1,0:T(8,128)(2,1)}, u32[]{:S(2)}, u32[]{:S(2)}) collective-permute-start(bf16[256,512]{1,0:T(8,128)(2,1)} %get-tuple-element.55), channel_id=1, source_target_pairs={{0,1},{1,0},{2,3},{3,2},{4,5},{5,4},{6,7},{7,6},{8,9},{9,8},{10,11... | collective-permute-start | bytes 786440 | tf_op jit(solution)/shard_map/ppermute | solution.py:43
  137.7 23.2 %all-to-all-start.2 = ((bf16[16,16,1024]{2,1,0:T(8,128)(2,1)}), bf16[16,16,1024]{2,1,0:T(8,128)(2,1)S(1)}, u32[]{:S(2)}, u32[]{:S(2)}) async-start(bf16[16,16,1024]{2,1,0:T(8,128)(2,1)} %broadcast_in_dim.22), calls=%async_computation.2 | async-start | bytes 1048576 | tf_op jit(solution)/shard_map/all_to_all | solution.py:93
  146.9 6.1 %collective-permute-start.26 = (bf16[256,512]{1,0:T(8,128)(2,1)}, bf16[256,512]{1,0:T(8,128)(2,1)S(1)}, u32[]{:S(2)}, u32[]{:S(2)}) collective-permute-start(bf16[256,512]{1,0:T(8,128)(2,1)} %get-tuple-element.71), channel_id=1, source_target_pairs={{0,1},{1,0},{2,3},{3,2},{4,5},{5,4},{6,7},{7,6},{8,9},{9,8},{10,11... | collective-permute-start | bytes 786440 | tf_op jit(solution)/shard_map/ppermute | solution.py:43
  147.0 6.0 %copy-start.19 = (bf16[256,512]{1,0:T(8,128)(2,1)S(1)}, bf16[256,512]{1,0:T(8,128)(2,1)}, u32[]{:S(2)}) copy-start(bf16[256,512]{1,0:T(8,128)(2,1)} %get-tuple-element.71) | copy-start | bytes 786436
  147.0 29.1 %collective-permute-start.32 = (bf16[512,1024]{1,0:T(8,128)(2,1)}, bf16[512,1024]{1,0:T(8,128)(2,1)}, u32[]{:S(2)}, u32[]{:S(2)}) collective-permute-start(bf16[512,1024]{1,0:T(8,128)(2,1)} %get-tuple-element.46), channel_id=1, source_target_pairs={{0,192},{64,128},{1,193},{65,129},{2,194},{66,130},{3,195},{67,131... | collective-permute-start | bytes 3145736 | tf_op jit(solution)/shard_map/ppermute | solution.py:47
  160.9 23.5 %collective-permute-start.31 = (bf16[256,1024]{1,0:T(8,128)(2,1)S(1)}, bf16[256,1024]{1,0:T(8,128)(2,1)S(1)}, u32[]{:S(2)}, u32[]{:S(2)}) collective-permute-start(bf16[256,1024]{1,0:T(8,128)(2,1)S(1)} %bitcast.84), channel_id=1, source_target_pairs={{192,0},{128,64},{193,1},{129,65},{194,2},{130,66},{195,3},{131,67... | collective-permute-start | bytes 1572872 | tf_op jit(solution)/shard_map/ppermute | solution.py:51
  164.0 14.7 %collective-permute-start.27 = (bf16[256,512]{1,0:T(8,128)(2,1)S(1)}, bf16[256,512]{1,0:T(8,128)(2,1)S(1)}, u32[]{:S(2)}, u32[]{:S(2)}) collective-permute-start(bf16[256,512]{1,0:T(8,128)(2,1)S(1)} %convolution_convert_fusion.3), channel_id=1, source_target_pairs={{0,1},{1,0},{2,3},{3,2},{4,5},{5,4},{6,7},{7,6},{8,9},{9,8},{10,11... | collective-permute-start | bytes 786440 | tf_op jit(solution)/shard_map/ppermute | solution.py:43
  164.3 14.3 %copy-start.2 = (bf16[1024,1024]{1,0:T(8,128)(2,1)S(1)}, bf16[1024,1024]{1,0:T(8,128)(2,1)}, u32[]{:S(2)}) copy-start(bf16[1024,1024]{1,0:T(8,128)(2,1)} %maximum_select_fusion) | copy-start | bytes 6291460
  178.6 5.8 %copy-start.6 = (bf16[256,1024]{1,0:T(8,128)(2,1)S(1)}, bf16[256,1024]{1,0:T(8,128)(2,1)}, u32[]{:S(2)}) copy-start(bf16[256,1024]{1,0:T(8,128)(2,1)} %copy-done.5) | copy-start | bytes 1572868
  178.6 5.8 %copy-start.14 = (bf16[512,1024]{1,0:T(8,128)(2,1)S(1)}, bf16[512,1024]{1,0:T(8,128)(2,1)}, u32[]{:S(2)}) copy-start(bf16[512,1024]{1,0:T(8,128)(2,1)} %maximum_maximum_fusion) | copy-start | bytes 3145732
  179.2 10.8 %collective-permute-start.30 = (bf16[256,512]{1,0:T(8,128)(2,1)S(1)}, bf16[256,512]{1,0:T(8,128)(2,1)S(1)}, u32[]{:S(2)}, u32[]{:S(2)}) collective-permute-start(bf16[256,512]{1,0:T(8,128)(2,1)S(1)} %get-tuple-element.82), channel_id=1, source_target_pairs={{0,4},{2,6},{4,0},{6,2},{1,5},{3,7},{5,1},{7,3},{8,12},{10,14},{12... | collective-permute-start | bytes 786440 | tf_op jit(solution)/shard_map/ppermute | solution.py:76
  182.4 12.1 %collective-permute-start.29 = (bf16[256,512]{1,0:T(8,128)(2,1)S(1)}, bf16[256,512]{1,0:T(8,128)(2,1)S(1)}, u32[]{:S(2)}, u32[]{:S(2)}) collective-permute-start(bf16[256,512]{1,0:T(8,128)(2,1)S(1)} %get-tuple-element.82), channel_id=1, source_target_pairs={{0,6},{2,0},{4,2},{6,4},{1,7},{3,1},{5,3},{7,5},{8,14},{10,8},{12,... | collective-permute-start | bytes 786440 | tf_op jit(solution)/shard_map/ppermute | solution.py:76
  183.5 11.0 %collective-permute-start.28 = (bf16[256,512]{1,0:T(8,128)(2,1)S(1)}, bf16[256,512]{1,0:T(8,128)(2,1)S(1)}, u32[]{:S(2)}, u32[]{:S(2)}) collective-permute-start(bf16[256,512]{1,0:T(8,128)(2,1)S(1)} %get-tuple-element.82), channel_id=1, source_target_pairs={{0,2},{2,4},{4,6},{6,0},{1,3},{3,5},{5,7},{7,1},{8,10},{10,12},{12... | collective-permute-start | bytes 786440 | tf_op jit(solution)/shard_map/ppermute | solution.py:76
  187.1 7.6 %copy-start.4 = (f32[256,512]{1,0:T(8,128)S(1)}, f32[256,512]{1,0:T(8,128)}, u32[]{:S(2)}) copy-start(f32[256,512]{1,0:T(8,128)} %copy-done.3) | copy-start | bytes 1572868
  187.1 7.6 %copy-start.23 = (bf16[256,512]{1,0:T(8,128)(2,1)S(1)}, bf16[256,512]{1,0:T(8,128)(2,1)}, u32[]{:S(2)}) copy-start(bf16[256,512]{1,0:T(8,128)(2,1)} %copy-done.22) | copy-start | bytes 786436
  195.1 2.1 collective-permute-start.33
  195.2 11.6 %collective-permute-start.34 = (bf16[256,512]{1,0:T(8,128)(2,1)S(1)}, bf16[256,512]{1,0:T(8,128)(2,1)S(1)}, u32[]{:S(2)}, u32[]{:S(2)}) collective-permute-start(bf16[256,512]{1,0:T(8,128)(2,1)S(1)} %multiply_convert_fusion), channel_id=1, source_target_pairs={{192,0},{128,64},{193,1},{129,65},{194,2},{130,66},{195,3},{131,67... | collective-permute-start | bytes 786440 | tf_op jit(solution)/shard_map/ppermute | solution.py:51
  197.1 9.8 %copy-start.16 = (bf16[256,512]{1,0:T(8,128)(2,1)S(1)}, bf16[256,512]{1,0:T(8,128)(2,1)}, u32[]{:S(2)}) copy-start(bf16[256,512]{1,0:T(8,128)(2,1)} %copy-done.15) | copy-start | bytes 786436
  197.1 11.3 %copy-start.12 = (bf16[256,512]{1,0:T(8,128)(2,1)S(1)}, bf16[256,512]{1,0:T(8,128)(2,1)}, u32[]{:S(2)}) copy-start(bf16[256,512]{1,0:T(8,128)(2,1)} %copy-done.11) | copy-start | bytes 786436
  197.1 11.3 %copy-start.18 = (bf16[256,512]{1,0:T(8,128)(2,1)S(1)}, bf16[256,512]{1,0:T(8,128)(2,1)}, u32[]{:S(2)}) copy-start(bf16[256,512]{1,0:T(8,128)(2,1)} %copy-done.17) | copy-start | bytes 786436
  198.5 10.0 %copy-start.8 = (bf16[16,1,16,1024]{3,2,1,0:T(8,128)(2,1)S(1)}, bf16[16,1,16,1024]{3,2,1,0:T(8,128)(2,1)}, u32[]{:S(2)}) copy-start(bf16[16,1,16,1024]{3,2,1,0:T(8,128)(2,1)} %copy-done.7) | copy-start | bytes 1572868
  198.5 10.0 %copy-start.10 = (bf16[16,1,16,1024]{3,2,1,0:T(8,128)(2,1)S(1)}, bf16[16,1,16,1024]{3,2,1,0:T(8,128)(2,1)}, u32[]{:S(2)}) copy-start(bf16[16,1,16,1024]{3,2,1,0:T(8,128)(2,1)} %copy-done.9) | copy-start | bytes 1572868
  198.5 24.1 %all-to-all-start.3 = ((bf16[16,16,1024]{2,1,0:T(8,128)(2,1)}), bf16[16,16,1024]{2,1,0:T(8,128)(2,1)S(1)}, u32[]{:S(2)}, u32[]{:S(2)}) async-start(bf16[16,16,1024]{2,1,0:T(8,128)(2,1)} %bitcast.18), calls=%async_computation.3 | async-start | bytes 1048576 | tf_op jit(solution)/shard_map/all_to_all | solution.py:82
  206.8 15.9 %collective-permute-start.24 = (bf16[16,1024]{1,0:T(8,128)(2,1)S(1)}, bf16[16,1024]{1,0:T(8,128)(2,1)S(1)}, u32[]{:S(2)}, u32[]{:S(2)}) collective-permute-start(bf16[16,1024]{1,0:T(8,128)(2,1)S(1)} %add_convert_fusion.1), channel_id=1, source_target_pairs={{0,128},{128,0},{1,129},{129,1},{2,130},{130,2},{3,131},{131,3},{4... | collective-permute-start | bytes 98312 | tf_op jit(solution)/shard_map/ppermute | solution.py:196
  206.8 1.6 collective-permute-start.35
  222.7 5.5 %collective-permute-start.36 = (bf16[16,1024]{1,0:T(8,128)(2,1)S(1)}, bf16[16,1024]{1,0:T(8,128)(2,1)S(1)}, u32[]{:S(2)}, u32[]{:S(2)}) collective-permute-start(bf16[16,1024]{1,0:T(8,128)(2,1)S(1)} %get-tuple-element.54), channel_id=1, source_target_pairs={{0,128},{128,0},{1,129},{129,1},{2,130},{130,2},{3,131},{131,3},{4... | collective-permute-start | bytes 98312 | tf_op jit(solution)/shard_map/ppermute | solution.py:197
  (1 other events, 0.7 us)

commit v5 on v4

--- a/solution.py
+++ b/solution.py
@@ -35,10 +35,6 @@
     return lax.optimization_barrier(values)
 
 
-def after(value, *others):
-    return together(value, *others)[0]
-
-
 def other_core(block):
     return lax.ppermute(block, "core", [(0, 1), (1, 0)])
 
@@ -67,14 +63,15 @@
     )
 
 
-def narrow_total(mine, theirs):
+def narrow_terms(mine, theirs):
     pair = mine + other_core(theirs.astype(jnp.bfloat16)).astype(jnp.float32)
     sent = pair.astype(jnp.bfloat16)
-    total = pair
-    for distance in (1, 3, 2):
-        route = [(i, (i + distance) % X) for i in range(X)]
-        total = total + lax.ppermute(sent, "x", route).astype(jnp.float32)
-    return total
+    routes = [[(i, (i + distance) % X) for i in range(X)] for distance in (1, 3, 2)]
+    return [pair] + [lax.ppermute(sent, "x", route) for route in routes]
+
+
+def add_terms(terms):
+    return sum(term.astype(jnp.float32) for term in terms)
 
 
 def spread_wide(partial):
@@ -98,7 +95,7 @@
 def back_total(whole, down_halves):
     theirs = contract(whole, down_halves[1], 1, 1)
     mine = contract(whole, down_halves[0], 1, 1)
-    return narrow_total(mine, theirs)
+    return add_terms(narrow_terms(mine, theirs))
 
 
 def slope_of(total, slopes):
@@ -118,62 +115,49 @@
     def pick(upper, lower):
         return jnp.where(is_upper, upper, lower)
 
-    tokens = saved_inputs.shape[1]
-    part = upstream.shape[0] // 2
-    by_part = saved_inputs[0].reshape(WIDE, 2, part, -1)
-    saved = [by_part[:, c].reshape(tokens // 2, -1) for c in range(2)]
+    def by_part(block):
+        rows, cols = block.shape
+        split = block.reshape(WIDE, 2, rows // (2 * WIDE), cols)
+        return [split[:, c].reshape(rows // 2, cols) for c in range(2)]
+
     w_up, w_down = up_weight[0], down_weight[0]
     up_halves, down_halves = halves(w_up, 1), halves(w_down, 0)
-
-    half = w_down.shape[0] // 2
-    down_pieces = [to_upper(w_down[:half])]
-
-    early, late = upstream[:part], upstream[part:]
-    gathered = gather_wide(pick(early, late))
-
-    def pre_total(rows):
-        theirs = contract(rows, up_halves[1], 1, 0)
-        mine = contract(rows, up_halves[0], 1, 0)
-        return narrow_total(mine, theirs)
-
-    hidden, slopes = [], []
-
-    def keep(total):
-        act, slope = gelu_parts(total)
-        act = act.astype(jnp.bfloat16)
-        hidden.append((act, other_core(act)))
-        slopes.append(slope)
-
-    keep(pre_total(saved[0]))
-    gathered, *down_pieces = together(gathered, *down_pieces)
-    top_total = back_total(gathered, down_halves)
-    top_total, top_rest = together(top_total, to_upper(gathered))
-    top_slope = slope_of(top_total, slopes[0])
-    top_slope, late_total = together(top_slope, pre_total(after(saved[1], gathered)))
-    keep(late_total)
+    saved = by_part(saved_inputs[0])
+    first, last = slice(0, saved[0].shape[0]), slice(saved[0].shape[0], None)
+
+    sent_down = to_upper(w_down)
+
+    theirs = jnp.concatenate([contract(rows, up_halves[1], 1, 0) for rows in saved], axis=0)
+    mine = jnp.concatenate([contract(rows, up_halves[0], 1, 0) for rows in saved], axis=0)
+    pre = narrow_terms(mine, theirs)
+    gathered, pre[1], pre[2] = together(gather_wide(upstream), pre[1], pre[2])
+    act, slopes = gelu_parts(add_terms(pre))
+    act = act.astype(jnp.bfloat16)
+    hidden = in_order(act, other_core(act))
+
+    top = by_part(gathered)
+    top_slope = slope_of(back_total(top[0], down_halves), slopes[first])
     moved = to_lower(back_through_up(top_slope, up_halves))
-    rest_total = back_total(top_rest, down_halves)
-    rest_total, piece = together(rest_total, to_upper(after(w_down[half:], top_rest)))
-    down_pieces.append(piece)
-    top_slope_rest = slope_of(rest_total, slopes[1])
-    partial = pick(back_through_up(top_slope_rest, up_halves), moved)
-    blocks, lower_slopes, *up_pieces = together(
-        spread_wide(partial),
-        to_upper(after(slopes[1].astype(jnp.bfloat16), rest_total)),
-        to_upper(after(w_up[:half], rest_total)),
-    )
-    lower_slopes = pick(lower_slopes.astype(jnp.float32), slopes[0])
-    middle = (pick(late, early).astype(jnp.float32) + add_blocks(blocks)).astype(jnp.bfloat16)
-    up_pieces.append(to_upper(after(w_up[half:], blocks)))
-
-    hidden = jnp.concatenate([in_order(*block) for block in hidden], axis=0)
-    low_down = pick(jnp.concatenate(down_pieces, axis=0), w_down)
-    low, hidden, low_down = together(gather_wide(middle), hidden, low_down)
+    late_slopes, _ = together(slopes[last], top_slope[0])
+    top_slope_rest = slope_of(back_total(top[1], down_halves), late_slopes)
+    blocks = spread_wide(pick(back_through_up(top_slope_rest, up_halves), moved))
+    sent_up = to_upper(together(w_up, sent_down)[0])
+    part = upstream.shape[0] // 2
+    middle = (
+        pick(upstream[part:], upstream[:part]).astype(jnp.float32) + add_blocks(blocks)
+    ).astype(jnp.bfloat16)
+
+    low_down = pick(sent_down, w_down)
+    low_up = pick(sent_up, w_up)
+    lower_slopes = to_upper(slopes[last].astype(jnp.bfloat16))
+    low, hidden, low_down, lower_slopes = together(
+        gather_wide(middle), hidden, low_down, lower_slopes
+    )
+    lower_slopes = pick(lower_slopes.astype(jnp.float32), slopes[first])
     low_rest = to_lower(low)
     low_total = back_total(low, halves(low_down, 0))
-    incoming = jnp.concatenate([pick(gathered, low), pick(top_rest, low_rest)], axis=0)
+    incoming = jnp.concatenate([pick(top[0], low), pick(top[1], low_rest)], axis=0)
     grad_down = contract(hidden, incoming, 0, 0).astype(jnp.bfloat16)
-    low_up = pick(jnp.concatenate(up_pieces, axis=0), w_up)
     low_total, grad_down, low_up = together(low_total, grad_down, low_up)
     low_slope = slope_of(low_total, lower_slopes)
     low_slope_rest = to_lower(low_slope[0])

time: 230 us -> 211 us (0.917)
  starting transfers between devices: 78.2 us -> 59.7 us
  waiting for transfers between devices: 105 us -> 98.9 us
  other arithmetic: 16 us -> 20.2 us
  matrix products: 19.6 us -> 22.7 us
    ppermute x6 -> x3, waiting for transfers between devices: 53.7 us -> 25.4 us  [to_upper(): return lax.ppermute(block, CROSS_AXES, [(0, 3), (1, 2)])]
    ppermute x15 -> x12, waiting for transfers between devices: 24.1 us -> 40.2 us  [narrow_terms(): return [pair] + [lax.ppermute(sent, 'x', route) for route in routes]]
    all_to_all x2, waiting for transfers between devices: 11.5 us -> 20.3 us  [spread_wide(): lax.all_to_all(partial.reshape(WIDE, rows // WIDE, cols), WIDE_AXES, 0, 0...]
    ppermute x15 -> x12, starting transfers between devices: 25.4 us -> 19.8 us  [narrow_terms(): return [pair] + [lax.ppermute(sent, 'x', route) for route in routes]]
    all_to_all x2, waiting for transfers between devices: 6.74 us -> 1.52 us  [gather_wide(): lax.all_to_all(jnp.broadcast_to(block[None], (WIDE, rows, cols)), WIDE_AX...]
    ppermute x6 -> x3, starting transfers between devices: 7.96 us -> 3.85 us  [to_upper(): return lax.ppermute(block, CROSS_AXES, [(0, 3), (1, 2)])]
    ppermute x3, waiting for transfers between devices: 0.01 us -> 3.33 us  [to_lower(): return lax.ppermute(block, CROSS_AXES, [(3, 0), (2, 1)])]
    dot_general x18, matrix products: 19.6 us -> 22.7 us  [contract(): lax.dot_general(first_op, second_op, (((first_dim,), (second_dim,)), ((),...]
  transfers between devices with their start and end apart: 41 -> 33, of which waited for: 16 -> 21; matrix products, arithmetic and copies ran while one was open for 18% -> 21% of each run, Pallas kernels for 0% -> 0%
where the time goes in v5:
time: 211 us; the launch traced here: 210 us
  waiting for transfers between devices  98.9 us (47%)
  starting transfers between devices  59.7 us (28%)
  matrix products  22.7 us (11%)
  other arithmetic  20.2 us (10%)
  local copies, waits for them, and re-layouts  7.34 us (3%)
    ppermute x12, waiting for transfers between devices, narrow_terms(): return [pair] + [lax.ppermute(sent, 'x', route) for route in routes]  40.2 us
    ppermute x3, waiting for transfers between devices, to_upper(): return lax.ppermute(block, CROSS_AXES, [(0, 3), (1, 2)])  25.4 us
    dot_general x18, matrix products, contract(): lax.dot_general(first_op, second_op, (((first_dim,), (second_dim,)), ((),...  22.7 us
    all_to_all x2, waiting for transfers between devices, spread_wide(): lax.all_to_all(partial.reshape(WIDE, rows // WIDE, cols), WIDE_AXES, 0, 0...  20.3 us
    ppermute x12, starting transfers between devices, narrow_terms(): return [pair] + [lax.ppermute(sent, 'x', route) for route in routes]  19.8 us
    all_to_all x2, starting transfers between devices, gather_wide(): lax.all_to_all(jnp.broadcast_to(block[None], (WIDE, rows, cols)), WIDE_AX...  14.5 us
    all_to_all x2, starting transfers between devices, spread_wide(): lax.all_to_all(partial.reshape(WIDE, rows // WIDE, cols), WIDE_AXES, 0, 0...  14 us
    select_n x6, other arithmetic, pick(): return jnp.where(is_upper, upper, lower)  8.1 us
  transfers between devices with their start and end apart: 33, of which 21 were waited for; matrix products, arithmetic and copies ran while one was open for 21% of the time, Pallas kernels for 0%

profile of v5, /device:TPU:56, one launch (start us, length us, event | category | flops | bytes accessed | tf_op | source)
XLA Modules:
  0.0 210.1 jit_solution(18196177321743738686)
XLA Ops:
  0.6 1.9 broadcast_in_dim.10
  2.6 9.6 %all-to-all-start = ((bf16[16,32,1024]{2,1,0:T(8,128)(2,1)}), bf16[16,32,1024]{2,1,0:T(8,128)(2,1)}, u32[]{:S(2)}, u32[]{:S(2)}) async-start(bf16[16,32,1024]{2,1,0:T(8,128)(2,1)} %broadcast_in_dim.10), calls=%async_computation | async-start | bytes 2097152 | tf_op jit(solution)/shard_map/all_to_all | solution.py:90
  12.2 1.3 fusion.80
  14.4 0.8 pad_maximum_fusion.1
  15.3 1.5 convolution_bitcast_fusion
  17.5 1.2 fusion.57
  18.8 2.8 %collective-permute-start.2 = (bf16[512,512]{1,0:T(8,128)(2,1)S(1)}, bf16[512,512]{1,0:T(8,128)(2,1)}, u32[]{:S(2)}, u32[]{:S(2)}) collective-permute-start(bf16[512,512]{1,0:T(8,128)(2,1)S(1)} %fusion.57), channel_id=1, source_target_pairs={{0,6},{2,0},{4,2},{6,4},{1,7},{3,1},{5,3},{7,5},{8,14},{10,8},{12,... | collective-permute-start | bytes 1572872 | tf_op jit(solution)/shard_map/ppermute | solution.py:70
  21.6 11.8 %collective-permute-done.2 = bf16[512,512]{1,0:T(8,128)(2,1)} collective-permute-done((bf16[512,512]{1,0:T(8,128)(2,1)S(1)}, bf16[512,512]{1,0:T(8,128)(2,1)}, u32[]{:S(2)}, u32[]{:S(2)}) %collective-permute-start.2) | collective-permute-done | bytes 524320 | tf_op jit(solution)/shard_map/ppermute | solution.py:70
  33.4 3.5 %collective-permute-done.1 = bf16[512,512]{1,0:T(8,128)(2,1)} collective-permute-done((bf16[512,512]{1,0:T(8,128)(2,1)S(1)}, bf16[512,512]{1,0:T(8,128)(2,1)}, u32[]{:S(2)}, u32[]{:S(2)}) %collective-permute-start.1) | collective-permute-done | bytes 524320 | tf_op jit(solution)/shard_map/ppermute | solution.py:70
  36.9 1.5 all-to-all-done
  38.5 1.4 fusion.78
  39.8 1.9 convolution_convert_fusion.5
  41.9 3.1 %collective-permute-start.7 = (bf16[512,512]{1,0:T(8,128)(2,1)S(1)}, bf16[512,512]{1,0:T(8,128)(2,1)S(1)}, u32[]{:S(2)}, u32[]{:S(2)}) collective-permute-start(bf16[512,512]{1,0:T(8,128)(2,1)S(1)} %copy-done.20), channel_id=1, source_target_pairs={{0,4},{2,6},{4,0},{6,2},{1,5},{3,7},{5,1},{7,3},{8,12},{10,14},{12... | collective-permute-start | bytes 1572872 | tf_op jit(solution)/shard_map/ppermute | solution.py:70
  45.0 1.3 collective-permute-start.17
  46.3 1.8 convolution_convert_fusion.6
  48.3 1.7 fusion.59
  50.6 2.8 %collective-permute-start.10 = (bf16[256,512]{1,0:T(8,128)(2,1)S(1)}, bf16[256,512]{1,0:T(8,128)(2,1)S(1)}, u32[]{:S(2)}, u32[]{:S(2)}) collective-permute-start(bf16[256,512]{1,0:T(8,128)(2,1)S(1)} %get-tuple-element.47), channel_id=1, source_target_pairs={{0,6},{2,0},{4,2},{6,4},{1,7},{3,1},{5,3},{7,5},{8,14},{10,8},{12,... | collective-permute-start | bytes 786440 | tf_op jit(solution)/shard_map/ppermute | solution.py:70
  53.4 4.8 %collective-permute-done.7 = bf16[512,512]{1,0:T(8,128)(2,1)S(1)} collective-permute-done((bf16[512,512]{1,0:T(8,128)(2,1)S(1)}, bf16[512,512]{1,0:T(8,128)(2,1)S(1)}, u32[]{:S(2)}, u32[]{:S(2)}) %collective-permute-start.7) | collective-permute-done | bytes 524320 | tf_op jit(solution)/shard_map/ppermute | solution.py:70
  58.2 1.6 collective-permute-start.9
  59.8 3.1 %multiply_convert_fusion = (bf16[512,512]{1,0:T(8,128)(2,1)}, f32[512,512]{1,0:T(8,128)S(1)}) fusion(bf16[512,512]{1,0:T(8,128)(2,1)S(1)} %collective-permute-done.7, bf16[512,512]{1,0:T(8,128)(2,1)} %collective-permute-done.2, bf16[512,512]{1,0:T(8,128)(2,1)} %collective-permute-done.1, bf16[512,512]{1,0:T(8,128)(2,1)} %collective-permute-done, ...), kind=kLoop, calls=%fused_computation.65 | loop fusion | flops 7340032 | bytes 4718592 | tf_op jit(solution)/shard_map/convert_element_type | solution.py:135
  62.9 1.0 collective-permute-done.11
  63.8 5.3 %collective-permute-done.10 = bf16[256,512]{1,0:T(8,128)(2,1)S(1)} collective-permute-done((bf16[256,512]{1,0:T(8,128)(2,1)S(1)}, bf16[256,512]{1,0:T(8,128)(2,1)S(1)}, u32[]{:S(2)}, u32[]{:S(2)}) %collective-permute-start.10) | collective-permute-done | bytes 262176 | tf_op jit(solution)/shard_map/ppermute | solution.py:70
  69.4 1.7 fusion.58
  71.2 3.1 %collective-permute-start.6 = (bf16[256,512]{1,0:T(8,128)(2,1)S(1)}, bf16[256,512]{1,0:T(8,128)(2,1)S(1)}, u32[]{:S(2)}, u32[]{:S(2)}) collective-permute-start(bf16[256,512]{1,0:T(8,128)(2,1)S(1)} %get-tuple-element.49), channel_id=1, source_target_pairs={{0,4},{2,6},{4,0},{6,2},{1,5},{3,7},{5,1},{7,3},{8,12},{10,14},{12... | collective-permute-start | bytes 786440 | tf_op jit(solution)/shard_map/ppermute | solution.py:70
  74.3 1.1 collective-permute-start.5
  75.4 0.9 collective-permute-start.4
  76.8 1.3 fusion.1
  78.1 3.0 %collective-permute-start.14 = (bf16[256,1024]{1,0:T(8,128)(2,1)}, bf16[256,1024]{1,0:T(8,128)(2,1)}, u32[]{:S(2)}, u32[]{:S(2)}) collective-permute-start(bf16[256,1024]{1,0:T(8,128)(2,1)} %fusion.1), channel_id=1, source_target_pairs={{192,0},{128,64},{193,1},{129,65},{194,2},{130,66},{195,3},{131,67... | collective-permute-start | bytes 1572872 | tf_op jit(solution)/shard_map/ppermute | solution.py:47
  81.1 0.8 collective-permute-done.6
  81.9 5.2 %collective-permute-done.5 = bf16[256,512]{1,0:T(8,128)(2,1)S(1)} collective-permute-done((bf16[256,512]{1,0:T(8,128)(2,1)S(1)}, bf16[256,512]{1,0:T(8,128)(2,1)S(1)}, u32[]{:S(2)}, u32[]{:S(2)}) %collective-permute-start.5) | collective-permute-done | bytes 262176 | tf_op jit(solution)/shard_map/ppermute | solution.py:70
  87.5 1.4 collective-permute-done.12
  89.5 2.1 %collective-permute-done.14 = bf16[256,1024]{1,0:T(8,128)(2,1)} collective-permute-done((bf16[256,1024]{1,0:T(8,128)(2,1)}, bf16[256,1024]{1,0:T(8,128)(2,1)}, u32[]{:S(2)}, u32[]{:S(2)}) %collective-permute-start.14) | collective-permute-done | bytes 524320 | tf_op jit(solution)/shard_map/ppermute | solution.py:47
  91.6 1.3 fusion.3
  92.9 5.7 %all-to-all-start.1 = ((bf16[16,16,1024]{2,1,0:T(8,128)(2,1)}), bf16[16,16,1024]{2,1,0:T(8,128)(2,1)S(1)}, u32[]{:S(2)}, u32[]{:S(2)}) async-start(bf16[16,16,1024]{2,1,0:T(8,128)(2,1)} %bitcast.15), calls=%async_computation.1 | async-start | bytes 1048576 | tf_op jit(solution)/shard_map/all_to_all | solution.py:79
  98.6 1.3 collective-permute-start.24
  99.9 1.8 slice.45
  101.7 1.3 collective-permute-start.18
  103.1 9.8 %all-to-all-done.1 = bf16[16,16,1024]{2,1,0:T(8,128)(2,1)S(1)} async-done(((bf16[16,16,1024]{2,1,0:T(8,128)(2,1)}), bf16[16,16,1024]{2,1,0:T(8,128)(2,1)S(1)}, u32[]{:S(2)}, u32[]{:S(2)}) %all-to-all-start.1) | async-done | bytes 524320 | tf_op jit(solution)/shard_map/all_to_all | solution.py:79
  113.0 0.9 broadcast_in_dim.22
  113.9 4.9 %all-to-all-start.2 = ((bf16[16,16,1024]{2,1,0:T(8,128)(2,1)}), bf16[16,16,1024]{2,1,0:T(8,128)(2,1)S(1)}, u32[]{:S(2)}, u32[]{:S(2)}) async-start(bf16[16,16,1024]{2,1,0:T(8,128)(2,1)} %broadcast_in_dim.22), calls=%async_computation.2 | async-start | bytes 1048576 | tf_op jit(solution)/shard_map/all_to_all | solution.py:90
  118.8 3.8 %broadcast_select_fusion.1 = bf16[1024,1024]{1,0:T(8,128)(2,1)} fusion(bf16[1024,1024]{1,0:T(8,128)(2,1)} %collective-permute-done.17, pred[]{:T(512)S(6)} %eq.8, bf16[1,1024,1024]{2,1,0:T(8,128)(2,1)} %param.7), kind=kLoop, calls=%fused_computation.1 | loop fusion | flops 1048576 | bytes 6291457 | tf_op jit(solution)/shard_map/jit(_where)/select_n | solution.py:116
  122.6 1.3 broadcast_select_fusion.3
  123.8 1.2 pad_maximum_fusion
  125.0 25.4 %collective-permute-done.24 = bf16[1024,1024]{1,0:T(8,128)(2,1)} collective-permute-done((bf16[1024,1024]{1,0:T(8,128)(2,1)S(1)}, bf16[1024,1024]{1,0:T(8,128)(2,1)}, u32[]{:S(2)}, u32[]{:S(2)}) %collective-permute-start.24) | collective-permute-done | bytes 2097184 | tf_op jit(solution)/shard_map/ppermute | solution.py:43
  150.4 3.1 %broadcast_select_fusion = bf16[1024,1024]{1,0:T(8,128)(2,1)} fusion(bf16[1024,1024]{1,0:T(8,128)(2,1)} %collective-permute-done.24, pred[]{:T(512)S(6)} %eq.8, bf16[1,1024,1024]{2,1,0:T(8,128)(2,1)S(1)} %copy-done), kind=kLoop, calls=%fused_computation | loop fusion | flops 1048576 | bytes 6291457 | tf_op jit(solution)/shard_map/jit(_where)/select_n | solution.py:116
  153.5 1.5 collective-permute-start.23
  155.0 1.7 convolution_convert_fusion.4
  156.8 1.1 broadcast_select_fusion.5
  158.8 1.8 collective-permute-start.22
  160.6 1.3 collective-permute-start.21
  161.9 0.8 collective-permute-start.20
  162.7 1.2 collective-permute-done.23
  164.0 2.6 %convolution_convert_fusion.1 = bf16[1024,1024]{1,0:T(8,128)(2,1)} fusion(bf16[512,1024]{1,0:T(8,128)(2,1)S(1)} %copy-done.15, bf16[256,1024]{1,0:T(8,128)(2,1)S(1)} %broadcast_select_fusion.4, bf16[256,1024]{1,0:T(8,128)(2,1)S(1)} %broadcast_select_fusion.5), kind=kOutput, calls=%fused_computation.3 | convolution fusion | flops 1076887552 | bytes 4194304 | tf_op jit(solution)/shard_map/dot_general | solution.py:26
  166.6 3.0 %collective-permute-done.22 = bf16[256,512]{1,0:T(8,128)(2,1)S(1)} collective-permute-done((bf16[256,512]{1,0:T(8,128)(2,1)S(1)}, bf16[256,512]{1,0:T(8,128)(2,1)S(1)}, u32[]{:S(2)}, u32[]{:S(2)}) %collective-permute-start.22) | collective-permute-done | bytes 262176 | tf_op jit(solution)/shard_map/ppermute | solution.py:70
  169.6 4.6 %collective-permute-done.21 = bf16[256,512]{1,0:T(8,128)(2,1)S(1)} collective-permute-done((bf16[256,512]{1,0:T(8,128)(2,1)S(1)}, bf16[256,512]{1,0:T(8,128)(2,1)S(1)}, u32[]{:S(2)}, u32[]{:S(2)}) %collective-permute-start.21) | collective-permute-done | bytes 262176 | tf_op jit(solution)/shard_map/ppermute | solution.py:70
  174.5 1.1 multiply_convert_fusion.1
  175.7 2.0 collective-permute-start.26
  178.3 1.3 fusion.2
  179.6 8.3 %all-to-all-start.3 = ((bf16[16,16,1024]{2,1,0:T(8,128)(2,1)}), bf16[16,16,1024]{2,1,0:T(8,128)(2,1)S(1)}, u32[]{:S(2)}, u32[]{:S(2)}) async-start(bf16[16,16,1024]{2,1,0:T(8,128)(2,1)} %bitcast.92), calls=%async_computation.3 | async-start | bytes 1048576 | tf_op jit(solution)/shard_map/all_to_all | solution.py:79
  188.0 1.0 broadcast_select_fusion.9
  189.7 1.0 broadcast_select_fusion.7
  190.7 2.6 %convolution_convert_fusion = bf16[1024,1024]{1,0:T(8,128)(2,1)} fusion(bf16[256,1024]{1,0:T(8,128)(2,1)S(1)} %bitcast.91, bf16[256,1024]{1,0:T(8,128)(2,1)S(1)} %bitcast.88, bf16[256,512]{1,0:T(8,128)(2,1)S(1)} %get-tuple-element.38, bf16[256,512]{1,0:T(8,128)(2,1)S(1)} %get-tuple-element.37, bf16[256,512]{1,0:T(8,128)(2,1)S(1)} %get-tuple-element.36, ...), kind=kOutput, calls=%fused_computation.2 | convolution fusion | flops 1081081856 | bytes 4194304 | tf_op jit(solution)/shard_map/dot_general | solution.py:26
  193.3 10.5 %all-to-all-done.3 = bf16[16,16,1024]{2,1,0:T(8,128)(2,1)S(1)} async-done(((bf16[16,16,1024]{2,1,0:T(8,128)(2,1)}), bf16[16,16,1024]{2,1,0:T(8,128)(2,1)S(1)}, u32[]{:S(2)}, u32[]{:S(2)}) %all-to-all-start.3) | async-done | bytes 524320 | tf_op jit(solution)/shard_map/all_to_all | solution.py:79
  204.0 5.4 %collective-permute-done.28 = bf16[16,1024]{1,0:T(8,128)(2,1)S(1)} collective-permute-done((bf16[16,1024]{1,0:T(8,128)(2,1)S(1)}, bf16[16,1024]{1,0:T(8,128)(2,1)S(1)}, u32[]{:S(2)}, u32[]{:S(2)}) %collective-permute-start.28) | collective-permute-done | bytes 32800 | tf_op jit(solution)/shard_map/ppermute | solution.py:181
  (90 shorter events, 8.2 us)
Async XLA Ops:
  2.6 11.0 %copy-start = (bf16[1,1024,1024]{2,1,0:T(8,128)(2,1)S(1)}, bf16[1,1024,1024]{2,1,0:T(8,128)(2,1)}, u32[]{:S(2)}) copy-start(bf16[1,1024,1024]{2,1,0:T(8,128)(2,1)} %param.6) | copy-start | bytes 6291460
  2.6 35.9 %all-to-all-start = ((bf16[16,32,1024]{2,1,0:T(8,128)(2,1)}), bf16[16,32,1024]{2,1,0:T(8,128)(2,1)}, u32[]{:S(2)}, u32[]{:S(2)}) async-start(bf16[16,32,1024]{2,1,0:T(8,128)(2,1)} %broadcast_in_dim.10), calls=%async_computation | async-start | bytes 2097152 | tf_op jit(solution)/shard_map/all_to_all | solution.py:90
  13.5 1.8 copy-start.8
  13.5 1.8 copy-start.11
  15.3 2.3 %collective-permute-start = (bf16[512,512]{1,0:T(8,128)(2,1)}, bf16[512,512]{1,0:T(8,128)(2,1)}, u32[]{:S(2)}, u32[]{:S(2)}) collective-permute-start(bf16[512,512]{1,0:T(8,128)(2,1)} %pad_maximum_fusion.1), channel_id=1, source_target_pairs={{0,1},{1,0},{2,3},{3,2},{4,5},{5,4},{6,7},{7,6},{8,9},{9,8},{10,11... | collective-permute-start | bytes 1572872 | tf_op jit(solution)/shard_map/ppermute | solution.py:39
  15.3 1.6 copy-start.9
  17.3 21.2 %copy-start.6 = (f32[256,512]{1,0:T(8,128)}, f32[256,512]{1,0:T(8,128)S(1)}, u32[]{:S(2)}) copy-start(f32[256,512]{1,0:T(8,128)S(1)} %convolution_bitcast_fusion.1) | copy-start | bytes 1572868
  18.7 2.9 %copy-start.19 = (bf16[512,512]{1,0:T(8,128)(2,1)}, bf16[512,512]{1,0:T(8,128)(2,1)S(1)}, u32[]{:S(2)}) copy-start(bf16[512,512]{1,0:T(8,128)(2,1)S(1)} %fusion.57) | copy-start | bytes 1572868
  18.8 14.7 %collective-permute-start.2 = (bf16[512,512]{1,0:T(8,128)(2,1)S(1)}, bf16[512,512]{1,0:T(8,128)(2,1)}, u32[]{:S(2)}, u32[]{:S(2)}) collective-permute-start(bf16[512,512]{1,0:T(8,128)(2,1)S(1)} %fusion.57), channel_id=1, source_target_pairs={{0,6},{2,0},{4,2},{6,4},{1,7},{3,1},{5,3},{7,5},{8,14},{10,8},{12,... | collective-permute-start | bytes 1572872 | tf_op jit(solution)/shard_map/ppermute | solution.py:70
  21.6 15.4 %collective-permute-start.1 = (bf16[512,512]{1,0:T(8,128)(2,1)S(1)}, bf16[512,512]{1,0:T(8,128)(2,1)}, u32[]{:S(2)}, u32[]{:S(2)}) collective-permute-start(bf16[512,512]{1,0:T(8,128)(2,1)S(1)} %fusion.57), channel_id=1, source_target_pairs={{0,2},{2,4},{4,6},{6,0},{1,3},{3,5},{5,7},{7,1},{8,10},{10,12},{12... | collective-permute-start | bytes 1572872 | tf_op jit(solution)/shard_map/ppermute | solution.py:70
  38.5 3.4 %copy-start.20 = (bf16[512,512]{1,0:T(8,128)(2,1)S(1)}, bf16[512,512]{1,0:T(8,128)(2,1)}, u32[]{:S(2)}) copy-start(bf16[512,512]{1,0:T(8,128)(2,1)} %copy-done.19) | copy-start | bytes 1572868
  39.8 10.1 %copy-start.3 = (bf16[16,1,16,1024]{3,2,1,0:T(8,128)(2,1)}, bf16[16,1,16,1024]{3,2,1,0:T(8,128)(2,1)S(1)}, u32[]{:S(2)}) copy-start(bf16[16,1,16,1024]{3,2,1,0:T(8,128)(2,1)S(1)} %get-tuple-element.42) | copy-start | bytes 1572868
  41.7 6.5 %collective-permute-start.8 = (bf16[256,512]{1,0:T(8,128)(2,1)S(1)}, bf16[256,512]{1,0:T(8,128)(2,1)S(1)}, u32[]{:S(2)}, u32[]{:S(2)}) collective-permute-start(bf16[256,512]{1,0:T(8,128)(2,1)S(1)} %convolution_convert_fusion.5), channel_id=1, source_target_pairs={{0,1},{1,0},{2,3},{3,2},{4,5},{5,4},{6,7},{7,6},{8,9},{9,8},{10,11... | collective-permute-start | bytes 786440 | tf_op jit(solution)/shard_map/ppermute | solution.py:39
  41.9 16.3 %collective-permute-start.7 = (bf16[512,512]{1,0:T(8,128)(2,1)S(1)}, bf16[512,512]{1,0:T(8,128)(2,1)S(1)}, u32[]{:S(2)}, u32[]{:S(2)}) collective-permute-start(bf16[512,512]{1,0:T(8,128)(2,1)S(1)} %copy-done.20), channel_id=1, source_target_pairs={{0,4},{2,6},{4,0},{6,2},{1,5},{3,7},{5,1},{7,3},{8,12},{10,14},{12... | collective-permute-start | bytes 1572872 | tf_op jit(solution)/shard_map/ppermute | solution.py:70
  45.0 53.7 %collective-permute-start.17 = (bf16[1024,1024]{1,0:T(8,128)(2,1)}, bf16[1024,1024]{1,0:T(8,128)(2,1)}, u32[]{:S(2)}, u32[]{:S(2)}) collective-permute-start(bf16[1024,1024]{1,0:T(8,128)(2,1)} %bitcast.17), channel_id=1, source_target_pairs={{0,192},{64,128},{1,193},{65,129},{2,194},{66,130},{3,195},{67,131... | collective-permute-start | bytes 6291464 | tf_op jit(solution)/shard_map/ppermute | solution.py:43
  46.2 13.5 %copy-start.7 = (f32[256,512]{1,0:T(8,128)S(1)}, f32[256,512]{1,0:T(8,128)}, u32[]{:S(2)}) copy-start(f32[256,512]{1,0:T(8,128)} %copy-done.6) | copy-start | bytes 1572868
  48.0 21.4 %collective-permute-start.3 = (bf16[256,512]{1,0:T(8,128)(2,1)S(1)}, bf16[256,512]{1,0:T(8,128)(2,1)S(1)}, u32[]{:S(2)}, u32[]{:S(2)}) collective-permute-start(bf16[256,512]{1,0:T(8,128)(2,1)S(1)} %convolution_convert_fusion.6), channel_id=1, source_target_pairs={{0,1},{1,0},{2,3},{3,2},{4,5},{5,4},{6,7},{7,6},{8,9},{9,8},{10,11... | collective-permute-start | bytes 786440 | tf_op jit(solution)/shard_map/ppermute | solution.py:39
  50.0 13.8 %collective-permute-start.11 = (bf16[256,512]{1,0:T(8,128)(2,1)S(1)}, bf16[256,512]{1,0:T(8,128)(2,1)S(1)}, u32[]{:S(2)}, u32[]{:S(2)}) collective-permute-start(bf16[256,512]{1,0:T(8,128)(2,1)S(1)} %get-tuple-element.47), channel_id=1, source_target_pairs={{0,4},{2,6},{4,0},{6,2},{1,5},{3,7},{5,1},{7,3},{8,12},{10,14},{12... | collective-permute-start | bytes 786440 | tf_op jit(solution)/shard_map/ppermute | solution.py:70
  50.6 18.5 %collective-permute-start.10 = (bf16[256,512]{1,0:T(8,128)(2,1)S(1)}, bf16[256,512]{1,0:T(8,128)(2,1)S(1)}, u32[]{:S(2)}, u32[]{:S(2)}) collective-permute-start(bf16[256,512]{1,0:T(8,128)(2,1)S(1)} %get-tuple-element.47), channel_id=1, source_target_pairs={{0,6},{2,0},{4,2},{6,4},{1,7},{3,1},{5,3},{7,5},{8,14},{10,8},{12,... | collective-permute-start | bytes 786440 | tf_op jit(solution)/shard_map/ppermute | solution.py:70
  58.2 10.9 %collective-permute-start.9 = (bf16[256,512]{1,0:T(8,128)(2,1)S(1)}, bf16[256,512]{1,0:T(8,128)(2,1)S(1)}, u32[]{:S(2)}, u32[]{:S(2)}) collective-permute-start(bf16[256,512]{1,0:T(8,128)(2,1)S(1)} %get-tuple-element.47), channel_id=1, source_target_pairs={{0,2},{2,4},{4,6},{6,0},{1,3},{3,5},{5,7},{7,1},{8,10},{10,12},{12... | collective-permute-start | bytes 786440 | tf_op jit(solution)/shard_map/ppermute | solution.py:70
  62.9 8.3 %copy-start.4 = (f32[512,512]{1,0:T(8,128)}, f32[512,512]{1,0:T(8,128)S(1)}, u32[]{:S(2)}) copy-start(f32[512,512]{1,0:T(8,128)S(1)} %get-tuple-element.34) | copy-start | bytes 3145732
  69.3 7.5 %copy-start.13 = (bf16[256,512]{1,0:T(8,128)(2,1)}, bf16[256,512]{1,0:T(8,128)(2,1)S(1)}, u32[]{:S(2)}) copy-start(bf16[256,512]{1,0:T(8,128)(2,1)S(1)} %get-tuple-element.44) | copy-start | bytes 786436
  69.3 6.9 %collective-permute-start.13 = (bf16[256,512]{1,0:T(8,128)(2,1)S(1)}, bf16[256,512]{1,0:T(8,128)(2,1)S(1)}, u32[]{:S(2)}, u32[]{:S(2)}) collective-permute-start(bf16[256,512]{1,0:T(8,128)(2,1)S(1)} %get-tuple-element.44), channel_id=1, source_target_pairs={{0,1},{1,0},{2,3},{3,2},{4,5},{5,4},{6,7},{7,6},{8,9},{9,8},{10,11... | collective-permute-start | bytes 786440 | tf_op jit(solution)/shard_map/ppermute | solution.py:39
  71.2 10.7 %collective-permute-start.6 = (bf16[256,512]{1,0:T(8,128)(2,1)S(1)}, bf16[256,512]{1,0:T(8,128)(2,1)S(1)}, u32[]{:S(2)}, u32[]{:S(2)}) collective-permute-start(bf16[256,512]{1,0:T(8,128)(2,1)S(1)} %get-tuple-element.49), channel_id=1, source_target_pairs={{0,4},{2,6},{4,0},{6,2},{1,5},{3,7},{5,1},{7,3},{8,12},{10,14},{12... | collective-permute-start | bytes 786440 | tf_op jit(solution)/shard_map/ppermute | solution.py:70
  74.3 12.8 %collective-permute-start.5 = (bf16[256,512]{1,0:T(8,128)(2,1)S(1)}, bf16[256,512]{1,0:T(8,128)(2,1)S(1)}, u32[]{:S(2)}, u32[]{:S(2)}) collective-permute-start(bf16[256,512]{1,0:T(8,128)(2,1)S(1)} %get-tuple-element.49), channel_id=1, source_target_pairs={{0,6},{2,0},{4,2},{6,4},{1,7},{3,1},{5,3},{7,5},{8,14},{10,8},{12,... | collective-permute-start | bytes 786440 | tf_op jit(solution)/shard_map/ppermute | solution.py:70
  75.4 11.7 %collective-permute-start.4 = (bf16[256,512]{1,0:T(8,128)(2,1)S(1)}, bf16[256,512]{1,0:T(8,128)(2,1)S(1)}, u32[]{:S(2)}, u32[]{:S(2)}) collective-permute-start(bf16[256,512]{1,0:T(8,128)(2,1)S(1)} %get-tuple-element.49), channel_id=1, source_target_pairs={{0,2},{2,4},{4,6},{6,0},{1,3},{3,5},{5,7},{7,1},{8,10},{10,12},{12... | collective-permute-start | bytes 786440 | tf_op jit(solution)/shard_map/ppermute | solution.py:70
  76.3 1.8 copy-start.16
  78.1 13.5 %collective-permute-start.14 = (bf16[256,1024]{1,0:T(8,128)(2,1)}, bf16[256,1024]{1,0:T(8,128)(2,1)}, u32[]{:S(2)}, u32[]{:S(2)}) collective-permute-start(bf16[256,1024]{1,0:T(8,128)(2,1)} %fusion.1), channel_id=1, source_target_pairs={{192,0},{128,64},{193,1},{129,65},{194,2},{130,66},{195,3},{131,67... | collective-permute-start | bytes 1572872 | tf_op jit(solution)/shard_map/ppermute | solution.py:47
  87.3 1.6 collective-permute-start.12
  89.0 3.9 %copy-start.17 = (bf16[256,512]{1,0:T(8,128)(2,1)}, bf16[256,512]{1,0:T(8,128)(2,1)S(1)}, u32[]{:S(2)}) copy-start(bf16[256,512]{1,0:T(8,128)(2,1)S(1)} %collective-permute-done.12) | copy-start | bytes 786436
  89.4 23.6 %copy-start.21 = (bf16[32,1024]{1,0:T(8,128)(2,1)S(1)}, bf16[32,1024]{1,0:T(8,128)(2,1)}, u32[]{:S(2)}) copy-start(bf16[32,1024]{1,0:T(8,128)(2,1)} %param.5) | copy-start | bytes 196612
  92.9 20.0 %all-to-all-start.1 = ((bf16[16,16,1024]{2,1,0:T(8,128)(2,1)}), bf16[16,16,1024]{2,1,0:T(8,128)(2,1)S(1)}, u32[]{:S(2)}, u32[]{:S(2)}) async-start(bf16[16,16,1024]{2,1,0:T(8,128)(2,1)} %bitcast.15), calls=%async_computation.1 | async-start | bytes 1048576 | tf_op jit(solution)/shard_map/all_to_all | solution.py:79
  98.6 51.8 %collective-permute-start.24 = (bf16[1024,1024]{1,0:T(8,128)(2,1)S(1)}, bf16[1024,1024]{1,0:T(8,128)(2,1)}, u32[]{:S(2)}, u32[]{:S(2)}) collective-permute-start(bf16[1024,1024]{1,0:T(8,128)(2,1)S(1)} %bitcast.77), channel_id=1, source_target_pairs={{0,192},{64,128},{1,193},{65,129},{2,194},{66,130},{3,195},{67,131... | collective-permute-start | bytes 6291464 | tf_op jit(solution)/shard_map/ppermute | solution.py:43
  101.7 51.8 %collective-permute-start.18 = (bf16[256,512]{1,0:T(8,128)(2,1)}, bf16[256,512]{1,0:T(8,128)(2,1)}, u32[]{:S(2)}, u32[]{:S(2)}) collective-permute-start(bf16[256,512]{1,0:T(8,128)(2,1)} %slice.45), channel_id=1, source_target_pairs={{0,192},{64,128},{1,193},{65,129},{2,194},{66,130},{3,195},{67,131... | collective-permute-start | bytes 786440 | tf_op jit(solution)/shard_map/ppermute | solution.py:43
  103.0 19.6 %collective-permute-start.16 = (bf16[512,512]{1,0:T(8,128)(2,1)}, bf16[512,512]{1,0:T(8,128)(2,1)}, u32[]{:S(2)}, u32[]{:S(2)}) collective-permute-start(bf16[512,512]{1,0:T(8,128)(2,1)} %get-tuple-element.33), channel_id=1, source_target_pairs={{0,1},{1,0},{2,3},{3,2},{4,5},{5,4},{6,7},{7,6},{8,9},{9,8},{10,11... | collective-permute-start | bytes 1572872 | tf_op jit(solution)/shard_map/ppermute | solution.py:39
  113.9 39.6 %all-to-all-start.2 = ((bf16[16,16,1024]{2,1,0:T(8,128)(2,1)}), bf16[16,16,1024]{2,1,0:T(8,128)(2,1)S(1)}, u32[]{:S(2)}, u32[]{:S(2)}) async-start(bf16[16,16,1024]{2,1,0:T(8,128)(2,1)} %broadcast_in_dim.22), calls=%async_computation.2 | async-start | bytes 1048576 | tf_op jit(solution)/shard_map/all_to_all | solution.py:90
  153.5 4.8 %copy-start.2 = (bf16[1024,1024]{1,0:T(8,128)(2,1)S(1)}, bf16[1024,1024]{1,0:T(8,128)(2,1)}, u32[]{:S(2)}) copy-start(bf16[1024,1024]{1,0:T(8,128)(2,1)} %broadcast_select_fusion.1) | copy-start | bytes 6291460
  153.5 10.3 %collective-permute-start.23 = (bf16[256,1024]{1,0:T(8,128)(2,1)S(1)}, bf16[256,1024]{1,0:T(8,128)(2,1)S(1)}, u32[]{:S(2)}, u32[]{:S(2)}) collective-permute-start(bf16[256,1024]{1,0:T(8,128)(2,1)S(1)} %bitcast.78), channel_id=1, source_target_pairs={{192,0},{128,64},{193,1},{129,65},{194,2},{130,66},{195,3},{131,67... | collective-permute-start | bytes 1572872 | tf_op jit(solution)/shard_map/ppermute | solution.py:47
  156.7 1.6 collective-permute-start.19
  157.9 6.0 %copy-start.15 = (bf16[512,1024]{1,0:T(8,128)(2,1)S(1)}, bf16[512,1024]{1,0:T(8,128)(2,1)}, u32[]{:S(2)}) copy-start(bf16[512,1024]{1,0:T(8,128)(2,1)} %pad_maximum_fusion) | copy-start | bytes 3145732
  158.8 10.8 %collective-permute-start.22 = (bf16[256,512]{1,0:T(8,128)(2,1)S(1)}, bf16[256,512]{1,0:T(8,128)(2,1)S(1)}, u32[]{:S(2)}, u32[]{:S(2)}) collective-permute-start(bf16[256,512]{1,0:T(8,128)(2,1)S(1)} %get-tuple-element.51), channel_id=1, source_target_pairs={{0,4},{2,6},{4,0},{6,2},{1,5},{3,7},{5,1},{7,3},{8,12},{10,14},{12... | collective-permute-start | bytes 786440 | tf_op jit(solution)/shard_map/ppermute | solution.py:70
  160.6 13.6 %collective-permute-start.21 = (bf16[256,512]{1,0:T(8,128)(2,1)S(1)}, bf16[256,512]{1,0:T(8,128)(2,1)S(1)}, u32[]{:S(2)}, u32[]{:S(2)}) collective-permute-start(bf16[256,512]{1,0:T(8,128)(2,1)S(1)} %get-tuple-element.51), channel_id=1, source_target_pairs={{0,6},{2,0},{4,2},{6,4},{1,7},{3,1},{5,3},{7,5},{8,14},{10,8},{12,... | collective-permute-start | bytes 786440 | tf_op jit(solution)/shard_map/ppermute | solution.py:70
  161.9 12.5 %collective-permute-start.20 = (bf16[256,512]{1,0:T(8,128)(2,1)S(1)}, bf16[256,512]{1,0:T(8,128)(2,1)S(1)}, u32[]{:S(2)}, u32[]{:S(2)}) collective-permute-start(bf16[256,512]{1,0:T(8,128)(2,1)S(1)} %get-tuple-element.51), channel_id=1, source_target_pairs={{0,2},{2,4},{4,6},{6,0},{1,3},{3,5},{5,7},{7,1},{8,10},{10,12},{12... | collective-permute-start | bytes 786440 | tf_op jit(solution)/shard_map/ppermute | solution.py:70
  164.0 10.6 %copy-start.5 = (f32[512,512]{1,0:T(8,128)S(1)}, f32[512,512]{1,0:T(8,128)}, u32[]{:S(2)}) copy-start(f32[512,512]{1,0:T(8,128)} %copy-done.4) | copy-start | bytes 3145732
  166.6 11.1 %copy-start.1 = (bf16[1024,1024]{1,0:T(8,128)(2,1)S(1)}, bf16[1024,1024]{1,0:T(8,128)(2,1)}, u32[]{:S(2)}) copy-start(bf16[1024,1024]{1,0:T(8,128)(2,1)} %broadcast_select_fusion) | copy-start | bytes 6291460
  175.6 2.6 %collective-permute-start.25 = (bf16[256,512]{1,0:T(8,128)(2,1)S(1)}, bf16[256,512]{1,0:T(8,128)(2,1)S(1)}, u32[]{:S(2)}, u32[]{:S(2)}) collective-permute-start(bf16[256,512]{1,0:T(8,128)(2,1)S(1)} %multiply_convert_fusion.1), channel_id=1, source_target_pairs={{0,1},{1,0},{2,3},{3,2},{4,5},{5,4},{6,7},{7,6},{8,9},{9,8},{10,11... | collective-permute-start | bytes 786440 | tf_op jit(solution)/shard_map/ppermute | solution.py:39
  175.7 12.1 %collective-permute-start.26 = (bf16[256,512]{1,0:T(8,128)(2,1)S(1)}, bf16[256,512]{1,0:T(8,128)(2,1)}, u32[]{:S(2)}, u32[]{:S(2)}) collective-permute-start(bf16[256,512]{1,0:T(8,128)(2,1)S(1)} %multiply_convert_fusion.1), channel_id=1, source_target_pairs={{192,0},{128,64},{193,1},{129,65},{194,2},{130,66},{195,3},{131,67... | collective-permute-start | bytes 786440 | tf_op jit(solution)/shard_map/ppermute | solution.py:47
  178.2 9.7 %copy-start.14 = (bf16[256,512]{1,0:T(8,128)(2,1)S(1)}, bf16[256,512]{1,0:T(8,128)(2,1)}, u32[]{:S(2)}) copy-start(bf16[256,512]{1,0:T(8,128)(2,1)} %copy-done.13) | copy-start | bytes 786436
  178.2 1.3 copy-start.18
  179.6 11.1 %copy-start.10 = (bf16[16,1,16,1024]{3,2,1,0:T(8,128)(2,1)S(1)}, bf16[16,1,16,1024]{3,2,1,0:T(8,128)(2,1)}, u32[]{:S(2)}) copy-start(bf16[16,1,16,1024]{3,2,1,0:T(8,128)(2,1)} %copy-done.8) | copy-start | bytes 1572868
  179.6 11.1 %copy-start.12 = (bf16[16,1,16,1024]{3,2,1,0:T(8,128)(2,1)S(1)}, bf16[16,1,16,1024]{3,2,1,0:T(8,128)(2,1)}, u32[]{:S(2)}) copy-start(bf16[16,1,16,1024]{3,2,1,0:T(8,128)(2,1)} %copy-done.11) | copy-start | bytes 1572868
  179.6 24.3 %all-to-all-start.3 = ((bf16[16,16,1024]{2,1,0:T(8,128)(2,1)}), bf16[16,16,1024]{2,1,0:T(8,128)(2,1)S(1)}, u32[]{:S(2)}, u32[]{:S(2)}) async-start(bf16[16,16,1024]{2,1,0:T(8,128)(2,1)} %bitcast.92), calls=%async_computation.3 | async-start | bytes 1048576 | tf_op jit(solution)/shard_map/all_to_all | solution.py:79
  187.8 16.1 %collective-permute-start.15 = (bf16[16,1024]{1,0:T(8,128)(2,1)S(1)}, bf16[16,1024]{1,0:T(8,128)(2,1)S(1)}, u32[]{:S(2)}, u32[]{:S(2)}) collective-permute-start(bf16[16,1024]{1,0:T(8,128)(2,1)S(1)} %add_convert_fusion.1), channel_id=1, source_target_pairs={{0,128},{128,0},{1,129},{129,1},{2,130},{130,2},{3,131},{131,3},{4... | collective-permute-start | bytes 98312 | tf_op jit(solution)/shard_map/ppermute | solution.py:180
  187.8 1.8 collective-permute-start.27
  203.9 5.5 %collective-permute-start.28 = (bf16[16,1024]{1,0:T(8,128)(2,1)S(1)}, bf16[16,1024]{1,0:T(8,128)(2,1)S(1)}, u32[]{:S(2)}, u32[]{:S(2)}) collective-permute-start(bf16[16,1024]{1,0:T(8,128)(2,1)S(1)} %get-tuple-element.32), channel_id=1, source_target_pairs={{0,128},{128,0},{1,129},{129,1},{2,130},{130,2},{3,131},{131,3},{4... | collective-permute-start | bytes 98312 | tf_op jit(solution)/shard_map/ppermute | solution.py:181

commit v6 on v5

--- a/solution.py
+++ b/solution.py
@@ -63,15 +63,48 @@
     )
 
 
-def narrow_terms(mine, theirs):
-    pair = mine + other_core(theirs.astype(jnp.bfloat16)).astype(jnp.float32)
-    sent = pair.astype(jnp.bfloat16)
-    routes = [[(i, (i + distance) % X) for i in range(X)] for distance in (1, 3, 2)]
-    return [pair] + [lax.ppermute(sent, "x", route) for route in routes]
-
-
-def add_terms(terms):
-    return sum(term.astype(jnp.float32) for term in terms)
+def pair_sum(mine, theirs):
+    return mine + other_core(theirs.astype(jnp.bfloat16)).astype(jnp.float32)
+
+
+def spread_x(partial):
+    rows, cols = partial.shape
+    blocks = lax.all_to_all(
+        partial.astype(jnp.bfloat16).reshape(X, rows // X, cols), "x", 0, 0, tiled=True
+    )
+    return jnp.sum(blocks.astype(jnp.float32), axis=0)
+
+
+def gather_x(block):
+    rows, cols = block.shape
+    return lax.all_to_all(
+        jnp.broadcast_to(block[None], (X, rows, cols)), "x", 0, 0, tiled=True
+    ).reshape(X * rows, cols)
+
+
+def step_x(block, distance):
+    return lax.ppermute(block, "x", [(i, (i + distance) % X) for i in range(X)])
+
+
+def spread_x_beside(partial):
+    rows, cols = partial.shape
+    x = lax.axis_index("x")
+    blocks = partial.reshape(X, rows // X, cols)
+    total = lax.dynamic_index_in_dim(blocks, x, 0, keepdims=False)
+    sent = blocks.astype(jnp.bfloat16)
+    for distance in (1, 3, 2):
+        target = lax.rem(x + distance, X)
+        block = lax.dynamic_index_in_dim(sent, target, 0, keepdims=False)
+        total = total + step_x(block, distance).astype(jnp.float32)
+    return total
+
+
+def gather_x_beside(block):
+    rows, cols = block.shape
+    found = [block] + [step_x(block, X - distance) for distance in (1, 2, 3)]
+    twice = jnp.stack(found + found[:-1])
+    start = lax.rem(X - lax.axis_index("x"), X)
+    return lax.dynamic_slice_in_dim(twice, start, X, 0).reshape(X * rows, cols)
 
 
 def spread_wide(partial):
@@ -92,15 +125,10 @@
     ).reshape(WIDE * rows, cols)
 
 
-def back_total(whole, down_halves):
+def back_share(whole, down_halves):
     theirs = contract(whole, down_halves[1], 1, 1)
     mine = contract(whole, down_halves[0], 1, 1)
-    return add_terms(narrow_terms(mine, theirs))
-
-
-def slope_of(total, slopes):
-    mine = (total * slopes).astype(jnp.bfloat16)
-    return mine, other_core(mine)
+    return spread_x(pair_sum(mine, theirs))
 
 
 def back_through_up(slope, up_halves):
@@ -115,64 +143,73 @@
     def pick(upper, lower):
         return jnp.where(is_upper, upper, lower)
 
-    def by_part(block):
+    part = upstream.shape[0] // 2
+
+    def part_of(block, index):
         rows, cols = block.shape
-        split = block.reshape(WIDE, 2, rows // (2 * WIDE), cols)
-        return [split[:, c].reshape(rows // 2, cols) for c in range(2)]
-
+        split = block.reshape(rows // (2 * part), 2, part, cols)
+        return split[:, index].reshape(rows // 2, cols)
+
+    def both_parts(early, late):
+        rows, cols = early.shape
+        pair = [block.reshape(rows // part, part, cols) for block in (early, late)]
+        return jnp.stack(pair, axis=1).reshape(2 * rows, cols)
+
+    saved = saved_inputs[0]
     w_up, w_down = up_weight[0], down_weight[0]
     up_halves, down_halves = halves(w_up, 1), halves(w_down, 0)
-    saved = by_part(saved_inputs[0])
-    first, last = slice(0, saved[0].shape[0]), slice(saved[0].shape[0], None)
-
-    sent_down = to_upper(w_down)
-
-    theirs = jnp.concatenate([contract(rows, up_halves[1], 1, 0) for rows in saved], axis=0)
-    mine = jnp.concatenate([contract(rows, up_halves[0], 1, 0) for rows in saved], axis=0)
-    pre = narrow_terms(mine, theirs)
-    gathered, pre[1], pre[2] = together(gather_wide(upstream), pre[1], pre[2])
-    act, slopes = gelu_parts(add_terms(pre))
-    act = act.astype(jnp.bfloat16)
-    hidden = in_order(act, other_core(act))
-
-    top = by_part(gathered)
-    top_slope = slope_of(back_total(top[0], down_halves), slopes[first])
-    moved = to_lower(back_through_up(top_slope, up_halves))
-    late_slopes, _ = together(slopes[last], top_slope[0])
-    top_slope_rest = slope_of(back_total(top[1], down_halves), late_slopes)
-    blocks = spread_wide(pick(back_through_up(top_slope_rest, up_halves), moved))
-    sent_up = to_upper(together(w_up, sent_down)[0])
-    part = upstream.shape[0] // 2
+
+    depth = w_down.shape[0]
+    some = w_up.shape[0] // 2
+    most = to_upper(jnp.concatenate([w_down, w_up[:some]], axis=0))
+
+    theirs = contract(saved, up_halves[1], 1, 0)
+    mine = contract(saved, up_halves[0], 1, 0)
+    pre = spread_x_beside(pair_sum(mine, theirs))
+    gathered, pre = together(gather_wide(upstream), pre)
+    act, slopes = gelu_parts(pre)
+
+    top_mine = gather_x((back_share(gathered, down_halves) * slopes).astype(jnp.bfloat16))
+    top_slope = [part_of(top_mine, c) for c in range(2)]
+    top_slope = [(block, other_core(block)) for block in top_slope]
+    moved = to_lower(back_through_up(top_slope[0], up_halves))
+    partial = pick(back_through_up(top_slope[1], up_halves), moved)
+    partial, act = together(partial, act.astype(jnp.bfloat16))
+    blocks = spread_wide(partial)
     middle = (
         pick(upstream[part:], upstream[:part]).astype(jnp.float32) + add_blocks(blocks)
     ).astype(jnp.bfloat16)
 
-    low_down = pick(sent_down, w_down)
-    low_up = pick(sent_up, w_up)
-    lower_slopes = to_upper(slopes[last].astype(jnp.bfloat16))
+    rest = to_upper(together(w_up[some:], most, blocks)[0])
+    low_down = pick(most[:depth], w_down)
+    lower_slopes = to_upper(part_of(slopes, 1).astype(jnp.bfloat16))
+    hidden = gather_x_beside(act)
     low, hidden, low_down, lower_slopes = together(
         gather_wide(middle), hidden, low_down, lower_slopes
     )
-    lower_slopes = pick(lower_slopes.astype(jnp.float32), slopes[first])
+    hidden = in_order(hidden, other_core(hidden))
+    lower_slopes = pick(lower_slopes.astype(jnp.float32), part_of(slopes, 0))
     low_rest = to_lower(low)
-    low_total = back_total(low, halves(low_down, 0))
-    incoming = jnp.concatenate([pick(top[0], low), pick(top[1], low_rest)], axis=0)
+    low_share = back_share(low, halves(low_down, 0))
+    incoming = pick(gathered, both_parts(low, low_rest))
     grad_down = contract(hidden, incoming, 0, 0).astype(jnp.bfloat16)
-    low_total, grad_down, low_up = together(low_total, grad_down, low_up)
-    low_slope = slope_of(low_total, lower_slopes)
-    low_slope_rest = to_lower(low_slope[0])
-    low_blocks = spread_wide(back_through_up(low_slope, halves(low_up, 1)))
-    slope_grad = jnp.concatenate(
-        [
-            in_order(*[pick(u, l) for u, l in zip(top_slope, low_slope)]),
-            in_order(
-                pick(top_slope_rest[0], low_slope_rest),
-                pick(top_slope_rest[1], other_core(low_slope_rest)),
-            ),
-        ],
-        axis=0,
-    )
-    grad_up = contract(jnp.concatenate(saved, axis=0), slope_grad, 0, 0).astype(jnp.bfloat16)
+    low_share, rest = together(low_share, rest)
+    low_mine = gather_x((low_share * lower_slopes).astype(jnp.bfloat16))
+    low_up = [pick(most[depth:], w_up[:some]), pick(rest, w_up[some:])]
+    low_mine, grad_down, *low_up = together(low_mine, grad_down, *low_up)
+    low_slope = (low_mine, other_core(low_mine))
+    low_slope_rest = to_lower(low_mine)
+    low_blocks = spread_wide(
+        jnp.concatenate([back_through_up(low_slope, halves(piece, 1)) for piece in low_up], axis=1)
+    )
+    slope_grad = both_parts(
+        in_order(*[pick(u, l) for u, l in zip(top_slope[0], low_slope)]),
+        in_order(
+            pick(top_slope[1][0], low_slope_rest),
+            pick(top_slope[1][1], other_core(low_slope_rest)),
+        ),
+    )
+    grad_up = contract(saved, slope_grad, 0, 0).astype(jnp.bfloat16)
     low_blocks, grad_up = together(low_blocks, grad_up)
     bottom = (middle.astype(jnp.float32) + add_blocks(low_blocks)).astype(jnp.bfloat16)
 

time: 211 us -> 227 us (1.076)
  waiting for transfers between devices: 98.9 us -> 70.3 us
  blocking collectives: 0 us -> 24.4 us
  local copies, waits for them, and re-layouts: 7.34 us -> 22.4 us
  starting transfers between devices: 59.7 us -> 64 us
    ppermute x12 -> x6, waiting for transfers between devices: 40.2 us -> 8.66 us  [step_x(): return lax.ppermute(block, 'x', [(i, (i + distance) % X) for i in range(X)])]
    all_to_all x0 -> x2, blocking collectives: none -> 24.4 us  [the longest x1 13.5 us: spread_x(): lax.all_to_all(partial.astype(jnp.bfloat16).reshape(X, rows // X, cols),...]
    all_to_all x2, waiting for transfers between devices: 1.52 us -> 12.6 us  [gather_wide(): lax.all_to_all(jnp.broadcast_to(block[None], (WIDE, rows, cols)), WIDE_AX...]
    unnamed x44 -> x41, local copies, waits for them, and re-layouts: 0.09 us -> 11 us
    ppermute x12 -> x6, starting transfers between devices: 19.8 us -> 9.5 us  [step_x(): return lax.ppermute(block, 'x', [(i, (i + distance) % X) for i in range(X)])]
    ppermute x3, starting transfers between devices: 6.45 us -> 15.3 us  [to_lower(): return lax.ppermute(block, CROSS_AXES, [(3, 0), (2, 1)])]
    all_to_all x2, waiting for transfers between devices: 20.3 us -> 11.5 us  [spread_wide(): lax.all_to_all(partial.reshape(WIDE, rows // WIDE, cols), WIDE_AXES, 0, 0...]
    ppermute x3, waiting for transfers between devices: 25.4 us -> 17.5 us  [to_upper(): return lax.ppermute(block, CROSS_AXES, [(0, 3), (1, 2)])]
  transfers between devices with their start and end apart: 33 -> 28, of which waited for: 21 -> 17; matrix products, arithmetic and copies ran while one was open for 21% -> 25% of each run, Pallas kernels for 0% -> 0%
where the time goes in v6:
time: 227 us; the launch traced here: 225 us
  waiting for transfers between devices  70.3 us (31%)
  starting transfers between devices  64 us (28%)
  blocking collectives  24.4 us (11%)
  local copies, waits for them, and re-layouts  22.4 us (10%)
  matrix products  21.8 us (10%)
  other arithmetic  20.8 us (9%)
    dot_general x16, matrix products, contract(): lax.dot_general(first_op, second_op, (((first_dim,), (second_dim,)), ((),...  21.8 us
    ppermute x3, waiting for transfers between devices, to_upper(): return lax.ppermute(block, CROSS_AXES, [(0, 3), (1, 2)])  17.5 us
    ppermute x3, starting transfers between devices, to_lower(): return lax.ppermute(block, CROSS_AXES, [(3, 0), (2, 1)])  15.3 us
    all_to_all x2, starting transfers between devices, gather_wide(): lax.all_to_all(jnp.broadcast_to(block[None], (WIDE, rows, cols)), WIDE_AX...  14.8 us
    all_to_all x1, blocking collectives, spread_x(): lax.all_to_all(partial.astype(jnp.bfloat16).reshape(X, rows // X, cols),...  13.5 us
    all_to_all x2, starting transfers between devices, spread_wide(): lax.all_to_all(partial.reshape(WIDE, rows // WIDE, cols), WIDE_AXES, 0, 0...  13.1 us
    all_to_all x2, waiting for transfers between devices, gather_wide(): lax.all_to_all(jnp.broadcast_to(block[None], (WIDE, rows, cols)), WIDE_AX...  12.6 us
    all_to_all x2, waiting for transfers between devices, spread_wide(): lax.all_to_all(partial.reshape(WIDE, rows // WIDE, cols), WIDE_AXES, 0, 0...  11.5 us
  transfers between devices with their start and end apart: 28, of which 17 were waited for; matrix products, arithmetic and copies ran while one was open for 25% of the time, Pallas kernels for 0%

profile of v6, /device:TPU:56, one launch (start us, length us, event | category | flops | bytes accessed | tf_op | source)
XLA Modules:
  0.0 224.8 jit_solution(14820960961753064195)
XLA Ops:
  0.7 2.1 broadcast_in_dim.14
  2.7 9.5 %all-to-all-start = ((bf16[16,32,1024]{2,1,0:T(8,128)(2,1)}), bf16[16,32,1024]{2,1,0:T(8,128)(2,1)}, u32[]{:S(2)}, u32[]{:S(2)}) async-start(bf16[16,32,1024]{2,1,0:T(8,128)(2,1)} %broadcast_in_dim.14), calls=%async_computation | async-start | bytes 2097152 | tf_op jit(solution)/shard_map/all_to_all | solution.py:123
  12.2 1.5 fusion.2
  13.8 2.2 %collective-permute-done = bf16[512,512]{1,0:T(8,128)(2,1)} collective-permute-done((bf16[512,512]{1,0:T(8,128)(2,1)}, bf16[512,512]{1,0:T(8,128)(2,1)}, u32[]{:S(2)}, u32[]{:S(2)}) %collective-permute-start) | collective-permute-done | bytes 524320 | tf_op jit(solution)/shard_map/ppermute | solution.py:39
  16.0 1.7 convert_add_fusion
  17.8 1.0 copy-done.11
  19.6 3.0 %collective-permute-start.3 = (bf16[128,512]{1,0:T(8,128)(2,1)}, bf16[128,512]{1,0:T(8,128)(2,1)S(1)}, u32[]{:S(2)}, u32[]{:S(2)}) collective-permute-start(bf16[128,512]{1,0:T(8,128)(2,1)} %get-tuple-element.61), channel_id=1, source_target_pairs={{0,4},{2,6},{4,0},{6,2},{1,5},{3,7},{5,1},{7,3},{8,12},{10,14},{12... | collective-permute-start | bytes 393224 | tf_op jit(solution)/shard_map/ppermute | solution.py:86
  22.6 1.1 collective-permute-start.2
  23.7 0.9 collective-permute-start.1
  24.6 3.0 %collective-permute-done.3 = bf16[128,512]{1,0:T(8,128)(2,1)S(1)} collective-permute-done((bf16[128,512]{1,0:T(8,128)(2,1)}, bf16[128,512]{1,0:T(8,128)(2,1)S(1)}, u32[]{:S(2)}, u32[]{:S(2)}) %collective-permute-start.3) | collective-permute-done | bytes 131104 | tf_op jit(solution)/shard_map/ppermute | solution.py:86
  27.6 2.1 collective-permute-done.2
  30.4 1.1 fusion.52
  31.5 7.0 %all-to-all-done = bf16[16,32,1024]{2,1,0:T(8,128)(2,1)} async-done(((bf16[16,32,1024]{2,1,0:T(8,128)(2,1)}), bf16[16,32,1024]{2,1,0:T(8,128)(2,1)}, u32[]{:S(2)}, u32[]{:S(2)}) %all-to-all-start) | async-done | bytes 1048608 | tf_op jit(solution)/shard_map/all_to_all | solution.py:123
  38.5 2.3 %convolution_convert_fusion.2 = bf16[512,512]{1,0:T(8,128)(2,1)S(1)} fusion(bf16[512,1024]{1,0:T(8,128)(2,1)} %bitcast, bf16[1,1024,1024]{2,1,0:T(8,128)(2,1)} %param.7, s32[]{:T(128)S(6)} %select_n.141), kind=kOutput, calls=%fused_computation.10 | convolution fusion | flops 537133056 | bytes 2621444 | tf_op jit(solution)/shard_map/dot_general | solution.py:26
  40.9 1.1 slice_bitcast_fusion
  42.8 2.0 pad_maximum_fusion
  44.7 1.3 collective-permute-start.12
  46.0 2.0 add_convert_fusion
  48.0 13.5 %all_to_all.40 = bf16[4,128,512]{2,1,0:T(8,128)(2,1)S(1)} all-to-all(bf16[4,128,512]{2,1,0:T(8,128)(2,1)S(1)} %bitcast.145), channel_id=1, replica_groups=mesh['section'=2,'ylo'=2,'z'=8,'x'=4,'core'=2] {'x'}, dimensions={0} | all-to-all | bytes 1048576 | tf_op jit(solution)/shard_map/all_to_all | solution.py:72
  61.6 0.9 fusion.50
  62.6 10.9 %all_to_all.41 = bf16[4,128,512]{2,1,0:T(8,128)(2,1)S(1)} all-to-all(bf16[4,128,512]{2,1,0:T(8,128)(2,1)S(1)} %broadcast_in_dim.15), channel_id=1, replica_groups=mesh['section'=2,'ylo'=2,'z'=8,'x'=4,'core'=2] {'x'}, dimensions={0} | all-to-all | bytes 1048576 | tf_op jit(solution)/shard_map/all_to_all | solution.py:80
  75.1 1.3 fusion.1
  76.4 7.5 %collective-permute-start.7 = (bf16[256,1024]{1,0:T(8,128)(2,1)}, bf16[256,1024]{1,0:T(8,128)(2,1)}, u32[]{:S(2)}, u32[]{:S(2)}) collective-permute-start(bf16[256,1024]{1,0:T(8,128)(2,1)} %fusion.1), channel_id=1, source_target_pairs={{192,0},{128,64},{193,1},{129,65},{194,2},{130,66},{195,3},{131,67... | collective-permute-start | bytes 1572872 | tf_op jit(solution)/shard_map/ppermute | solution.py:47
  83.9 1.5 slice.68
  85.5 1.3 collective-permute-start.13
  87.3 7.6 %collective-permute-done.7 = bf16[256,1024]{1,0:T(8,128)(2,1)} collective-permute-done((bf16[256,1024]{1,0:T(8,128)(2,1)}, bf16[256,1024]{1,0:T(8,128)(2,1)}, u32[]{:S(2)}, u32[]{:S(2)}) %collective-permute-start.7) | collective-permute-done | bytes 524320 | tf_op jit(solution)/shard_map/ppermute | solution.py:47
  94.9 2.3 %fusion.3 = bf16[256,1024]{1,0:T(8,128)(2,1)} fusion(bf16[256,1024]{1,0:T(8,128)(2,1)} %collective-permute-done.7, f32[256,1024]{1,0:T(8,128)S(1)} %fusion.21, bf16[256,512]{1,0:T(8,128)(2,1)} %collective-permute-done.5, bf16[1,1024,1024]{2,1,0:T(8,128)(2,1)S(1)} %copy-done.1, s32[]{:T(128)S(6)} %select_n.141, pred[]{:T(512)S(6)} %eq.8), kind=kOutput, calls=%fused_computation.13 | convolution fusion | flops 269221888 | bytes 3407877 | tf_op jit(solution)/shard_map/dot_general | solution.py:26
  97.2 5.3 %all-to-all-start.3 = ((bf16[16,16,1024]{2,1,0:T(8,128)(2,1)}), bf16[16,16,1024]{2,1,0:T(8,128)(2,1)}, u32[]{:S(2)}, u32[]{:S(2)}) async-start(bf16[16,16,1024]{2,1,0:T(8,128)(2,1)} %bitcast.133), calls=%async_computation.3 | async-start | bytes 1048576 | tf_op jit(solution)/shard_map/all_to_all | solution.py:112
  102.5 16.1 %collective-permute-done.12 = bf16[1536,1024]{1,0:T(8,128)(2,1)} collective-permute-done((bf16[1536,1024]{1,0:T(8,128)(2,1)}, bf16[1536,1024]{1,0:T(8,128)(2,1)}, u32[]{:S(2)}, u32[]{:S(2)}) %collective-permute-start.12) | collective-permute-done | bytes 3145760 | tf_op jit(solution)/shard_map/ppermute | solution.py:43
  118.6 3.8 %slice_select_fusion = bf16[1024,1024]{1,0:T(8,128)(2,1)} fusion(bf16[1536,1024]{1,0:T(8,128)(2,1)} %collective-permute-done.12, pred[]{:T(512)S(6)} %eq.8, bf16[1,1024,1024]{2,1,0:T(8,128)(2,1)} %param.7), kind=kLoop, calls=%fused_computation.1 | loop fusion | flops 1048576 | bytes 6291457 | tf_op jit(solution)/shard_map/jit(_where)/select_n | solution.py:144
  122.4 2.8 %collective-permute-start.9 = (bf16[128,512]{1,0:T(8,128)(2,1)S(1)}, bf16[128,512]{1,0:T(8,128)(2,1)S(1)}, u32[]{:S(2)}, u32[]{:S(2)}) collective-permute-start(bf16[128,512]{1,0:T(8,128)(2,1)S(1)} %get-tuple-element.23), channel_id=1, source_target_pairs={{0,6},{2,0},{4,2},{6,4},{1,7},{3,1},{5,3},{7,5},{8,14},{10,8},{12,... | collective-permute-start | bytes 393224 | tf_op jit(solution)/shard_map/ppermute | solution.py:86
  126.0 0.9 collective-permute-start.11
  127.5 1.7 collective-permute-done.9
  129.9 1.8 collective-permute-done.10
  132.4 1.1 convert_reduce_fusion.1
  134.9 0.9 broadcast_in_dim.16
  135.8 5.3 %all-to-all-start.4 = ((bf16[16,16,1024]{2,1,0:T(8,128)(2,1)}), bf16[16,16,1024]{2,1,0:T(8,128)(2,1)}, u32[]{:S(2)}, u32[]{:S(2)}) async-start(bf16[16,16,1024]{2,1,0:T(8,128)(2,1)} %broadcast_in_dim.16), calls=%async_computation.4 | async-start | bytes 1048576 | tf_op jit(solution)/shard_map/all_to_all | solution.py:123
  141.2 1.6 bitcast_dynamic-update-slice_fusion
  144.7 1.9 constant_dynamic-slice_fusion
  146.6 1.3 collective-permute-start.15
  147.9 5.7 %all-to-all-done.4 = bf16[16,16,1024]{2,1,0:T(8,128)(2,1)} async-done(((bf16[16,16,1024]{2,1,0:T(8,128)(2,1)}), bf16[16,16,1024]{2,1,0:T(8,128)(2,1)}, u32[]{:S(2)}, u32[]{:S(2)}) %all-to-all-start.4) | async-done | bytes 524320 | tf_op jit(solution)/shard_map/all_to_all | solution.py:123
  153.6 1.9 convolution_convert_fusion.3
  155.6 1.5 collective-permute-done.14
  157.1 2.6 %fusion.4 = bf16[256,512]{1,0:T(8,128)(2,1)} fusion(bf16[256,1024]{1,0:T(8,128)(2,1)} %bitcast.18, bf16[1024,1024]{1,0:T(8,128)(2,1)} %slice_select_fusion, s32[]{:T(128)S(6)} %select_n.140, bf16[256,512]{1,0:T(8,128)(2,1)S(1)} %collective-permute-done.14), kind=kOutput, calls=%fused_computation.16 | convolution fusion | flops 268828672 | bytes 2097156 | tf_op jit(solution)/shard_map/dot_general | solution.py:26
  159.7 3.4 %all-to-all-start.5 = ((bf16[4,64,512]{2,1,0:T(8,128)(2,1)}), bf16[4,64,512]{2,1,0:T(8,128)(2,1)S(1)}, u32[]{:S(2)}, u32[]{:S(2)}) async-start(bf16[4,64,512]{2,1,0:T(8,128)(2,1)} %bitcast.28), calls=%async_computation.5 | async-start | bytes 524288 | tf_op jit(solution)/shard_map/all_to_all | solution.py:72
  163.1 2.1 collective-permute-start.17
  165.2 1.6 slice.55
  166.9 3.4 %all-to-all-done.5 = bf16[4,64,512]{2,1,0:T(8,128)(2,1)S(1)} async-done(((bf16[4,64,512]{2,1,0:T(8,128)(2,1)}), bf16[4,64,512]{2,1,0:T(8,128)(2,1)S(1)}, u32[]{:S(2)}, u32[]{:S(2)}) %all-to-all-start.5) | async-done | bytes 262176 | tf_op jit(solution)/shard_map/all_to_all | solution.py:72
  170.3 1.3 collective-permute-done.15
  171.7 0.9 fusion.54
  173.3 3.4 %all-to-all-start.6 = ((bf16[4,64,512]{2,1,0:T(8,128)(2,1)}), bf16[4,64,512]{2,1,0:T(8,128)(2,1)S(1)}, u32[]{:S(2)}, u32[]{:S(2)}) async-start(bf16[4,64,512]{2,1,0:T(8,128)(2,1)} %broadcast_in_dim.17), calls=%async_computation.6 | async-start | bytes 524288 | tf_op jit(solution)/shard_map/all_to_all | solution.py:80
  177.1 1.3 pad_maximum_fusion.1
  178.5 3.6 %broadcast_select_fusion = (bf16[512,1024]{1,0:T(8,128)(2,1)}, bf16[512,1024]{1,0:T(8,128)(2,1)}, bf16[512,1024]{1,0:T(8,128)(2,1)S(1)}) fusion(bf16[512,1024]{1,0:T(8,128)(2,1)} %collective-permute-done.15, pred[]{:T(512)S(6)} %eq.8, bf16[1,1024,1024]{2,1,0:T(8,128)(2,1)S(1)} %copy-done.1, bf16[1536,1024]{1,0:T(8,128)(2,1)} %collective-permute-done.12, ...), kind=kLoop, calls=%fused_computation.52 | loop fusion | flops 1572864 | bytes 9437185 | tf_op jit(solution)/shard_map/jit(_where)/select_n | solution.py:144
  182.0 1.2 broadcast_select_fusion.2
  183.2 2.6 %convolution_convert_fusion = bf16[1024,1024]{1,0:T(8,128)(2,1)} fusion(bf16[512,1024]{1,0:T(8,128)(2,1)S(1)} %get-tuple-element.66, bf16[512,512]{1,0:T(8,128)(2,1)S(1)} %get-tuple-element.57, bf16[512,512]{1,0:T(8,128)(2,1)S(1)} %get-tuple-element.56), kind=kOutput, calls=%fused_computation.3 | convolution fusion | flops 1076887552 | bytes 4194304 | tf_op jit(solution)/shard_map/dot_general | solution.py:26
  185.9 5.7 %collective-permute-start.19 = (bf16[256,512]{1,0:T(8,128)(2,1)S(1)}, bf16[256,512]{1,0:T(8,128)(2,1)}, u32[]{:S(2)}, u32[]{:S(2)}) collective-permute-start(bf16[256,512]{1,0:T(8,128)(2,1)S(1)} %bitcast.125), channel_id=1, source_target_pairs={{192,0},{128,64},{193,1},{129,65},{194,2},{130,66},{195,3},{131,67... | collective-permute-start | bytes 786440 | tf_op jit(solution)/shard_map/ppermute | solution.py:47
  193.9 7.8 %all-to-all-start.7 = ((bf16[16,16,1024]{2,1,0:T(8,128)(2,1)}), bf16[16,16,1024]{2,1,0:T(8,128)(2,1)}, u32[]{:S(2)}, u32[]{:S(2)}) async-start(bf16[16,16,1024]{2,1,0:T(8,128)(2,1)} %bitcast.35), calls=%async_computation.7 | async-start | bytes 1048576 | tf_op jit(solution)/shard_map/all_to_all | solution.py:112
  201.9 1.6 collective-permute-done.20
  203.5 1.0 broadcast_select_fusion.8
  204.7 1.3 convert_bitcast_fusion
  206.0 11.5 %all-to-all-done.7 = bf16[16,16,1024]{2,1,0:T(8,128)(2,1)} async-done(((bf16[16,16,1024]{2,1,0:T(8,128)(2,1)}), bf16[16,16,1024]{2,1,0:T(8,128)(2,1)}, u32[]{:S(2)}, u32[]{:S(2)}) %all-to-all-start.7) | async-done | bytes 524320 | tf_op jit(solution)/shard_map/all_to_all | solution.py:112
  217.5 1.1 convert_reduce_fusion
  218.7 2.6 %copy.12 = bf16[1,1024,1024]{2,1,0:T(8,128)(2,1)} copy(bf16[1,1024,1024]{1,2,0:T(8,128)(2,1)S(1)} %bitcast.136) | data formatting | bytes 4194304
  221.3 2.8 %collective-permute-done.21 = bf16[16,1024]{1,0:T(8,128)(2,1)S(1)} collective-permute-done((bf16[16,1024]{1,0:T(8,128)(2,1)S(1)}, bf16[16,1024]{1,0:T(8,128)(2,1)S(1)}, u32[]{:S(2)}, u32[]{:S(2)}) %collective-permute-start.21) | collective-permute-done | bytes 32800 | tf_op jit(solution)/shard_map/ppermute | solution.py:218
  (85 shorter events, 15.6 us)
Async XLA Ops:
  0.6 11.6 %copy-start = (bf16[1,512,1024]{2,1,0:T(8,128)(2,1)S(1)}, bf16[1,512,1024]{2,1,0:T(8,128)(2,1)}, u32[]{:S(2)}) copy-start(bf16[1,512,1024]{2,1,0:T(8,128)(2,1)} %param.4) | copy-start | bytes 3145732
  0.6 11.6 %copy-start.1 = (bf16[1,1024,1024]{2,1,0:T(8,128)(2,1)S(1)}, bf16[1,1024,1024]{2,1,0:T(8,128)(2,1)}, u32[]{:S(2)}) copy-start(bf16[1,1024,1024]{2,1,0:T(8,128)(2,1)} %param.6) | copy-start | bytes 6291460
  2.7 35.8 %all-to-all-start = ((bf16[16,32,1024]{2,1,0:T(8,128)(2,1)}), bf16[16,32,1024]{2,1,0:T(8,128)(2,1)}, u32[]{:S(2)}, u32[]{:S(2)}) async-start(bf16[16,32,1024]{2,1,0:T(8,128)(2,1)} %broadcast_in_dim.14), calls=%async_computation | async-start | bytes 2097152 | tf_op jit(solution)/shard_map/all_to_all | solution.py:123
  13.8 2.3 %collective-permute-start = (bf16[512,512]{1,0:T(8,128)(2,1)}, bf16[512,512]{1,0:T(8,128)(2,1)}, u32[]{:S(2)}, u32[]{:S(2)}) collective-permute-start(bf16[512,512]{1,0:T(8,128)(2,1)} %fusion.2), channel_id=1, source_target_pairs={{0,1},{1,0},{2,3},{3,2},{4,5},{5,4},{6,7},{7,6},{8,9},{9,8},{10,11... | collective-permute-start | bytes 1572872 | tf_op jit(solution)/shard_map/ppermute | solution.py:39
  17.8 1.0 copy-start.11
  19.6 8.1 %collective-permute-start.3 = (bf16[128,512]{1,0:T(8,128)(2,1)}, bf16[128,512]{1,0:T(8,128)(2,1)S(1)}, u32[]{:S(2)}, u32[]{:S(2)}) collective-permute-start(bf16[128,512]{1,0:T(8,128)(2,1)} %get-tuple-element.61), channel_id=1, source_target_pairs={{0,4},{2,6},{4,0},{6,2},{1,5},{3,7},{5,1},{7,3},{8,12},{10,14},{12... | collective-permute-start | bytes 393224 | tf_op jit(solution)/shard_map/ppermute | solution.py:86
  22.6 7.1 %collective-permute-start.2 = (bf16[128,512]{1,0:T(8,128)(2,1)}, bf16[128,512]{1,0:T(8,128)(2,1)S(1)}, u32[]{:S(2)}, u32[]{:S(2)}) collective-permute-start(bf16[128,512]{1,0:T(8,128)(2,1)} %get-tuple-element.62), channel_id=1, source_target_pairs={{0,6},{2,0},{4,2},{6,4},{1,7},{3,1},{5,3},{7,5},{8,14},{10,8},{12,... | collective-permute-start | bytes 393224 | tf_op jit(solution)/shard_map/ppermute | solution.py:86
  23.7 6.7 %collective-permute-start.1 = (bf16[128,512]{1,0:T(8,128)(2,1)S(1)}, bf16[128,512]{1,0:T(8,128)(2,1)}, u32[]{:S(2)}, u32[]{:S(2)}) collective-permute-start(bf16[128,512]{1,0:T(8,128)(2,1)S(1)} %get-tuple-element.60), channel_id=1, source_target_pairs={{0,2},{2,4},{4,6},{6,0},{1,3},{3,5},{5,7},{7,1},{8,10},{10,12},{12... | collective-permute-start | bytes 393224 | tf_op jit(solution)/shard_map/ppermute | solution.py:86
  29.7 0.7 copy-start.16
  40.8 2.0 copy-start.2
  40.8 5.2 %collective-permute-start.4 = (bf16[512,512]{1,0:T(8,128)(2,1)S(1)}, bf16[512,512]{1,0:T(8,128)(2,1)S(1)}, u32[]{:S(2)}, u32[]{:S(2)}) collective-permute-start(bf16[512,512]{1,0:T(8,128)(2,1)S(1)} %convolution_convert_fusion.2), channel_id=1, source_target_pairs={{0,1},{1,0},{2,3},{3,2},{4,5},{5,4},{6,7},{7,6},{8,9},{9,8},{10,11... | collective-permute-start | bytes 1572872 | tf_op jit(solution)/shard_map/ppermute | solution.py:39
  44.7 73.9 %collective-permute-start.12 = (bf16[1536,1024]{1,0:T(8,128)(2,1)}, bf16[1536,1024]{1,0:T(8,128)(2,1)}, u32[]{:S(2)}, u32[]{:S(2)}) collective-permute-start(bf16[1536,1024]{1,0:T(8,128)(2,1)} %pad_maximum_fusion), channel_id=1, source_target_pairs={{0,192},{64,128},{1,193},{65,129},{2,194},{66,130},{3,195},{67,131... | collective-permute-start | bytes 9437192 | tf_op jit(solution)/shard_map/ppermute | solution.py:43
  73.5 0.7 copy-start.7
  73.5 13.3 %copy-start.5 = (bf16[16,1,16,512]{3,2,1,0:T(8,128)(2,1)}, bf16[16,1,16,512]{3,2,1,0:T(8,128)(2,1)S(1)}, u32[]{:S(2)}) copy-start(bf16[16,1,16,512]{3,2,1,0:T(8,128)(2,1)S(1)} %get-tuple-element.58) | copy-start | bytes 786436
  73.5 1.6 collective-permute-start.6
  75.1 8.8 %copy-start.12 = (bf16[256,512]{1,0:T(8,128)(2,1)}, bf16[256,512]{1,0:T(8,128)(2,1)S(1)}, u32[]{:S(2)}) copy-start(bf16[256,512]{1,0:T(8,128)(2,1)S(1)} %collective-permute-done.6) | copy-start | bytes 786436
  76.4 18.5 %collective-permute-start.7 = (bf16[256,1024]{1,0:T(8,128)(2,1)}, bf16[256,1024]{1,0:T(8,128)(2,1)}, u32[]{:S(2)}, u32[]{:S(2)}) collective-permute-start(bf16[256,1024]{1,0:T(8,128)(2,1)} %fusion.1), channel_id=1, source_target_pairs={{192,0},{128,64},{193,1},{129,65},{194,2},{130,66},{195,3},{131,67... | collective-permute-start | bytes 1572872 | tf_op jit(solution)/shard_map/ppermute | solution.py:47
  83.9 3.3 %collective-permute-start.5 = (bf16[256,512]{1,0:T(8,128)(2,1)S(1)}, bf16[256,512]{1,0:T(8,128)(2,1)}, u32[]{:S(2)}, u32[]{:S(2)}) collective-permute-start(bf16[256,512]{1,0:T(8,128)(2,1)S(1)} %bitcast.129), channel_id=1, source_target_pairs={{0,1},{1,0},{2,3},{3,2},{4,5},{5,4},{6,7},{7,6},{8,9},{9,8},{10,11... | collective-permute-start | bytes 786440 | tf_op jit(solution)/shard_map/ppermute | solution.py:39
  85.5 62.4 %collective-permute-start.13 = (bf16[64,512]{1,0:T(8,128)(2,1)}, bf16[64,512]{1,0:T(8,128)(2,1)}, u32[]{:S(2)}, u32[]{:S(2)}) collective-permute-start(bf16[64,512]{1,0:T(8,128)(2,1)} %bitcast.27), channel_id=1, source_target_pairs={{0,192},{64,128},{1,193},{65,129},{2,194},{66,130},{3,195},{67,131... | collective-permute-start | bytes 196616 | tf_op jit(solution)/shard_map/ppermute | solution.py:43
  97.2 35.2 %all-to-all-start.3 = ((bf16[16,16,1024]{2,1,0:T(8,128)(2,1)}), bf16[16,16,1024]{2,1,0:T(8,128)(2,1)}, u32[]{:S(2)}, u32[]{:S(2)}) async-start(bf16[16,16,1024]{2,1,0:T(8,128)(2,1)} %bitcast.133), calls=%async_computation.3 | async-start | bytes 1048576 | tf_op jit(solution)/shard_map/all_to_all | solution.py:112
  122.4 6.8 %collective-permute-start.9 = (bf16[128,512]{1,0:T(8,128)(2,1)S(1)}, bf16[128,512]{1,0:T(8,128)(2,1)S(1)}, u32[]{:S(2)}, u32[]{:S(2)}) collective-permute-start(bf16[128,512]{1,0:T(8,128)(2,1)S(1)} %get-tuple-element.23), channel_id=1, source_target_pairs={{0,6},{2,0},{4,2},{6,4},{1,7},{3,1},{5,3},{7,5},{8,14},{10,8},{12,... | collective-permute-start | bytes 393224 | tf_op jit(solution)/shard_map/ppermute | solution.py:86
  125.2 6.6 %collective-permute-start.10 = (bf16[128,512]{1,0:T(8,128)(2,1)S(1)}, bf16[128,512]{1,0:T(8,128)(2,1)S(1)}, u32[]{:S(2)}, u32[]{:S(2)}) collective-permute-start(bf16[128,512]{1,0:T(8,128)(2,1)S(1)} %get-tuple-element.23), channel_id=1, source_target_pairs={{0,4},{2,6},{4,0},{6,2},{1,5},{3,7},{5,1},{7,3},{8,12},{10,14},{12... | collective-permute-start | bytes 393224 | tf_op jit(solution)/shard_map/ppermute | solution.py:86
  126.0 15.2 %collective-permute-start.11 = (bf16[128,512]{1,0:T(8,128)(2,1)S(1)}, bf16[128,512]{1,0:T(8,128)(2,1)}, u32[]{:S(2)}, u32[]{:S(2)}) collective-permute-start(bf16[128,512]{1,0:T(8,128)(2,1)S(1)} %get-tuple-element.23), channel_id=1, source_target_pairs={{0,2},{2,4},{4,6},{6,0},{1,3},{3,5},{5,7},{7,1},{8,10},{10,12},{12... | collective-permute-start | bytes 393224 | tf_op jit(solution)/shard_map/ppermute | solution.py:86
  134.3 0.6 copy-start.14
  135.8 17.8 %all-to-all-start.4 = ((bf16[16,16,1024]{2,1,0:T(8,128)(2,1)}), bf16[16,16,1024]{2,1,0:T(8,128)(2,1)}, u32[]{:S(2)}, u32[]{:S(2)}) async-start(bf16[16,16,1024]{2,1,0:T(8,128)(2,1)} %broadcast_in_dim.16), calls=%async_computation.4 | async-start | bytes 1048576 | tf_op jit(solution)/shard_map/all_to_all | solution.py:123
  146.6 25.0 %collective-permute-start.15 = (bf16[512,1024]{1,0:T(8,128)(2,1)}, bf16[512,1024]{1,0:T(8,128)(2,1)}, u32[]{:S(2)}, u32[]{:S(2)}) collective-permute-start(bf16[512,1024]{1,0:T(8,128)(2,1)} %get-tuple-element.26), channel_id=1, source_target_pairs={{0,192},{64,128},{1,193},{65,129},{2,194},{66,130},{3,195},{67,131... | collective-permute-start | bytes 3145736 | tf_op jit(solution)/shard_map/ppermute | solution.py:43
  153.6 13.2 %copy-start.15 = (bf16[16,1024]{1,0:T(8,128)(2,1)S(1)}, bf16[16,1024]{1,0:T(8,128)(2,1)}, u32[]{:S(2)}) copy-start(bf16[16,1024]{1,0:T(8,128)(2,1)} %copy-done.14) | copy-start | bytes 98308
  155.5 1.6 collective-permute-start.14
  159.7 10.6 %all-to-all-start.5 = ((bf16[4,64,512]{2,1,0:T(8,128)(2,1)}), bf16[4,64,512]{2,1,0:T(8,128)(2,1)S(1)}, u32[]{:S(2)}, u32[]{:S(2)}) async-start(bf16[4,64,512]{2,1,0:T(8,128)(2,1)} %bitcast.28), calls=%async_computation.5 | async-start | bytes 524288 | tf_op jit(solution)/shard_map/all_to_all | solution.py:72
  163.1 14.1 %collective-permute-start.17 = (bf16[256,1024]{1,0:T(8,128)(2,1)}, bf16[256,1024]{1,0:T(8,128)(2,1)}, u32[]{:S(2)}, u32[]{:S(2)}) collective-permute-start(bf16[256,1024]{1,0:T(8,128)(2,1)} %bitcast.18), channel_id=1, source_target_pairs={{192,0},{128,64},{193,1},{129,65},{194,2},{130,66},{195,3},{131,67... | collective-permute-start | bytes 1572872 | tf_op jit(solution)/shard_map/ppermute | solution.py:47
  166.8 51.8 %collective-permute-start.8 = (bf16[16,1024]{1,0:T(8,128)(2,1)S(1)}, bf16[16,1024]{1,0:T(8,128)(2,1)S(1)}, u32[]{:S(2)}, u32[]{:S(2)}) collective-permute-start(bf16[16,1024]{1,0:T(8,128)(2,1)S(1)} %copy-done.15), channel_id=1, source_target_pairs={{0,128},{128,0},{1,129},{129,1},{2,130},{130,2},{3,131},{131,3},{4... | collective-permute-start | bytes 98312 | tf_op jit(solution)/shard_map/ppermute | solution.py:217
  166.8 15.3 %collective-permute-start.16 = (bf16[512,512]{1,0:T(8,128)(2,1)}, bf16[512,512]{1,0:T(8,128)(2,1)}, u32[]{:S(2)}, u32[]{:S(2)}) collective-permute-start(bf16[512,512]{1,0:T(8,128)(2,1)} %bitcast.134), channel_id=1, source_target_pairs={{0,1},{1,0},{2,3},{3,2},{4,5},{5,4},{6,7},{7,6},{8,9},{9,8},{10,11... | collective-permute-start | bytes 1572872 | tf_op jit(solution)/shard_map/ppermute | solution.py:39
  173.3 12.5 %all-to-all-start.6 = ((bf16[4,64,512]{2,1,0:T(8,128)(2,1)}), bf16[4,64,512]{2,1,0:T(8,128)(2,1)S(1)}, u32[]{:S(2)}, u32[]{:S(2)}) async-start(bf16[4,64,512]{2,1,0:T(8,128)(2,1)} %broadcast_in_dim.17), calls=%async_computation.6 | async-start | bytes 524288 | tf_op jit(solution)/shard_map/all_to_all | solution.py:80
  178.5 3.6 %copy-start.10 = (bf16[4,128,512]{2,1,0:T(8,128)(2,1)S(1)}, bf16[4,128,512]{2,1,0:T(8,128)(2,1)}, u32[]{:S(2)}) copy-start(bf16[4,128,512]{2,1,0:T(8,128)(2,1)} %constant_dynamic-slice_fusion) | copy-start | bytes 1572868
  183.2 8.3 %copy-start.4 = (bf16[512,1024]{1,0:T(8,128)(2,1)S(1)}, bf16[512,1024]{1,0:T(8,128)(2,1)}, u32[]{:S(2)}) copy-start(bf16[512,1024]{1,0:T(8,128)(2,1)} %get-tuple-element.33) | copy-start | bytes 3145732
  183.2 8.7 %copy-start.3 = (bf16[512,1024]{1,0:T(8,128)(2,1)S(1)}, bf16[512,1024]{1,0:T(8,128)(2,1)}, u32[]{:S(2)}) copy-start(bf16[512,1024]{1,0:T(8,128)(2,1)} %get-tuple-element.32) | copy-start | bytes 3145732
  185.9 6.4 %collective-permute-start.18 = (bf16[256,512]{1,0:T(8,128)(2,1)S(1)}, bf16[256,512]{1,0:T(8,128)(2,1)S(1)}, u32[]{:S(2)}, u32[]{:S(2)}) collective-permute-start(bf16[256,512]{1,0:T(8,128)(2,1)S(1)} %bitcast.124), channel_id=1, source_target_pairs={{0,1},{1,0},{2,3},{3,2},{4,5},{5,4},{6,7},{7,6},{8,9},{9,8},{10,11... | collective-permute-start | bytes 786440 | tf_op jit(solution)/shard_map/ppermute | solution.py:39
  185.9 15.8 %collective-permute-start.19 = (bf16[256,512]{1,0:T(8,128)(2,1)S(1)}, bf16[256,512]{1,0:T(8,128)(2,1)}, u32[]{:S(2)}, u32[]{:S(2)}) collective-permute-start(bf16[256,512]{1,0:T(8,128)(2,1)S(1)} %bitcast.125), channel_id=1, source_target_pairs={{192,0},{128,64},{193,1},{129,65},{194,2},{130,66},{195,3},{131,67... | collective-permute-start | bytes 786440 | tf_op jit(solution)/shard_map/ppermute | solution.py:47
  192.3 1.6 copy-start.9
  192.7 9.1 %copy-start.8 = (bf16[16,1,16,512]{3,2,1,0:T(8,128)(2,1)S(1)}, bf16[16,1,16,512]{3,2,1,0:T(8,128)(2,1)}, u32[]{:S(2)}) copy-start(bf16[16,1,16,512]{3,2,1,0:T(8,128)(2,1)} %copy-done.7) | copy-start | bytes 786436
  192.7 9.1 %copy-start.13 = (bf16[256,512]{1,0:T(8,128)(2,1)S(1)}, bf16[256,512]{1,0:T(8,128)(2,1)}, u32[]{:S(2)}) copy-start(bf16[256,512]{1,0:T(8,128)(2,1)} %copy-done.12) | copy-start | bytes 786436
  193.9 9.6 %copy-start.6 = (bf16[16,1,16,512]{3,2,1,0:T(8,128)(2,1)S(1)}, bf16[16,1,16,512]{3,2,1,0:T(8,128)(2,1)}, u32[]{:S(2)}) copy-start(bf16[16,1,16,512]{3,2,1,0:T(8,128)(2,1)} %copy-done.5) | copy-start | bytes 786436
  193.9 23.6 %all-to-all-start.7 = ((bf16[16,16,1024]{2,1,0:T(8,128)(2,1)}), bf16[16,16,1024]{2,1,0:T(8,128)(2,1)}, u32[]{:S(2)}, u32[]{:S(2)}) async-start(bf16[16,16,1024]{2,1,0:T(8,128)(2,1)} %bitcast.35), calls=%async_computation.7 | async-start | bytes 1048576 | tf_op jit(solution)/shard_map/all_to_all | solution.py:112
  201.7 1.8 collective-permute-start.20
  218.6 5.5 %collective-permute-start.21 = (bf16[16,1024]{1,0:T(8,128)(2,1)S(1)}, bf16[16,1024]{1,0:T(8,128)(2,1)S(1)}, u32[]{:S(2)}, u32[]{:S(2)}) collective-permute-start(bf16[16,1024]{1,0:T(8,128)(2,1)S(1)} %get-tuple-element.47), channel_id=1, source_target_pairs={{0,128},{128,0},{1,129},{129,1},{2,130},{130,2},{3,131},{131,3},{4... | collective-permute-start | bytes 98312 | tf_op jit(solution)/shard_map/ppermute | solution.py:218

commit v7 on v6

--- a/solution.py
+++ b/solution.py
@@ -43,17 +43,25 @@
     return lax.ppermute(block, CROSS_AXES, [(0, 3), (1, 2)])
 
 
+def pair_weights(block):
+    pairs = [[0, 3], [1, 2]]
+    return lax.all_gather(block, CROSS_AXES, axis=0, tiled=True, axis_index_groups=pairs)
+
+
 def to_lower(block):
     return lax.ppermute(block, CROSS_AXES, [(3, 0), (2, 1)])
 
 
-def halves(weight, dim):
-    size = weight.shape[dim] // CORES
+def halves(weight, dim, depth=None):
+    rows, cols = depth or weight.shape[0], weight.shape[1]
     core = lax.axis_index("core")
-    return (
-        lax.dynamic_slice_in_dim(weight, core * size, size, dim),
-        lax.dynamic_slice_in_dim(weight, (1 - core) * size, size, dim),
-    )
+
+    def half(index):
+        if dim == 0:
+            return lax.dynamic_slice(weight, (index * (rows // CORES), 0), (rows // CORES, cols))
+        return lax.dynamic_slice(weight, (0, index * (cols // CORES)), (rows, cols // CORES))
+
+    return half(core), half(1 - core)
 
 
 def in_order(mine, theirs):
@@ -159,49 +167,44 @@
     w_up, w_down = up_weight[0], down_weight[0]
     up_halves, down_halves = halves(w_up, 1), halves(w_down, 0)
 
-    depth = w_down.shape[0]
-    some = w_up.shape[0] // 2
-    most = to_upper(jnp.concatenate([w_down, w_up[:some]], axis=0))
+    low_down = pair_weights(w_down)
 
     theirs = contract(saved, up_halves[1], 1, 0)
     mine = contract(saved, up_halves[0], 1, 0)
     pre = spread_x_beside(pair_sum(mine, theirs))
-    gathered, pre = together(gather_wide(upstream), pre)
     act, slopes = gelu_parts(pre)
-
-    top_mine = gather_x((back_share(gathered, down_halves) * slopes).astype(jnp.bfloat16))
-    top_slope = [part_of(top_mine, c) for c in range(2)]
-    top_slope = [(block, other_core(block)) for block in top_slope]
+    act = act.astype(jnp.bfloat16)
+    slopes = [part_of(slopes, c) for c in range(2)]
+    gathered, act, *slopes = together(gather_wide(upstream), act, *slopes)
+    low_up = pair_weights(together(w_up, act)[0])
+
+    share = back_share(gathered, down_halves)
+    top_mine = [
+        gather_x((part_of(share, c) * slopes[c]).astype(jnp.bfloat16)) for c in range(2)
+    ]
+    top_slope = [(block, other_core(block)) for block in top_mine]
     moved = to_lower(back_through_up(top_slope[0], up_halves))
     partial = pick(back_through_up(top_slope[1], up_halves), moved)
-    partial, act = together(partial, act.astype(jnp.bfloat16))
+    partial, act, sent = together(partial, act, slopes[1].astype(jnp.bfloat16))
     blocks = spread_wide(partial)
     middle = (
         pick(upstream[part:], upstream[:part]).astype(jnp.float32) + add_blocks(blocks)
     ).astype(jnp.bfloat16)
 
-    rest = to_upper(together(w_up[some:], most, blocks)[0])
-    low_down = pick(most[:depth], w_down)
-    lower_slopes = to_upper(part_of(slopes, 1).astype(jnp.bfloat16))
     hidden = gather_x_beside(act)
-    low, hidden, low_down, lower_slopes = together(
-        gather_wide(middle), hidden, low_down, lower_slopes
-    )
+    low, hidden, sent = together(gather_wide(middle), hidden, to_upper(sent))
     hidden = in_order(hidden, other_core(hidden))
-    lower_slopes = pick(lower_slopes.astype(jnp.float32), part_of(slopes, 0))
     low_rest = to_lower(low)
-    low_share = back_share(low, halves(low_down, 0))
+    low_share = back_share(low, halves(low_down, 0, w_down.shape[0]))
     incoming = pick(gathered, both_parts(low, low_rest))
     grad_down = contract(hidden, incoming, 0, 0).astype(jnp.bfloat16)
-    low_share, rest = together(low_share, rest)
-    low_mine = gather_x((low_share * lower_slopes).astype(jnp.bfloat16))
-    low_up = [pick(most[depth:], w_up[:some]), pick(rest, w_up[some:])]
-    low_mine, grad_down, *low_up = together(low_mine, grad_down, *low_up)
+    low_mine = gather_x(
+        (low_share * pick(sent.astype(jnp.float32), slopes[0])).astype(jnp.bfloat16)
+    )
+    low_mine, grad_down = together(low_mine, grad_down)
     low_slope = (low_mine, other_core(low_mine))
     low_slope_rest = to_lower(low_mine)
-    low_blocks = spread_wide(
-        jnp.concatenate([back_through_up(low_slope, halves(piece, 1)) for piece in low_up], axis=1)
-    )
+    low_blocks = spread_wide(back_through_up(low_slope, halves(low_up, 1, w_up.shape[0])))
     slope_grad = both_parts(
         in_order(*[pick(u, l) for u, l in zip(top_slope[0], low_slope)]),
         in_order(
@@ -213,10 +216,8 @@
     low_blocks, grad_up = together(low_blocks, grad_up)
     bottom = (middle.astype(jnp.float32) + add_blocks(low_blocks)).astype(jnp.bfloat16)
 
-    swap = [(0, 1), (1, 0)]
-    upper_first = lax.ppermute(middle, "section", swap)
-    lower_last = lax.ppermute(bottom, "section", swap)
-    grad_in = jnp.concatenate([pick(upper_first, bottom), pick(middle, lower_last)], axis=0)
+    other = lax.ppermute(pick(bottom, middle), "section", [(0, 1), (1, 0)])
+    grad_in = jnp.concatenate([pick(other, bottom), pick(middle, other)], axis=0)
     return grad_in[None], grad_up[None], grad_down[None]
 
 

time: 227 us -> 237 us (1.044)
  waiting for transfers between devices: 70.3 us -> 84.4 us
  between operations: 1.09 us -> 14.5 us
  local copies, waits for them, and re-layouts: 22.4 us -> 10.6 us
  other arithmetic: 20.8 us -> 10.8 us
  blocking collectives: 24.4 us -> 32.9 us
  starting transfers between devices: 64 us -> 56.4 us
  matrix products: 21.8 us -> 25.6 us
    ppermute x3 -> x1, waiting for transfers between devices: 17.5 us -> 0.01 us  [to_upper(): return lax.ppermute(block, CROSS_AXES, [(0, 3), (1, 2)])]
    ppermute x3, waiting for transfers between devices: 8 us -> 24 us  [to_lower(): return lax.ppermute(block, CROSS_AXES, [(3, 0), (2, 1)])]
    all_to_all x1 -> x2, blocking collectives: 10.9 us -> 19.1 us  [gather_x(): lax.all_to_all(jnp.broadcast_to(block[None], (X, rows, cols)), 'x', 0, 0,...]
    select_n x4 -> x3, other arithmetic: 7.36 us -> 1.37 us  [pick(): return jnp.where(is_upper, upper, lower)]
    all_to_all x2, waiting for transfers between devices: 12.6 us -> 18.6 us  [gather_wide(): lax.all_to_all(jnp.broadcast_to(block[None], (WIDE, rows, cols)), WIDE_AX...]
    all_to_all x2, waiting for transfers between devices: 11.5 us -> 17.4 us  [spread_wide(): lax.all_to_all(partial.reshape(WIDE, rows // WIDE, cols), WIDE_AXES, 0, 0...]
    unnamed x41 -> x33, local copies, waits for them, and re-layouts: 11 us -> 5.36 us
    dot_general x16 -> x14, matrix products: 21.8 us -> 25.6 us  [contract(): lax.dot_general(first_op, second_op, (((first_dim,), (second_dim,)), ((),...]
  transfers between devices with their start and end apart: 28 -> 27, of which waited for: 17 -> 19; matrix products, arithmetic and copies ran while one was open for 25% -> 18% of each run, Pallas kernels for 0% -> 0%
where the time goes in v7:
time: 237 us; the launch traced here: 235 us
  waiting for transfers between devices  84.4 us (36%)
  starting transfers between devices  56.4 us (24%)
  blocking collectives  32.9 us (14%)
  matrix products  25.6 us (11%)
  between operations  14.5 us (6%)
  other arithmetic  10.8 us (5%)
  local copies, waits for them, and re-layouts  10.6 us (4%)
    dot_general x14, matrix products, contract(): lax.dot_general(first_op, second_op, (((first_dim,), (second_dim,)), ((),...  25.6 us
    ppermute x3, waiting for transfers between devices, to_lower(): return lax.ppermute(block, CROSS_AXES, [(3, 0), (2, 1)])  24 us
    all_to_all x2, blocking collectives, gather_x(): lax.all_to_all(jnp.broadcast_to(block[None], (X, rows, cols)), 'x', 0, 0,...  19.1 us
    all_to_all x2, waiting for transfers between devices, gather_wide(): lax.all_to_all(jnp.broadcast_to(block[None], (WIDE, rows, cols)), WIDE_AX...  18.6 us
    all_to_all x2, waiting for transfers between devices, spread_wide(): lax.all_to_all(partial.reshape(WIDE, rows // WIDE, cols), WIDE_AXES, 0, 0...  17.4 us
    all_to_all x2, starting transfers between devices, gather_wide(): lax.all_to_all(jnp.broadcast_to(block[None], (WIDE, rows, cols)), WIDE_AX...  14.4 us
    all_to_all x1, blocking collectives, spread_x(): lax.all_to_all(partial.astype(jnp.bfloat16).reshape(X, rows // X, cols),...  13.9 us
    ppermute x3, starting transfers between devices, to_lower(): return lax.ppermute(block, CROSS_AXES, [(3, 0), (2, 1)])  12.8 us
  transfers between devices with their start and end apart: 27, of which 19 were waited for; matrix products, arithmetic and copies ran while one was open for 18% of the time, Pallas kernels for 0%

profile of v7, /device:TPU:56, one launch (start us, length us, event | category | flops | bytes accessed | tf_op | source)
XLA Modules:
  0.0 235.3 jit_solution(7432366755647723117)
XLA Ops:
  7.2 2.1 broadcast_in_dim.16
  9.3 9.5 %all-to-all-start = ((bf16[16,32,1024]{2,1,0:T(8,128)(2,1)}), bf16[16,32,1024]{2,1,0:T(8,128)(2,1)}, u32[]{:S(2)}, u32[]{:S(2)}) async-start(bf16[16,32,1024]{2,1,0:T(8,128)(2,1)} %broadcast_in_dim.16), calls=%async_computation | async-start | bytes 2097152 | tf_op jit(solution)/shard_map/all_to_all | solution.py:131
  18.8 1.5 fusion.3
  20.4 2.2 collective-permute-done
  22.6 1.8 convert_add_fusion
  24.4 1.0 copy-done.3
  25.5 3.1 %collective-permute-start.3 = (bf16[128,512]{1,0:T(8,128)(2,1)S(1)}, bf16[128,512]{1,0:T(8,128)(2,1)}, u32[]{:S(2)}, u32[]{:S(2)}) collective-permute-start(bf16[128,512]{1,0:T(8,128)(2,1)S(1)} %get-tuple-element.51), channel_id=1, source_target_pairs={{0,4},{2,6},{4,0},{6,2},{1,5},{3,7},{5,1},{7,3},{8,12},{10,14},{12... | collective-permute-start | bytes 393224 | tf_op jit(solution)/shard_map/ppermute | solution.py:94
  28.6 1.1 collective-permute-start.2
  29.7 0.9 collective-permute-start.1
  30.6 2.9 %collective-permute-done.3 = bf16[128,512]{1,0:T(8,128)(2,1)} collective-permute-done((bf16[128,512]{1,0:T(8,128)(2,1)S(1)}, bf16[128,512]{1,0:T(8,128)(2,1)}, u32[]{:S(2)}, u32[]{:S(2)}) %collective-permute-start.3) | collective-permute-done | bytes 131104 | tf_op jit(solution)/shard_map/ppermute | solution.py:94
  33.5 2.1 collective-permute-done.2
  36.2 2.0 fusion.48
  38.9 6.2 %all-to-all-done = bf16[16,32,1024]{2,1,0:T(8,128)(2,1)} async-done(((bf16[16,32,1024]{2,1,0:T(8,128)(2,1)}), bf16[16,32,1024]{2,1,0:T(8,128)(2,1)}, u32[]{:S(2)}, u32[]{:S(2)}) %all-to-all-start) | async-done | bytes 1048608 | tf_op jit(solution)/shard_map/all_to_all | solution.py:131
  45.0 2.6 %convolution_convert_fusion.2 = bf16[512,512]{1,0:T(8,128)(2,1)S(1)} fusion(bf16[512,1024]{1,0:T(8,128)(2,1)} %bitcast, bf16[1,1024,1024]{2,1,0:T(8,128)(2,1)} %param.7, s32[]{:T(128)S(6)} %select_n.131), kind=kOutput, calls=%fused_computation.10 | convolution fusion | flops 537133056 | bytes 2621444 | tf_op jit(solution)/shard_map/dot_general | solution.py:26
  47.8 1.9 collective-permute-done.4
  49.7 2.0 add_convert_fusion
  51.7 13.9 %all_to_all.45 = bf16[4,128,512]{2,1,0:T(8,128)(2,1)S(1)} all-to-all(bf16[4,128,512]{2,1,0:T(8,128)(2,1)S(1)} %bitcast.147), channel_id=1, replica_groups=mesh['section'=2,'ylo'=2,'z'=8,'x'=4,'core'=2] {'x'}, dimensions={0} | all-to-all | bytes 1048576 | tf_op jit(solution)/shard_map/all_to_all | solution.py:80
  65.7 9.1 %all_to_all.46 = bf16[4,64,512]{2,1,0:T(8,128)(2,1)S(1)} all-to-all(bf16[4,64,512]{2,1,0:T(8,128)(2,1)S(1)} %broadcast_in_dim.18), channel_id=1, replica_groups=mesh['section'=2,'ylo'=2,'z'=8,'x'=4,'core'=2] {'x'}, dimensions={0} | all-to-all | bytes 524288 | tf_op jit(solution)/shard_map/all_to_all | solution.py:88
  75.3 1.0 collective-permute-done.6
  76.3 1.3 fusion.1
  77.6 3.1 %collective-permute-start.7 = (bf16[256,1024]{1,0:T(8,128)(2,1)}, bf16[256,1024]{1,0:T(8,128)(2,1)}, u32[]{:S(2)}, u32[]{:S(2)}) collective-permute-start(bf16[256,1024]{1,0:T(8,128)(2,1)} %fusion.1), channel_id=1, source_target_pairs={{192,0},{128,64},{193,1},{129,65},{194,2},{130,66},{195,3},{131,67... | collective-permute-start | bytes 1572872 | tf_op jit(solution)/shard_map/ppermute | solution.py:52
  81.4 10.0 %all_to_all.47 = bf16[4,64,512]{2,1,0:T(8,128)(2,1)} all-to-all(bf16[4,64,512]{2,1,0:T(8,128)(2,1)S(1)} %broadcast_in_dim.17), channel_id=1, replica_groups=mesh['section'=2,'ylo'=2,'z'=8,'x'=4,'core'=2] {'x'}, dimensions={0} | all-to-all | bytes 524288 | tf_op jit(solution)/shard_map/all_to_all | solution.py:88
  91.4 1.4 fusion.22
  93.3 8.6 %collective-permute-done.7 = bf16[256,1024]{1,0:T(8,128)(2,1)} collective-permute-done((bf16[256,1024]{1,0:T(8,128)(2,1)}, bf16[256,1024]{1,0:T(8,128)(2,1)}, u32[]{:S(2)}, u32[]{:S(2)}) %collective-permute-start.7) | collective-permute-done | bytes 524320 | tf_op jit(solution)/shard_map/ppermute | solution.py:52
  101.9 2.2 fusion.4
  104.1 7.1 %all-to-all-start.4 = ((bf16[16,16,1024]{2,1,0:T(8,128)(2,1)}), bf16[16,16,1024]{2,1,0:T(8,128)(2,1)S(1)}, u32[]{:S(2)}, u32[]{:S(2)}) async-start(bf16[16,16,1024]{2,1,0:T(8,128)(2,1)} %bitcast.136), calls=%async_computation.4 | async-start | bytes 1048576 | tf_op jit(solution)/shard_map/all_to_all | solution.py:120
  111.3 0.7 all-gather.4.cloned.1.call-update
  112.0 1.3 collective-permute-start.8
  113.3 1.5 collective-permute-start.9
  114.8 1.3 collective-permute-start.11
  116.1 1.6 collective-permute-done.8
  117.7 2.4 %collective-permute-done.9 = bf16[128,512]{1,0:T(8,128)(2,1)S(1)} collective-permute-done((bf16[128,512]{1,0:T(8,128)(2,1)S(1)}, bf16[128,512]{1,0:T(8,128)(2,1)S(1)}, u32[]{:S(2)}, u32[]{:S(2)}) %collective-permute-start.9) | collective-permute-done | bytes 131104 | tf_op jit(solution)/shard_map/ppermute | solution.py:94
  120.1 6.0 %all-to-all-done.4 = bf16[16,16,1024]{2,1,0:T(8,128)(2,1)S(1)} async-done(((bf16[16,16,1024]{2,1,0:T(8,128)(2,1)}), bf16[16,16,1024]{2,1,0:T(8,128)(2,1)S(1)}, u32[]{:S(2)}, u32[]{:S(2)}) %all-to-all-start.4) | async-done | bytes 524320 | tf_op jit(solution)/shard_map/all_to_all | solution.py:120
  126.3 0.9 broadcast_in_dim.19
  127.1 4.9 %all-to-all-start.5 = ((bf16[16,16,1024]{2,1,0:T(8,128)(2,1)}), bf16[16,16,1024]{2,1,0:T(8,128)(2,1)S(1)}, u32[]{:S(2)}, u32[]{:S(2)}) async-start(bf16[16,16,1024]{2,1,0:T(8,128)(2,1)} %broadcast_in_dim.19), calls=%async_computation.5 | async-start | bytes 1048576 | tf_op jit(solution)/shard_map/all_to_all | solution.py:131
  132.0 0.9 bitcast_dynamic-update-slice_fusion
  133.0 0.8 constant_dynamic-slice_fusion
  133.8 12.4 %all-to-all-done.5 = bf16[16,16,1024]{2,1,0:T(8,128)(2,1)S(1)} async-done(((bf16[16,16,1024]{2,1,0:T(8,128)(2,1)}), bf16[16,16,1024]{2,1,0:T(8,128)(2,1)S(1)}, u32[]{:S(2)}, u32[]{:S(2)}) %all-to-all-start.5) | async-done | bytes 524320 | tf_op jit(solution)/shard_map/all_to_all | solution.py:131
  146.2 1.7 convolution_convert_fusion.3
  148.1 1.5 collective-permute-done.12
  149.6 2.4 %fusion.5 = bf16[256,512]{1,0:T(8,128)(2,1)} fusion(bf16[256,1024]{1,0:T(8,128)(2,1)S(1)} %bitcast.127, bf16[1,2048,1024]{2,1,0:T(8,128)(2,1)} %all-gather.6.cloned.1.call-done, s32[]{:T(128)S(6)} %select_n.138, bf16[256,512]{1,0:T(8,128)(2,1)S(1)} %collective-permute-done.12), kind=kOutput, calls=%fused_computation.14 | convolution fusion | flops 268828672 | bytes 2097156 | tf_op jit(solution)/shard_map/dot_general | solution.py:26
  152.0 3.4 %all-to-all-start.6 = ((bf16[4,64,512]{2,1,0:T(8,128)(2,1)}), bf16[4,64,512]{2,1,0:T(8,128)(2,1)S(1)}, u32[]{:S(2)}, u32[]{:S(2)}) async-start(bf16[4,64,512]{2,1,0:T(8,128)(2,1)} %bitcast.31), calls=%async_computation.6 | async-start | bytes 524288 | tf_op jit(solution)/shard_map/all_to_all | solution.py:80
  155.4 4.5 %collective-permute-start.14 = (bf16[256,1024]{1,0:T(8,128)(2,1)S(1)}, bf16[256,1024]{1,0:T(8,128)(2,1)S(1)}, u32[]{:S(2)}, u32[]{:S(2)}) collective-permute-start(bf16[256,1024]{1,0:T(8,128)(2,1)S(1)} %bitcast.128), channel_id=1, source_target_pairs={{192,0},{128,64},{193,1},{129,65},{194,2},{130,66},{195,3},{131,67... | collective-permute-start | bytes 1572872 | tf_op jit(solution)/shard_map/ppermute | solution.py:52
  160.0 2.6 %all-to-all-done.6 = bf16[4,64,512]{2,1,0:T(8,128)(2,1)S(1)} async-done(((bf16[4,64,512]{2,1,0:T(8,128)(2,1)}), bf16[4,64,512]{2,1,0:T(8,128)(2,1)S(1)}, u32[]{:S(2)}, u32[]{:S(2)}) %all-to-all-start.6) | async-done | bytes 262176 | tf_op jit(solution)/shard_map/all_to_all | solution.py:80
  162.7 0.9 multiply_convert_fusion.1
  163.5 0.7 broadcast_in_dim.20
  164.3 3.4 %all-to-all-start.7 = ((bf16[4,64,512]{2,1,0:T(8,128)(2,1)}), bf16[4,64,512]{2,1,0:T(8,128)(2,1)S(1)}, u32[]{:S(2)}, u32[]{:S(2)}) async-start(bf16[4,64,512]{2,1,0:T(8,128)(2,1)} %broadcast_in_dim.20), calls=%async_computation.7 | async-start | bytes 524288 | tf_op jit(solution)/shard_map/all_to_all | solution.py:88
  167.7 15.4 %collective-permute-done.14 = bf16[256,1024]{1,0:T(8,128)(2,1)S(1)} collective-permute-done((bf16[256,1024]{1,0:T(8,128)(2,1)S(1)}, bf16[256,1024]{1,0:T(8,128)(2,1)S(1)}, u32[]{:S(2)}, u32[]{:S(2)}) %collective-permute-start.14) | collective-permute-done | bytes 524320 | tf_op jit(solution)/shard_map/ppermute | solution.py:52
  183.1 0.8 copy-done.10
  183.9 1.1 pad_maximum_fusion
  185.0 1.3 broadcast_select_fusion.1
  186.3 1.3 bitcast_select_fusion
  187.7 2.6 %convolution_convert_fusion = bf16[1024,1024]{1,0:T(8,128)(2,1)} fusion(bf16[512,1024]{1,0:T(8,128)(2,1)S(1)} %bitcast_select_fusion, bf16[512,512]{1,0:T(8,128)(2,1)S(1)} %get-tuple-element.49, bf16[512,512]{1,0:T(8,128)(2,1)S(1)} %get-tuple-element.48), kind=kOutput, calls=%fused_computation.1 | convolution fusion | flops 1076887552 | bytes 4194304 | tf_op jit(solution)/shard_map/dot_general | solution.py:26
  190.3 5.2 %collective-permute-start.16 = (bf16[256,512]{1,0:T(8,128)(2,1)S(1)}, bf16[256,512]{1,0:T(8,128)(2,1)}, u32[]{:S(2)}, u32[]{:S(2)}) collective-permute-start(bf16[256,512]{1,0:T(8,128)(2,1)S(1)} %bitcast.133), channel_id=1, source_target_pairs={{192,0},{128,64},{193,1},{129,65},{194,2},{130,66},{195,3},{131,67... | collective-permute-start | bytes 786440 | tf_op jit(solution)/shard_map/ppermute | solution.py:52
  195.4 1.7 fusion.28
  197.2 2.5 %fusion.2 = bf16[256,1024]{1,0:T(8,128)(2,1)} fusion(f32[256,1024]{1,0:T(8,128)S(1)} %fusion.28, bf16[256,512]{1,0:T(8,128)(2,1)S(1)} %collective-permute-done.15, bf16[2048,1024]{1,0:T(8,128)(2,1)} %all-gather.4.cloned.1.call-done, s32[]{:T(128)S(6)} %select_n.131), kind=kOutput, calls=%fused_computation.8 | convolution fusion | flops 268959744 | bytes 2883588 | tf_op jit(solution)/shard_map/dot_general | solution.py:26
  199.7 5.6 %all-to-all-start.8 = ((bf16[16,16,1024]{2,1,0:T(8,128)(2,1)}), bf16[16,16,1024]{2,1,0:T(8,128)(2,1)}, u32[]{:S(2)}, u32[]{:S(2)}) async-start(bf16[16,16,1024]{2,1,0:T(8,128)(2,1)} %bitcast.37), calls=%async_computation.8 | async-start | bytes 1048576 | tf_op jit(solution)/shard_map/all_to_all | solution.py:120
  205.5 1.6 collective-permute-done.17
  207.1 1.1 broadcast_select_fusion.7
  208.4 1.3 convert_bitcast_fusion
  209.7 11.4 %all-to-all-done.8 = bf16[16,16,1024]{2,1,0:T(8,128)(2,1)} async-done(((bf16[16,16,1024]{2,1,0:T(8,128)(2,1)}), bf16[16,16,1024]{2,1,0:T(8,128)(2,1)}, u32[]{:S(2)}, u32[]{:S(2)}) %all-to-all-start.8) | async-done | bytes 524320 | tf_op jit(solution)/shard_map/all_to_all | solution.py:120
  221.1 1.1 convert_reduce_fusion
  222.3 2.6 %copy.12 = bf16[1,1024,1024]{2,1,0:T(8,128)(2,1)} copy(bf16[1,1024,1024]{1,2,0:T(8,128)(2,1)S(1)} %bitcast.137) | data formatting | bytes 4194304
  224.9 2.8 %collective-permute-done.18 = bf16[16,1024]{1,0:T(8,128)(2,1)S(1)} collective-permute-done((bf16[16,1024]{1,0:T(8,128)(2,1)S(1)}, bf16[16,1024]{1,0:T(8,128)(2,1)S(1)}, u32[]{:S(2)}, u32[]{:S(2)}) %collective-permute-start.18) | collective-permute-done | bytes 32800 | tf_op jit(solution)/shard_map/ppermute | solution.py:219
  (73 shorter events, 4.8 us)
Async XLA Ops:
  7.2 11.7 %copy-start = (bf16[1,512,1024]{2,1,0:T(8,128)(2,1)S(1)}, bf16[1,512,1024]{2,1,0:T(8,128)(2,1)}, u32[]{:S(2)}) copy-start(bf16[1,512,1024]{2,1,0:T(8,128)(2,1)} %param.4) | copy-start | bytes 3145732
  7.2 11.7 %copy-start.1 = (bf16[1,1024,1024]{2,1,0:T(8,128)(2,1)S(1)}, bf16[1,1024,1024]{2,1,0:T(8,128)(2,1)}, u32[]{:S(2)}) copy-start(bf16[1,1024,1024]{2,1,0:T(8,128)(2,1)} %param.6) | copy-start | bytes 6291460
  9.3 35.8 %all-to-all-start = ((bf16[16,32,1024]{2,1,0:T(8,128)(2,1)}), bf16[16,32,1024]{2,1,0:T(8,128)(2,1)}, u32[]{:S(2)}, u32[]{:S(2)}) async-start(bf16[16,32,1024]{2,1,0:T(8,128)(2,1)} %broadcast_in_dim.16), calls=%async_computation | async-start | bytes 2097152 | tf_op jit(solution)/shard_map/all_to_all | solution.py:131
  18.8 127.5 %all-gather.6.cloned.1.call-start = ((), (), s32[]{:S(2)}) async-start(), calls=%async_computation.10 | async-start | bytes 6291456 | tf_op jit(solution)/shard_map/all_gather | solution.py:48
  20.4 2.3 collective-permute-start
  24.4 1.0 copy-start.3
  25.5 8.0 %collective-permute-start.3 = (bf16[128,512]{1,0:T(8,128)(2,1)S(1)}, bf16[128,512]{1,0:T(8,128)(2,1)}, u32[]{:S(2)}, u32[]{:S(2)}) collective-permute-start(bf16[128,512]{1,0:T(8,128)(2,1)S(1)} %get-tuple-element.51), channel_id=1, source_target_pairs={{0,4},{2,6},{4,0},{6,2},{1,5},{3,7},{5,1},{7,3},{8,12},{10,14},{12... | collective-permute-start | bytes 393224 | tf_op jit(solution)/shard_map/ppermute | solution.py:94
  28.6 7.0 %collective-permute-start.2 = (bf16[128,512]{1,0:T(8,128)(2,1)S(1)}, bf16[128,512]{1,0:T(8,128)(2,1)}, u32[]{:S(2)}, u32[]{:S(2)}) collective-permute-start(bf16[128,512]{1,0:T(8,128)(2,1)S(1)} %get-tuple-element.52), channel_id=1, source_target_pairs={{0,6},{2,0},{4,2},{6,4},{1,7},{3,1},{5,3},{7,5},{8,14},{10,8},{12,... | collective-permute-start | bytes 393224 | tf_op jit(solution)/shard_map/ppermute | solution.py:94
  29.7 6.5 %collective-permute-start.1 = (bf16[128,512]{1,0:T(8,128)(2,1)S(1)}, bf16[128,512]{1,0:T(8,128)(2,1)}, u32[]{:S(2)}, u32[]{:S(2)}) collective-permute-start(bf16[128,512]{1,0:T(8,128)(2,1)S(1)} %get-tuple-element.50), channel_id=1, source_target_pairs={{0,2},{2,4},{4,6},{6,0},{1,3},{3,5},{5,7},{7,1},{8,10},{10,12},{12... | collective-permute-start | bytes 393224 | tf_op jit(solution)/shard_map/ppermute | solution.py:94
  45.0 4.6 %copy-start.2 = (bf16[1,1024,1024]{2,1,0:T(8,128)(2,1)S(1)}, bf16[1,1024,1024]{2,1,0:T(8,128)(2,1)}, u32[]{:S(2)}) copy-start(bf16[1,1024,1024]{2,1,0:T(8,128)(2,1)} %param.7) | copy-start | bytes 6291460
  47.7 2.0 collective-permute-start.4
  74.8 6.0 %copy-start.7 = (f32[4,1,16,512]{3,2,1,0:T(8,128)S(1)}, f32[4,1,16,512]{3,2,1,0:T(8,128)}, u32[]{:S(2)}) copy-start(f32[4,1,16,512]{3,2,1,0:T(8,128)} %get-tuple-element.55) | copy-start | bytes 393220
  74.8 1.5 collective-permute-start.6
  76.3 15.1 %copy-start.5 = (bf16[256,512]{1,0:T(8,128)(2,1)}, bf16[256,512]{1,0:T(8,128)(2,1)S(1)}, u32[]{:S(2)}) copy-start(bf16[256,512]{1,0:T(8,128)(2,1)S(1)} %collective-permute-done.6) | copy-start | bytes 786436
  77.6 24.3 %collective-permute-start.7 = (bf16[256,1024]{1,0:T(8,128)(2,1)}, bf16[256,1024]{1,0:T(8,128)(2,1)}, u32[]{:S(2)}, u32[]{:S(2)}) collective-permute-start(bf16[256,1024]{1,0:T(8,128)(2,1)} %fusion.1), channel_id=1, source_target_pairs={{192,0},{128,64},{193,1},{129,65},{194,2},{130,66},{195,3},{131,67... | collective-permute-start | bytes 1572872 | tf_op jit(solution)/shard_map/ppermute | solution.py:52
  91.4 1.9 collective-permute-start.5
  104.1 7.9 %copy-start.4 = (bf16[128,512]{1,0:T(8,128)(2,1)S(1)}, bf16[128,512]{1,0:T(8,128)(2,1)}, u32[]{:S(2)}) copy-start(bf16[128,512]{1,0:T(8,128)(2,1)} %get-tuple-element.23) | copy-start | bytes 393220
  104.1 10.7 %copy-start.12 = (bf16[64,512]{1,0:T(8,128)(2,1)S(1)}, bf16[64,512]{1,0:T(8,128)(2,1)}, u32[]{:S(2)}) copy-start(bf16[64,512]{1,0:T(8,128)(2,1)} %get-tuple-element.24) | copy-start | bytes 196612
  104.1 22.1 %copy-start.11 = (bf16[32,1024]{1,0:T(8,128)(2,1)S(1)}, bf16[32,1024]{1,0:T(8,128)(2,1)}, u32[]{:S(2)}) copy-start(bf16[32,1024]{1,0:T(8,128)(2,1)} %param.5) | copy-start | bytes 196612
  104.1 22.0 %all-to-all-start.4 = ((bf16[16,16,1024]{2,1,0:T(8,128)(2,1)}), bf16[16,16,1024]{2,1,0:T(8,128)(2,1)S(1)}, u32[]{:S(2)}, u32[]{:S(2)}) async-start(bf16[16,16,1024]{2,1,0:T(8,128)(2,1)} %bitcast.136), calls=%async_computation.4 | async-start | bytes 1048576 | tf_op jit(solution)/shard_map/all_to_all | solution.py:120
  111.2 84.2 %all-gather.4.cloned.1.call-start = ((), (), s32[]{:S(2)}) async-start(), calls=%async_computation.9 | async-start | bytes 6291456 | tf_op jit(solution)/shard_map/all_gather | solution.py:48
  112.0 5.7 %collective-permute-start.8 = (bf16[128,512]{1,0:T(8,128)(2,1)S(1)}, bf16[128,512]{1,0:T(8,128)(2,1)S(1)}, u32[]{:S(2)}, u32[]{:S(2)}) collective-permute-start(bf16[128,512]{1,0:T(8,128)(2,1)S(1)} %copy-done.4), channel_id=1, source_target_pairs={{0,6},{2,0},{4,2},{6,4},{1,7},{3,1},{5,3},{7,5},{8,14},{10,8},{12,... | collective-permute-start | bytes 393224 | tf_op jit(solution)/shard_map/ppermute | solution.py:94
  113.3 6.8 %collective-permute-start.9 = (bf16[128,512]{1,0:T(8,128)(2,1)S(1)}, bf16[128,512]{1,0:T(8,128)(2,1)S(1)}, u32[]{:S(2)}, u32[]{:S(2)}) collective-permute-start(bf16[128,512]{1,0:T(8,128)(2,1)S(1)} %copy-done.4), channel_id=1, source_target_pairs={{0,4},{2,6},{4,0},{6,2},{1,5},{3,7},{5,1},{7,3},{8,12},{10,14},{12... | collective-permute-start | bytes 393224 | tf_op jit(solution)/shard_map/ppermute | solution.py:94
  114.8 17.2 %collective-permute-start.10 = (bf16[128,512]{1,0:T(8,128)(2,1)S(1)}, bf16[128,512]{1,0:T(8,128)(2,1)}, u32[]{:S(2)}, u32[]{:S(2)}) collective-permute-start(bf16[128,512]{1,0:T(8,128)(2,1)S(1)} %copy-done.4), channel_id=1, source_target_pairs={{0,2},{2,4},{4,6},{6,0},{1,3},{3,5},{5,7},{7,1},{8,10},{10,12},{12... | collective-permute-start | bytes 393224 | tf_op jit(solution)/shard_map/ppermute | solution.py:94
  114.8 19.0 %collective-permute-start.11 = (bf16[64,512]{1,0:T(8,128)(2,1)S(1)}, bf16[64,512]{1,0:T(8,128)(2,1)}, u32[]{:S(2)}, u32[]{:S(2)}) collective-permute-start(bf16[64,512]{1,0:T(8,128)(2,1)S(1)} %copy-done.12), channel_id=1, source_target_pairs={{0,192},{64,128},{1,193},{65,129},{2,194},{66,130},{3,195},{67,131... | collective-permute-start | bytes 196616 | tf_op jit(solution)/shard_map/ppermute | solution.py:43
  126.2 21.7 %copy-start.8 = (bf16[16,1024]{1,0:T(8,128)(2,1)}, bf16[16,1024]{1,0:T(8,128)(2,1)S(1)}, u32[]{:S(2)}) copy-start(bf16[16,1024]{1,0:T(8,128)(2,1)S(1)} %add_convert_fusion.2) | copy-start | bytes 98308
  127.1 19.1 %all-to-all-start.5 = ((bf16[16,16,1024]{2,1,0:T(8,128)(2,1)}), bf16[16,16,1024]{2,1,0:T(8,128)(2,1)S(1)}, u32[]{:S(2)}, u32[]{:S(2)}) async-start(bf16[16,16,1024]{2,1,0:T(8,128)(2,1)} %broadcast_in_dim.19), calls=%async_computation.5 | async-start | bytes 1048576 | tf_op jit(solution)/shard_map/all_to_all | solution.py:131
  148.0 1.6 collective-permute-start.12
  152.0 10.6 %all-to-all-start.6 = ((bf16[4,64,512]{2,1,0:T(8,128)(2,1)}), bf16[4,64,512]{2,1,0:T(8,128)(2,1)S(1)}, u32[]{:S(2)}, u32[]{:S(2)}) async-start(bf16[4,64,512]{2,1,0:T(8,128)(2,1)} %bitcast.31), calls=%async_computation.6 | async-start | bytes 524288 | tf_op jit(solution)/shard_map/all_to_all | solution.py:80
  155.4 27.7 %collective-permute-start.14 = (bf16[256,1024]{1,0:T(8,128)(2,1)S(1)}, bf16[256,1024]{1,0:T(8,128)(2,1)S(1)}, u32[]{:S(2)}, u32[]{:S(2)}) collective-permute-start(bf16[256,1024]{1,0:T(8,128)(2,1)S(1)} %bitcast.128), channel_id=1, source_target_pairs={{192,0},{128,64},{193,1},{129,65},{194,2},{130,66},{195,3},{131,67... | collective-permute-start | bytes 1572872 | tf_op jit(solution)/shard_map/ppermute | solution.py:52
  159.9 25.1 %collective-permute-start.13 = (bf16[512,512]{1,0:T(8,128)(2,1)}, bf16[512,512]{1,0:T(8,128)(2,1)}, u32[]{:S(2)}, u32[]{:S(2)}) collective-permute-start(bf16[512,512]{1,0:T(8,128)(2,1)} %bitcast.28), channel_id=1, source_target_pairs={{0,1},{1,0},{2,3},{3,2},{4,5},{5,4},{6,7},{7,6},{8,9},{9,8},{10,11... | collective-permute-start | bytes 1572872 | tf_op jit(solution)/shard_map/ppermute | solution.py:39
  164.3 26.0 %all-to-all-start.7 = ((bf16[4,64,512]{2,1,0:T(8,128)(2,1)}), bf16[4,64,512]{2,1,0:T(8,128)(2,1)S(1)}, u32[]{:S(2)}, u32[]{:S(2)}) async-start(bf16[4,64,512]{2,1,0:T(8,128)(2,1)} %broadcast_in_dim.20), calls=%async_computation.7 | async-start | bytes 524288 | tf_op jit(solution)/shard_map/all_to_all | solution.py:88
  183.1 0.8 copy-start.10
  190.3 6.9 %collective-permute-start.15 = (bf16[256,512]{1,0:T(8,128)(2,1)S(1)}, bf16[256,512]{1,0:T(8,128)(2,1)S(1)}, u32[]{:S(2)}, u32[]{:S(2)}) collective-permute-start(bf16[256,512]{1,0:T(8,128)(2,1)S(1)} %bitcast.132), channel_id=1, source_target_pairs={{0,1},{1,0},{2,3},{3,2},{4,5},{5,4},{6,7},{7,6},{8,9},{9,8},{10,11... | collective-permute-start | bytes 786440 | tf_op jit(solution)/shard_map/ppermute | solution.py:39
  190.3 15.0 %collective-permute-start.16 = (bf16[256,512]{1,0:T(8,128)(2,1)S(1)}, bf16[256,512]{1,0:T(8,128)(2,1)}, u32[]{:S(2)}, u32[]{:S(2)}) collective-permute-start(bf16[256,512]{1,0:T(8,128)(2,1)S(1)} %bitcast.133), channel_id=1, source_target_pairs={{192,0},{128,64},{193,1},{129,65},{194,2},{130,66},{195,3},{131,67... | collective-permute-start | bytes 786440 | tf_op jit(solution)/shard_map/ppermute | solution.py:52
  197.1 8.2 %copy-start.6 = (bf16[256,512]{1,0:T(8,128)(2,1)S(1)}, bf16[256,512]{1,0:T(8,128)(2,1)}, u32[]{:S(2)}) copy-start(bf16[256,512]{1,0:T(8,128)(2,1)} %copy-done.5) | copy-start | bytes 786436
  199.7 21.4 %all-to-all-start.8 = ((bf16[16,16,1024]{2,1,0:T(8,128)(2,1)}), bf16[16,16,1024]{2,1,0:T(8,128)(2,1)}, u32[]{:S(2)}, u32[]{:S(2)}) async-start(bf16[16,16,1024]{2,1,0:T(8,128)(2,1)} %bitcast.37), calls=%async_computation.8 | async-start | bytes 1048576 | tf_op jit(solution)/shard_map/all_to_all | solution.py:120
  205.3 1.8 collective-permute-start.17
  208.4 13.8 %copy-start.9 = (bf16[16,1024]{1,0:T(8,128)(2,1)S(1)}, bf16[16,1024]{1,0:T(8,128)(2,1)}, u32[]{:S(2)}) copy-start(bf16[16,1024]{1,0:T(8,128)(2,1)} %copy-done.8) | copy-start | bytes 98308
  222.2 5.5 %collective-permute-start.18 = (bf16[16,1024]{1,0:T(8,128)(2,1)S(1)}, bf16[16,1024]{1,0:T(8,128)(2,1)S(1)}, u32[]{:S(2)}, u32[]{:S(2)}) collective-permute-start(bf16[16,1024]{1,0:T(8,128)(2,1)S(1)} %broadcast_select_fusion.12), channel_id=1, source_target_pairs={{0,128},{128,0},{1,129},{129,1},{2,130},{130,2},{3,131},{131,3},{4... | collective-permute-start | bytes 98312 | tf_op jit(solution)/shard_map/ppermute | solution.py:219
Sparse Core Ops, SparseCore 0:
  30.7 70.0 all-gather.5
  113.9 71.1 all-gather.3

commit v8 on v7

--- a/solution.py
+++ b/solution.py
@@ -43,25 +43,17 @@
     return lax.ppermute(block, CROSS_AXES, [(0, 3), (1, 2)])
 
 
-def pair_weights(block):
-    pairs = [[0, 3], [1, 2]]
-    return lax.all_gather(block, CROSS_AXES, axis=0, tiled=True, axis_index_groups=pairs)
-
-
 def to_lower(block):
     return lax.ppermute(block, CROSS_AXES, [(3, 0), (2, 1)])
 
 
-def halves(weight, dim, depth=None):
-    rows, cols = depth or weight.shape[0], weight.shape[1]
+def halves(weight, dim):
+    size = weight.shape[dim] // CORES
     core = lax.axis_index("core")
-
-    def half(index):
-        if dim == 0:
-            return lax.dynamic_slice(weight, (index * (rows // CORES), 0), (rows // CORES, cols))
-        return lax.dynamic_slice(weight, (0, index * (cols // CORES)), (rows, cols // CORES))
-
-    return half(core), half(1 - core)
+    return (
+        lax.dynamic_slice_in_dim(weight, core * size, size, dim),
+        lax.dynamic_slice_in_dim(weight, (1 - core) * size, size, dim),
+    )
 
 
 def in_order(mine, theirs):
@@ -167,7 +159,9 @@
     w_up, w_down = up_weight[0], down_weight[0]
     up_halves, down_halves = halves(w_up, 1), halves(w_down, 0)
 
-    low_down = pair_weights(w_down)
+    crossed = []
+    for piece in (down_halves[1], down_halves[0], up_halves[0], up_halves[1]):
+        crossed.append(to_upper(together(piece, *crossed[-1:])[0]))
 
     theirs = contract(saved, up_halves[1], 1, 0)
     mine = contract(saved, up_halves[0], 1, 0)
@@ -176,7 +170,6 @@
     act = act.astype(jnp.bfloat16)
     slopes = [part_of(slopes, c) for c in range(2)]
     gathered, act, *slopes = together(gather_wide(upstream), act, *slopes)
-    low_up = pair_weights(together(w_up, act)[0])
 
     share = back_share(gathered, down_halves)
     top_mine = [
@@ -195,7 +188,8 @@
     low, hidden, sent = together(gather_wide(middle), hidden, to_upper(sent))
     hidden = in_order(hidden, other_core(hidden))
     low_rest = to_lower(low)
-    low_share = back_share(low, halves(low_down, 0, w_down.shape[0]))
+    low_down = [pick(crossed[1], down_halves[0]), pick(crossed[0], down_halves[1])]
+    low_share = back_share(low, low_down)
     incoming = pick(gathered, both_parts(low, low_rest))
     grad_down = contract(hidden, incoming, 0, 0).astype(jnp.bfloat16)
     low_mine = gather_x(
@@ -204,7 +198,8 @@
     low_mine, grad_down = together(low_mine, grad_down)
     low_slope = (low_mine, other_core(low_mine))
     low_slope_rest = to_lower(low_mine)
-    low_blocks = spread_wide(back_through_up(low_slope, halves(low_up, 1, w_up.shape[0])))
+    low_up = [pick(crossed[2], up_halves[0]), pick(crossed[3], up_halves[1])]
+    low_blocks = spread_wide(back_through_up(low_slope, low_up))
     slope_grad = both_parts(
         in_order(*[pick(u, l) for u, l in zip(top_slope[0], low_slope)]),
         in_order(

time: 237 us -> 221 us (0.932)
  blocking collectives: 32.9 us -> 9.07 us
  starting transfers between devices: 56.4 us -> 75.3 us
  waiting for transfers between devices: 84.4 us -> 69.6 us
  local copies, waits for them, and re-layouts: 10.6 us -> 24.5 us
  between operations: 14.5 us -> 1.02 us
  other arithmetic: 10.8 us -> 13.6 us
    ppermute x3, waiting for transfers between devices: 24 us -> 2.83 us  [to_lower(): return lax.ppermute(block, CROSS_AXES, [(3, 0), (2, 1)])]
    all_to_all x1 -> x0, blocking collectives: 13.9 us -> none  [spread_x(): lax.all_to_all(partial.astype(jnp.bfloat16).reshape(X, rows // X, cols),...]
    ppermute x1 -> x5, waiting for transfers between devices: 0.01 us -> 13.1 us  [to_upper(): return lax.ppermute(block, CROSS_AXES, [(0, 3), (1, 2)])]
    all_to_all x2 -> x1, blocking collectives: 19.1 us -> 9.07 us  [gather_x(): lax.all_to_all(jnp.broadcast_to(block[None], (X, rows, cols)), 'x', 0, 0,...]
    unnamed x33 -> x37, local copies, waits for them, and re-layouts: 5.36 us -> 12.8 us
    all_to_all x2, waiting for transfers between devices: 18.6 us -> 11.3 us  [gather_wide(): lax.all_to_all(jnp.broadcast_to(block[None], (WIDE, rows, cols)), WIDE_AX...]
    all_to_all x1 -> x2, waiting for transfers between devices: 2.6 us -> 8.68 us  [spread_x(): lax.all_to_all(partial.astype(jnp.bfloat16).reshape(X, rows // X, cols),...]
    all_to_all x2, waiting for transfers between devices: 17.4 us -> 11.5 us  [spread_wide(): lax.all_to_all(partial.reshape(WIDE, rows // WIDE, cols), WIDE_AXES, 0, 0...]
  transfers between devices with their start and end apart: 27 -> 31, of which waited for: 19 -> 19; matrix products, arithmetic and copies ran while one was open for 18% -> 24% of each run, Pallas kernels for 0% -> 0%
where the time goes in v8:
time: 221 us; the launch traced here: 219 us
  starting transfers between devices  75.3 us (34%)
  waiting for transfers between devices  69.6 us (31%)
  matrix products  25.6 us (12%)
  local copies, waits for them, and re-layouts  24.5 us (11%)
  other arithmetic  13.6 us (6%)
  blocking collectives  9.07 us (4%)
    dot_general x14, matrix products, contract(): lax.dot_general(first_op, second_op, (((first_dim,), (second_dim,)), ((),...  25.6 us
    ppermute x3, starting transfers between devices, to_lower(): return lax.ppermute(block, CROSS_AXES, [(3, 0), (2, 1)])  16.2 us
    all_to_all x2, starting transfers between devices, gather_wide(): lax.all_to_all(jnp.broadcast_to(block[None], (WIDE, rows, cols)), WIDE_AX...  14.7 us
    ppermute x5, waiting for transfers between devices, to_upper(): return lax.ppermute(block, CROSS_AXES, [(0, 3), (1, 2)])  13.1 us
    unnamed x37, local copies, waits for them, and re-layouts  12.8 us
    all_to_all x2, waiting for transfers between devices, spread_wide(): lax.all_to_all(partial.reshape(WIDE, rows // WIDE, cols), WIDE_AXES, 0, 0...  11.5 us
    all_to_all x2, waiting for transfers between devices, gather_wide(): lax.all_to_all(jnp.broadcast_to(block[None], (WIDE, rows, cols)), WIDE_AX...  11.3 us
    all_to_all x2, starting transfers between devices, spread_wide(): lax.all_to_all(partial.reshape(WIDE, rows // WIDE, cols), WIDE_AXES, 0, 0...  10.7 us
  transfers between devices with their start and end apart: 31, of which 19 were waited for; matrix products, arithmetic and copies ran while one was open for 24% of the time, Pallas kernels for 0%

profile of v8, /device:TPU:56, one launch (start us, length us, event | category | flops | bytes accessed | tf_op | source)
XLA Modules:
  0.0 218.8 jit_solution(554384888160563769)
XLA Ops:
  0.6 2.0 broadcast_in_dim.16
  2.7 9.5 %all-to-all-start = ((bf16[16,32,1024]{2,1,0:T(8,128)(2,1)}), bf16[16,32,1024]{2,1,0:T(8,128)(2,1)}, u32[]{:S(2)}, u32[]{:S(2)}) async-start(bf16[16,32,1024]{2,1,0:T(8,128)(2,1)} %broadcast_in_dim.16), calls=%async_computation | async-start | bytes 2097152 | tf_op jit(solution)/shard_map/all_to_all | solution.py:123
  12.2 1.7 dynamic-slice_bitcast_fusion.2
  13.8 1.5 fusion.3
  15.4 2.2 %collective-permute-done = bf16[512,512]{1,0:T(8,128)(2,1)} collective-permute-done((bf16[512,512]{1,0:T(8,128)(2,1)}, bf16[512,512]{1,0:T(8,128)(2,1)}, u32[]{:S(2)}, u32[]{:S(2)}) %collective-permute-start) | collective-permute-done | bytes 524320 | tf_op jit(solution)/shard_map/ppermute | solution.py:39
  17.6 1.7 convert_add_fusion
  19.5 3.1 %collective-permute-start.3 = (bf16[128,512]{1,0:T(8,128)(2,1)S(1)}, bf16[128,512]{1,0:T(8,128)(2,1)S(1)}, u32[]{:S(2)}, u32[]{:S(2)}) collective-permute-start(bf16[128,512]{1,0:T(8,128)(2,1)S(1)} %get-tuple-element.59), channel_id=1, source_target_pairs={{0,4},{2,6},{4,0},{6,2},{1,5},{3,7},{5,1},{7,3},{8,12},{10,14},{12... | collective-permute-start | bytes 393224 | tf_op jit(solution)/shard_map/ppermute | solution.py:86
  22.6 1.1 collective-permute-start.2
  24.6 1.5 dynamic-slice_bitcast_fusion
  26.1 1.3 collective-permute-done.3
  27.4 2.1 collective-permute-done.2
  31.6 6.8 %all-to-all-done = bf16[16,32,1024]{2,1,0:T(8,128)(2,1)} async-done(((bf16[16,32,1024]{2,1,0:T(8,128)(2,1)}), bf16[16,32,1024]{2,1,0:T(8,128)(2,1)}, u32[]{:S(2)}, u32[]{:S(2)}) %all-to-all-start) | async-done | bytes 1048608 | tf_op jit(solution)/shard_map/all_to_all | solution.py:123
  38.4 2.4 %convolution_convert_fusion.2 = bf16[512,512]{1,0:T(8,128)(2,1)S(1)} fusion(bf16[512,1024]{1,0:T(8,128)(2,1)} %bitcast, bf16[512,1024]{1,0:T(8,128)(2,1)} %get-tuple-element.46), kind=kOutput, calls=%fused_computation.10 | convolution fusion | flops 537133056 | bytes 2621440 | tf_op jit(solution)/shard_map/dot_general | solution.py:26
  40.9 1.9 collective-permute-done.4
  42.8 2.8 %add_convert_fusion = bf16[512,512]{1,0:T(8,128)(2,1)} fusion(bf16[512,512]{1,0:T(8,128)(2,1)S(1)} %collective-permute-done.4, bf16[512,1024]{1,0:T(8,128)(2,1)} %bitcast, bf16[512,1024]{1,0:T(8,128)(2,1)S(1)} %copy-done.2), kind=kOutput, calls=%fused_computation.33 | convolution fusion | flops 537657344 | bytes 3145728 | tf_op jit(solution)/shard_map/dot_general | solution.py:26
  45.6 4.3 %all-to-all-start.1 = ((bf16[4,128,512]{2,1,0:T(8,128)(2,1)}), bf16[4,128,512]{2,1,0:T(8,128)(2,1)}, u32[]{:S(2)}, u32[]{:S(2)}) async-start(bf16[4,128,512]{2,1,0:T(8,128)(2,1)} %bitcast.123), calls=%async_computation.1 | async-start | bytes 1048576 | tf_op jit(solution)/shard_map/all_to_all | solution.py:72
  49.9 1.3 collective-permute-start.12
  51.2 8.7 %all-to-all-done.1 = bf16[4,128,512]{2,1,0:T(8,128)(2,1)} async-done(((bf16[4,128,512]{2,1,0:T(8,128)(2,1)}), bf16[4,128,512]{2,1,0:T(8,128)(2,1)}, u32[]{:S(2)}, u32[]{:S(2)}) %all-to-all-start.1) | async-done | bytes 524320 | tf_op jit(solution)/shard_map/all_to_all | solution.py:72
  59.9 1.1 convert_reduce_fusion.2
  61.1 9.1 %all_to_all.45 = bf16[4,64,512]{2,1,0:T(8,128)(2,1)S(1)} all-to-all(bf16[4,64,512]{2,1,0:T(8,128)(2,1)S(1)} %broadcast_in_dim.18), channel_id=1, replica_groups=mesh['section'=2,'ylo'=2,'z'=8,'x'=4,'core'=2] {'x'}, dimensions={0} | all-to-all | bytes 524288 | tf_op jit(solution)/shard_map/all_to_all | solution.py:80
  70.7 1.1 collective-permute-done.6
  71.7 1.3 fusion.1
  73.0 3.1 %collective-permute-start.7 = (bf16[256,1024]{1,0:T(8,128)(2,1)}, bf16[256,1024]{1,0:T(8,128)(2,1)}, u32[]{:S(2)}, u32[]{:S(2)}) collective-permute-start(bf16[256,1024]{1,0:T(8,128)(2,1)} %fusion.1), channel_id=1, source_target_pairs={{192,0},{128,64},{193,1},{129,65},{194,2},{130,66},{195,3},{131,67... | collective-permute-start | bytes 1572872 | tf_op jit(solution)/shard_map/ppermute | solution.py:47
  77.5 4.0 %all-to-all-start.2 = ((bf16[4,64,512]{2,1,0:T(8,128)(2,1)}), bf16[4,64,512]{2,1,0:T(8,128)(2,1)}, u32[]{:S(2)}, u32[]{:S(2)}) async-start(bf16[4,64,512]{2,1,0:T(8,128)(2,1)} %broadcast_in_dim.17), calls=%async_computation.2 | async-start | bytes 524288 | tf_op jit(solution)/shard_map/all_to_all | solution.py:80
  81.5 1.3 collective-permute-start.13
  82.8 5.7 %all-to-all-done.2 = bf16[4,64,512]{2,1,0:T(8,128)(2,1)} async-done(((bf16[4,64,512]{2,1,0:T(8,128)(2,1)}), bf16[4,64,512]{2,1,0:T(8,128)(2,1)}, u32[]{:S(2)}, u32[]{:S(2)}) %all-to-all-start.2) | async-done | bytes 262176 | tf_op jit(solution)/shard_map/all_to_all | solution.py:80
  88.5 1.4 fusion.34
  90.3 1.3 fusion.4
  91.6 5.2 %all-to-all-start.4 = ((bf16[16,16,1024]{2,1,0:T(8,128)(2,1)}), bf16[16,16,1024]{2,1,0:T(8,128)(2,1)}, u32[]{:S(2)}, u32[]{:S(2)}) async-start(bf16[16,16,1024]{2,1,0:T(8,128)(2,1)} %bitcast.113), calls=%async_computation.4 | async-start | bytes 1048576 | tf_op jit(solution)/shard_map/all_to_all | solution.py:112
  96.8 13.0 %collective-permute-done.13 = bf16[512,1024]{1,0:T(8,128)(2,1)} collective-permute-done((bf16[512,1024]{1,0:T(8,128)(2,1)}, bf16[512,1024]{1,0:T(8,128)(2,1)}, u32[]{:S(2)}, u32[]{:S(2)}) %collective-permute-start.13) | collective-permute-done | bytes 1048608 | tf_op jit(solution)/shard_map/ppermute | solution.py:43
  109.9 1.3 collective-permute-start.17
  111.1 3.0 %collective-permute-start.8 = (bf16[128,512]{1,0:T(8,128)(2,1)}, bf16[128,512]{1,0:T(8,128)(2,1)S(1)}, u32[]{:S(2)}, u32[]{:S(2)}) collective-permute-start(bf16[128,512]{1,0:T(8,128)(2,1)} %get-tuple-element.25), channel_id=1, source_target_pairs={{0,6},{2,0},{4,2},{6,4},{1,7},{3,1},{5,3},{7,5},{8,14},{10,8},{12,... | collective-permute-start | bytes 393224 | tf_op jit(solution)/shard_map/ppermute | solution.py:86
  115.8 1.3 collective-permute-start.11
  117.1 1.6 bitcast_dynamic-update-slice_fusion.5
  122.4 1.1 convert_reduce_fusion.1
  125.9 5.2 %all-to-all-start.5 = ((bf16[16,16,1024]{2,1,0:T(8,128)(2,1)}), bf16[16,16,1024]{2,1,0:T(8,128)(2,1)}, u32[]{:S(2)}, u32[]{:S(2)}) async-start(bf16[16,16,1024]{2,1,0:T(8,128)(2,1)} %broadcast_in_dim.19), calls=%async_computation.5 | async-start | bytes 1048576 | tf_op jit(solution)/shard_map/all_to_all | solution.py:123
  131.1 1.6 bitcast_dynamic-update-slice_fusion
  132.7 1.6 bitcast_dynamic-update-slice_fusion.6
  134.2 1.6 bitcast_dynamic-update-slice_fusion.4
  135.8 1.6 bitcast_dynamic-update-slice_fusion.2
  137.4 1.9 constant_dynamic-slice_fusion
  139.3 4.5 %all-to-all-done.5 = bf16[16,16,1024]{2,1,0:T(8,128)(2,1)} async-done(((bf16[16,16,1024]{2,1,0:T(8,128)(2,1)}), bf16[16,16,1024]{2,1,0:T(8,128)(2,1)}, u32[]{:S(2)}, u32[]{:S(2)}) %all-to-all-start.5) | async-done | bytes 524320 | tf_op jit(solution)/shard_map/all_to_all | solution.py:123
  143.8 1.9 convolution_convert_fusion.3
  145.8 1.5 collective-permute-done.14
  147.3 2.6 %fusion.5 = bf16[256,512]{1,0:T(8,128)(2,1)} fusion(bf16[256,1024]{1,0:T(8,128)(2,1)} %bitcast.23, bf16[512,1024]{1,0:T(8,128)(2,1)} %collective-permute-done.13, bf16[512,1024]{1,0:T(8,128)(2,1)S(1)} %copy-done.3, pred[]{:T(512)S(6)} %eq.8, bf16[256,512]{1,0:T(8,128)(2,1)S(1)} %collective-permute-done.14), kind=kOutput, calls=%fused_computation.14 | convolution fusion | flops 269352960 | bytes 3145729 | tf_op jit(solution)/shard_map/dot_general | solution.py:26
  149.9 4.0 %all-to-all-start.6 = ((bf16[4,64,512]{2,1,0:T(8,128)(2,1)}), bf16[4,64,512]{2,1,0:T(8,128)(2,1)}, u32[]{:S(2)}, u32[]{:S(2)}) async-start(bf16[4,64,512]{2,1,0:T(8,128)(2,1)} %bitcast.125), calls=%async_computation.6 | async-start | bytes 524288 | tf_op jit(solution)/shard_map/all_to_all | solution.py:72
  154.2 1.3 collective-permute-start.19
  155.5 7.9 %collective-permute-start.16 = (bf16[256,1024]{1,0:T(8,128)(2,1)}, bf16[256,1024]{1,0:T(8,128)(2,1)}, u32[]{:S(2)}, u32[]{:S(2)}) collective-permute-start(bf16[256,1024]{1,0:T(8,128)(2,1)} %bitcast.23), channel_id=1, source_target_pairs={{192,0},{128,64},{193,1},{129,65},{194,2},{130,66},{195,3},{131,67... | collective-permute-start | bytes 1572872 | tf_op jit(solution)/shard_map/ppermute | solution.py:47
  166.0 4.5 %all-to-all-start.7 = ((bf16[4,64,512]{2,1,0:T(8,128)(2,1)}), bf16[4,64,512]{2,1,0:T(8,128)(2,1)}, u32[]{:S(2)}, u32[]{:S(2)}) async-start(bf16[4,64,512]{2,1,0:T(8,128)(2,1)} %broadcast_in_dim.20), calls=%async_computation.7 | async-start | bytes 524288 | tf_op jit(solution)/shard_map/all_to_all | solution.py:80
  170.5 1.3 broadcast_select_fusion.1
  171.8 2.8 %collective-permute-done.16 = bf16[256,1024]{1,0:T(8,128)(2,1)} collective-permute-done((bf16[256,1024]{1,0:T(8,128)(2,1)}, bf16[256,1024]{1,0:T(8,128)(2,1)}, u32[]{:S(2)}, u32[]{:S(2)}) %collective-permute-start.16) | collective-permute-done | bytes 524320 | tf_op jit(solution)/shard_map/ppermute | solution.py:47
  174.6 1.3 pad_maximum_fusion
  175.9 1.3 bitcast_select_fusion
  177.3 2.6 %convolution_convert_fusion = bf16[1024,1024]{1,0:T(8,128)(2,1)} fusion(bf16[512,1024]{1,0:T(8,128)(2,1)S(1)} %bitcast_select_fusion, bf16[512,512]{1,0:T(8,128)(2,1)S(1)} %get-tuple-element.57, bf16[512,512]{1,0:T(8,128)(2,1)S(1)} %get-tuple-element.56), kind=kOutput, calls=%fused_computation.1 | convolution fusion | flops 1076887552 | bytes 4194304 | tf_op jit(solution)/shard_map/dot_general | solution.py:26
  179.9 5.2 %collective-permute-start.20 = (bf16[256,512]{1,0:T(8,128)(2,1)}, bf16[256,512]{1,0:T(8,128)(2,1)}, u32[]{:S(2)}, u32[]{:S(2)}) collective-permute-start(bf16[256,512]{1,0:T(8,128)(2,1)} %bitcast.30), channel_id=1, source_target_pairs={{192,0},{128,64},{193,1},{129,65},{194,2},{130,66},{195,3},{131,67... | collective-permute-start | bytes 786440 | tf_op jit(solution)/shard_map/ppermute | solution.py:47
  185.7 1.7 fusion.12
  187.5 2.7 %fusion.2 = bf16[256,1024]{1,0:T(8,128)(2,1)} fusion(f32[256,1024]{1,0:T(8,128)S(1)} %fusion.12, bf16[256,512]{1,0:T(8,128)(2,1)} %bitcast.30, bf16[1024,512]{1,0:T(8,128)(2,1)} %collective-permute-done.17, bf16[1024,512]{1,0:T(8,128)(2,1)S(1)} %get-tuple-element.32, pred[]{:T(512)S(6)} %eq.8), kind=kOutput, calls=%fused_computation.8 | convolution fusion | flops 269484032 | bytes 3932161 | tf_op jit(solution)/shard_map/dot_general | solution.py:26
  190.1 5.5 %all-to-all-start.8 = ((bf16[16,16,1024]{2,1,0:T(8,128)(2,1)}), bf16[16,16,1024]{2,1,0:T(8,128)(2,1)}, u32[]{:S(2)}, u32[]{:S(2)}) async-start(bf16[16,16,1024]{2,1,0:T(8,128)(2,1)} %bitcast.34), calls=%async_computation.8 | async-start | bytes 1048576 | tf_op jit(solution)/shard_map/all_to_all | solution.py:112
  195.9 1.6 collective-permute-done.21
  198.7 1.3 convert_bitcast_fusion
  200.0 11.5 %all-to-all-done.8 = bf16[16,16,1024]{2,1,0:T(8,128)(2,1)} async-done(((bf16[16,16,1024]{2,1,0:T(8,128)(2,1)}), bf16[16,16,1024]{2,1,0:T(8,128)(2,1)}, u32[]{:S(2)}, u32[]{:S(2)}) %all-to-all-start.8) | async-done | bytes 524320 | tf_op jit(solution)/shard_map/all_to_all | solution.py:112
  211.5 1.1 convert_reduce_fusion
  212.7 2.6 %copy.12 = bf16[1,1024,1024]{2,1,0:T(8,128)(2,1)} copy(bf16[1,1024,1024]{1,2,0:T(8,128)(2,1)S(1)} %bitcast.112) | data formatting | bytes 4194304
  215.3 2.8 %collective-permute-done.22 = bf16[16,1024]{1,0:T(8,128)(2,1)S(1)} collective-permute-done((bf16[16,1024]{1,0:T(8,128)(2,1)S(1)}, bf16[16,1024]{1,0:T(8,128)(2,1)S(1)}, u32[]{:S(2)}, u32[]{:S(2)}) %collective-permute-start.22) | collective-permute-done | bytes 32800 | tf_op jit(solution)/shard_map/ppermute | solution.py:214
  (83 shorter events, 19.0 us)
Async XLA Ops:
  0.6 13.2 %copy-start = (bf16[1,512,1024]{2,1,0:T(8,128)(2,1)S(1)}, bf16[1,512,1024]{2,1,0:T(8,128)(2,1)}, u32[]{:S(2)}) copy-start(bf16[1,512,1024]{2,1,0:T(8,128)(2,1)} %param.4) | copy-start | bytes 3145732
  2.7 35.8 %all-to-all-start = ((bf16[16,32,1024]{2,1,0:T(8,128)(2,1)}), bf16[16,32,1024]{2,1,0:T(8,128)(2,1)}, u32[]{:S(2)}, u32[]{:S(2)}) async-start(bf16[16,32,1024]{2,1,0:T(8,128)(2,1)} %broadcast_in_dim.16), calls=%async_computation | async-start | bytes 2097152 | tf_op jit(solution)/shard_map/all_to_all | solution.py:123
  15.4 2.3 %collective-permute-start = (bf16[512,512]{1,0:T(8,128)(2,1)}, bf16[512,512]{1,0:T(8,128)(2,1)}, u32[]{:S(2)}, u32[]{:S(2)}) collective-permute-start(bf16[512,512]{1,0:T(8,128)(2,1)} %fusion.3), channel_id=1, source_target_pairs={{0,1},{1,0},{2,3},{3,2},{4,5},{5,4},{6,7},{7,6},{8,9},{9,8},{10,11... | collective-permute-start | bytes 1572872 | tf_op jit(solution)/shard_map/ppermute | solution.py:39
  19.4 5.3 %copy-start.1 = (bf16[1,1024,1024]{2,1,0:T(8,128)(2,1)S(1)}, bf16[1,1024,1024]{2,1,0:T(8,128)(2,1)}, u32[]{:S(2)}) copy-start(bf16[1,1024,1024]{2,1,0:T(8,128)(2,1)} %param.7) | copy-start | bytes 6291460
  19.5 7.9 %collective-permute-start.3 = (bf16[128,512]{1,0:T(8,128)(2,1)S(1)}, bf16[128,512]{1,0:T(8,128)(2,1)S(1)}, u32[]{:S(2)}, u32[]{:S(2)}) collective-permute-start(bf16[128,512]{1,0:T(8,128)(2,1)S(1)} %get-tuple-element.59), channel_id=1, source_target_pairs={{0,4},{2,6},{4,0},{6,2},{1,5},{3,7},{5,1},{7,3},{8,12},{10,14},{12... | collective-permute-start | bytes 393224 | tf_op jit(solution)/shard_map/ppermute | solution.py:86
  22.6 6.9 %collective-permute-start.2 = (bf16[128,512]{1,0:T(8,128)(2,1)S(1)}, bf16[128,512]{1,0:T(8,128)(2,1)S(1)}, u32[]{:S(2)}, u32[]{:S(2)}) collective-permute-start(bf16[128,512]{1,0:T(8,128)(2,1)S(1)} %get-tuple-element.60), channel_id=1, source_target_pairs={{0,6},{2,0},{4,2},{6,4},{1,7},{3,1},{5,3},{7,5},{8,14},{10,8},{12,... | collective-permute-start | bytes 393224 | tf_op jit(solution)/shard_map/ppermute | solution.py:86
  23.7 6.3 %collective-permute-start.1 = (bf16[128,512]{1,0:T(8,128)(2,1)S(1)}, bf16[128,512]{1,0:T(8,128)(2,1)S(1)}, u32[]{:S(2)}, u32[]{:S(2)}) collective-permute-start(bf16[128,512]{1,0:T(8,128)(2,1)S(1)} %get-tuple-element.58), channel_id=1, source_target_pairs={{0,2},{2,4},{4,6},{6,0},{1,3},{3,5},{5,7},{7,1},{8,10},{10,12},{12... | collective-permute-start | bytes 393224 | tf_op jit(solution)/shard_map/ppermute | solution.py:86
  38.4 4.4 %copy-start.2 = (bf16[512,1024]{1,0:T(8,128)(2,1)S(1)}, bf16[512,1024]{1,0:T(8,128)(2,1)}, u32[]{:S(2)}) copy-start(bf16[512,1024]{1,0:T(8,128)(2,1)} %get-tuple-element.28) | copy-start | bytes 3145732
  40.8 2.0 collective-permute-start.4
  45.6 14.3 %all-to-all-start.1 = ((bf16[4,128,512]{2,1,0:T(8,128)(2,1)}), bf16[4,128,512]{2,1,0:T(8,128)(2,1)}, u32[]{:S(2)}, u32[]{:S(2)}) async-start(bf16[4,128,512]{2,1,0:T(8,128)(2,1)} %bitcast.123), calls=%async_computation.1 | async-start | bytes 1048576 | tf_op jit(solution)/shard_map/all_to_all | solution.py:72
  49.9 31.6 %collective-permute-start.12 = (bf16[512,1024]{1,0:T(8,128)(2,1)}, bf16[512,1024]{1,0:T(8,128)(2,1)}, u32[]{:S(2)}, u32[]{:S(2)}) collective-permute-start(bf16[512,1024]{1,0:T(8,128)(2,1)} %get-tuple-element.46), channel_id=1, source_target_pairs={{0,192},{64,128},{1,193},{65,129},{2,194},{66,130},{3,195},{67,131... | collective-permute-start | bytes 3145736 | tf_op jit(solution)/shard_map/ppermute | solution.py:43
  70.2 5.9 %copy-start.10 = (f32[4,1,16,512]{3,2,1,0:T(8,128)S(1)}, f32[4,1,16,512]{3,2,1,0:T(8,128)}, u32[]{:S(2)}) copy-start(f32[4,1,16,512]{3,2,1,0:T(8,128)} %get-tuple-element.63) | copy-start | bytes 393220
  70.2 1.5 collective-permute-start.6
  71.7 1.3 copy-start.8
  73.0 17.3 %collective-permute-start.7 = (bf16[256,1024]{1,0:T(8,128)(2,1)}, bf16[256,1024]{1,0:T(8,128)(2,1)}, u32[]{:S(2)}, u32[]{:S(2)}) collective-permute-start(bf16[256,1024]{1,0:T(8,128)(2,1)} %fusion.1), channel_id=1, source_target_pairs={{192,0},{128,64},{193,1},{129,65},{194,2},{130,66},{195,3},{131,67... | collective-permute-start | bytes 1572872 | tf_op jit(solution)/shard_map/ppermute | solution.py:47
  77.5 11.1 %all-to-all-start.2 = ((bf16[4,64,512]{2,1,0:T(8,128)(2,1)}), bf16[4,64,512]{2,1,0:T(8,128)(2,1)}, u32[]{:S(2)}, u32[]{:S(2)}) async-start(bf16[4,64,512]{2,1,0:T(8,128)(2,1)} %broadcast_in_dim.17), calls=%async_computation.2 | async-start | bytes 524288 | tf_op jit(solution)/shard_map/all_to_all | solution.py:80
  81.5 28.3 %collective-permute-start.13 = (bf16[512,1024]{1,0:T(8,128)(2,1)}, bf16[512,1024]{1,0:T(8,128)(2,1)}, u32[]{:S(2)}, u32[]{:S(2)}) collective-permute-start(bf16[512,1024]{1,0:T(8,128)(2,1)} %get-tuple-element.28), channel_id=1, source_target_pairs={{0,192},{64,128},{1,193},{65,129},{2,194},{66,130},{3,195},{67,131... | collective-permute-start | bytes 3145736 | tf_op jit(solution)/shard_map/ppermute | solution.py:43
  88.5 1.7 collective-permute-start.5
  90.3 1.3 copy-start.4
  91.6 30.9 %all-to-all-start.4 = ((bf16[16,16,1024]{2,1,0:T(8,128)(2,1)}), bf16[16,16,1024]{2,1,0:T(8,128)(2,1)}, u32[]{:S(2)}, u32[]{:S(2)}) async-start(bf16[16,16,1024]{2,1,0:T(8,128)(2,1)} %bitcast.113), calls=%async_computation.4 | async-start | bytes 1048576 | tf_op jit(solution)/shard_map/all_to_all | solution.py:112
  109.9 44.3 %collective-permute-start.17 = (bf16[1024,512]{1,0:T(8,128)(2,1)S(1)}, bf16[1024,512]{1,0:T(8,128)(2,1)}, u32[]{:S(2)}, u32[]{:S(2)}) collective-permute-start(bf16[1024,512]{1,0:T(8,128)(2,1)S(1)} %get-tuple-element.32), channel_id=1, source_target_pairs={{0,192},{64,128},{1,193},{65,129},{2,194},{66,130},{3,195},{67,131... | collective-permute-start | bytes 3145736 | tf_op jit(solution)/shard_map/ppermute | solution.py:43
  111.1 7.9 %collective-permute-start.8 = (bf16[128,512]{1,0:T(8,128)(2,1)}, bf16[128,512]{1,0:T(8,128)(2,1)S(1)}, u32[]{:S(2)}, u32[]{:S(2)}) collective-permute-start(bf16[128,512]{1,0:T(8,128)(2,1)} %get-tuple-element.25), channel_id=1, source_target_pairs={{0,6},{2,0},{4,2},{6,4},{1,7},{3,1},{5,3},{7,5},{8,14},{10,8},{12,... | collective-permute-start | bytes 393224 | tf_op jit(solution)/shard_map/ppermute | solution.py:86
  114.1 7.0 %collective-permute-start.9 = (bf16[128,512]{1,0:T(8,128)(2,1)}, bf16[128,512]{1,0:T(8,128)(2,1)S(1)}, u32[]{:S(2)}, u32[]{:S(2)}) collective-permute-start(bf16[128,512]{1,0:T(8,128)(2,1)} %get-tuple-element.25), channel_id=1, source_target_pairs={{0,4},{2,6},{4,0},{6,2},{1,5},{3,7},{5,1},{7,3},{8,12},{10,14},{12... | collective-permute-start | bytes 393224 | tf_op jit(solution)/shard_map/ppermute | solution.py:86
  115.0 16.1 %collective-permute-start.10 = (bf16[128,512]{1,0:T(8,128)(2,1)}, bf16[128,512]{1,0:T(8,128)(2,1)}, u32[]{:S(2)}, u32[]{:S(2)}) collective-permute-start(bf16[128,512]{1,0:T(8,128)(2,1)} %get-tuple-element.25), channel_id=1, source_target_pairs={{0,2},{2,4},{4,6},{6,0},{1,3},{3,5},{5,7},{7,1},{8,10},{10,12},{12... | collective-permute-start | bytes 393224 | tf_op jit(solution)/shard_map/ppermute | solution.py:86
  115.8 23.4 %collective-permute-start.11 = (bf16[64,512]{1,0:T(8,128)(2,1)}, bf16[64,512]{1,0:T(8,128)(2,1)}, u32[]{:S(2)}, u32[]{:S(2)}) collective-permute-start(bf16[64,512]{1,0:T(8,128)(2,1)} %get-tuple-element.26), channel_id=1, source_target_pairs={{0,192},{64,128},{1,193},{65,129},{2,194},{66,130},{3,195},{67,131... | collective-permute-start | bytes 196616 | tf_op jit(solution)/shard_map/ppermute | solution.py:43
  119.0 0.6 copy-start.11
  121.1 0.7 copy-start.12
  124.4 0.6 copy-start.13
  125.9 17.9 %all-to-all-start.5 = ((bf16[16,16,1024]{2,1,0:T(8,128)(2,1)}), bf16[16,16,1024]{2,1,0:T(8,128)(2,1)}, u32[]{:S(2)}, u32[]{:S(2)}) async-start(bf16[16,16,1024]{2,1,0:T(8,128)(2,1)} %broadcast_in_dim.19), calls=%async_computation.5 | async-start | bytes 1048576 | tf_op jit(solution)/shard_map/all_to_all | solution.py:123
  143.8 3.6 %copy-start.3 = (bf16[512,1024]{1,0:T(8,128)(2,1)S(1)}, bf16[512,1024]{1,0:T(8,128)(2,1)}, u32[]{:S(2)}) copy-start(bf16[512,1024]{1,0:T(8,128)(2,1)} %get-tuple-element.28) | copy-start | bytes 3145732
  145.7 1.6 collective-permute-start.14
  149.9 13.5 %all-to-all-start.6 = ((bf16[4,64,512]{2,1,0:T(8,128)(2,1)}), bf16[4,64,512]{2,1,0:T(8,128)(2,1)}, u32[]{:S(2)}, u32[]{:S(2)}) async-start(bf16[4,64,512]{2,1,0:T(8,128)(2,1)} %bitcast.125), calls=%async_computation.6 | async-start | bytes 524288 | tf_op jit(solution)/shard_map/all_to_all | solution.py:72
  153.9 16.6 %collective-permute-start.15 = (bf16[512,512]{1,0:T(8,128)(2,1)}, bf16[512,512]{1,0:T(8,128)(2,1)}, u32[]{:S(2)}, u32[]{:S(2)}) collective-permute-start(bf16[512,512]{1,0:T(8,128)(2,1)} %bitcast.110), channel_id=1, source_target_pairs={{0,1},{1,0},{2,3},{3,2},{4,5},{5,4},{6,7},{7,6},{8,9},{9,8},{10,11... | collective-permute-start | bytes 1572872 | tf_op jit(solution)/shard_map/ppermute | solution.py:39
  154.2 30.9 %collective-permute-start.19 = (bf16[1024,512]{1,0:T(8,128)(2,1)S(1)}, bf16[1024,512]{1,0:T(8,128)(2,1)}, u32[]{:S(2)}, u32[]{:S(2)}) collective-permute-start(bf16[1024,512]{1,0:T(8,128)(2,1)S(1)} %get-tuple-element.33), channel_id=1, source_target_pairs={{0,192},{64,128},{1,193},{65,129},{2,194},{66,130},{3,195},{67,131... | collective-permute-start | bytes 3145736 | tf_op jit(solution)/shard_map/ppermute | solution.py:43
  155.5 19.1 %collective-permute-start.16 = (bf16[256,1024]{1,0:T(8,128)(2,1)}, bf16[256,1024]{1,0:T(8,128)(2,1)}, u32[]{:S(2)}, u32[]{:S(2)}) collective-permute-start(bf16[256,1024]{1,0:T(8,128)(2,1)} %bitcast.23), channel_id=1, source_target_pairs={{192,0},{128,64},{193,1},{129,65},{194,2},{130,66},{195,3},{131,67... | collective-permute-start | bytes 1572872 | tf_op jit(solution)/shard_map/ppermute | solution.py:47
  166.0 13.9 %all-to-all-start.7 = ((bf16[4,64,512]{2,1,0:T(8,128)(2,1)}), bf16[4,64,512]{2,1,0:T(8,128)(2,1)}, u32[]{:S(2)}, u32[]{:S(2)}) async-start(bf16[4,64,512]{2,1,0:T(8,128)(2,1)} %broadcast_in_dim.20), calls=%async_computation.7 | async-start | bytes 524288 | tf_op jit(solution)/shard_map/all_to_all | solution.py:80
  179.9 5.2 %collective-permute-start.18 = (bf16[256,512]{1,0:T(8,128)(2,1)}, bf16[256,512]{1,0:T(8,128)(2,1)S(1)}, u32[]{:S(2)}, u32[]{:S(2)}) collective-permute-start(bf16[256,512]{1,0:T(8,128)(2,1)} %bitcast.30), channel_id=1, source_target_pairs={{0,1},{1,0},{2,3},{3,2},{4,5},{5,4},{6,7},{7,6},{8,9},{9,8},{10,11... | collective-permute-start | bytes 786440 | tf_op jit(solution)/shard_map/ppermute | solution.py:39
  179.9 15.8 %collective-permute-start.20 = (bf16[256,512]{1,0:T(8,128)(2,1)}, bf16[256,512]{1,0:T(8,128)(2,1)}, u32[]{:S(2)}, u32[]{:S(2)}) collective-permute-start(bf16[256,512]{1,0:T(8,128)(2,1)} %bitcast.30), channel_id=1, source_target_pairs={{192,0},{128,64},{193,1},{129,65},{194,2},{130,66},{195,3},{131,67... | collective-permute-start | bytes 786440 | tf_op jit(solution)/shard_map/ppermute | solution.py:47
  185.0 0.7 copy-start.6
  187.5 8.3 %copy-start.7 = (bf16[256,512]{1,0:T(8,128)(2,1)S(1)}, bf16[256,512]{1,0:T(8,128)(2,1)}, u32[]{:S(2)}) copy-start(bf16[256,512]{1,0:T(8,128)(2,1)} %copy-done.6) | copy-start | bytes 786436
  187.5 8.3 %copy-start.9 = (bf16[256,512]{1,0:T(8,128)(2,1)S(1)}, bf16[256,512]{1,0:T(8,128)(2,1)}, u32[]{:S(2)}) copy-start(bf16[256,512]{1,0:T(8,128)(2,1)} %copy-done.8) | copy-start | bytes 786436
  190.1 7.3 %copy-start.5 = (bf16[256,512]{1,0:T(8,128)(2,1)S(1)}, bf16[256,512]{1,0:T(8,128)(2,1)}, u32[]{:S(2)}) copy-start(bf16[256,512]{1,0:T(8,128)(2,1)} %copy-done.4) | copy-start | bytes 786436
  190.1 21.3 %all-to-all-start.8 = ((bf16[16,16,1024]{2,1,0:T(8,128)(2,1)}), bf16[16,16,1024]{2,1,0:T(8,128)(2,1)}, u32[]{:S(2)}, u32[]{:S(2)}) async-start(bf16[16,16,1024]{2,1,0:T(8,128)(2,1)} %bitcast.34), calls=%async_computation.8 | async-start | bytes 1048576 | tf_op jit(solution)/shard_map/all_to_all | solution.py:112
  195.6 1.8 collective-permute-start.21
  198.7 13.9 %copy-start.14 = (bf16[16,1024]{1,0:T(8,128)(2,1)S(1)}, bf16[16,1024]{1,0:T(8,128)(2,1)}, u32[]{:S(2)}) copy-start(bf16[16,1024]{1,0:T(8,128)(2,1)} %copy-done.13) | copy-start | bytes 98308
  212.6 5.5 %collective-permute-start.22 = (bf16[16,1024]{1,0:T(8,128)(2,1)S(1)}, bf16[16,1024]{1,0:T(8,128)(2,1)S(1)}, u32[]{:S(2)}, u32[]{:S(2)}) collective-permute-start(bf16[16,1024]{1,0:T(8,128)(2,1)S(1)} %broadcast_select_fusion.12), channel_id=1, source_target_pairs={{0,128},{128,0},{1,129},{129,1},{2,130},{130,2},{3,131},{131,3},{4... | collective-permute-start | bytes 98312 | tf_op jit(solution)/shard_map/ppermute | solution.py:214

commit v9 on v8

--- a/solution.py
+++ b/solution.py
@@ -101,10 +101,13 @@
 
 def gather_x_beside(block):
     rows, cols = block.shape
-    found = [block] + [step_x(block, X - distance) for distance in (1, 2, 3)]
-    twice = jnp.stack(found + found[:-1])
-    start = lax.rem(X - lax.axis_index("x"), X)
-    return lax.dynamic_slice_in_dim(twice, start, X, 0).reshape(X * rows, cols)
+    found = [block] + [step_x(block, distance) for distance in (1, 2, 3)]
+    source = lax.broadcasted_iota(jnp.int32, (X, 1, 1), 0)
+    passed = lax.rem(lax.axis_index("x") - source + X, X)
+    placed = found[0][None]
+    for distance in (1, 2, 3):
+        placed = jnp.where(passed == distance, found[distance][None], placed)
+    return placed.reshape(X * rows, cols)
 
 
 def spread_wide(partial):
@@ -159,9 +162,10 @@
     w_up, w_down = up_weight[0], down_weight[0]
     up_halves, down_halves = halves(w_up, 1), halves(w_down, 0)
 
-    crossed = []
-    for piece in (down_halves[1], down_halves[0], up_halves[0], up_halves[1]):
-        crossed.append(to_upper(together(piece, *crossed[-1:])[0]))
+    sent_down = to_upper(w_down)
+    sent_up = []
+    for piece in up_halves:
+        sent_up.append(to_upper(together(piece, *(sent_up or [sent_down]))[0]))
 
     theirs = contract(saved, up_halves[1], 1, 0)
     mine = contract(saved, up_halves[0], 1, 0)
@@ -178,8 +182,8 @@
     top_slope = [(block, other_core(block)) for block in top_mine]
     moved = to_lower(back_through_up(top_slope[0], up_halves))
     partial = pick(back_through_up(top_slope[1], up_halves), moved)
-    partial, act, sent = together(partial, act, slopes[1].astype(jnp.bfloat16))
-    blocks = spread_wide(partial)
+    partial, sent = together(partial, slopes[1].astype(jnp.bfloat16))
+    blocks, act, sent_down = together(spread_wide(partial), act, sent_down)
     middle = (
         pick(upstream[part:], upstream[:part]).astype(jnp.float32) + add_blocks(blocks)
     ).astype(jnp.bfloat16)
@@ -188,7 +192,7 @@
     low, hidden, sent = together(gather_wide(middle), hidden, to_upper(sent))
     hidden = in_order(hidden, other_core(hidden))
     low_rest = to_lower(low)
-    low_down = [pick(crossed[1], down_halves[0]), pick(crossed[0], down_halves[1])]
+    low_down = [pick(u, l) for u, l in zip(halves(sent_down, 0), down_halves)]
     low_share = back_share(low, low_down)
     incoming = pick(gathered, both_parts(low, low_rest))
     grad_down = contract(hidden, incoming, 0, 0).astype(jnp.bfloat16)
@@ -198,7 +202,7 @@
     low_mine, grad_down = together(low_mine, grad_down)
     low_slope = (low_mine, other_core(low_mine))
     low_slope_rest = to_lower(low_mine)
-    low_up = [pick(crossed[2], up_halves[0]), pick(crossed[3], up_halves[1])]
+    low_up = [pick(u, l) for u, l in zip(sent_up, up_halves)]
     low_blocks = spread_wide(back_through_up(low_slope, low_up))
     slope_grad = both_parts(
         in_order(*[pick(u, l) for u, l in zip(top_slope[0], low_slope)]),

time: 221 us -> 230 us (1.041)
  waiting for transfers between devices: 69.6 us -> 81.8 us
  local copies, waits for them, and re-layouts: 24.5 us -> 13.2 us
  blocking collectives: 9.07 us -> 13.9 us
    ppermute x5 -> x4, waiting for transfers between devices: 13.1 us -> 30.3 us  [to_upper(): return lax.ppermute(block, CROSS_AXES, [(0, 3), (1, 2)])]
    all_to_all x2 -> x1, waiting for transfers between devices: 8.68 us -> 0.01 us  [spread_x(): lax.all_to_all(partial.astype(jnp.bfloat16).reshape(X, rows // X, cols),...]
    unnamed x37 -> x29, local copies, waits for them, and re-layouts: 12.8 us -> 4.86 us
    all_to_all x2, waiting for transfers between devices: 11.3 us -> 4.59 us  [gather_wide(): lax.all_to_all(jnp.broadcast_to(block[None], (WIDE, rows, cols)), WIDE_AX...]
    all_to_all x2 -> x3, waiting for transfers between devices: 5.72 us -> 12.2 us  [gather_x(): lax.all_to_all(jnp.broadcast_to(block[None], (X, rows, cols)), 'x', 0, 0,...]
    all_to_all x1, blocking collectives: 9.07 us -> 13.9 us  [spread_x(): lax.all_to_all(partial.astype(jnp.bfloat16).reshape(X, rows // X, cols),...]
    all_to_all x2 -> x1, starting transfers between devices: 8.32 us -> 4.04 us  [spread_x(): lax.all_to_all(partial.astype(jnp.bfloat16).reshape(X, rows // X, cols),...]
    ppermute x6, waiting for transfers between devices: 5.09 us -> 9.21 us  [step_x(): return lax.ppermute(block, 'x', [(i, (i + distance) % X) for i in range(X)])]
  transfers between devices with their start and end apart: 31 -> 30, of which waited for: 19 -> 20; matrix products, arithmetic and copies ran while one was open for 24% -> 17% of each run, Pallas kernels for 0% -> 0%
where the time goes in v9:
time: 230 us; the launch traced here: 228 us
  waiting for transfers between devices  81.8 us (36%)
  starting transfers between devices  77.1 us (34%)
  matrix products  25.3 us (11%)
  other arithmetic  15.6 us (7%)
  blocking collectives  13.9 us (6%)
  local copies, waits for them, and re-layouts  13.2 us (6%)
    ppermute x4, waiting for transfers between devices, to_upper(): return lax.ppermute(block, CROSS_AXES, [(0, 3), (1, 2)])  30.3 us
    dot_general x14, matrix products, contract(): lax.dot_general(first_op, second_op, (((first_dim,), (second_dim,)), ((),...  25.3 us
    ppermute x3, starting transfers between devices, to_lower(): return lax.ppermute(block, CROSS_AXES, [(3, 0), (2, 1)])  15.9 us
    all_to_all x2, starting transfers between devices, gather_wide(): lax.all_to_all(jnp.broadcast_to(block[None], (WIDE, rows, cols)), WIDE_AX...  14.8 us
    all_to_all x1, blocking collectives, spread_x(): lax.all_to_all(partial.astype(jnp.bfloat16).reshape(X, rows // X, cols),...  13.9 us
    all_to_all x2, starting transfers between devices, spread_wide(): lax.all_to_all(partial.reshape(WIDE, rows // WIDE, cols), WIDE_AXES, 0, 0...  13.5 us
    all_to_all x3, waiting for transfers between devices, gather_x(): lax.all_to_all(jnp.broadcast_to(block[None], (X, rows, cols)), 'x', 0, 0,...  12.2 us
    all_to_all x3, starting transfers between devices, gather_x(): lax.all_to_all(jnp.broadcast_to(block[None], (X, rows, cols)), 'x', 0, 0,...  12.1 us
  transfers between devices with their start and end apart: 30, of which 20 were waited for; matrix products, arithmetic and copies ran while one was open for 17% of the time, Pallas kernels for 0%

profile of v9, /device:TPU:56, one launch (start us, length us, event | category | flops | bytes accessed | tf_op | source)
XLA Modules:
  0.0 227.9 jit_solution(1989216725737620008)
XLA Ops:
  0.6 2.0 broadcast_in_dim.113
  2.7 9.5 %all-to-all-start = ((bf16[16,32,1024]{2,1,0:T(8,128)(2,1)}), bf16[16,32,1024]{2,1,0:T(8,128)(2,1)}, u32[]{:S(2)}, u32[]{:S(2)}) async-start(bf16[16,32,1024]{2,1,0:T(8,128)(2,1)} %broadcast_in_dim.113), calls=%async_computation | async-start | bytes 2097152 | tf_op jit(solution)/shard_map/all_to_all | solution.py:126
  12.2 1.7 dynamic-slice_bitcast_fusion
  13.8 1.5 fusion.3
  15.4 2.2 collective-permute-done
  17.6 1.7 convert_add_fusion
  19.4 1.0 copy-done.1
  20.4 3.1 %collective-permute-start.3 = (bf16[128,512]{1,0:T(8,128)(2,1)S(1)}, bf16[128,512]{1,0:T(8,128)(2,1)}, u32[]{:S(2)}, u32[]{:S(2)}) collective-permute-start(bf16[128,512]{1,0:T(8,128)(2,1)S(1)} %get-tuple-element.59), channel_id=1, source_target_pairs={{0,4},{2,6},{4,0},{6,2},{1,5},{3,7},{5,1},{7,3},{8,12},{10,14},{12... | collective-permute-start | bytes 393224 | tf_op jit(solution)/shard_map/ppermute | solution.py:86
  23.6 1.1 collective-permute-start.2
  24.7 0.9 collective-permute-start.1
  25.6 2.9 %collective-permute-done.3 = bf16[128,512]{1,0:T(8,128)(2,1)} collective-permute-done((bf16[128,512]{1,0:T(8,128)(2,1)S(1)}, bf16[128,512]{1,0:T(8,128)(2,1)}, u32[]{:S(2)}, u32[]{:S(2)}) %collective-permute-start.3) | collective-permute-done | bytes 131104 | tf_op jit(solution)/shard_map/ppermute | solution.py:86
  28.5 2.1 collective-permute-done.2
  31.1 2.0 fusion.36
  33.8 4.6 %all-to-all-done = bf16[16,32,1024]{2,1,0:T(8,128)(2,1)} async-done(((bf16[16,32,1024]{2,1,0:T(8,128)(2,1)}), bf16[16,32,1024]{2,1,0:T(8,128)(2,1)}, u32[]{:S(2)}, u32[]{:S(2)}) %all-to-all-start) | async-done | bytes 1048608 | tf_op jit(solution)/shard_map/all_to_all | solution.py:126
  38.4 2.4 %convolution_convert_fusion.2 = bf16[512,512]{1,0:T(8,128)(2,1)S(1)} fusion(bf16[512,1024]{1,0:T(8,128)(2,1)} %bitcast, bf16[1,1024,1024]{2,1,0:T(8,128)(2,1)} %param.7, s32[]{:T(128)S(6)} %select_n.156), kind=kOutput, calls=%fused_computation.10 | convolution fusion | flops 537133056 | bytes 2621444 | tf_op jit(solution)/shard_map/dot_general | solution.py:26
  41.0 1.9 collective-permute-done.4
  42.9 2.0 add_convert_fusion
  44.9 13.9 %all_to_all.45 = bf16[4,128,512]{2,1,0:T(8,128)(2,1)S(1)} all-to-all(bf16[4,128,512]{2,1,0:T(8,128)(2,1)S(1)} %bitcast.134), channel_id=1, replica_groups=mesh['section'=2,'ylo'=2,'z'=8,'x'=4,'core'=2] {'x'}, dimensions={0} | all-to-all | bytes 1048576 | tf_op jit(solution)/shard_map/all_to_all | solution.py:72
  60.3 3.4 %all-to-all-start.3 = ((bf16[4,64,512]{2,1,0:T(8,128)(2,1)}), bf16[4,64,512]{2,1,0:T(8,128)(2,1)S(1)}, u32[]{:S(2)}, u32[]{:S(2)}) async-start(bf16[4,64,512]{2,1,0:T(8,128)(2,1)} %broadcast_in_dim.115), calls=%async_computation.3 | async-start | bytes 524288 | tf_op jit(solution)/shard_map/all_to_all | solution.py:80
  63.7 1.3 collective-permute-start.8
  65.0 5.3 %all-to-all-done.3 = bf16[4,64,512]{2,1,0:T(8,128)(2,1)S(1)} async-done(((bf16[4,64,512]{2,1,0:T(8,128)(2,1)}), bf16[4,64,512]{2,1,0:T(8,128)(2,1)S(1)}, u32[]{:S(2)}, u32[]{:S(2)}) %all-to-all-start.3) | async-done | bytes 262176 | tf_op jit(solution)/shard_map/all_to_all | solution.py:80
  70.8 1.1 collective-permute-done.6
  71.9 1.3 fusion.1
  73.1 3.1 %collective-permute-start.7 = (bf16[256,1024]{1,0:T(8,128)(2,1)}, bf16[256,1024]{1,0:T(8,128)(2,1)}, u32[]{:S(2)}, u32[]{:S(2)}) collective-permute-start(bf16[256,1024]{1,0:T(8,128)(2,1)} %fusion.1), channel_id=1, source_target_pairs={{192,0},{128,64},{193,1},{129,65},{194,2},{130,66},{195,3},{131,67... | collective-permute-start | bytes 1572872 | tf_op jit(solution)/shard_map/ppermute | solution.py:47
  77.6 4.2 %all-to-all-start.2 = ((bf16[4,64,512]{2,1,0:T(8,128)(2,1)}), bf16[4,64,512]{2,1,0:T(8,128)(2,1)}, u32[]{:S(2)}, u32[]{:S(2)}) async-start(bf16[4,64,512]{2,1,0:T(8,128)(2,1)} %broadcast_in_dim.114), calls=%async_computation.2 | async-start | bytes 524288 | tf_op jit(solution)/shard_map/all_to_all | solution.py:80
  81.8 6.9 %all-to-all-done.2 = bf16[4,64,512]{2,1,0:T(8,128)(2,1)} async-done(((bf16[4,64,512]{2,1,0:T(8,128)(2,1)}), bf16[4,64,512]{2,1,0:T(8,128)(2,1)}, u32[]{:S(2)}, u32[]{:S(2)}) %all-to-all-start.2) | async-done | bytes 262176 | tf_op jit(solution)/shard_map/all_to_all | solution.py:80
  88.7 1.4 fusion.50
  90.5 1.3 fusion.4
  91.8 5.2 %all-to-all-start.4 = ((bf16[16,16,1024]{2,1,0:T(8,128)(2,1)}), bf16[16,16,1024]{2,1,0:T(8,128)(2,1)}, u32[]{:S(2)}, u32[]{:S(2)}) async-start(bf16[16,16,1024]{2,1,0:T(8,128)(2,1)} %bitcast.125), calls=%async_computation.4 | async-start | bytes 1048576 | tf_op jit(solution)/shard_map/all_to_all | solution.py:115
  97.0 16.4 %collective-permute-done.8 = bf16[1024,1024]{1,0:T(8,128)(2,1)} collective-permute-done((bf16[1024,1024]{1,0:T(8,128)(2,1)}, bf16[1024,1024]{1,0:T(8,128)(2,1)}, u32[]{:S(2)}, u32[]{:S(2)}) %collective-permute-start.8) | collective-permute-done | bytes 2097184 | tf_op jit(solution)/shard_map/ppermute | solution.py:43
  113.3 1.1 convert_reduce_fusion.1
  116.7 5.3 %all-to-all-start.5 = ((bf16[16,16,1024]{2,1,0:T(8,128)(2,1)}), bf16[16,16,1024]{2,1,0:T(8,128)(2,1)}, u32[]{:S(2)}, u32[]{:S(2)}) async-start(bf16[16,16,1024]{2,1,0:T(8,128)(2,1)} %broadcast_in_dim.116), calls=%async_computation.5 | async-start | bytes 1048576 | tf_op jit(solution)/shard_map/all_to_all | solution.py:126
  122.2 1.3 collective-permute-start.16
  123.5 1.3 collective-permute-start.12
  124.8 1.8 collective-permute-start.11
  126.5 2.7 %collective-permute-start.10 = (bf16[128,512]{1,0:T(8,128)(2,1)}, bf16[128,512]{1,0:T(8,128)(2,1)S(1)}, u32[]{:S(2)}, u32[]{:S(2)}) collective-permute-start(bf16[128,512]{1,0:T(8,128)(2,1)} %get-tuple-element.27), channel_id=1, source_target_pairs={{0,4},{2,6},{4,0},{6,2},{1,5},{3,7},{5,1},{7,3},{8,12},{10,14},{12... | collective-permute-start | bytes 393224 | tf_op jit(solution)/shard_map/ppermute | solution.py:86
  129.2 1.5 collective-permute-start.9
  131.6 2.2 collective-permute-done.10
  134.4 2.0 fusion.31
  136.4 14.0 %collective-permute-done.12 = bf16[64,512]{1,0:T(8,128)(2,1)} collective-permute-done((bf16[64,512]{1,0:T(8,128)(2,1)}, bf16[64,512]{1,0:T(8,128)(2,1)}, u32[]{:S(2)}, u32[]{:S(2)}) %collective-permute-start.12) | collective-permute-done | bytes 65568 | tf_op jit(solution)/shard_map/ppermute | solution.py:43
  150.3 2.3 %convolution_convert_fusion.3 = bf16[256,512]{1,0:T(8,128)(2,1)S(1)} fusion(bf16[256,1024]{1,0:T(8,128)(2,1)} %bitcast.24, bf16[1024,1024]{1,0:T(8,128)(2,1)} %collective-permute-done.8, s32[]{:T(128)S(6)} %select_n.156, pred[]{:T(512)S(6)} %eq.32, bf16[1,1024,1024]{2,1,0:T(8,128)(2,1)} %param.7), kind=kOutput, calls=%fused_computation.15 | convolution fusion | flops 269090816 | bytes 2883589 | tf_op jit(solution)/shard_map/dot_general | solution.py:26
  152.8 1.5 collective-permute-done.13
  154.3 2.6 %fusion.5 = bf16[256,512]{1,0:T(8,128)(2,1)} fusion(bf16[256,1024]{1,0:T(8,128)(2,1)} %bitcast.24, bf16[1024,1024]{1,0:T(8,128)(2,1)} %collective-permute-done.8, s32[]{:T(128)S(6)} %select_n.155, pred[]{:T(512)S(6)} %eq.32, bf16[1,1024,1024]{2,1,0:T(8,128)(2,1)S(1)} %copy-done.13, bf16[256,512]{1,0:T(8,128)(2,1)S(1)} %collective-permute-done.13), kind=kOutput, calls=%fused_computation.14 | convolution fusion | flops 269352960 | bytes 3145733 | tf_op jit(solution)/shard_map/dot_general | solution.py:26
  156.9 4.0 %all-to-all-start.6 = ((bf16[4,64,512]{2,1,0:T(8,128)(2,1)}), bf16[4,64,512]{2,1,0:T(8,128)(2,1)}, u32[]{:S(2)}, u32[]{:S(2)}) async-start(bf16[4,64,512]{2,1,0:T(8,128)(2,1)} %bitcast.136), calls=%async_computation.6 | async-start | bytes 524288 | tf_op jit(solution)/shard_map/all_to_all | solution.py:72
  161.2 1.3 collective-permute-start.18
  162.5 7.6 %collective-permute-start.15 = (bf16[256,1024]{1,0:T(8,128)(2,1)}, bf16[256,1024]{1,0:T(8,128)(2,1)}, u32[]{:S(2)}, u32[]{:S(2)}) collective-permute-start(bf16[256,1024]{1,0:T(8,128)(2,1)} %bitcast.24), channel_id=1, source_target_pairs={{192,0},{128,64},{193,1},{129,65},{194,2},{130,66},{195,3},{131,67... | collective-permute-start | bytes 1572872 | tf_op jit(solution)/shard_map/ppermute | solution.py:47
  170.0 1.0 convert_reduce_fusion.3
  172.6 4.5 %all-to-all-start.7 = ((bf16[4,64,512]{2,1,0:T(8,128)(2,1)}), bf16[4,64,512]{2,1,0:T(8,128)(2,1)}, u32[]{:S(2)}, u32[]{:S(2)}) async-start(bf16[4,64,512]{2,1,0:T(8,128)(2,1)} %broadcast_in_dim.134), calls=%async_computation.7 | async-start | bytes 524288 | tf_op jit(solution)/shard_map/all_to_all | solution.py:80
  177.2 1.3 broadcast_select_fusion.1
  178.4 2.5 %collective-permute-done.15 = bf16[256,1024]{1,0:T(8,128)(2,1)} collective-permute-done((bf16[256,1024]{1,0:T(8,128)(2,1)}, bf16[256,1024]{1,0:T(8,128)(2,1)}, u32[]{:S(2)}, u32[]{:S(2)}) %collective-permute-start.15) | collective-permute-done | bytes 524320 | tf_op jit(solution)/shard_map/ppermute | solution.py:47
  180.9 1.3 pad_maximum_fusion
  182.2 1.3 bitcast_select_fusion
  183.6 2.6 %convolution_convert_fusion = bf16[1024,1024]{1,0:T(8,128)(2,1)} fusion(bf16[512,1024]{1,0:T(8,128)(2,1)S(1)} %bitcast_select_fusion, bf16[512,512]{1,0:T(8,128)(2,1)S(1)} %get-tuple-element.57, bf16[512,512]{1,0:T(8,128)(2,1)S(1)} %get-tuple-element.56), kind=kOutput, calls=%fused_computation.1 | convolution fusion | flops 1076887552 | bytes 4194304 | tf_op jit(solution)/shard_map/dot_general | solution.py:26
  186.2 5.2 %collective-permute-start.19 = (bf16[256,512]{1,0:T(8,128)(2,1)}, bf16[256,512]{1,0:T(8,128)(2,1)}, u32[]{:S(2)}, u32[]{:S(2)}) collective-permute-start(bf16[256,512]{1,0:T(8,128)(2,1)} %bitcast.33), channel_id=1, source_target_pairs={{192,0},{128,64},{193,1},{129,65},{194,2},{130,66},{195,3},{131,67... | collective-permute-start | bytes 786440 | tf_op jit(solution)/shard_map/ppermute | solution.py:47
  192.1 1.7 fusion.15
  193.8 2.7 %fusion.2 = bf16[256,1024]{1,0:T(8,128)(2,1)} fusion(f32[256,1024]{1,0:T(8,128)S(1)} %fusion.15, bf16[256,512]{1,0:T(8,128)(2,1)} %bitcast.33, bf16[1024,512]{1,0:T(8,128)(2,1)} %collective-permute-done.16, bf16[1024,512]{1,0:T(8,128)(2,1)S(1)} %get-tuple-element.34, pred[]{:T(512)S(6)} %eq.32), kind=kOutput, calls=%fused_computation.8 | convolution fusion | flops 269484032 | bytes 3932161 | tf_op jit(solution)/shard_map/dot_general | solution.py:26
  196.4 8.3 %all-to-all-start.8 = ((bf16[16,16,1024]{2,1,0:T(8,128)(2,1)}), bf16[16,16,1024]{2,1,0:T(8,128)(2,1)}, u32[]{:S(2)}, u32[]{:S(2)}) async-start(bf16[16,16,1024]{2,1,0:T(8,128)(2,1)} %bitcast.37), calls=%async_computation.8 | async-start | bytes 1048576 | tf_op jit(solution)/shard_map/all_to_all | solution.py:115
  205.0 1.6 collective-permute-done.20
  206.6 1.0 broadcast_select_fusion.7
  207.8 1.3 convert_bitcast_fusion
  209.1 11.5 %all-to-all-done.8 = bf16[16,16,1024]{2,1,0:T(8,128)(2,1)} async-done(((bf16[16,16,1024]{2,1,0:T(8,128)(2,1)}), bf16[16,16,1024]{2,1,0:T(8,128)(2,1)}, u32[]{:S(2)}, u32[]{:S(2)}) %all-to-all-start.8) | async-done | bytes 524320 | tf_op jit(solution)/shard_map/all_to_all | solution.py:115
  220.5 1.1 convert_reduce_fusion
  221.8 2.6 %copy.12 = bf16[1,1024,1024]{2,1,0:T(8,128)(2,1)} copy(bf16[1,1024,1024]{1,2,0:T(8,128)(2,1)S(1)} %bitcast.123) | data formatting | bytes 4194304
  224.4 2.8 %collective-permute-done.21 = bf16[16,1024]{1,0:T(8,128)(2,1)S(1)} collective-permute-done((bf16[16,1024]{1,0:T(8,128)(2,1)S(1)}, bf16[16,1024]{1,0:T(8,128)(2,1)S(1)}, u32[]{:S(2)}, u32[]{:S(2)}) %collective-permute-start.21) | collective-permute-done | bytes 32800 | tf_op jit(solution)/shard_map/ppermute | solution.py:218
  (76 shorter events, 12.8 us)
Async XLA Ops:
  0.6 13.2 %copy-start = (bf16[1,512,1024]{2,1,0:T(8,128)(2,1)S(1)}, bf16[1,512,1024]{2,1,0:T(8,128)(2,1)}, u32[]{:S(2)}) copy-start(bf16[1,512,1024]{2,1,0:T(8,128)(2,1)} %param.4) | copy-start | bytes 3145732
  2.7 35.8 %all-to-all-start = ((bf16[16,32,1024]{2,1,0:T(8,128)(2,1)}), bf16[16,32,1024]{2,1,0:T(8,128)(2,1)}, u32[]{:S(2)}, u32[]{:S(2)}) async-start(bf16[16,32,1024]{2,1,0:T(8,128)(2,1)} %broadcast_in_dim.113), calls=%async_computation | async-start | bytes 2097152 | tf_op jit(solution)/shard_map/all_to_all | solution.py:126
  15.4 2.3 collective-permute-start
  19.4 1.0 copy-start.1
  20.4 8.0 %collective-permute-start.3 = (bf16[128,512]{1,0:T(8,128)(2,1)S(1)}, bf16[128,512]{1,0:T(8,128)(2,1)}, u32[]{:S(2)}, u32[]{:S(2)}) collective-permute-start(bf16[128,512]{1,0:T(8,128)(2,1)S(1)} %get-tuple-element.59), channel_id=1, source_target_pairs={{0,4},{2,6},{4,0},{6,2},{1,5},{3,7},{5,1},{7,3},{8,12},{10,14},{12... | collective-permute-start | bytes 393224 | tf_op jit(solution)/shard_map/ppermute | solution.py:86
  23.6 7.0 %collective-permute-start.2 = (bf16[128,512]{1,0:T(8,128)(2,1)S(1)}, bf16[128,512]{1,0:T(8,128)(2,1)}, u32[]{:S(2)}, u32[]{:S(2)}) collective-permute-start(bf16[128,512]{1,0:T(8,128)(2,1)S(1)} %get-tuple-element.60), channel_id=1, source_target_pairs={{0,6},{2,0},{4,2},{6,4},{1,7},{3,1},{5,3},{7,5},{8,14},{10,8},{12,... | collective-permute-start | bytes 393224 | tf_op jit(solution)/shard_map/ppermute | solution.py:86
  24.7 6.4 %collective-permute-start.1 = (bf16[128,512]{1,0:T(8,128)(2,1)S(1)}, bf16[128,512]{1,0:T(8,128)(2,1)}, u32[]{:S(2)}, u32[]{:S(2)}) collective-permute-start(bf16[128,512]{1,0:T(8,128)(2,1)S(1)} %get-tuple-element.58), channel_id=1, source_target_pairs={{0,2},{2,4},{4,6},{6,0},{1,3},{3,5},{5,7},{7,1},{8,10},{10,12},{12... | collective-permute-start | bytes 393224 | tf_op jit(solution)/shard_map/ppermute | solution.py:86
  38.4 4.4 %copy-start.12 = (bf16[1,1024,1024]{2,1,0:T(8,128)(2,1)S(1)}, bf16[1,1024,1024]{2,1,0:T(8,128)(2,1)}, u32[]{:S(2)}) copy-start(bf16[1,1024,1024]{2,1,0:T(8,128)(2,1)} %param.7) | copy-start | bytes 6291460
  40.9 2.0 collective-permute-start.4
  60.3 10.1 %all-to-all-start.3 = ((bf16[4,64,512]{2,1,0:T(8,128)(2,1)}), bf16[4,64,512]{2,1,0:T(8,128)(2,1)S(1)}, u32[]{:S(2)}, u32[]{:S(2)}) async-start(bf16[4,64,512]{2,1,0:T(8,128)(2,1)} %broadcast_in_dim.115), calls=%async_computation.3 | async-start | bytes 524288 | tf_op jit(solution)/shard_map/all_to_all | solution.py:80
  63.7 49.7 %collective-permute-start.8 = (bf16[1024,1024]{1,0:T(8,128)(2,1)}, bf16[1024,1024]{1,0:T(8,128)(2,1)}, u32[]{:S(2)}, u32[]{:S(2)}) collective-permute-start(bf16[1024,1024]{1,0:T(8,128)(2,1)} %bitcast.137), channel_id=1, source_target_pairs={{0,192},{64,128},{1,193},{65,129},{2,194},{66,130},{3,195},{67,131... | collective-permute-start | bytes 6291464 | tf_op jit(solution)/shard_map/ppermute | solution.py:43
  70.3 5.9 %copy-start.8 = (f32[4,1,16,512]{3,2,1,0:T(8,128)S(1)}, f32[4,1,16,512]{3,2,1,0:T(8,128)}, u32[]{:S(2)}) copy-start(f32[4,1,16,512]{3,2,1,0:T(8,128)} %get-tuple-element.63) | copy-start | bytes 393220
  70.3 5.9 %copy-start.9 = (f32[4,1,16,512]{3,2,1,0:T(8,128)S(1)}, f32[4,1,16,512]{3,2,1,0:T(8,128)}, u32[]{:S(2)}) copy-start(f32[4,1,16,512]{3,2,1,0:T(8,128)} %get-tuple-element.61) | copy-start | bytes 393220
  70.3 1.5 collective-permute-start.6
  71.9 1.3 copy-start.6
  73.1 17.3 %collective-permute-start.7 = (bf16[256,1024]{1,0:T(8,128)(2,1)}, bf16[256,1024]{1,0:T(8,128)(2,1)}, u32[]{:S(2)}, u32[]{:S(2)}) collective-permute-start(bf16[256,1024]{1,0:T(8,128)(2,1)} %fusion.1), channel_id=1, source_target_pairs={{192,0},{128,64},{193,1},{129,65},{194,2},{130,66},{195,3},{131,67... | collective-permute-start | bytes 1572872 | tf_op jit(solution)/shard_map/ppermute | solution.py:47
  77.6 11.1 %all-to-all-start.2 = ((bf16[4,64,512]{2,1,0:T(8,128)(2,1)}), bf16[4,64,512]{2,1,0:T(8,128)(2,1)}, u32[]{:S(2)}, u32[]{:S(2)}) async-start(bf16[4,64,512]{2,1,0:T(8,128)(2,1)} %broadcast_in_dim.114), calls=%async_computation.2 | async-start | bytes 524288 | tf_op jit(solution)/shard_map/all_to_all | solution.py:80
  88.7 1.7 collective-permute-start.5
  90.4 1.3 copy-start.2
  91.8 21.6 %all-to-all-start.4 = ((bf16[16,16,1024]{2,1,0:T(8,128)(2,1)}), bf16[16,16,1024]{2,1,0:T(8,128)(2,1)}, u32[]{:S(2)}, u32[]{:S(2)}) async-start(bf16[16,16,1024]{2,1,0:T(8,128)(2,1)} %bitcast.125), calls=%async_computation.4 | async-start | bytes 1048576 | tf_op jit(solution)/shard_map/all_to_all | solution.py:115
  115.3 0.6 copy-start.10
  116.7 33.6 %all-to-all-start.5 = ((bf16[16,16,1024]{2,1,0:T(8,128)(2,1)}), bf16[16,16,1024]{2,1,0:T(8,128)(2,1)}, u32[]{:S(2)}, u32[]{:S(2)}) async-start(bf16[16,16,1024]{2,1,0:T(8,128)(2,1)} %broadcast_in_dim.116), calls=%async_computation.5 | async-start | bytes 1048576 | tf_op jit(solution)/shard_map/all_to_all | solution.py:126
  122.2 39.0 %collective-permute-start.16 = (bf16[1024,512]{1,0:T(8,128)(2,1)S(1)}, bf16[1024,512]{1,0:T(8,128)(2,1)}, u32[]{:S(2)}, u32[]{:S(2)}) collective-permute-start(bf16[1024,512]{1,0:T(8,128)(2,1)S(1)} %get-tuple-element.34), channel_id=1, source_target_pairs={{0,192},{64,128},{1,193},{65,129},{2,194},{66,130},{3,195},{67,131... | collective-permute-start | bytes 3145736 | tf_op jit(solution)/shard_map/ppermute | solution.py:43
  123.5 26.9 %collective-permute-start.12 = (bf16[64,512]{1,0:T(8,128)(2,1)}, bf16[64,512]{1,0:T(8,128)(2,1)}, u32[]{:S(2)}, u32[]{:S(2)}) collective-permute-start(bf16[64,512]{1,0:T(8,128)(2,1)} %get-tuple-element.28), channel_id=1, source_target_pairs={{0,192},{64,128},{1,193},{65,129},{2,194},{66,130},{3,195},{67,131... | collective-permute-start | bytes 196616 | tf_op jit(solution)/shard_map/ppermute | solution.py:43
  124.8 6.8 %collective-permute-start.11 = (bf16[128,512]{1,0:T(8,128)(2,1)}, bf16[128,512]{1,0:T(8,128)(2,1)S(1)}, u32[]{:S(2)}, u32[]{:S(2)}) collective-permute-start(bf16[128,512]{1,0:T(8,128)(2,1)} %get-tuple-element.27), channel_id=1, source_target_pairs={{0,2},{2,4},{4,6},{6,0},{1,3},{3,5},{5,7},{7,1},{8,10},{10,12},{12... | collective-permute-start | bytes 393224 | tf_op jit(solution)/shard_map/ppermute | solution.py:86
  126.5 7.2 %collective-permute-start.10 = (bf16[128,512]{1,0:T(8,128)(2,1)}, bf16[128,512]{1,0:T(8,128)(2,1)S(1)}, u32[]{:S(2)}, u32[]{:S(2)}) collective-permute-start(bf16[128,512]{1,0:T(8,128)(2,1)} %get-tuple-element.27), channel_id=1, source_target_pairs={{0,4},{2,6},{4,0},{6,2},{1,5},{3,7},{5,1},{7,3},{8,12},{10,14},{12... | collective-permute-start | bytes 393224 | tf_op jit(solution)/shard_map/ppermute | solution.py:86
  129.2 5.2 %collective-permute-start.9 = (bf16[128,512]{1,0:T(8,128)(2,1)}, bf16[128,512]{1,0:T(8,128)(2,1)S(1)}, u32[]{:S(2)}, u32[]{:S(2)}) collective-permute-start(bf16[128,512]{1,0:T(8,128)(2,1)} %get-tuple-element.27), channel_id=1, source_target_pairs={{0,6},{2,0},{4,2},{6,4},{1,7},{3,1},{5,3},{7,5},{8,14},{10,8},{12,... | collective-permute-start | bytes 393224 | tf_op jit(solution)/shard_map/ppermute | solution.py:86
  150.3 4.0 %copy-start.13 = (bf16[1,1024,1024]{2,1,0:T(8,128)(2,1)S(1)}, bf16[1,1024,1024]{2,1,0:T(8,128)(2,1)}, u32[]{:S(2)}) copy-start(bf16[1,1024,1024]{2,1,0:T(8,128)(2,1)} %param.7) | copy-start | bytes 6291460
  152.7 1.6 collective-permute-start.13
  156.9 13.1 %all-to-all-start.6 = ((bf16[4,64,512]{2,1,0:T(8,128)(2,1)}), bf16[4,64,512]{2,1,0:T(8,128)(2,1)}, u32[]{:S(2)}, u32[]{:S(2)}) async-start(bf16[4,64,512]{2,1,0:T(8,128)(2,1)} %bitcast.136), calls=%async_computation.6 | async-start | bytes 524288 | tf_op jit(solution)/shard_map/all_to_all | solution.py:72
  160.9 16.2 %collective-permute-start.14 = (bf16[512,512]{1,0:T(8,128)(2,1)}, bf16[512,512]{1,0:T(8,128)(2,1)}, u32[]{:S(2)}, u32[]{:S(2)}) collective-permute-start(bf16[512,512]{1,0:T(8,128)(2,1)} %fusion.31), channel_id=1, source_target_pairs={{0,1},{1,0},{2,3},{3,2},{4,5},{5,4},{6,7},{7,6},{8,9},{9,8},{10,11... | collective-permute-start | bytes 1572872 | tf_op jit(solution)/shard_map/ppermute | solution.py:39
  161.2 30.2 %collective-permute-start.18 = (bf16[1024,512]{1,0:T(8,128)(2,1)S(1)}, bf16[1024,512]{1,0:T(8,128)(2,1)}, u32[]{:S(2)}, u32[]{:S(2)}) collective-permute-start(bf16[1024,512]{1,0:T(8,128)(2,1)S(1)} %get-tuple-element.35), channel_id=1, source_target_pairs={{0,192},{64,128},{1,193},{65,129},{2,194},{66,130},{3,195},{67,131... | collective-permute-start | bytes 3145736 | tf_op jit(solution)/shard_map/ppermute | solution.py:43
  162.5 18.5 %collective-permute-start.15 = (bf16[256,1024]{1,0:T(8,128)(2,1)}, bf16[256,1024]{1,0:T(8,128)(2,1)}, u32[]{:S(2)}, u32[]{:S(2)}) collective-permute-start(bf16[256,1024]{1,0:T(8,128)(2,1)} %bitcast.24), channel_id=1, source_target_pairs={{192,0},{128,64},{193,1},{129,65},{194,2},{130,66},{195,3},{131,67... | collective-permute-start | bytes 1572872 | tf_op jit(solution)/shard_map/ppermute | solution.py:47
  172.6 13.6 %all-to-all-start.7 = ((bf16[4,64,512]{2,1,0:T(8,128)(2,1)}), bf16[4,64,512]{2,1,0:T(8,128)(2,1)}, u32[]{:S(2)}, u32[]{:S(2)}) async-start(bf16[4,64,512]{2,1,0:T(8,128)(2,1)} %broadcast_in_dim.134), calls=%async_computation.7 | async-start | bytes 524288 | tf_op jit(solution)/shard_map/all_to_all | solution.py:80
  186.2 5.2 %collective-permute-start.17 = (bf16[256,512]{1,0:T(8,128)(2,1)}, bf16[256,512]{1,0:T(8,128)(2,1)S(1)}, u32[]{:S(2)}, u32[]{:S(2)}) collective-permute-start(bf16[256,512]{1,0:T(8,128)(2,1)} %bitcast.33), channel_id=1, source_target_pairs={{0,1},{1,0},{2,3},{3,2},{4,5},{5,4},{6,7},{7,6},{8,9},{9,8},{10,11... | collective-permute-start | bytes 786440 | tf_op jit(solution)/shard_map/ppermute | solution.py:39
  186.2 18.5 %collective-permute-start.19 = (bf16[256,512]{1,0:T(8,128)(2,1)}, bf16[256,512]{1,0:T(8,128)(2,1)}, u32[]{:S(2)}, u32[]{:S(2)}) collective-permute-start(bf16[256,512]{1,0:T(8,128)(2,1)} %bitcast.33), channel_id=1, source_target_pairs={{192,0},{128,64},{193,1},{129,65},{194,2},{130,66},{195,3},{131,67... | collective-permute-start | bytes 786440 | tf_op jit(solution)/shard_map/ppermute | solution.py:47
  191.4 0.7 copy-start.4
  193.8 11.1 %copy-start.5 = (bf16[256,512]{1,0:T(8,128)(2,1)S(1)}, bf16[256,512]{1,0:T(8,128)(2,1)}, u32[]{:S(2)}) copy-start(bf16[256,512]{1,0:T(8,128)(2,1)} %copy-done.4) | copy-start | bytes 786436
  193.8 11.1 %copy-start.7 = (bf16[256,512]{1,0:T(8,128)(2,1)S(1)}, bf16[256,512]{1,0:T(8,128)(2,1)}, u32[]{:S(2)}) copy-start(bf16[256,512]{1,0:T(8,128)(2,1)} %copy-done.6) | copy-start | bytes 786436
  196.4 10.1 %copy-start.3 = (bf16[256,512]{1,0:T(8,128)(2,1)S(1)}, bf16[256,512]{1,0:T(8,128)(2,1)}, u32[]{:S(2)}) copy-start(bf16[256,512]{1,0:T(8,128)(2,1)} %copy-done.2) | copy-start | bytes 786436
  196.4 24.1 %all-to-all-start.8 = ((bf16[16,16,1024]{2,1,0:T(8,128)(2,1)}), bf16[16,16,1024]{2,1,0:T(8,128)(2,1)}, u32[]{:S(2)}, u32[]{:S(2)}) async-start(bf16[16,16,1024]{2,1,0:T(8,128)(2,1)} %bitcast.37), calls=%async_computation.8 | async-start | bytes 1048576 | tf_op jit(solution)/shard_map/all_to_all | solution.py:115
  204.7 1.8 collective-permute-start.20
  207.7 13.9 %copy-start.11 = (bf16[16,1024]{1,0:T(8,128)(2,1)S(1)}, bf16[16,1024]{1,0:T(8,128)(2,1)}, u32[]{:S(2)}) copy-start(bf16[16,1024]{1,0:T(8,128)(2,1)} %copy-done.10) | copy-start | bytes 98308
  221.7 5.5 %collective-permute-start.21 = (bf16[16,1024]{1,0:T(8,128)(2,1)S(1)}, bf16[16,1024]{1,0:T(8,128)(2,1)S(1)}, u32[]{:S(2)}, u32[]{:S(2)}) collective-permute-start(bf16[16,1024]{1,0:T(8,128)(2,1)S(1)} %broadcast_select_fusion.12), channel_id=1, source_target_pairs={{0,128},{128,0},{1,129},{129,1},{2,130},{130,2},{3,131},{131,3},{4... | collective-permute-start | bytes 98312 | tf_op jit(solution)/shard_map/ppermute | solution.py:218

commit v10 on v5

--- a/solution.py
+++ b/solution.py
@@ -140,15 +140,17 @@
     moved = to_lower(back_through_up(top_slope, up_halves))
     late_slopes, _ = together(slopes[last], top_slope[0])
     top_slope_rest = slope_of(back_total(top[1], down_halves), late_slopes)
-    blocks = spread_wide(pick(back_through_up(top_slope_rest, up_halves), moved))
-    sent_up = to_upper(together(w_up, sent_down)[0])
+    partial = pick(back_through_up(top_slope_rest, up_halves), moved)
+    half = w_up.shape[0] // 2
+    sent_up = [to_upper(together(w_up[:half], sent_down)[0])]
+    sent_up.append(to_upper(together(w_up[half:], sent_up[0])[0]))
+    blocks, sent_down = together(spread_wide(partial), sent_down)
     part = upstream.shape[0] // 2
     middle = (
         pick(upstream[part:], upstream[:part]).astype(jnp.float32) + add_blocks(blocks)
     ).astype(jnp.bfloat16)
 
     low_down = pick(sent_down, w_down)
-    low_up = pick(sent_up, w_up)
     lower_slopes = to_upper(slopes[last].astype(jnp.bfloat16))
     low, hidden, low_down, lower_slopes = together(
         gather_wide(middle), hidden, low_down, lower_slopes
@@ -158,7 +160,8 @@
     low_total = back_total(low, halves(low_down, 0))
     incoming = jnp.concatenate([pick(top[0], low), pick(top[1], low_rest)], axis=0)
     grad_down = contract(hidden, incoming, 0, 0).astype(jnp.bfloat16)
-    low_total, grad_down, low_up = together(low_total, grad_down, low_up)
+    low_total, grad_down, sent_up[1] = together(low_total, grad_down, sent_up[1])
+    low_up = pick(jnp.concatenate(sent_up, axis=0), w_up)
     low_slope = slope_of(low_total, lower_slopes)
     low_slope_rest = to_lower(low_slope[0])
     low_blocks = spread_wide(back_through_up(low_slope, halves(low_up, 1)))

time: 211 us -> 200 us (0.948)
  waiting for transfers between devices: 98.9 us -> 82 us
  starting transfers between devices: 59.7 us -> 66.5 us
  other arithmetic: 20.2 us -> 17.7 us
    ppermute x3 -> x4, waiting for transfers between devices: 25.4 us -> 6.07 us  [to_upper(): return lax.ppermute(block, CROSS_AXES, [(0, 3), (1, 2)])]
    ppermute x3, starting transfers between devices: 6.45 us -> 11.3 us  [to_lower(): return lax.ppermute(block, CROSS_AXES, [(3, 0), (2, 1)])]
    all_to_all x2, waiting for transfers between devices: 20.3 us -> 22.8 us  [spread_wide(): lax.all_to_all(partial.reshape(WIDE, rows // WIDE, cols), WIDE_AXES, 0, 0...]
    all_to_all x2, waiting for transfers between devices: 1.52 us -> 4 us  [gather_wide(): lax.all_to_all(jnp.broadcast_to(block[None], (WIDE, rows, cols)), WIDE_AX...]
    ppermute x12, waiting for transfers between devices: 40.2 us -> 37.8 us  [narrow_terms(): return [pair] + [lax.ppermute(sent, 'x', route) for route in routes]]
    ppermute x3 -> x4, starting transfers between devices: 3.85 us -> 5.13 us  [to_upper(): return lax.ppermute(block, CROSS_AXES, [(0, 3), (1, 2)])]
  transfers between devices with their start and end apart: 33 -> 34, of which waited for: 21 -> 18; matrix products, arithmetic and copies ran while one was open for 21% -> 21% of each run, Pallas kernels for 0% -> 0%
where the time goes in v10:
time: 200 us; the launch traced here: 199 us
  waiting for transfers between devices  82 us (41%)
  starting transfers between devices  66.5 us (33%)
  matrix products  22.7 us (11%)
  other arithmetic  17.7 us (9%)
  local copies, waits for them, and re-layouts  8.84 us (4%)
    ppermute x12, waiting for transfers between devices, narrow_terms(): return [pair] + [lax.ppermute(sent, 'x', route) for route in routes]  37.8 us
    all_to_all x2, waiting for transfers between devices, spread_wide(): lax.all_to_all(partial.reshape(WIDE, rows // WIDE, cols), WIDE_AXES, 0, 0...  22.8 us
    dot_general x18, matrix products, contract(): lax.dot_general(first_op, second_op, (((first_dim,), (second_dim,)), ((),...  22.7 us
    ppermute x12, starting transfers between devices, narrow_terms(): return [pair] + [lax.ppermute(sent, 'x', route) for route in routes]  21 us
    all_to_all x2, starting transfers between devices, gather_wide(): lax.all_to_all(jnp.broadcast_to(block[None], (WIDE, rows, cols)), WIDE_AX...  14.5 us
    all_to_all x2, starting transfers between devices, spread_wide(): lax.all_to_all(partial.reshape(WIDE, rows // WIDE, cols), WIDE_AXES, 0, 0...  13.5 us
    ppermute x3, starting transfers between devices, to_lower(): return lax.ppermute(block, CROSS_AXES, [(3, 0), (2, 1)])  11.3 us
    select_n x6, other arithmetic, pick(): return jnp.where(is_upper, upper, lower)  7.51 us
  transfers between devices with their start and end apart: 34, of which 18 were waited for; matrix products, arithmetic and copies ran while one was open for 21% of the time, Pallas kernels for 0%

profile of v10, /device:TPU:56, one launch (start us, length us, event | category | flops | bytes accessed | tf_op | source)
XLA Modules:
  0.0 199.0 jit_solution(14647051819232726787)
XLA Ops:
  0.6 1.9 broadcast_in_dim.10
  2.6 9.6 %all-to-all-start = ((bf16[16,32,1024]{2,1,0:T(8,128)(2,1)}), bf16[16,32,1024]{2,1,0:T(8,128)(2,1)}, u32[]{:S(2)}, u32[]{:S(2)}) async-start(bf16[16,32,1024]{2,1,0:T(8,128)(2,1)} %broadcast_in_dim.10), calls=%async_computation | async-start | bytes 2097152 | tf_op jit(solution)/shard_map/all_to_all | solution.py:90
  12.2 1.3 fusion.80
  14.4 0.8 pad_maximum_fusion.1
  15.3 1.5 convolution_bitcast_fusion
  17.5 1.2 fusion.57
  18.8 1.6 collective-permute-start.1
  20.3 2.0 collective-permute-start.2
  22.3 12.2 %collective-permute-done.1 = bf16[512,512]{1,0:T(8,128)(2,1)} collective-permute-done((bf16[512,512]{1,0:T(8,128)(2,1)S(1)}, bf16[512,512]{1,0:T(8,128)(2,1)}, u32[]{:S(2)}, u32[]{:S(2)}) %collective-permute-start.1) | collective-permute-done | bytes 524320 | tf_op jit(solution)/shard_map/ppermute | solution.py:70
  34.5 4.0 %all-to-all-done = bf16[16,32,1024]{2,1,0:T(8,128)(2,1)} async-done(((bf16[16,32,1024]{2,1,0:T(8,128)(2,1)}), bf16[16,32,1024]{2,1,0:T(8,128)(2,1)}, u32[]{:S(2)}, u32[]{:S(2)}) %all-to-all-start) | async-done | bytes 1048608 | tf_op jit(solution)/shard_map/all_to_all | solution.py:90
  38.5 1.4 fusion.78
  39.8 1.9 convolution_convert_fusion.5
  41.9 3.1 %collective-permute-start.7 = (bf16[512,512]{1,0:T(8,128)(2,1)S(1)}, bf16[512,512]{1,0:T(8,128)(2,1)S(1)}, u32[]{:S(2)}, u32[]{:S(2)}) collective-permute-start(bf16[512,512]{1,0:T(8,128)(2,1)S(1)} %copy-done.22), channel_id=1, source_target_pairs={{0,4},{2,6},{4,0},{6,2},{1,5},{3,7},{5,1},{7,3},{8,12},{10,14},{12... | collective-permute-start | bytes 1572872 | tf_op jit(solution)/shard_map/ppermute | solution.py:70
  45.0 1.3 collective-permute-start.15
  46.3 1.8 convolution_convert_fusion.6
  48.3 1.7 fusion.59
  50.6 2.8 %collective-permute-start.10 = (bf16[256,512]{1,0:T(8,128)(2,1)S(1)}, bf16[256,512]{1,0:T(8,128)(2,1)S(1)}, u32[]{:S(2)}, u32[]{:S(2)}) collective-permute-start(bf16[256,512]{1,0:T(8,128)(2,1)S(1)} %get-tuple-element.55), channel_id=1, source_target_pairs={{0,6},{2,0},{4,2},{6,4},{1,7},{3,1},{5,3},{7,5},{8,14},{10,8},{12,... | collective-permute-start | bytes 786440 | tf_op jit(solution)/shard_map/ppermute | solution.py:70
  53.4 4.8 %collective-permute-done.7 = bf16[512,512]{1,0:T(8,128)(2,1)S(1)} collective-permute-done((bf16[512,512]{1,0:T(8,128)(2,1)S(1)}, bf16[512,512]{1,0:T(8,128)(2,1)S(1)}, u32[]{:S(2)}, u32[]{:S(2)}) %collective-permute-start.7) | collective-permute-done | bytes 524320 | tf_op jit(solution)/shard_map/ppermute | solution.py:70
  58.2 1.6 collective-permute-start.9
  59.8 3.1 %multiply_convert_fusion = (bf16[512,512]{1,0:T(8,128)(2,1)}, f32[512,512]{1,0:T(8,128)S(1)}) fusion(bf16[512,512]{1,0:T(8,128)(2,1)S(1)} %collective-permute-done.7, bf16[512,512]{1,0:T(8,128)(2,1)} %collective-permute-done.2, bf16[512,512]{1,0:T(8,128)(2,1)} %collective-permute-done.1, bf16[512,512]{1,0:T(8,128)(2,1)} %collective-permute-done, ...), kind=kLoop, calls=%fused_computation.67 | loop fusion | flops 7340032 | bytes 4718592 | tf_op jit(solution)/shard_map/convert_element_type | solution.py:135
  62.9 0.9 collective-permute-done.11
  63.8 5.3 %collective-permute-done.10 = bf16[256,512]{1,0:T(8,128)(2,1)S(1)} collective-permute-done((bf16[256,512]{1,0:T(8,128)(2,1)S(1)}, bf16[256,512]{1,0:T(8,128)(2,1)S(1)}, u32[]{:S(2)}, u32[]{:S(2)}) %collective-permute-start.10) | collective-permute-done | bytes 262176 | tf_op jit(solution)/shard_map/ppermute | solution.py:70
  69.4 1.7 fusion.58
  71.2 3.1 %collective-permute-start.6 = (bf16[256,512]{1,0:T(8,128)(2,1)S(1)}, bf16[256,512]{1,0:T(8,128)(2,1)S(1)}, u32[]{:S(2)}, u32[]{:S(2)}) collective-permute-start(bf16[256,512]{1,0:T(8,128)(2,1)S(1)} %get-tuple-element.57), channel_id=1, source_target_pairs={{0,4},{2,6},{4,0},{6,2},{1,5},{3,7},{5,1},{7,3},{8,12},{10,14},{12... | collective-permute-start | bytes 786440 | tf_op jit(solution)/shard_map/ppermute | solution.py:70
  74.3 1.1 collective-permute-start.5
  75.4 0.9 collective-permute-start.4
  76.8 1.3 fusion.1
  78.1 3.0 %collective-permute-start.14 = (bf16[256,1024]{1,0:T(8,128)(2,1)}, bf16[256,1024]{1,0:T(8,128)(2,1)}, u32[]{:S(2)}, u32[]{:S(2)}) collective-permute-start(bf16[256,1024]{1,0:T(8,128)(2,1)} %fusion.1), channel_id=1, source_target_pairs={{192,0},{128,64},{193,1},{129,65},{194,2},{130,66},{195,3},{131,67... | collective-permute-start | bytes 1572872 | tf_op jit(solution)/shard_map/ppermute | solution.py:47
  81.1 0.8 collective-permute-done.6
  81.9 5.2 %collective-permute-done.5 = bf16[256,512]{1,0:T(8,128)(2,1)S(1)} collective-permute-done((bf16[256,512]{1,0:T(8,128)(2,1)S(1)}, bf16[256,512]{1,0:T(8,128)(2,1)S(1)}, u32[]{:S(2)}, u32[]{:S(2)}) %collective-permute-start.5) | collective-permute-done | bytes 262176 | tf_op jit(solution)/shard_map/ppermute | solution.py:70
  87.5 1.4 collective-permute-done.12
  89.4 2.2 %collective-permute-done.14 = bf16[256,1024]{1,0:T(8,128)(2,1)} collective-permute-done((bf16[256,1024]{1,0:T(8,128)(2,1)}, bf16[256,1024]{1,0:T(8,128)(2,1)}, u32[]{:S(2)}, u32[]{:S(2)}) %collective-permute-start.14) | collective-permute-done | bytes 524320 | tf_op jit(solution)/shard_map/ppermute | solution.py:47
  91.6 1.3 fusion.3
  92.9 5.2 %all-to-all-start.1 = ((bf16[16,16,1024]{2,1,0:T(8,128)(2,1)}), bf16[16,16,1024]{2,1,0:T(8,128)(2,1)S(1)}, u32[]{:S(2)}, u32[]{:S(2)}) async-start(bf16[16,16,1024]{2,1,0:T(8,128)(2,1)} %bitcast.15), calls=%async_computation.1 | async-start | bytes 1048576 | tf_op jit(solution)/shard_map/all_to_all | solution.py:79
  98.1 1.5 slice_bitcast_fusion
  99.6 1.3 collective-permute-start.24
  101.0 11.4 %all-to-all-done.1 = bf16[16,16,1024]{2,1,0:T(8,128)(2,1)S(1)} async-done(((bf16[16,16,1024]{2,1,0:T(8,128)(2,1)}), bf16[16,16,1024]{2,1,0:T(8,128)(2,1)S(1)}, u32[]{:S(2)}, u32[]{:S(2)}) %all-to-all-start.1) | async-done | bytes 524320 | tf_op jit(solution)/shard_map/all_to_all | solution.py:79
  112.5 0.9 broadcast_in_dim.22
  113.4 4.9 %all-to-all-start.2 = ((bf16[16,16,1024]{2,1,0:T(8,128)(2,1)}), bf16[16,16,1024]{2,1,0:T(8,128)(2,1)S(1)}, u32[]{:S(2)}, u32[]{:S(2)}) async-start(bf16[16,16,1024]{2,1,0:T(8,128)(2,1)} %broadcast_in_dim.22), calls=%async_computation.2 | async-start | bytes 1048576 | tf_op jit(solution)/shard_map/all_to_all | solution.py:90
  118.3 1.1 slice.63
  119.4 1.3 collective-permute-start.18
  120.7 1.3 broadcast_select_fusion.2
  122.0 1.1 pad_maximum_fusion
  123.1 6.1 %collective-permute-done.24 = bf16[512,1024]{1,0:T(8,128)(2,1)} collective-permute-done((bf16[512,1024]{1,0:T(8,128)(2,1)}, bf16[512,1024]{1,0:T(8,128)(2,1)}, u32[]{:S(2)}, u32[]{:S(2)}) %collective-permute-start.24) | collective-permute-done | bytes 1048608 | tf_op jit(solution)/shard_map/ppermute | solution.py:43
  129.2 1.3 collective-permute-start.25
  130.4 3.8 %broadcast_select_fusion = bf16[1024,1024]{1,0:T(8,128)(2,1)} fusion(bf16[1024,1024]{1,0:T(8,128)(2,1)} %collective-permute-done.15, pred[]{:T(512)S(6)} %eq.8, bf16[1,1024,1024]{2,1,0:T(8,128)(2,1)} %param.7), kind=kLoop, calls=%fused_computation.1 | loop fusion | flops 1048576 | bytes 6291457 | tf_op jit(solution)/shard_map/jit(_where)/select_n | solution.py:116
  134.2 6.3 %collective-permute-start.23 = (bf16[256,1024]{1,0:T(8,128)(2,1)S(1)}, bf16[256,1024]{1,0:T(8,128)(2,1)S(1)}, u32[]{:S(2)}, u32[]{:S(2)}) collective-permute-start(bf16[256,1024]{1,0:T(8,128)(2,1)S(1)} %bitcast.81), channel_id=1, source_target_pairs={{192,0},{128,64},{193,1},{129,65},{194,2},{130,66},{195,3},{131,67... | collective-permute-start | bytes 1572872 | tf_op jit(solution)/shard_map/ppermute | solution.py:47
  140.5 1.7 convolution_convert_fusion.4
  142.3 1.1 broadcast_select_fusion.4
  144.4 2.3 %collective-permute-start.22 = (bf16[256,512]{1,0:T(8,128)(2,1)S(1)}, bf16[256,512]{1,0:T(8,128)(2,1)S(1)}, u32[]{:S(2)}, u32[]{:S(2)}) collective-permute-start(bf16[256,512]{1,0:T(8,128)(2,1)S(1)} %get-tuple-element.59), channel_id=1, source_target_pairs={{0,4},{2,6},{4,0},{6,2},{1,5},{3,7},{5,1},{7,3},{8,12},{10,14},{12... | collective-permute-start | bytes 786440 | tf_op jit(solution)/shard_map/ppermute | solution.py:70
  146.6 1.1 collective-permute-start.21
  147.8 0.9 collective-permute-start.20
  148.7 2.6 %convolution_convert_fusion.1 = bf16[1024,1024]{1,0:T(8,128)(2,1)} fusion(bf16[512,1024]{1,0:T(8,128)(2,1)S(1)} %copy-done.14, bf16[256,1024]{1,0:T(8,128)(2,1)S(1)} %broadcast_select_fusion.3, bf16[256,1024]{1,0:T(8,128)(2,1)S(1)} %broadcast_select_fusion.4), kind=kOutput, calls=%fused_computation.3 | convolution fusion | flops 1076887552 | bytes 4194304 | tf_op jit(solution)/shard_map/dot_general | solution.py:26
  151.4 3.8 %collective-permute-done.22 = bf16[256,512]{1,0:T(8,128)(2,1)S(1)} collective-permute-done((bf16[256,512]{1,0:T(8,128)(2,1)S(1)}, bf16[256,512]{1,0:T(8,128)(2,1)S(1)}, u32[]{:S(2)}, u32[]{:S(2)}) %collective-permute-start.22) | collective-permute-done | bytes 262176 | tf_op jit(solution)/shard_map/ppermute | solution.py:70
  155.1 4.9 %collective-permute-done.21 = bf16[256,512]{1,0:T(8,128)(2,1)S(1)} collective-permute-done((bf16[256,512]{1,0:T(8,128)(2,1)S(1)}, bf16[256,512]{1,0:T(8,128)(2,1)S(1)}, u32[]{:S(2)}, u32[]{:S(2)}) %collective-permute-start.21) | collective-permute-done | bytes 262176 | tf_op jit(solution)/shard_map/ppermute | solution.py:70
  160.2 1.1 multiply_convert_fusion.1
  161.4 2.0 %collective-permute-start.27 = (bf16[256,512]{1,0:T(8,128)(2,1)S(1)}, bf16[256,512]{1,0:T(8,128)(2,1)}, u32[]{:S(2)}, u32[]{:S(2)}) collective-permute-start(bf16[256,512]{1,0:T(8,128)(2,1)S(1)} %multiply_convert_fusion.1), channel_id=1, source_target_pairs={{192,0},{128,64},{193,1},{129,65},{194,2},{130,66},{195,3},{131,67... | collective-permute-start | bytes 786440 | tf_op jit(solution)/shard_map/ppermute | solution.py:47
  163.4 2.5 %maximum_select_fusion = bf16[1024,1024]{1,0:T(8,128)(2,1)S(1)} fusion(bf16[512,1024]{1,0:T(8,128)(2,1)} %collective-permute-done.25, bf16[512,1024]{1,0:T(8,128)(2,1)} %collective-permute-done.24, bf16[1,1024,1024]{2,1,0:T(8,128)(2,1)S(1)} %copy-done, pred[]{:T(512)S(6)} %eq.8), kind=kLoop, calls=%fused_computation | loop fusion | flops 5242880 | bytes 6291457 | tf_op jit(solution)/shard_map/jit(_where)/select_n | solution.py:116
  167.2 1.3 fusion.2
  168.5 8.3 %all-to-all-start.3 = ((bf16[16,16,1024]{2,1,0:T(8,128)(2,1)}), bf16[16,16,1024]{2,1,0:T(8,128)(2,1)S(1)}, u32[]{:S(2)}, u32[]{:S(2)}) async-start(bf16[16,16,1024]{2,1,0:T(8,128)(2,1)} %bitcast.21), calls=%async_computation.3 | async-start | bytes 1048576 | tf_op jit(solution)/shard_map/all_to_all | solution.py:79
  177.0 1.6 collective-permute-done.28
  178.7 2.6 %convolution_convert_fusion = bf16[1024,1024]{1,0:T(8,128)(2,1)} fusion(bf16[256,1024]{1,0:T(8,128)(2,1)S(1)} %bitcast.94, bf16[256,1024]{1,0:T(8,128)(2,1)S(1)} %bitcast.91, bf16[256,512]{1,0:T(8,128)(2,1)S(1)} %get-tuple-element.46, bf16[256,512]{1,0:T(8,128)(2,1)S(1)} %get-tuple-element.45, bf16[256,512]{1,0:T(8,128)(2,1)S(1)} %get-tuple-element.44, ...), kind=kOutput, calls=%fused_computation.2 | convolution fusion | flops 1081081856 | bytes 4194304 | tf_op jit(solution)/shard_map/dot_general | solution.py:26
  181.3 11.4 %all-to-all-done.3 = bf16[16,16,1024]{2,1,0:T(8,128)(2,1)S(1)} async-done(((bf16[16,16,1024]{2,1,0:T(8,128)(2,1)}), bf16[16,16,1024]{2,1,0:T(8,128)(2,1)S(1)}, u32[]{:S(2)}, u32[]{:S(2)}) %all-to-all-start.3) | async-done | bytes 524320 | tf_op jit(solution)/shard_map/all_to_all | solution.py:79
  193.0 5.4 %collective-permute-done.29 = bf16[16,1024]{1,0:T(8,128)(2,1)S(1)} collective-permute-done((bf16[16,1024]{1,0:T(8,128)(2,1)S(1)}, bf16[16,1024]{1,0:T(8,128)(2,1)S(1)}, u32[]{:S(2)}, u32[]{:S(2)}) %collective-permute-start.29) | collective-permute-done | bytes 32800 | tf_op jit(solution)/shard_map/ppermute | solution.py:184
  (97 shorter events, 8.1 us)
Async XLA Ops:
  2.6 11.0 %copy-start = (bf16[1,1024,1024]{2,1,0:T(8,128)(2,1)S(1)}, bf16[1,1024,1024]{2,1,0:T(8,128)(2,1)}, u32[]{:S(2)}) copy-start(bf16[1,1024,1024]{2,1,0:T(8,128)(2,1)} %param.6) | copy-start | bytes 6291460
  2.6 35.9 %all-to-all-start = ((bf16[16,32,1024]{2,1,0:T(8,128)(2,1)}), bf16[16,32,1024]{2,1,0:T(8,128)(2,1)}, u32[]{:S(2)}, u32[]{:S(2)}) async-start(bf16[16,32,1024]{2,1,0:T(8,128)(2,1)} %broadcast_in_dim.10), calls=%async_computation | async-start | bytes 2097152 | tf_op jit(solution)/shard_map/all_to_all | solution.py:90
  13.5 1.8 copy-start.7
  13.5 1.8 copy-start.10
  15.3 2.3 %collective-permute-start = (bf16[512,512]{1,0:T(8,128)(2,1)}, bf16[512,512]{1,0:T(8,128)(2,1)}, u32[]{:S(2)}, u32[]{:S(2)}) collective-permute-start(bf16[512,512]{1,0:T(8,128)(2,1)} %pad_maximum_fusion.1), channel_id=1, source_target_pairs={{0,1},{1,0},{2,3},{3,2},{4,5},{5,4},{6,7},{7,6},{8,9},{9,8},{10,11... | collective-permute-start | bytes 1572872 | tf_op jit(solution)/shard_map/ppermute | solution.py:39
  15.3 1.6 copy-start.8
  17.3 21.2 %copy-start.5 = (f32[256,512]{1,0:T(8,128)}, f32[256,512]{1,0:T(8,128)S(1)}, u32[]{:S(2)}) copy-start(f32[256,512]{1,0:T(8,128)S(1)} %convolution_bitcast_fusion.1) | copy-start | bytes 1572868
  18.7 1.6 copy-start.21
  18.8 15.7 %collective-permute-start.1 = (bf16[512,512]{1,0:T(8,128)(2,1)S(1)}, bf16[512,512]{1,0:T(8,128)(2,1)}, u32[]{:S(2)}, u32[]{:S(2)}) collective-permute-start(bf16[512,512]{1,0:T(8,128)(2,1)S(1)} %fusion.57), channel_id=1, source_target_pairs={{0,2},{2,4},{4,6},{6,0},{1,3},{3,5},{5,7},{7,1},{8,10},{10,12},{12... | collective-permute-start | bytes 1572872 | tf_op jit(solution)/shard_map/ppermute | solution.py:70
  20.3 14.1 %collective-permute-start.2 = (bf16[512,512]{1,0:T(8,128)(2,1)S(1)}, bf16[512,512]{1,0:T(8,128)(2,1)}, u32[]{:S(2)}, u32[]{:S(2)}) collective-permute-start(bf16[512,512]{1,0:T(8,128)(2,1)S(1)} %fusion.57), channel_id=1, source_target_pairs={{0,6},{2,0},{4,2},{6,4},{1,7},{3,1},{5,3},{7,5},{8,14},{10,8},{12,... | collective-permute-start | bytes 1572872 | tf_op jit(solution)/shard_map/ppermute | solution.py:70
  38.5 3.4 %copy-start.22 = (bf16[512,512]{1,0:T(8,128)(2,1)S(1)}, bf16[512,512]{1,0:T(8,128)(2,1)}, u32[]{:S(2)}) copy-start(bf16[512,512]{1,0:T(8,128)(2,1)} %copy-done.21) | copy-start | bytes 1572868
  39.8 10.1 %copy-start.2 = (bf16[16,1,16,1024]{3,2,1,0:T(8,128)(2,1)}, bf16[16,1,16,1024]{3,2,1,0:T(8,128)(2,1)S(1)}, u32[]{:S(2)}) copy-start(bf16[16,1,16,1024]{3,2,1,0:T(8,128)(2,1)S(1)} %get-tuple-element.50) | copy-start | bytes 1572868
  41.7 6.5 %collective-permute-start.8 = (bf16[256,512]{1,0:T(8,128)(2,1)S(1)}, bf16[256,512]{1,0:T(8,128)(2,1)S(1)}, u32[]{:S(2)}, u32[]{:S(2)}) collective-permute-start(bf16[256,512]{1,0:T(8,128)(2,1)S(1)} %convolution_convert_fusion.5), channel_id=1, source_target_pairs={{0,1},{1,0},{2,3},{3,2},{4,5},{5,4},{6,7},{7,6},{8,9},{9,8},{10,11... | collective-permute-start | bytes 786440 | tf_op jit(solution)/shard_map/ppermute | solution.py:39
  41.9 16.3 %collective-permute-start.7 = (bf16[512,512]{1,0:T(8,128)(2,1)S(1)}, bf16[512,512]{1,0:T(8,128)(2,1)S(1)}, u32[]{:S(2)}, u32[]{:S(2)}) collective-permute-start(bf16[512,512]{1,0:T(8,128)(2,1)S(1)} %copy-done.22), channel_id=1, source_target_pairs={{0,4},{2,6},{4,0},{6,2},{1,5},{3,7},{5,1},{7,3},{8,12},{10,14},{12... | collective-permute-start | bytes 1572872 | tf_op jit(solution)/shard_map/ppermute | solution.py:70
  45.0 54.7 %collective-permute-start.15 = (bf16[1024,1024]{1,0:T(8,128)(2,1)}, bf16[1024,1024]{1,0:T(8,128)(2,1)}, u32[]{:S(2)}, u32[]{:S(2)}) collective-permute-start(bf16[1024,1024]{1,0:T(8,128)(2,1)} %bitcast.16), channel_id=1, source_target_pairs={{0,192},{64,128},{1,193},{65,129},{2,194},{66,130},{3,195},{67,131... | collective-permute-start | bytes 6291464 | tf_op jit(solution)/shard_map/ppermute | solution.py:43
  46.2 13.5 %copy-start.6 = (f32[256,512]{1,0:T(8,128)S(1)}, f32[256,512]{1,0:T(8,128)}, u32[]{:S(2)}) copy-start(f32[256,512]{1,0:T(8,128)} %copy-done.5) | copy-start | bytes 1572868
  48.0 21.4 %collective-permute-start.3 = (bf16[256,512]{1,0:T(8,128)(2,1)S(1)}, bf16[256,512]{1,0:T(8,128)(2,1)S(1)}, u32[]{:S(2)}, u32[]{:S(2)}) collective-permute-start(bf16[256,512]{1,0:T(8,128)(2,1)S(1)} %convolution_convert_fusion.6), channel_id=1, source_target_pairs={{0,1},{1,0},{2,3},{3,2},{4,5},{5,4},{6,7},{7,6},{8,9},{9,8},{10,11... | collective-permute-start | bytes 786440 | tf_op jit(solution)/shard_map/ppermute | solution.py:39
  50.0 13.8 %collective-permute-start.11 = (bf16[256,512]{1,0:T(8,128)(2,1)S(1)}, bf16[256,512]{1,0:T(8,128)(2,1)S(1)}, u32[]{:S(2)}, u32[]{:S(2)}) collective-permute-start(bf16[256,512]{1,0:T(8,128)(2,1)S(1)} %get-tuple-element.55), channel_id=1, source_target_pairs={{0,4},{2,6},{4,0},{6,2},{1,5},{3,7},{5,1},{7,3},{8,12},{10,14},{12... | collective-permute-start | bytes 786440 | tf_op jit(solution)/shard_map/ppermute | solution.py:70
  50.6 18.5 %collective-permute-start.10 = (bf16[256,512]{1,0:T(8,128)(2,1)S(1)}, bf16[256,512]{1,0:T(8,128)(2,1)S(1)}, u32[]{:S(2)}, u32[]{:S(2)}) collective-permute-start(bf16[256,512]{1,0:T(8,128)(2,1)S(1)} %get-tuple-element.55), channel_id=1, source_target_pairs={{0,6},{2,0},{4,2},{6,4},{1,7},{3,1},{5,3},{7,5},{8,14},{10,8},{12,... | collective-permute-start | bytes 786440 | tf_op jit(solution)/shard_map/ppermute | solution.py:70
  58.2 10.9 %collective-permute-start.9 = (bf16[256,512]{1,0:T(8,128)(2,1)S(1)}, bf16[256,512]{1,0:T(8,128)(2,1)S(1)}, u32[]{:S(2)}, u32[]{:S(2)}) collective-permute-start(bf16[256,512]{1,0:T(8,128)(2,1)S(1)} %get-tuple-element.55), channel_id=1, source_target_pairs={{0,2},{2,4},{4,6},{6,0},{1,3},{3,5},{5,7},{7,1},{8,10},{10,12},{12... | collective-permute-start | bytes 786440 | tf_op jit(solution)/shard_map/ppermute | solution.py:70
  62.9 8.3 %copy-start.3 = (f32[512,512]{1,0:T(8,128)}, f32[512,512]{1,0:T(8,128)S(1)}, u32[]{:S(2)}) copy-start(f32[512,512]{1,0:T(8,128)S(1)} %get-tuple-element.40) | copy-start | bytes 3145732
  69.3 7.5 %copy-start.12 = (bf16[256,512]{1,0:T(8,128)(2,1)}, bf16[256,512]{1,0:T(8,128)(2,1)S(1)}, u32[]{:S(2)}) copy-start(bf16[256,512]{1,0:T(8,128)(2,1)S(1)} %get-tuple-element.52) | copy-start | bytes 786436
  69.3 6.9 %collective-permute-start.13 = (bf16[256,512]{1,0:T(8,128)(2,1)S(1)}, bf16[256,512]{1,0:T(8,128)(2,1)S(1)}, u32[]{:S(2)}, u32[]{:S(2)}) collective-permute-start(bf16[256,512]{1,0:T(8,128)(2,1)S(1)} %get-tuple-element.52), channel_id=1, source_target_pairs={{0,1},{1,0},{2,3},{3,2},{4,5},{5,4},{6,7},{7,6},{8,9},{9,8},{10,11... | collective-permute-start | bytes 786440 | tf_op jit(solution)/shard_map/ppermute | solution.py:39
  71.2 10.7 %collective-permute-start.6 = (bf16[256,512]{1,0:T(8,128)(2,1)S(1)}, bf16[256,512]{1,0:T(8,128)(2,1)S(1)}, u32[]{:S(2)}, u32[]{:S(2)}) collective-permute-start(bf16[256,512]{1,0:T(8,128)(2,1)S(1)} %get-tuple-element.57), channel_id=1, source_target_pairs={{0,4},{2,6},{4,0},{6,2},{1,5},{3,7},{5,1},{7,3},{8,12},{10,14},{12... | collective-permute-start | bytes 786440 | tf_op jit(solution)/shard_map/ppermute | solution.py:70
  74.3 12.8 %collective-permute-start.5 = (bf16[256,512]{1,0:T(8,128)(2,1)S(1)}, bf16[256,512]{1,0:T(8,128)(2,1)S(1)}, u32[]{:S(2)}, u32[]{:S(2)}) collective-permute-start(bf16[256,512]{1,0:T(8,128)(2,1)S(1)} %get-tuple-element.57), channel_id=1, source_target_pairs={{0,6},{2,0},{4,2},{6,4},{1,7},{3,1},{5,3},{7,5},{8,14},{10,8},{12,... | collective-permute-start | bytes 786440 | tf_op jit(solution)/shard_map/ppermute | solution.py:70
  75.4 11.7 %collective-permute-start.4 = (bf16[256,512]{1,0:T(8,128)(2,1)S(1)}, bf16[256,512]{1,0:T(8,128)(2,1)S(1)}, u32[]{:S(2)}, u32[]{:S(2)}) collective-permute-start(bf16[256,512]{1,0:T(8,128)(2,1)S(1)} %get-tuple-element.57), channel_id=1, source_target_pairs={{0,2},{2,4},{4,6},{6,0},{1,3},{3,5},{5,7},{7,1},{8,10},{10,12},{12... | collective-permute-start | bytes 786440 | tf_op jit(solution)/shard_map/ppermute | solution.py:70
  76.3 1.8 copy-start.15
  78.1 13.5 %collective-permute-start.14 = (bf16[256,1024]{1,0:T(8,128)(2,1)}, bf16[256,1024]{1,0:T(8,128)(2,1)}, u32[]{:S(2)}, u32[]{:S(2)}) collective-permute-start(bf16[256,1024]{1,0:T(8,128)(2,1)} %fusion.1), channel_id=1, source_target_pairs={{192,0},{128,64},{193,1},{129,65},{194,2},{130,66},{195,3},{131,67... | collective-permute-start | bytes 1572872 | tf_op jit(solution)/shard_map/ppermute | solution.py:47
  87.3 1.6 collective-permute-start.12
  89.0 3.9 %copy-start.17 = (bf16[256,512]{1,0:T(8,128)(2,1)}, bf16[256,512]{1,0:T(8,128)(2,1)S(1)}, u32[]{:S(2)}) copy-start(bf16[256,512]{1,0:T(8,128)(2,1)S(1)} %collective-permute-done.12) | copy-start | bytes 786436
  92.9 19.5 %all-to-all-start.1 = ((bf16[16,16,1024]{2,1,0:T(8,128)(2,1)}), bf16[16,16,1024]{2,1,0:T(8,128)(2,1)S(1)}, u32[]{:S(2)}, u32[]{:S(2)}) async-start(bf16[16,16,1024]{2,1,0:T(8,128)(2,1)} %bitcast.15), calls=%async_computation.1 | async-start | bytes 1048576 | tf_op jit(solution)/shard_map/all_to_all | solution.py:79
  98.1 14.4 %copy-start.23 = (bf16[32,1024]{1,0:T(8,128)(2,1)S(1)}, bf16[32,1024]{1,0:T(8,128)(2,1)}, u32[]{:S(2)}) copy-start(bf16[32,1024]{1,0:T(8,128)(2,1)} %param.5) | copy-start | bytes 196612
  99.6 29.5 %collective-permute-start.24 = (bf16[512,1024]{1,0:T(8,128)(2,1)}, bf16[512,1024]{1,0:T(8,128)(2,1)}, u32[]{:S(2)}, u32[]{:S(2)}) collective-permute-start(bf16[512,1024]{1,0:T(8,128)(2,1)} %get-tuple-element.29), channel_id=1, source_target_pairs={{0,192},{64,128},{1,193},{65,129},{2,194},{66,130},{3,195},{67,131... | collective-permute-start | bytes 3145736 | tf_op jit(solution)/shard_map/ppermute | solution.py:43
  100.9 19.8 %collective-permute-start.17 = (bf16[512,512]{1,0:T(8,128)(2,1)}, bf16[512,512]{1,0:T(8,128)(2,1)}, u32[]{:S(2)}, u32[]{:S(2)}) collective-permute-start(bf16[512,512]{1,0:T(8,128)(2,1)} %get-tuple-element.39), channel_id=1, source_target_pairs={{0,1},{1,0},{2,3},{3,2},{4,5},{5,4},{6,7},{7,6},{8,9},{9,8},{10,11... | collective-permute-start | bytes 1572872 | tf_op jit(solution)/shard_map/ppermute | solution.py:39
  113.4 20.8 %all-to-all-start.2 = ((bf16[16,16,1024]{2,1,0:T(8,128)(2,1)}), bf16[16,16,1024]{2,1,0:T(8,128)(2,1)S(1)}, u32[]{:S(2)}, u32[]{:S(2)}) async-start(bf16[16,16,1024]{2,1,0:T(8,128)(2,1)} %broadcast_in_dim.22), calls=%async_computation.2 | async-start | bytes 1048576 | tf_op jit(solution)/shard_map/all_to_all | solution.py:90
  119.4 14.8 %collective-permute-start.18 = (bf16[256,512]{1,0:T(8,128)(2,1)S(1)}, bf16[256,512]{1,0:T(8,128)(2,1)}, u32[]{:S(2)}, u32[]{:S(2)}) collective-permute-start(bf16[256,512]{1,0:T(8,128)(2,1)S(1)} %slice.63), channel_id=1, source_target_pairs={{0,192},{64,128},{1,193},{65,129},{2,194},{66,130},{3,195},{67,131... | collective-permute-start | bytes 786440 | tf_op jit(solution)/shard_map/ppermute | solution.py:43
  129.2 31.0 %collective-permute-start.25 = (bf16[512,1024]{1,0:T(8,128)(2,1)}, bf16[512,1024]{1,0:T(8,128)(2,1)}, u32[]{:S(2)}, u32[]{:S(2)}) collective-permute-start(bf16[512,1024]{1,0:T(8,128)(2,1)} %get-tuple-element.30), channel_id=1, source_target_pairs={{0,192},{64,128},{1,193},{65,129},{2,194},{66,130},{3,195},{67,131... | collective-permute-start | bytes 3145736 | tf_op jit(solution)/shard_map/ppermute | solution.py:43
  134.2 9.6 %copy-start.1 = (bf16[1024,1024]{1,0:T(8,128)(2,1)S(1)}, bf16[1024,1024]{1,0:T(8,128)(2,1)}, u32[]{:S(2)}) copy-start(bf16[1024,1024]{1,0:T(8,128)(2,1)} %broadcast_select_fusion) | copy-start | bytes 6291460
  134.2 14.4 %collective-permute-start.23 = (bf16[256,1024]{1,0:T(8,128)(2,1)S(1)}, bf16[256,1024]{1,0:T(8,128)(2,1)S(1)}, u32[]{:S(2)}, u32[]{:S(2)}) collective-permute-start(bf16[256,1024]{1,0:T(8,128)(2,1)S(1)} %bitcast.81), channel_id=1, source_target_pairs={{192,0},{128,64},{193,1},{129,65},{194,2},{130,66},{195,3},{131,67... | collective-permute-start | bytes 1572872 | tf_op jit(solution)/shard_map/ppermute | solution.py:47
  142.2 1.6 collective-permute-start.19
  143.4 5.3 %copy-start.14 = (bf16[512,1024]{1,0:T(8,128)(2,1)S(1)}, bf16[512,1024]{1,0:T(8,128)(2,1)}, u32[]{:S(2)}) copy-start(bf16[512,1024]{1,0:T(8,128)(2,1)} %pad_maximum_fusion) | copy-start | bytes 3145732
  144.4 10.8 %collective-permute-start.22 = (bf16[256,512]{1,0:T(8,128)(2,1)S(1)}, bf16[256,512]{1,0:T(8,128)(2,1)S(1)}, u32[]{:S(2)}, u32[]{:S(2)}) collective-permute-start(bf16[256,512]{1,0:T(8,128)(2,1)S(1)} %get-tuple-element.59), channel_id=1, source_target_pairs={{0,4},{2,6},{4,0},{6,2},{1,5},{3,7},{5,1},{7,3},{8,12},{10,14},{12... | collective-permute-start | bytes 786440 | tf_op jit(solution)/shard_map/ppermute | solution.py:70
  146.6 13.4 %collective-permute-start.21 = (bf16[256,512]{1,0:T(8,128)(2,1)S(1)}, bf16[256,512]{1,0:T(8,128)(2,1)S(1)}, u32[]{:S(2)}, u32[]{:S(2)}) collective-permute-start(bf16[256,512]{1,0:T(8,128)(2,1)S(1)} %get-tuple-element.59), channel_id=1, source_target_pairs={{0,6},{2,0},{4,2},{6,4},{1,7},{3,1},{5,3},{7,5},{8,14},{10,8},{12,... | collective-permute-start | bytes 786440 | tf_op jit(solution)/shard_map/ppermute | solution.py:70
  147.8 12.3 %collective-permute-start.20 = (bf16[256,512]{1,0:T(8,128)(2,1)S(1)}, bf16[256,512]{1,0:T(8,128)(2,1)S(1)}, u32[]{:S(2)}, u32[]{:S(2)}) collective-permute-start(bf16[256,512]{1,0:T(8,128)(2,1)S(1)} %get-tuple-element.59), channel_id=1, source_target_pairs={{0,2},{2,4},{4,6},{6,0},{1,3},{3,5},{5,7},{7,1},{8,10},{10,12},{12... | collective-permute-start | bytes 786440 | tf_op jit(solution)/shard_map/ppermute | solution.py:70
  151.4 8.8 %copy-start.4 = (f32[512,512]{1,0:T(8,128)S(1)}, f32[512,512]{1,0:T(8,128)}, u32[]{:S(2)}) copy-start(f32[512,512]{1,0:T(8,128)} %copy-done.3) | copy-start | bytes 3145732
  161.3 4.6 %collective-permute-start.26 = (bf16[256,512]{1,0:T(8,128)(2,1)S(1)}, bf16[256,512]{1,0:T(8,128)(2,1)S(1)}, u32[]{:S(2)}, u32[]{:S(2)}) collective-permute-start(bf16[256,512]{1,0:T(8,128)(2,1)S(1)} %multiply_convert_fusion.1), channel_id=1, source_target_pairs={{0,1},{1,0},{2,3},{3,2},{4,5},{5,4},{6,7},{7,6},{8,9},{9,8},{10,11... | collective-permute-start | bytes 786440 | tf_op jit(solution)/shard_map/ppermute | solution.py:39
  161.4 15.4 %collective-permute-start.27 = (bf16[256,512]{1,0:T(8,128)(2,1)S(1)}, bf16[256,512]{1,0:T(8,128)(2,1)}, u32[]{:S(2)}, u32[]{:S(2)}) collective-permute-start(bf16[256,512]{1,0:T(8,128)(2,1)S(1)} %multiply_convert_fusion.1), channel_id=1, source_target_pairs={{192,0},{128,64},{193,1},{129,65},{194,2},{130,66},{195,3},{131,67... | collective-permute-start | bytes 786440 | tf_op jit(solution)/shard_map/ppermute | solution.py:47
  165.9 0.7 copy-start.19
  167.1 9.7 %copy-start.13 = (bf16[256,512]{1,0:T(8,128)(2,1)S(1)}, bf16[256,512]{1,0:T(8,128)(2,1)}, u32[]{:S(2)}) copy-start(bf16[256,512]{1,0:T(8,128)(2,1)} %copy-done.12) | copy-start | bytes 786436
  167.1 9.7 %copy-start.16 = (bf16[256,512]{1,0:T(8,128)(2,1)S(1)}, bf16[256,512]{1,0:T(8,128)(2,1)}, u32[]{:S(2)}) copy-start(bf16[256,512]{1,0:T(8,128)(2,1)} %copy-done.15) | copy-start | bytes 786436
  167.1 9.7 %copy-start.20 = (bf16[256,512]{1,0:T(8,128)(2,1)S(1)}, bf16[256,512]{1,0:T(8,128)(2,1)}, u32[]{:S(2)}) copy-start(bf16[256,512]{1,0:T(8,128)(2,1)} %copy-done.19) | copy-start | bytes 786436
  167.2 11.4 %copy-start.18 = (bf16[256,512]{1,0:T(8,128)(2,1)S(1)}, bf16[256,512]{1,0:T(8,128)(2,1)}, u32[]{:S(2)}) copy-start(bf16[256,512]{1,0:T(8,128)(2,1)} %copy-done.17) | copy-start | bytes 786436
  168.5 10.2 %copy-start.9 = (bf16[16,1,16,1024]{3,2,1,0:T(8,128)(2,1)S(1)}, bf16[16,1,16,1024]{3,2,1,0:T(8,128)(2,1)}, u32[]{:S(2)}) copy-start(bf16[16,1,16,1024]{3,2,1,0:T(8,128)(2,1)} %copy-done.7) | copy-start | bytes 1572868
  168.5 10.2 %copy-start.11 = (bf16[16,1,16,1024]{3,2,1,0:T(8,128)(2,1)S(1)}, bf16[16,1,16,1024]{3,2,1,0:T(8,128)(2,1)}, u32[]{:S(2)}) copy-start(bf16[16,1,16,1024]{3,2,1,0:T(8,128)(2,1)} %copy-done.10) | copy-start | bytes 1572868
  168.5 24.3 %all-to-all-start.3 = ((bf16[16,16,1024]{2,1,0:T(8,128)(2,1)}), bf16[16,16,1024]{2,1,0:T(8,128)(2,1)S(1)}, u32[]{:S(2)}, u32[]{:S(2)}) async-start(bf16[16,16,1024]{2,1,0:T(8,128)(2,1)} %bitcast.21), calls=%async_computation.3 | async-start | bytes 1048576 | tf_op jit(solution)/shard_map/all_to_all | solution.py:79
  176.7 16.1 %collective-permute-start.16 = (bf16[16,1024]{1,0:T(8,128)(2,1)S(1)}, bf16[16,1024]{1,0:T(8,128)(2,1)S(1)}, u32[]{:S(2)}, u32[]{:S(2)}) collective-permute-start(bf16[16,1024]{1,0:T(8,128)(2,1)S(1)} %add_convert_fusion.1), channel_id=1, source_target_pairs={{0,128},{128,0},{1,129},{129,1},{2,130},{130,2},{3,131},{131,3},{4... | collective-permute-start | bytes 98312 | tf_op jit(solution)/shard_map/ppermute | solution.py:183
  176.8 1.8 collective-permute-start.28
  192.9 5.5 %collective-permute-start.29 = (bf16[16,1024]{1,0:T(8,128)(2,1)S(1)}, bf16[16,1024]{1,0:T(8,128)(2,1)S(1)}, u32[]{:S(2)}, u32[]{:S(2)}) collective-permute-start(bf16[16,1024]{1,0:T(8,128)(2,1)S(1)} %get-tuple-element.38), channel_id=1, source_target_pairs={{0,128},{128,0},{1,129},{129,1},{2,130},{130,2},{3,131},{131,3},{4... | collective-permute-start | bytes 98312 | tf_op jit(solution)/shard_map/ppermute | solution.py:184

commit v11 on v10

--- a/solution.py
+++ b/solution.py
@@ -63,11 +63,41 @@
     )
 
 
+def pair_sum(mine, theirs):
+    return mine + other_core(theirs.astype(jnp.bfloat16)).astype(jnp.float32)
+
+
+def step_x(block, distance):
+    return lax.ppermute(block, "x", [(i, (i + distance) % X) for i in range(X)])
+
+
 def narrow_terms(mine, theirs):
-    pair = mine + other_core(theirs.astype(jnp.bfloat16)).astype(jnp.float32)
+    pair = pair_sum(mine, theirs)
     sent = pair.astype(jnp.bfloat16)
-    routes = [[(i, (i + distance) % X) for i in range(X)] for distance in (1, 3, 2)]
-    return [pair] + [lax.ppermute(sent, "x", route) for route in routes]
+    return [pair] + [step_x(sent, distance) for distance in (1, 3, 2)]
+
+
+def spread_x(partial):
+    rows, cols = partial.shape
+    x = lax.axis_index("x")
+    blocks = partial.reshape(X, rows // X, cols)
+    total = lax.dynamic_index_in_dim(blocks, x, 0, keepdims=False)
+    sent = blocks.astype(jnp.bfloat16)
+    for distance in (1, 3, 2):
+        block = lax.dynamic_index_in_dim(sent, lax.rem(x + distance, X), 0, keepdims=False)
+        total = total + step_x(block, distance).astype(jnp.float32)
+    return total
+
+
+def gather_x(block):
+    rows, cols = block.shape
+    found = [block] + [step_x(block, distance) for distance in (1, 2, 3)]
+    source = lax.broadcasted_iota(jnp.int32, (X, 1, 1), 0)
+    passed = lax.rem(lax.axis_index("x") - source + X, X)
+    placed = found[0][None]
+    for distance in (1, 2, 3):
+        placed = jnp.where(passed == distance, found[distance][None], placed)
+    return placed.reshape(X * rows, cols)
 
 
 def add_terms(terms):
@@ -129,11 +159,10 @@
 
     theirs = jnp.concatenate([contract(rows, up_halves[1], 1, 0) for rows in saved], axis=0)
     mine = jnp.concatenate([contract(rows, up_halves[0], 1, 0) for rows in saved], axis=0)
-    pre = narrow_terms(mine, theirs)
-    gathered, pre[1], pre[2] = together(gather_wide(upstream), pre[1], pre[2])
-    act, slopes = gelu_parts(add_terms(pre))
+    act, slopes = gelu_parts(spread_x(pair_sum(mine, theirs)))
     act = act.astype(jnp.bfloat16)
-    hidden = in_order(act, other_core(act))
+    slopes = gather_x(slopes.astype(jnp.bfloat16))
+    gathered, act, slopes = together(gather_wide(upstream), act, slopes)
 
     top = by_part(gathered)
     top_slope = slope_of(back_total(top[0], down_halves), slopes[first])
@@ -144,6 +173,7 @@
     half = w_up.shape[0] // 2
     sent_up = [to_upper(together(w_up[:half], sent_down)[0])]
     sent_up.append(to_upper(together(w_up[half:], sent_up[0])[0]))
+    partial, act = together(partial, act)
     blocks, sent_down = together(spread_wide(partial), sent_down)
     part = upstream.shape[0] // 2
     middle = (
@@ -151,11 +181,13 @@
     ).astype(jnp.bfloat16)
 
     low_down = pick(sent_down, w_down)
-    lower_slopes = to_upper(slopes[last].astype(jnp.bfloat16))
+    lower_slopes = to_upper(slopes[last])
+    hidden = gather_x(act)
+    hidden = in_order(hidden, other_core(hidden))
     low, hidden, low_down, lower_slopes = together(
         gather_wide(middle), hidden, low_down, lower_slopes
     )
-    lower_slopes = pick(lower_slopes.astype(jnp.float32), slopes[first])
+    lower_slopes = pick(lower_slopes, slopes[first])
     low_rest = to_lower(low)
     low_total = back_total(low, halves(low_down, 0))
     incoming = jnp.concatenate([pick(top[0], low), pick(top[1], low_rest)], axis=0)

time: 200 us -> 202 us (1.010)
  starting transfers between devices: 66.5 us -> 75.4 us
  waiting for transfers between devices: 82 us -> 76.9 us
    all_to_all x2, waiting for transfers between devices: 22.8 us -> 11.7 us  [spread_wide(): lax.all_to_all(partial.reshape(WIDE, rows // WIDE, cols), WIDE_AXES, 0, 0...]
    ppermute x12 -> x18, starting transfers between devices: 21 us -> 27.6 us  [step_x(): return lax.ppermute(block, 'x', [(i, (i + distance) % X) for i in range(X)])]
    ppermute x4, waiting for transfers between devices: 6.07 us -> 10.8 us  [to_upper(): return lax.ppermute(block, CROSS_AXES, [(0, 3), (1, 2)])]
    all_to_all x2, starting transfers between devices: 14.5 us -> 17.6 us  [gather_wide(): lax.all_to_all(jnp.broadcast_to(block[None], (WIDE, rows, cols)), WIDE_AX...]
    convert_element_type x2, other arithmetic: 4.31 us -> 1.2 us  [the longest x1 1.13 us: body(): slopes = gather_x(slopes.astype(jnp.bfloat16))]
    ppermute x9, waiting for transfers between devices: 3.69 us -> 6.09 us  [other_core(): return lax.ppermute(block, 'core', [(0, 1), (1, 0)])]
    ppermute x3, waiting for transfers between devices: 2.16 us -> 4.33 us  [to_lower(): return lax.ppermute(block, CROSS_AXES, [(3, 0), (2, 1)])]
    ppermute x12 -> x18, waiting for transfers between devices: 37.8 us -> 35.7 us  [step_x(): return lax.ppermute(block, 'x', [(i, (i + distance) % X) for i in range(X)])]
  transfers between devices with their start and end apart: 34 -> 40, of which waited for: 18 -> 27; matrix products, arithmetic and copies ran while one was open for 21% -> 19% of each run, Pallas kernels for 0% -> 0%
where the time goes in v11:
time: 202 us; the launch traced here: 201 us
  waiting for transfers between devices  76.9 us (38%)
  starting transfers between devices  75.4 us (37%)
  matrix products  21.7 us (11%)
  other arithmetic  17.9 us (9%)
  local copies, waits for them, and re-layouts  8.12 us (4%)
    ppermute x18, waiting for transfers between devices, step_x(): return lax.ppermute(block, 'x', [(i, (i + distance) % X) for i in range(X)])  35.7 us
    ppermute x18, starting transfers between devices, step_x(): return lax.ppermute(block, 'x', [(i, (i + distance) % X) for i in range(X)])  27.6 us
    dot_general x18, matrix products, contract(): lax.dot_general(first_op, second_op, (((first_dim,), (second_dim,)), ((),...  21.7 us
    all_to_all x2, starting transfers between devices, gather_wide(): lax.all_to_all(jnp.broadcast_to(block[None], (WIDE, rows, cols)), WIDE_AX...  17.6 us
    all_to_all x2, starting transfers between devices, spread_wide(): lax.all_to_all(partial.reshape(WIDE, rows // WIDE, cols), WIDE_AXES, 0, 0...  13.8 us
    all_to_all x2, waiting for transfers between devices, spread_wide(): lax.all_to_all(partial.reshape(WIDE, rows // WIDE, cols), WIDE_AXES, 0, 0...  11.7 us
    ppermute x4, waiting for transfers between devices, to_upper(): return lax.ppermute(block, CROSS_AXES, [(0, 3), (1, 2)])  10.8 us
    ppermute x3, starting transfers between devices, to_lower(): return lax.ppermute(block, CROSS_AXES, [(3, 0), (2, 1)])  10.1 us
  transfers between devices with their start and end apart: 40, of which 27 were waited for; matrix products, arithmetic and copies ran while one was open for 19% of the time, Pallas kernels for 0%

profile of v11, /device:TPU:56, one launch (start us, length us, event | category | flops | bytes accessed | tf_op | source)
XLA Modules:
  0.0 201.1 jit_solution(407310837539492504)
XLA Ops:
  0.6 1.9 broadcast_in_dim.136
  2.6 9.6 %all-to-all-start = ((bf16[16,32,1024]{2,1,0:T(8,128)(2,1)}), bf16[16,32,1024]{2,1,0:T(8,128)(2,1)}, u32[]{:S(2)}, u32[]{:S(2)}) async-start(bf16[16,32,1024]{2,1,0:T(8,128)(2,1)} %broadcast_in_dim.136), calls=%async_computation | async-start | bytes 2097152 | tf_op jit(solution)/shard_map/all_to_all | solution.py:120
  12.2 1.3 fusion.86
  16.3 1.2 collective-permute-done
  17.5 1.2 maximum_add_fusion
  19.5 3.0 %collective-permute-start.3 = (bf16[128,512]{1,0:T(8,128)(2,1)}, bf16[128,512]{1,0:T(8,128)(2,1)S(1)}, u32[]{:S(2)}, u32[]{:S(2)}) collective-permute-start(bf16[128,512]{1,0:T(8,128)(2,1)} %get-tuple-element.58), channel_id=1, source_target_pairs={{0,4},{2,6},{4,0},{6,2},{1,5},{3,7},{5,1},{7,3},{8,12},{10,14},{12... | collective-permute-start | bytes 393224 | tf_op jit(solution)/shard_map/ppermute | solution.py:71
  22.6 1.1 collective-permute-start.2
  24.7 2.9 %collective-permute-done.3 = bf16[128,512]{1,0:T(8,128)(2,1)S(1)} collective-permute-done((bf16[128,512]{1,0:T(8,128)(2,1)}, bf16[128,512]{1,0:T(8,128)(2,1)S(1)}, u32[]{:S(2)}, u32[]{:S(2)}) %collective-permute-start.3) | collective-permute-done | bytes 131104 | tf_op jit(solution)/shard_map/ppermute | solution.py:71
  27.6 2.1 %collective-permute-done.2 = bf16[128,512]{1,0:T(8,128)(2,1)S(1)} collective-permute-done((bf16[128,512]{1,0:T(8,128)(2,1)}, bf16[128,512]{1,0:T(8,128)(2,1)S(1)}, u32[]{:S(2)}, u32[]{:S(2)}) %collective-permute-start.2) | collective-permute-done | bytes 131104 | tf_op jit(solution)/shard_map/ppermute | solution.py:71
  30.2 1.1 fusion.63
  32.4 2.6 %collective-permute-start.5 = (bf16[128,512]{1,0:T(8,128)(2,1)S(1)}, bf16[128,512]{1,0:T(8,128)(2,1)S(1)}, u32[]{:S(2)}, u32[]{:S(2)}) collective-permute-start(bf16[128,512]{1,0:T(8,128)(2,1)S(1)} %get-tuple-element.45), channel_id=1, source_target_pairs={{0,4},{2,6},{4,0},{6,2},{1,5},{3,7},{5,1},{7,3},{8,12},{10,14},{12... | collective-permute-start | bytes 393224 | tf_op jit(solution)/shard_map/ppermute | solution.py:71
  35.0 1.5 collective-permute-start.4
  37.6 3.7 %collective-permute-done.5 = bf16[128,512]{1,0:T(8,128)(2,1)S(1)} collective-permute-done((bf16[128,512]{1,0:T(8,128)(2,1)S(1)}, bf16[128,512]{1,0:T(8,128)(2,1)S(1)}, u32[]{:S(2)}, u32[]{:S(2)}) %collective-permute-start.5) | collective-permute-done | bytes 131104 | tf_op jit(solution)/shard_map/ppermute | solution.py:71
  41.6 1.5 fusion.85
  43.1 1.9 convolution_convert_fusion.5
  45.1 1.5 collective-permute-done.11
  46.7 1.7 fusion.57
  48.4 2.7 %collective-permute-start.14 = (bf16[256,512]{1,0:T(8,128)(2,1)S(1)}, bf16[256,512]{1,0:T(8,128)(2,1)S(1)}, u32[]{:S(2)}, u32[]{:S(2)}) collective-permute-start(bf16[256,512]{1,0:T(8,128)(2,1)S(1)} %get-tuple-element.60), channel_id=1, source_target_pairs={{0,4},{2,6},{4,0},{6,2},{1,5},{3,7},{5,1},{7,3},{8,12},{10,14},{12... | collective-permute-start | bytes 786440 | tf_op jit(solution)/shard_map/ppermute | solution.py:71
  51.1 1.3 collective-permute-start.13
  53.1 1.3 collective-permute-start.18
  54.5 1.8 convolution_convert_fusion.6
  56.6 2.6 %collective-permute-done.14 = bf16[256,512]{1,0:T(8,128)(2,1)S(1)} collective-permute-done((bf16[256,512]{1,0:T(8,128)(2,1)S(1)}, bf16[256,512]{1,0:T(8,128)(2,1)S(1)}, u32[]{:S(2)}, u32[]{:S(2)}) %collective-permute-start.14) | collective-permute-done | bytes 262176 | tf_op jit(solution)/shard_map/ppermute | solution.py:71
  59.2 4.8 %collective-permute-done.13 = bf16[256,512]{1,0:T(8,128)(2,1)S(1)} collective-permute-done((bf16[256,512]{1,0:T(8,128)(2,1)S(1)}, bf16[256,512]{1,0:T(8,128)(2,1)S(1)}, u32[]{:S(2)}, u32[]{:S(2)}) %collective-permute-start.13) | collective-permute-done | bytes 262176 | tf_op jit(solution)/shard_map/ppermute | solution.py:71
  64.4 1.7 fusion.56
  66.1 2.8 %collective-permute-start.10 = (bf16[256,512]{1,0:T(8,128)(2,1)S(1)}, bf16[256,512]{1,0:T(8,128)(2,1)S(1)}, u32[]{:S(2)}, u32[]{:S(2)}) collective-permute-start(bf16[256,512]{1,0:T(8,128)(2,1)S(1)} %get-tuple-element.62), channel_id=1, source_target_pairs={{0,4},{2,6},{4,0},{6,2},{1,5},{3,7},{5,1},{7,3},{8,12},{10,14},{12... | collective-permute-start | bytes 786440 | tf_op jit(solution)/shard_map/ppermute | solution.py:71
  68.8 1.3 collective-permute-start.9
  71.3 1.3 fusion.1
  72.6 2.9 %collective-permute-start.17 = (bf16[256,1024]{1,0:T(8,128)(2,1)}, bf16[256,1024]{1,0:T(8,128)(2,1)}, u32[]{:S(2)}, u32[]{:S(2)}) collective-permute-start(bf16[256,1024]{1,0:T(8,128)(2,1)} %fusion.1), channel_id=1, source_target_pairs={{192,0},{128,64},{193,1},{129,65},{194,2},{130,66},{195,3},{131,67... | collective-permute-start | bytes 1572872 | tf_op jit(solution)/shard_map/ppermute | solution.py:47
  75.5 1.3 collective-permute-done.10
  76.9 5.1 %collective-permute-done.9 = bf16[256,512]{1,0:T(8,128)(2,1)S(1)} collective-permute-done((bf16[256,512]{1,0:T(8,128)(2,1)S(1)}, bf16[256,512]{1,0:T(8,128)(2,1)S(1)}, u32[]{:S(2)}, u32[]{:S(2)}) %collective-permute-start.9) | collective-permute-done | bytes 262176 | tf_op jit(solution)/shard_map/ppermute | solution.py:71
  82.3 1.5 collective-permute-done.15
  84.3 1.8 collective-permute-done.17
  86.0 1.3 fusion.3
  87.4 8.1 %all-to-all-start.1 = ((bf16[16,16,1024]{2,1,0:T(8,128)(2,1)}), bf16[16,16,1024]{2,1,0:T(8,128)(2,1)S(1)}, u32[]{:S(2)}, u32[]{:S(2)}) async-start(bf16[16,16,1024]{2,1,0:T(8,128)(2,1)} %bitcast.144), calls=%async_computation.1 | async-start | bytes 1048576 | tf_op jit(solution)/shard_map/all_to_all | solution.py:109
  95.5 1.5 slice_bitcast_fusion
  97.0 6.4 %collective-permute-done.18 = bf16[1024,1024]{1,0:T(8,128)(2,1)} collective-permute-done((bf16[1024,1024]{1,0:T(8,128)(2,1)}, bf16[1024,1024]{1,0:T(8,128)(2,1)}, u32[]{:S(2)}, u32[]{:S(2)}) %collective-permute-start.18) | collective-permute-done | bytes 2097184 | tf_op jit(solution)/shard_map/ppermute | solution.py:43
  103.4 1.3 collective-permute-start.30
  105.6 3.1 %collective-permute-start.21 = (bf16[128,512]{1,0:T(8,128)(2,1)S(1)}, bf16[128,512]{1,0:T(8,128)(2,1)S(1)}, u32[]{:S(2)}, u32[]{:S(2)}) collective-permute-start(bf16[128,512]{1,0:T(8,128)(2,1)S(1)} %get-tuple-element.28), channel_id=1, source_target_pairs={{0,4},{2,6},{4,0},{6,2},{1,5},{3,7},{5,1},{7,3},{8,12},{10,14},{12... | collective-permute-start | bytes 393224 | tf_op jit(solution)/shard_map/ppermute | solution.py:71
  108.7 3.1 %collective-permute-done.22 = bf16[128,512]{1,0:T(8,128)(2,1)S(1)} collective-permute-done((bf16[128,512]{1,0:T(8,128)(2,1)S(1)}, bf16[128,512]{1,0:T(8,128)(2,1)S(1)}, u32[]{:S(2)}, u32[]{:S(2)}) %collective-permute-start.22) | collective-permute-done | bytes 131104 | tf_op jit(solution)/shard_map/ppermute | solution.py:71
  111.8 1.4 collective-permute-done.21
  116.5 8.0 %all-to-all-start.2 = ((bf16[16,16,1024]{2,1,0:T(8,128)(2,1)}), bf16[16,16,1024]{2,1,0:T(8,128)(2,1)S(1)}, u32[]{:S(2)}, u32[]{:S(2)}) async-start(bf16[16,16,1024]{2,1,0:T(8,128)(2,1)} %broadcast_in_dim.154), calls=%async_computation.2 | async-start | bytes 1048576 | tf_op jit(solution)/shard_map/all_to_all | solution.py:120
  124.6 1.3 collective-permute-start.24
  125.8 4.4 %collective-permute-done.30 = bf16[512,1024]{1,0:T(8,128)(2,1)} collective-permute-done((bf16[512,1024]{1,0:T(8,128)(2,1)}, bf16[512,1024]{1,0:T(8,128)(2,1)}, u32[]{:S(2)}, u32[]{:S(2)}) %collective-permute-start.30) | collective-permute-done | bytes 1048608 | tf_op jit(solution)/shard_map/ppermute | solution.py:43
  130.2 1.3 collective-permute-start.31
  131.5 1.3 broadcast_select_fusion.2
  132.8 1.1 pad_maximum_fusion
  134.0 3.8 %broadcast_select_fusion = bf16[1024,1024]{1,0:T(8,128)(2,1)} fusion(bf16[1024,1024]{1,0:T(8,128)(2,1)} %collective-permute-done.18, pred[]{:T(512)S(6)} %eq.35, bf16[1,1024,1024]{2,1,0:T(8,128)(2,1)} %param.7), kind=kLoop, calls=%fused_computation.1 | loop fusion | flops 1048576 | bytes 6291457 | tf_op jit(solution)/shard_map/jit(_where)/select_n | solution.py:146
  137.7 2.9 %all-to-all-done.2 = bf16[16,16,1024]{2,1,0:T(8,128)(2,1)S(1)} async-done(((bf16[16,16,1024]{2,1,0:T(8,128)(2,1)}), bf16[16,16,1024]{2,1,0:T(8,128)(2,1)S(1)}, u32[]{:S(2)}, u32[]{:S(2)}) %all-to-all-start.2) | async-done | bytes 524320 | tf_op jit(solution)/shard_map/all_to_all | solution.py:120
  140.6 5.9 %collective-permute-start.29 = (bf16[256,1024]{1,0:T(8,128)(2,1)S(1)}, bf16[256,1024]{1,0:T(8,128)(2,1)S(1)}, u32[]{:S(2)}, u32[]{:S(2)}) collective-permute-start(bf16[256,1024]{1,0:T(8,128)(2,1)S(1)} %bitcast.128), channel_id=1, source_target_pairs={{192,0},{128,64},{193,1},{129,65},{194,2},{130,66},{195,3},{131,67... | collective-permute-start | bytes 1572872 | tf_op jit(solution)/shard_map/ppermute | solution.py:47
  146.5 1.7 convolution_convert_fusion.4
  150.4 1.8 collective-permute-start.28
  152.2 1.4 collective-permute-start.27
  154.2 2.5 %collective-permute-done.29 = bf16[256,1024]{1,0:T(8,128)(2,1)S(1)} collective-permute-done((bf16[256,1024]{1,0:T(8,128)(2,1)S(1)}, bf16[256,1024]{1,0:T(8,128)(2,1)S(1)}, u32[]{:S(2)}, u32[]{:S(2)}) %collective-permute-start.29) | collective-permute-done | bytes 524320 | tf_op jit(solution)/shard_map/ppermute | solution.py:47
  156.9 2.6 %convolution_convert_fusion.1 = bf16[1024,1024]{1,0:T(8,128)(2,1)} fusion(bf16[512,1024]{1,0:T(8,128)(2,1)S(1)} %copy-done.11, bf16[256,1024]{1,0:T(8,128)(2,1)S(1)} %broadcast_select_fusion.3, bf16[256,1024]{1,0:T(8,128)(2,1)S(1)} %broadcast_select_fusion.4), kind=kOutput, calls=%fused_computation.3 | convolution fusion | flops 1076887552 | bytes 4194304 | tf_op jit(solution)/shard_map/dot_general | solution.py:26
  159.5 1.9 collective-permute-done.28
  161.4 4.5 %collective-permute-done.27 = bf16[256,512]{1,0:T(8,128)(2,1)S(1)} collective-permute-done((bf16[256,512]{1,0:T(8,128)(2,1)S(1)}, bf16[256,512]{1,0:T(8,128)(2,1)S(1)}, u32[]{:S(2)}, u32[]{:S(2)}) %collective-permute-start.27) | collective-permute-done | bytes 262176 | tf_op jit(solution)/shard_map/ppermute | solution.py:71
  167.5 1.3 collective-permute-start.33
  168.8 2.5 %maximum_select_fusion = bf16[1024,1024]{1,0:T(8,128)(2,1)S(1)} fusion(bf16[512,1024]{1,0:T(8,128)(2,1)} %collective-permute-done.31, bf16[512,1024]{1,0:T(8,128)(2,1)} %collective-permute-done.30, bf16[1,1024,1024]{2,1,0:T(8,128)(2,1)S(1)} %copy-done, pred[]{:T(512)S(6)} %eq.35), kind=kLoop, calls=%fused_computation | loop fusion | flops 5242880 | bytes 6291457 | tf_op jit(solution)/shard_map/jit(_where)/select_n | solution.py:146
  171.9 1.3 fusion.2
  173.2 5.7 %all-to-all-start.3 = ((bf16[16,16,1024]{2,1,0:T(8,128)(2,1)}), bf16[16,16,1024]{2,1,0:T(8,128)(2,1)S(1)}, u32[]{:S(2)}, u32[]{:S(2)}) async-start(bf16[16,16,1024]{2,1,0:T(8,128)(2,1)} %bitcast.37), calls=%async_computation.3 | async-start | bytes 1048576 | tf_op jit(solution)/shard_map/all_to_all | solution.py:109
  179.1 1.4 collective-permute-done.34
  180.6 2.6 %convolution_convert_fusion = bf16[1024,1024]{1,0:T(8,128)(2,1)} fusion(bf16[256,1024]{1,0:T(8,128)(2,1)S(1)} %bitcast.143, bf16[256,1024]{1,0:T(8,128)(2,1)S(1)} %bitcast.140, bf16[256,512]{1,0:T(8,128)(2,1)S(1)} %get-tuple-element.50, bf16[256,512]{1,0:T(8,128)(2,1)S(1)} %get-tuple-element.49, bf16[256,512]{1,0:T(8,128)(2,1)S(1)} %get-tuple-element.48, ...), kind=kOutput, calls=%fused_computation.2 | convolution fusion | flops 1081081856 | bytes 4194304 | tf_op jit(solution)/shard_map/dot_general | solution.py:26
  183.2 11.7 %all-to-all-done.3 = bf16[16,16,1024]{2,1,0:T(8,128)(2,1)S(1)} async-done(((bf16[16,16,1024]{2,1,0:T(8,128)(2,1)}), bf16[16,16,1024]{2,1,0:T(8,128)(2,1)S(1)}, u32[]{:S(2)}, u32[]{:S(2)}) %all-to-all-start.3) | async-done | bytes 524320 | tf_op jit(solution)/shard_map/all_to_all | solution.py:109
  195.1 5.4 %collective-permute-done.35 = bf16[16,1024]{1,0:T(8,128)(2,1)S(1)} collective-permute-done((bf16[16,1024]{1,0:T(8,128)(2,1)S(1)}, bf16[16,1024]{1,0:T(8,128)(2,1)S(1)}, u32[]{:S(2)}, u32[]{:S(2)}) %collective-permute-start.35) | collective-permute-done | bytes 32800 | tf_op jit(solution)/shard_map/ppermute | solution.py:216
  (104 shorter events, 21.3 us)
Async XLA Ops:
  2.6 10.9 %copy-start = (bf16[1,1024,1024]{2,1,0:T(8,128)(2,1)S(1)}, bf16[1,1024,1024]{2,1,0:T(8,128)(2,1)}, u32[]{:S(2)}) copy-start(bf16[1,1024,1024]{2,1,0:T(8,128)(2,1)} %param.6) | copy-start | bytes 6291460
  2.6 39.1 %all-to-all-start = ((bf16[16,32,1024]{2,1,0:T(8,128)(2,1)}), bf16[16,32,1024]{2,1,0:T(8,128)(2,1)}, u32[]{:S(2)}, u32[]{:S(2)}) async-start(bf16[16,32,1024]{2,1,0:T(8,128)(2,1)} %broadcast_in_dim.136), calls=%async_computation | async-start | bytes 2097152 | tf_op jit(solution)/shard_map/all_to_all | solution.py:120
  13.5 1.9 copy-start.5
  13.5 2.3 %copy-start.3 = (bf16[16,1,16,1024]{3,2,1,0:T(8,128)(2,1)}, bf16[16,1,16,1024]{3,2,1,0:T(8,128)(2,1)S(1)}, u32[]{:S(2)}) copy-start(bf16[16,1,16,1024]{3,2,1,0:T(8,128)(2,1)S(1)} %get-tuple-element.55) | copy-start | bytes 1572868
  15.3 2.3 %collective-permute-start = (bf16[512,512]{1,0:T(8,128)(2,1)}, bf16[512,512]{1,0:T(8,128)(2,1)}, u32[]{:S(2)}, u32[]{:S(2)}) collective-permute-start(bf16[512,512]{1,0:T(8,128)(2,1)} %pad_maximum_fusion.1), channel_id=1, source_target_pairs={{0,1},{1,0},{2,3},{3,2},{4,5},{5,4},{6,7},{7,6},{8,9},{9,8},{10,11... | collective-permute-start | bytes 1572872 | tf_op jit(solution)/shard_map/ppermute | solution.py:39
  19.5 8.1 %collective-permute-start.3 = (bf16[128,512]{1,0:T(8,128)(2,1)}, bf16[128,512]{1,0:T(8,128)(2,1)S(1)}, u32[]{:S(2)}, u32[]{:S(2)}) collective-permute-start(bf16[128,512]{1,0:T(8,128)(2,1)} %get-tuple-element.58), channel_id=1, source_target_pairs={{0,4},{2,6},{4,0},{6,2},{1,5},{3,7},{5,1},{7,3},{8,12},{10,14},{12... | collective-permute-start | bytes 393224 | tf_op jit(solution)/shard_map/ppermute | solution.py:71
  22.6 7.1 %collective-permute-start.2 = (bf16[128,512]{1,0:T(8,128)(2,1)}, bf16[128,512]{1,0:T(8,128)(2,1)S(1)}, u32[]{:S(2)}, u32[]{:S(2)}) collective-permute-start(bf16[128,512]{1,0:T(8,128)(2,1)} %get-tuple-element.59), channel_id=1, source_target_pairs={{0,6},{2,0},{4,2},{6,4},{1,7},{3,1},{5,3},{7,5},{8,14},{10,8},{12,... | collective-permute-start | bytes 393224 | tf_op jit(solution)/shard_map/ppermute | solution.py:71
  23.7 6.5 %collective-permute-start.1 = (bf16[128,512]{1,0:T(8,128)(2,1)S(1)}, bf16[128,512]{1,0:T(8,128)(2,1)}, u32[]{:S(2)}, u32[]{:S(2)}) collective-permute-start(bf16[128,512]{1,0:T(8,128)(2,1)S(1)} %get-tuple-element.57), channel_id=1, source_target_pairs={{0,2},{2,4},{4,6},{6,0},{1,3},{3,5},{5,7},{7,1},{8,10},{10,12},{12... | collective-permute-start | bytes 393224 | tf_op jit(solution)/shard_map/ppermute | solution.py:71
  31.4 6.3 %collective-permute-start.6 = (bf16[128,512]{1,0:T(8,128)(2,1)S(1)}, bf16[128,512]{1,0:T(8,128)(2,1)S(1)}, u32[]{:S(2)}, u32[]{:S(2)}) collective-permute-start(bf16[128,512]{1,0:T(8,128)(2,1)S(1)} %get-tuple-element.45), channel_id=1, source_target_pairs={{0,2},{2,4},{4,6},{6,0},{1,3},{3,5},{5,7},{7,1},{8,10},{10,12},{12... | collective-permute-start | bytes 393224 | tf_op jit(solution)/shard_map/ppermute | solution.py:71
  32.4 8.9 %collective-permute-start.5 = (bf16[128,512]{1,0:T(8,128)(2,1)S(1)}, bf16[128,512]{1,0:T(8,128)(2,1)S(1)}, u32[]{:S(2)}, u32[]{:S(2)}) collective-permute-start(bf16[128,512]{1,0:T(8,128)(2,1)S(1)} %get-tuple-element.45), channel_id=1, source_target_pairs={{0,4},{2,6},{4,0},{6,2},{1,5},{3,7},{5,1},{7,3},{8,12},{10,14},{12... | collective-permute-start | bytes 393224 | tf_op jit(solution)/shard_map/ppermute | solution.py:71
  35.0 6.3 %collective-permute-start.4 = (bf16[128,512]{1,0:T(8,128)(2,1)S(1)}, bf16[128,512]{1,0:T(8,128)(2,1)S(1)}, u32[]{:S(2)}, u32[]{:S(2)}) collective-permute-start(bf16[128,512]{1,0:T(8,128)(2,1)S(1)} %get-tuple-element.45), channel_id=1, source_target_pairs={{0,6},{2,0},{4,2},{6,4},{1,7},{3,1},{5,3},{7,5},{8,14},{10,8},{12,... | collective-permute-start | bytes 393224 | tf_op jit(solution)/shard_map/ppermute | solution.py:71
  41.6 22.3 %copy-start.7 = (bf16[512,512]{1,0:T(8,128)(2,1)}, bf16[512,512]{1,0:T(8,128)(2,1)S(1)}, u32[]{:S(2)}) copy-start(bf16[512,512]{1,0:T(8,128)(2,1)S(1)} %fusion.55) | copy-start | bytes 1572868
  43.1 5.3 %copy-start.2 = (bf16[16,1,16,1024]{3,2,1,0:T(8,128)(2,1)}, bf16[16,1,16,1024]{3,2,1,0:T(8,128)(2,1)S(1)}, u32[]{:S(2)}) copy-start(bf16[16,1,16,1024]{3,2,1,0:T(8,128)(2,1)S(1)} %get-tuple-element.54) | copy-start | bytes 1572868
  45.0 1.6 collective-permute-start.11
  48.4 10.8 %collective-permute-start.14 = (bf16[256,512]{1,0:T(8,128)(2,1)S(1)}, bf16[256,512]{1,0:T(8,128)(2,1)S(1)}, u32[]{:S(2)}, u32[]{:S(2)}) collective-permute-start(bf16[256,512]{1,0:T(8,128)(2,1)S(1)} %get-tuple-element.60), channel_id=1, source_target_pairs={{0,4},{2,6},{4,0},{6,2},{1,5},{3,7},{5,1},{7,3},{8,12},{10,14},{12... | collective-permute-start | bytes 786440 | tf_op jit(solution)/shard_map/ppermute | solution.py:71
  51.1 12.8 %collective-permute-start.13 = (bf16[256,512]{1,0:T(8,128)(2,1)S(1)}, bf16[256,512]{1,0:T(8,128)(2,1)S(1)}, u32[]{:S(2)}, u32[]{:S(2)}) collective-permute-start(bf16[256,512]{1,0:T(8,128)(2,1)S(1)} %get-tuple-element.60), channel_id=1, source_target_pairs={{0,6},{2,0},{4,2},{6,4},{1,7},{3,1},{5,3},{7,5},{8,14},{10,8},{12,... | collective-permute-start | bytes 786440 | tf_op jit(solution)/shard_map/ppermute | solution.py:71
  52.4 11.6 %collective-permute-start.12 = (bf16[256,512]{1,0:T(8,128)(2,1)S(1)}, bf16[256,512]{1,0:T(8,128)(2,1)S(1)}, u32[]{:S(2)}, u32[]{:S(2)}) collective-permute-start(bf16[256,512]{1,0:T(8,128)(2,1)S(1)} %get-tuple-element.60), channel_id=1, source_target_pairs={{0,2},{2,4},{4,6},{6,0},{1,3},{3,5},{5,7},{7,1},{8,10},{10,12},{12... | collective-permute-start | bytes 786440 | tf_op jit(solution)/shard_map/ppermute | solution.py:71
  53.1 50.2 %collective-permute-start.18 = (bf16[1024,1024]{1,0:T(8,128)(2,1)}, bf16[1024,1024]{1,0:T(8,128)(2,1)}, u32[]{:S(2)}, u32[]{:S(2)}) collective-permute-start(bf16[1024,1024]{1,0:T(8,128)(2,1)} %bitcast.28), channel_id=1, source_target_pairs={{0,192},{64,128},{1,193},{65,129},{2,194},{66,130},{3,195},{67,131... | collective-permute-start | bytes 6291464 | tf_op jit(solution)/shard_map/ppermute | solution.py:43
  54.4 27.5 %copy-start.16 = (bf16[256,512]{1,0:T(8,128)(2,1)}, bf16[256,512]{1,0:T(8,128)(2,1)S(1)}, u32[]{:S(2)}) copy-start(bf16[256,512]{1,0:T(8,128)(2,1)S(1)} %slice.43) | copy-start | bytes 786436
  56.3 8.1 %collective-permute-start.7 = (bf16[256,512]{1,0:T(8,128)(2,1)S(1)}, bf16[256,512]{1,0:T(8,128)(2,1)S(1)}, u32[]{:S(2)}, u32[]{:S(2)}) collective-permute-start(bf16[256,512]{1,0:T(8,128)(2,1)S(1)} %convolution_convert_fusion.6), channel_id=1, source_target_pairs={{0,1},{1,0},{2,3},{3,2},{4,5},{5,4},{6,7},{7,6},{8,9},{9,8},{10,11... | collective-permute-start | bytes 786440 | tf_op jit(solution)/shard_map/ppermute | solution.py:39
  64.2 6.7 %collective-permute-start.16 = (bf16[256,512]{1,0:T(8,128)(2,1)S(1)}, bf16[256,512]{1,0:T(8,128)(2,1)S(1)}, u32[]{:S(2)}, u32[]{:S(2)}) collective-permute-start(bf16[256,512]{1,0:T(8,128)(2,1)S(1)} %multiply_convert_fusion.2), channel_id=1, source_target_pairs={{0,1},{1,0},{2,3},{3,2},{4,5},{5,4},{6,7},{7,6},{8,9},{9,8},{10,11... | collective-permute-start | bytes 786440 | tf_op jit(solution)/shard_map/ppermute | solution.py:39
  66.1 10.8 %collective-permute-start.10 = (bf16[256,512]{1,0:T(8,128)(2,1)S(1)}, bf16[256,512]{1,0:T(8,128)(2,1)S(1)}, u32[]{:S(2)}, u32[]{:S(2)}) collective-permute-start(bf16[256,512]{1,0:T(8,128)(2,1)S(1)} %get-tuple-element.62), channel_id=1, source_target_pairs={{0,4},{2,6},{4,0},{6,2},{1,5},{3,7},{5,1},{7,3},{8,12},{10,14},{12... | collective-permute-start | bytes 786440 | tf_op jit(solution)/shard_map/ppermute | solution.py:71
  68.8 13.1 %collective-permute-start.9 = (bf16[256,512]{1,0:T(8,128)(2,1)S(1)}, bf16[256,512]{1,0:T(8,128)(2,1)S(1)}, u32[]{:S(2)}, u32[]{:S(2)}) collective-permute-start(bf16[256,512]{1,0:T(8,128)(2,1)S(1)} %get-tuple-element.62), channel_id=1, source_target_pairs={{0,6},{2,0},{4,2},{6,4},{1,7},{3,1},{5,3},{7,5},{8,14},{10,8},{12,... | collective-permute-start | bytes 786440 | tf_op jit(solution)/shard_map/ppermute | solution.py:71
  70.1 11.8 %collective-permute-start.8 = (bf16[256,512]{1,0:T(8,128)(2,1)S(1)}, bf16[256,512]{1,0:T(8,128)(2,1)S(1)}, u32[]{:S(2)}, u32[]{:S(2)}) collective-permute-start(bf16[256,512]{1,0:T(8,128)(2,1)S(1)} %get-tuple-element.62), channel_id=1, source_target_pairs={{0,2},{2,4},{4,6},{6,0},{1,3},{3,5},{5,7},{7,1},{8,10},{10,12},{12... | collective-permute-start | bytes 786440 | tf_op jit(solution)/shard_map/ppermute | solution.py:71
  70.9 1.8 copy-start.12
  72.6 13.4 %collective-permute-start.17 = (bf16[256,1024]{1,0:T(8,128)(2,1)}, bf16[256,1024]{1,0:T(8,128)(2,1)}, u32[]{:S(2)}, u32[]{:S(2)}) collective-permute-start(bf16[256,1024]{1,0:T(8,128)(2,1)} %fusion.1), channel_id=1, source_target_pairs={{192,0},{128,64},{193,1},{129,65},{194,2},{130,66},{195,3},{131,67... | collective-permute-start | bytes 1572872 | tf_op jit(solution)/shard_map/ppermute | solution.py:47
  82.1 5.2 %copy-start.9 = (bf16[256,512]{1,0:T(8,128)(2,1)}, bf16[256,512]{1,0:T(8,128)(2,1)S(1)}, u32[]{:S(2)}) copy-start(bf16[256,512]{1,0:T(8,128)(2,1)S(1)} %multiply_convert_fusion.1) | copy-start | bytes 786436
  82.2 1.6 collective-permute-start.15
  83.8 3.6 %copy-start.14 = (bf16[256,512]{1,0:T(8,128)(2,1)}, bf16[256,512]{1,0:T(8,128)(2,1)S(1)}, u32[]{:S(2)}) copy-start(bf16[256,512]{1,0:T(8,128)(2,1)S(1)} %collective-permute-done.15) | copy-start | bytes 786436
  87.4 27.4 %all-to-all-start.1 = ((bf16[16,16,1024]{2,1,0:T(8,128)(2,1)}), bf16[16,16,1024]{2,1,0:T(8,128)(2,1)S(1)}, u32[]{:S(2)}, u32[]{:S(2)}) async-start(bf16[16,16,1024]{2,1,0:T(8,128)(2,1)} %bitcast.144), calls=%async_computation.1 | async-start | bytes 1048576 | tf_op jit(solution)/shard_map/all_to_all | solution.py:109
  103.4 26.9 %collective-permute-start.30 = (bf16[512,1024]{1,0:T(8,128)(2,1)}, bf16[512,1024]{1,0:T(8,128)(2,1)}, u32[]{:S(2)}, u32[]{:S(2)}) collective-permute-start(bf16[512,1024]{1,0:T(8,128)(2,1)} %get-tuple-element.33), channel_id=1, source_target_pairs={{0,192},{64,128},{1,193},{65,129},{2,194},{66,130},{3,195},{67,131... | collective-permute-start | bytes 3145736 | tf_op jit(solution)/shard_map/ppermute | solution.py:43
  104.7 7.2 %collective-permute-start.22 = (bf16[128,512]{1,0:T(8,128)(2,1)S(1)}, bf16[128,512]{1,0:T(8,128)(2,1)S(1)}, u32[]{:S(2)}, u32[]{:S(2)}) collective-permute-start(bf16[128,512]{1,0:T(8,128)(2,1)S(1)} %get-tuple-element.28), channel_id=1, source_target_pairs={{0,2},{2,4},{4,6},{6,0},{1,3},{3,5},{5,7},{7,1},{8,10},{10,12},{12... | collective-permute-start | bytes 393224 | tf_op jit(solution)/shard_map/ppermute | solution.py:71
  105.6 7.6 %collective-permute-start.21 = (bf16[128,512]{1,0:T(8,128)(2,1)S(1)}, bf16[128,512]{1,0:T(8,128)(2,1)S(1)}, u32[]{:S(2)}, u32[]{:S(2)}) collective-permute-start(bf16[128,512]{1,0:T(8,128)(2,1)S(1)} %get-tuple-element.28), channel_id=1, source_target_pairs={{0,4},{2,6},{4,0},{6,2},{1,5},{3,7},{5,1},{7,3},{8,12},{10,14},{12... | collective-permute-start | bytes 393224 | tf_op jit(solution)/shard_map/ppermute | solution.py:71
  108.7 5.0 %collective-permute-start.20 = (bf16[128,512]{1,0:T(8,128)(2,1)S(1)}, bf16[128,512]{1,0:T(8,128)(2,1)S(1)}, u32[]{:S(2)}, u32[]{:S(2)}) collective-permute-start(bf16[128,512]{1,0:T(8,128)(2,1)S(1)} %get-tuple-element.28), channel_id=1, source_target_pairs={{0,6},{2,0},{4,2},{6,4},{1,7},{3,1},{5,3},{7,5},{8,14},{10,8},{12,... | collective-permute-start | bytes 393224 | tf_op jit(solution)/shard_map/ppermute | solution.py:71
  114.7 16.8 %collective-permute-start.23 = (bf16[512,512]{1,0:T(8,128)(2,1)}, bf16[512,512]{1,0:T(8,128)(2,1)}, u32[]{:S(2)}, u32[]{:S(2)}) collective-permute-start(bf16[512,512]{1,0:T(8,128)(2,1)} %fusion.53), channel_id=1, source_target_pairs={{0,1},{1,0},{2,3},{3,2},{4,5},{5,4},{6,7},{7,6},{8,9},{9,8},{10,11... | collective-permute-start | bytes 1572872 | tf_op jit(solution)/shard_map/ppermute | solution.py:39
  116.5 24.1 %all-to-all-start.2 = ((bf16[16,16,1024]{2,1,0:T(8,128)(2,1)}), bf16[16,16,1024]{2,1,0:T(8,128)(2,1)S(1)}, u32[]{:S(2)}, u32[]{:S(2)}) async-start(bf16[16,16,1024]{2,1,0:T(8,128)(2,1)} %broadcast_in_dim.154), calls=%async_computation.2 | async-start | bytes 1048576 | tf_op jit(solution)/shard_map/all_to_all | solution.py:120
  124.6 13.2 %collective-permute-start.24 = (bf16[256,512]{1,0:T(8,128)(2,1)}, bf16[256,512]{1,0:T(8,128)(2,1)}, u32[]{:S(2)}, u32[]{:S(2)}) collective-permute-start(bf16[256,512]{1,0:T(8,128)(2,1)} %copy-done.16), channel_id=1, source_target_pairs={{0,192},{64,128},{1,193},{65,129},{2,194},{66,130},{3,195},{67,131... | collective-permute-start | bytes 786440 | tf_op jit(solution)/shard_map/ppermute | solution.py:43
  130.2 36.0 %collective-permute-start.31 = (bf16[512,1024]{1,0:T(8,128)(2,1)}, bf16[512,1024]{1,0:T(8,128)(2,1)}, u32[]{:S(2)}, u32[]{:S(2)}) collective-permute-start(bf16[512,1024]{1,0:T(8,128)(2,1)} %get-tuple-element.34), channel_id=1, source_target_pairs={{0,192},{64,128},{1,193},{65,129},{2,194},{66,130},{3,195},{67,131... | collective-permute-start | bytes 3145736 | tf_op jit(solution)/shard_map/ppermute | solution.py:43
  140.6 9.3 %copy-start.1 = (bf16[1024,1024]{1,0:T(8,128)(2,1)S(1)}, bf16[1024,1024]{1,0:T(8,128)(2,1)}, u32[]{:S(2)}) copy-start(bf16[1024,1024]{1,0:T(8,128)(2,1)} %broadcast_select_fusion) | copy-start | bytes 6291460
  140.6 16.1 %collective-permute-start.29 = (bf16[256,1024]{1,0:T(8,128)(2,1)S(1)}, bf16[256,1024]{1,0:T(8,128)(2,1)S(1)}, u32[]{:S(2)}, u32[]{:S(2)}) collective-permute-start(bf16[256,1024]{1,0:T(8,128)(2,1)S(1)} %bitcast.128), channel_id=1, source_target_pairs={{192,0},{128,64},{193,1},{129,65},{194,2},{130,66},{195,3},{131,67... | collective-permute-start | bytes 1572872 | tf_op jit(solution)/shard_map/ppermute | solution.py:47
  148.3 1.6 collective-permute-start.25
  149.5 7.4 %copy-start.11 = (bf16[512,1024]{1,0:T(8,128)(2,1)S(1)}, bf16[512,1024]{1,0:T(8,128)(2,1)}, u32[]{:S(2)}) copy-start(bf16[512,1024]{1,0:T(8,128)(2,1)} %pad_maximum_fusion) | copy-start | bytes 3145732
  150.4 11.0 %collective-permute-start.28 = (bf16[256,512]{1,0:T(8,128)(2,1)S(1)}, bf16[256,512]{1,0:T(8,128)(2,1)S(1)}, u32[]{:S(2)}, u32[]{:S(2)}) collective-permute-start(bf16[256,512]{1,0:T(8,128)(2,1)S(1)} %get-tuple-element.64), channel_id=1, source_target_pairs={{0,4},{2,6},{4,0},{6,2},{1,5},{3,7},{5,1},{7,3},{8,12},{10,14},{12... | collective-permute-start | bytes 786440 | tf_op jit(solution)/shard_map/ppermute | solution.py:71
  152.2 13.7 %collective-permute-start.27 = (bf16[256,512]{1,0:T(8,128)(2,1)S(1)}, bf16[256,512]{1,0:T(8,128)(2,1)S(1)}, u32[]{:S(2)}, u32[]{:S(2)}) collective-permute-start(bf16[256,512]{1,0:T(8,128)(2,1)S(1)} %get-tuple-element.64), channel_id=1, source_target_pairs={{0,6},{2,0},{4,2},{6,4},{1,7},{3,1},{5,3},{7,5},{8,14},{10,8},{12,... | collective-permute-start | bytes 786440 | tf_op jit(solution)/shard_map/ppermute | solution.py:71
  153.6 12.5 %collective-permute-start.26 = (bf16[256,512]{1,0:T(8,128)(2,1)S(1)}, bf16[256,512]{1,0:T(8,128)(2,1)S(1)}, u32[]{:S(2)}, u32[]{:S(2)}) collective-permute-start(bf16[256,512]{1,0:T(8,128)(2,1)S(1)} %get-tuple-element.64), channel_id=1, source_target_pairs={{0,2},{2,4},{4,6},{6,0},{1,3},{3,5},{5,7},{7,1},{8,10},{10,12},{12... | collective-permute-start | bytes 786440 | tf_op jit(solution)/shard_map/ppermute | solution.py:71
  156.9 9.4 %copy-start.8 = (bf16[512,512]{1,0:T(8,128)(2,1)S(1)}, bf16[512,512]{1,0:T(8,128)(2,1)}, u32[]{:S(2)}) copy-start(bf16[512,512]{1,0:T(8,128)(2,1)} %copy-done.7) | copy-start | bytes 1572868
  167.4 4.0 %collective-permute-start.32 = (bf16[256,512]{1,0:T(8,128)(2,1)S(1)}, bf16[256,512]{1,0:T(8,128)(2,1)S(1)}, u32[]{:S(2)}, u32[]{:S(2)}) collective-permute-start(bf16[256,512]{1,0:T(8,128)(2,1)S(1)} %multiply_convert_fusion), channel_id=1, source_target_pairs={{0,1},{1,0},{2,3},{3,2},{4,5},{5,4},{6,7},{7,6},{8,9},{9,8},{10,11... | collective-permute-start | bytes 786440 | tf_op jit(solution)/shard_map/ppermute | solution.py:39
  167.5 11.4 %collective-permute-start.33 = (bf16[256,512]{1,0:T(8,128)(2,1)S(1)}, bf16[256,512]{1,0:T(8,128)(2,1)S(1)}, u32[]{:S(2)}, u32[]{:S(2)}) collective-permute-start(bf16[256,512]{1,0:T(8,128)(2,1)S(1)} %multiply_convert_fusion), channel_id=1, source_target_pairs={{192,0},{128,64},{193,1},{129,65},{194,2},{130,66},{195,3},{131,67... | collective-permute-start | bytes 786440 | tf_op jit(solution)/shard_map/ppermute | solution.py:47
  171.8 7.1 %copy-start.13 = (bf16[256,512]{1,0:T(8,128)(2,1)S(1)}, bf16[256,512]{1,0:T(8,128)(2,1)}, u32[]{:S(2)}) copy-start(bf16[256,512]{1,0:T(8,128)(2,1)} %copy-done.12) | copy-start | bytes 786436
  171.9 8.7 %copy-start.10 = (bf16[256,512]{1,0:T(8,128)(2,1)S(1)}, bf16[256,512]{1,0:T(8,128)(2,1)}, u32[]{:S(2)}) copy-start(bf16[256,512]{1,0:T(8,128)(2,1)} %copy-done.9) | copy-start | bytes 786436
  171.9 8.7 %copy-start.15 = (bf16[256,512]{1,0:T(8,128)(2,1)S(1)}, bf16[256,512]{1,0:T(8,128)(2,1)}, u32[]{:S(2)}) copy-start(bf16[256,512]{1,0:T(8,128)(2,1)} %copy-done.14) | copy-start | bytes 786436
  173.2 7.4 %copy-start.4 = (bf16[16,1,16,1024]{3,2,1,0:T(8,128)(2,1)S(1)}, bf16[16,1,16,1024]{3,2,1,0:T(8,128)(2,1)}, u32[]{:S(2)}) copy-start(bf16[16,1,16,1024]{3,2,1,0:T(8,128)(2,1)} %copy-done.3) | copy-start | bytes 1572868
  173.2 7.4 %copy-start.6 = (bf16[16,1,16,1024]{3,2,1,0:T(8,128)(2,1)S(1)}, bf16[16,1,16,1024]{3,2,1,0:T(8,128)(2,1)}, u32[]{:S(2)}) copy-start(bf16[16,1,16,1024]{3,2,1,0:T(8,128)(2,1)} %copy-done.5) | copy-start | bytes 1572868
  173.2 21.7 %all-to-all-start.3 = ((bf16[16,16,1024]{2,1,0:T(8,128)(2,1)}), bf16[16,16,1024]{2,1,0:T(8,128)(2,1)S(1)}, u32[]{:S(2)}, u32[]{:S(2)}) async-start(bf16[16,16,1024]{2,1,0:T(8,128)(2,1)} %bitcast.37), calls=%async_computation.3 | async-start | bytes 1048576 | tf_op jit(solution)/shard_map/all_to_all | solution.py:109
  178.9 16.1 %collective-permute-start.19 = (bf16[16,1024]{1,0:T(8,128)(2,1)S(1)}, bf16[16,1024]{1,0:T(8,128)(2,1)S(1)}, u32[]{:S(2)}, u32[]{:S(2)}) collective-permute-start(bf16[16,1024]{1,0:T(8,128)(2,1)S(1)} %add_convert_fusion.1), channel_id=1, source_target_pairs={{0,128},{128,0},{1,129},{129,1},{2,130},{130,2},{3,131},{131,3},{4... | collective-permute-start | bytes 98312 | tf_op jit(solution)/shard_map/ppermute | solution.py:215
  178.9 1.6 collective-permute-start.34
  195.0 5.5 %collective-permute-start.35 = (bf16[16,1024]{1,0:T(8,128)(2,1)S(1)}, bf16[16,1024]{1,0:T(8,128)(2,1)S(1)}, u32[]{:S(2)}, u32[]{:S(2)}) collective-permute-start(bf16[16,1024]{1,0:T(8,128)(2,1)S(1)} %get-tuple-element.42), channel_id=1, source_target_pairs={{0,128},{128,0},{1,129},{129,1},{2,130},{130,2},{3,131},{131,3},{4... | collective-permute-start | bytes 98312 | tf_op jit(solution)/shard_map/ppermute | solution.py:216

commit v12 on v11

--- a/solution.py
+++ b/solution.py
@@ -162,10 +162,13 @@
     act, slopes = gelu_parts(spread_x(pair_sum(mine, theirs)))
     act = act.astype(jnp.bfloat16)
     slopes = gather_x(slopes.astype(jnp.bfloat16))
-    gathered, act, slopes = together(gather_wide(upstream), act, slopes)
+    gathered, act = together(gather_wide(upstream), act)
 
     top = by_part(gathered)
-    top_slope = slope_of(back_total(top[0], down_halves), slopes[first])
+    theirs = contract(top[0], down_halves[1], 1, 1)
+    mine = contract(top[0], down_halves[0], 1, 1)
+    mine, slopes = together(mine, slopes)
+    top_slope = slope_of(add_terms(narrow_terms(mine, theirs)), slopes[first])
     moved = to_lower(back_through_up(top_slope, up_halves))
     late_slopes, _ = together(slopes[last], top_slope[0])
     top_slope_rest = slope_of(back_total(top[1], down_halves), late_slopes)
@@ -174,26 +177,24 @@
     sent_up = [to_upper(together(w_up[:half], sent_down)[0])]
     sent_up.append(to_upper(together(w_up[half:], sent_up[0])[0]))
     partial, act = together(partial, act)
-    blocks, sent_down = together(spread_wide(partial), sent_down)
+    blocks, low_down, lower_slopes = together(
+        spread_wide(partial), pick(sent_down, w_down), to_upper(slopes[last])
+    )
     part = upstream.shape[0] // 2
     middle = (
         pick(upstream[part:], upstream[:part]).astype(jnp.float32) + add_blocks(blocks)
     ).astype(jnp.bfloat16)
 
-    low_down = pick(sent_down, w_down)
-    lower_slopes = to_upper(slopes[last])
-    hidden = gather_x(act)
-    hidden = in_order(hidden, other_core(hidden))
-    low, hidden, low_down, lower_slopes = together(
-        gather_wide(middle), hidden, low_down, lower_slopes
-    )
+    hidden = gather_x(in_order(act, other_core(act)))
+    low, hidden = together(gather_wide(middle), hidden)
     lower_slopes = pick(lower_slopes, slopes[first])
     low_rest = to_lower(low)
     low_total = back_total(low, halves(low_down, 0))
     incoming = jnp.concatenate([pick(top[0], low), pick(top[1], low_rest)], axis=0)
+    incoming, sent_up[1] = together(incoming, sent_up[1])
     grad_down = contract(hidden, incoming, 0, 0).astype(jnp.bfloat16)
-    low_total, grad_down, sent_up[1] = together(low_total, grad_down, sent_up[1])
     low_up = pick(jnp.concatenate(sent_up, axis=0), w_up)
+    low_total, grad_down, low_up = together(low_total, grad_down, low_up)
     low_slope = slope_of(low_total, lower_slopes)
     low_slope_rest = to_lower(low_slope[0])
     low_blocks = spread_wide(back_through_up(low_slope, halves(low_up, 1)))

time: 202 us -> 197 us (0.975)
  waiting for transfers between devices: 76.9 us -> 72.4 us
  other arithmetic: 17.9 us -> 15.8 us
    ppermute x18, waiting for transfers between devices: 35.7 us -> 25.4 us  [step_x(): return lax.ppermute(block, 'x', [(i, (i + distance) % X) for i in range(X)])]
    ppermute x4, waiting for transfers between devices: 10.8 us -> 15.6 us  [to_upper(): return lax.ppermute(block, CROSS_AXES, [(0, 3), (1, 2)])]
  transfers between devices with their start and end apart: 40 -> 40, of which waited for: 27 -> 23; matrix products, arithmetic and copies ran while one was open for 19% -> 21% of each run, Pallas kernels for 0% -> 0%
where the time goes in v12:
time: 197 us; the launch traced here: 196 us
  starting transfers between devices  75.7 us (38%)
  waiting for transfers between devices  72.4 us (37%)
  matrix products  21.9 us (11%)
  other arithmetic  15.8 us (8%)
  local copies, waits for them, and re-layouts  8.58 us (4%)
    ppermute x18, starting transfers between devices, step_x(): return lax.ppermute(block, 'x', [(i, (i + distance) % X) for i in range(X)])  28.1 us
    ppermute x18, waiting for transfers between devices, step_x(): return lax.ppermute(block, 'x', [(i, (i + distance) % X) for i in range(X)])  25.4 us
    dot_general x18, matrix products, contract(): lax.dot_general(first_op, second_op, (((first_dim,), (second_dim,)), ((),...  21.9 us
    all_to_all x2, starting transfers between devices, gather_wide(): lax.all_to_all(jnp.broadcast_to(block[None], (WIDE, rows, cols)), WIDE_AX...  17 us
    ppermute x4, waiting for transfers between devices, to_upper(): return lax.ppermute(block, CROSS_AXES, [(0, 3), (1, 2)])  15.6 us
    all_to_all x2, starting transfers between devices, spread_wide(): lax.all_to_all(partial.reshape(WIDE, rows // WIDE, cols), WIDE_AXES, 0, 0...  14.8 us
    all_to_all x2, waiting for transfers between devices, spread_wide(): lax.all_to_all(partial.reshape(WIDE, rows // WIDE, cols), WIDE_AXES, 0, 0...  11.6 us
    ppermute x3, starting transfers between devices, to_lower(): return lax.ppermute(block, CROSS_AXES, [(3, 0), (2, 1)])  9.63 us
  transfers between devices with their start and end apart: 40, of which 23 were waited for; matrix products, arithmetic and copies ran while one was open for 21% of the time, Pallas kernels for 0%

profile of v12, /device:TPU:56, one launch (start us, length us, event | category | flops | bytes accessed | tf_op | source)
XLA Modules:
  0.0 195.7 jit_solution(6246581210025360454)
XLA Ops:
  0.6 1.9 broadcast_in_dim.157
  2.6 9.6 %all-to-all-start = ((bf16[16,32,1024]{2,1,0:T(8,128)(2,1)}), bf16[16,32,1024]{2,1,0:T(8,128)(2,1)}, u32[]{:S(2)}, u32[]{:S(2)}) async-start(bf16[16,32,1024]{2,1,0:T(8,128)(2,1)} %broadcast_in_dim.157), calls=%async_computation | async-start | bytes 2097152 | tf_op jit(solution)/shard_map/all_to_all | solution.py:120
  12.2 1.3 fusion.82
  16.3 1.2 collective-permute-done
  17.5 1.2 maximum_add_fusion
  19.5 3.0 %collective-permute-start.3 = (bf16[128,512]{1,0:T(8,128)(2,1)}, bf16[128,512]{1,0:T(8,128)(2,1)S(1)}, u32[]{:S(2)}, u32[]{:S(2)}) collective-permute-start(bf16[128,512]{1,0:T(8,128)(2,1)} %get-tuple-element.60), channel_id=1, source_target_pairs={{0,4},{2,6},{4,0},{6,2},{1,5},{3,7},{5,1},{7,3},{8,12},{10,14},{12... | collective-permute-start | bytes 393224 | tf_op jit(solution)/shard_map/ppermute | solution.py:71
  22.6 1.1 collective-permute-start.2
  24.7 2.9 %collective-permute-done.3 = bf16[128,512]{1,0:T(8,128)(2,1)S(1)} collective-permute-done((bf16[128,512]{1,0:T(8,128)(2,1)}, bf16[128,512]{1,0:T(8,128)(2,1)S(1)}, u32[]{:S(2)}, u32[]{:S(2)}) %collective-permute-start.3) | collective-permute-done | bytes 131104 | tf_op jit(solution)/shard_map/ppermute | solution.py:71
  27.6 2.1 %collective-permute-done.2 = bf16[128,512]{1,0:T(8,128)(2,1)S(1)} collective-permute-done((bf16[128,512]{1,0:T(8,128)(2,1)}, bf16[128,512]{1,0:T(8,128)(2,1)S(1)}, u32[]{:S(2)}, u32[]{:S(2)}) %collective-permute-start.2) | collective-permute-done | bytes 131104 | tf_op jit(solution)/shard_map/ppermute | solution.py:71
  30.3 1.2 fusion.60
  31.5 1.5 collective-permute-start.10
  33.0 2.7 %collective-permute-start.9 = (bf16[128,512]{1,0:T(8,128)(2,1)S(1)}, bf16[128,512]{1,0:T(8,128)(2,1)S(1)}, u32[]{:S(2)}, u32[]{:S(2)}) collective-permute-start(bf16[128,512]{1,0:T(8,128)(2,1)S(1)} %get-tuple-element.49), channel_id=1, source_target_pairs={{0,4},{2,6},{4,0},{6,2},{1,5},{3,7},{5,1},{7,3},{8,12},{10,14},{12... | collective-permute-start | bytes 393224 | tf_op jit(solution)/shard_map/ppermute | solution.py:71
  36.6 1.8 all-to-all-done
  38.5 1.3 fusion.81
  39.8 1.9 convolution_convert_fusion.5
  42.4 1.9 fusion.20
  44.4 2.9 %collective-permute-start.14 = (bf16[256,512]{1,0:T(8,128)(2,1)S(1)}, bf16[256,512]{1,0:T(8,128)(2,1)S(1)}, u32[]{:S(2)}, u32[]{:S(2)}) collective-permute-start(bf16[256,512]{1,0:T(8,128)(2,1)S(1)} %fusion.54), channel_id=1, source_target_pairs={{0,4},{2,6},{4,0},{6,2},{1,5},{3,7},{5,1},{7,3},{8,12},{10,14},{12... | collective-permute-start | bytes 786440 | tf_op jit(solution)/shard_map/ppermute | solution.py:71
  47.3 1.1 collective-permute-start.13
  49.3 1.3 collective-permute-start.18
  50.6 1.8 convolution_convert_fusion.6
  52.7 2.4 %collective-permute-done.14 = bf16[256,512]{1,0:T(8,128)(2,1)S(1)} collective-permute-done((bf16[256,512]{1,0:T(8,128)(2,1)S(1)}, bf16[256,512]{1,0:T(8,128)(2,1)S(1)}, u32[]{:S(2)}, u32[]{:S(2)}) %collective-permute-start.14) | collective-permute-done | bytes 262176 | tf_op jit(solution)/shard_map/ppermute | solution.py:71
  55.1 5.1 %collective-permute-done.13 = bf16[256,512]{1,0:T(8,128)(2,1)S(1)} collective-permute-done((bf16[256,512]{1,0:T(8,128)(2,1)S(1)}, bf16[256,512]{1,0:T(8,128)(2,1)S(1)}, u32[]{:S(2)}, u32[]{:S(2)}) %collective-permute-start.13) | collective-permute-done | bytes 262176 | tf_op jit(solution)/shard_map/ppermute | solution.py:71
  60.5 1.7 fusion.53
  62.2 3.1 %collective-permute-start.7 = (bf16[256,512]{1,0:T(8,128)(2,1)S(1)}, bf16[256,512]{1,0:T(8,128)(2,1)S(1)}, u32[]{:S(2)}, u32[]{:S(2)}) collective-permute-start(bf16[256,512]{1,0:T(8,128)(2,1)S(1)} %get-tuple-element.64), channel_id=1, source_target_pairs={{0,4},{2,6},{4,0},{6,2},{1,5},{3,7},{5,1},{7,3},{8,12},{10,14},{12... | collective-permute-start | bytes 786440 | tf_op jit(solution)/shard_map/ppermute | solution.py:71
  65.3 1.1 collective-permute-start.6
  67.9 1.3 fusion.1
  69.1 3.0 %collective-permute-start.17 = (bf16[256,1024]{1,0:T(8,128)(2,1)}, bf16[256,1024]{1,0:T(8,128)(2,1)}, u32[]{:S(2)}, u32[]{:S(2)}) collective-permute-start(bf16[256,1024]{1,0:T(8,128)(2,1)} %fusion.1), channel_id=1, source_target_pairs={{192,0},{128,64},{193,1},{129,65},{194,2},{130,66},{195,3},{131,67... | collective-permute-start | bytes 1572872 | tf_op jit(solution)/shard_map/ppermute | solution.py:47
  73.0 5.1 %collective-permute-done.6 = bf16[256,512]{1,0:T(8,128)(2,1)S(1)} collective-permute-done((bf16[256,512]{1,0:T(8,128)(2,1)S(1)}, bf16[256,512]{1,0:T(8,128)(2,1)S(1)}, u32[]{:S(2)}, u32[]{:S(2)}) %collective-permute-start.6) | collective-permute-done | bytes 262176 | tf_op jit(solution)/shard_map/ppermute | solution.py:71
  78.6 1.4 collective-permute-done.15
  80.5 2.2 %collective-permute-done.17 = bf16[256,1024]{1,0:T(8,128)(2,1)} collective-permute-done((bf16[256,1024]{1,0:T(8,128)(2,1)}, bf16[256,1024]{1,0:T(8,128)(2,1)}, u32[]{:S(2)}, u32[]{:S(2)}) %collective-permute-start.17) | collective-permute-done | bytes 524320 | tf_op jit(solution)/shard_map/ppermute | solution.py:47
  82.6 1.3 fusion.3
  83.9 6.5 %all-to-all-start.1 = ((bf16[16,16,1024]{2,1,0:T(8,128)(2,1)}), bf16[16,16,1024]{2,1,0:T(8,128)(2,1)S(1)}, u32[]{:S(2)}, u32[]{:S(2)}) async-start(bf16[16,16,1024]{2,1,0:T(8,128)(2,1)} %bitcast.143), calls=%async_computation.1 | async-start | bytes 1048576 | tf_op jit(solution)/shard_map/all_to_all | solution.py:109
  90.4 1.5 slice_bitcast_fusion
  91.9 1.3 collective-permute-start.19
  93.2 8.0 %collective-permute-done.18 = bf16[1024,1024]{1,0:T(8,128)(2,1)} collective-permute-done((bf16[1024,1024]{1,0:T(8,128)(2,1)}, bf16[1024,1024]{1,0:T(8,128)(2,1)}, u32[]{:S(2)}, u32[]{:S(2)}) %collective-permute-start.18) | collective-permute-done | bytes 2097184 | tf_op jit(solution)/shard_map/ppermute | solution.py:43
  101.2 1.3 collective-permute-start.30
  102.5 3.8 %broadcast_select_fusion = bf16[1024,1024]{1,0:T(8,128)(2,1)} fusion(bf16[1024,1024]{1,0:T(8,128)(2,1)} %collective-permute-done.18, pred[]{:T(512)S(6)} %eq.35, bf16[1,1024,1024]{2,1,0:T(8,128)(2,1)} %param.7), kind=kLoop, calls=%fused_computation.1 | loop fusion | flops 1048576 | bytes 6291457 | tf_op jit(solution)/shard_map/jit(_where)/select_n | solution.py:146
  108.1 7.3 %all-to-all-start.2 = ((bf16[16,16,1024]{2,1,0:T(8,128)(2,1)}), bf16[16,16,1024]{2,1,0:T(8,128)(2,1)S(1)}, u32[]{:S(2)}, u32[]{:S(2)}) async-start(bf16[16,16,1024]{2,1,0:T(8,128)(2,1)} %broadcast_in_dim.175), calls=%async_computation.2 | async-start | bytes 1048576 | tf_op jit(solution)/shard_map/all_to_all | solution.py:120
  115.4 1.5 collective-permute-done.21
  116.9 0.9 broadcast_select_fusion.12
  117.8 1.0 collective-permute-start.24
  118.8 3.6 %collective-permute-start.23 = (bf16[128,1024]{1,0:T(8,128)(2,1)S(1)}, bf16[128,1024]{1,0:T(8,128)(2,1)S(1)}, u32[]{:S(2)}, u32[]{:S(2)}) collective-permute-start(bf16[128,1024]{1,0:T(8,128)(2,1)S(1)} %pad_maximum_fusion.2), channel_id=1, source_target_pairs={{0,4},{2,6},{4,0},{6,2},{1,5},{3,7},{5,1},{7,3},{8,12},{10,14},{12... | collective-permute-start | bytes 786440 | tf_op jit(solution)/shard_map/ppermute | solution.py:71
  122.4 5.6 %collective-permute-done.30 = bf16[512,1024]{1,0:T(8,128)(2,1)} collective-permute-done((bf16[512,1024]{1,0:T(8,128)(2,1)}, bf16[512,1024]{1,0:T(8,128)(2,1)}, u32[]{:S(2)}, u32[]{:S(2)}) %collective-permute-start.30) | collective-permute-done | bytes 1048608 | tf_op jit(solution)/shard_map/ppermute | solution.py:43
  128.0 1.3 collective-permute-start.31
  129.3 5.1 %collective-permute-done.23 = bf16[128,1024]{1,0:T(8,128)(2,1)S(1)} collective-permute-done((bf16[128,1024]{1,0:T(8,128)(2,1)S(1)}, bf16[128,1024]{1,0:T(8,128)(2,1)S(1)}, u32[]{:S(2)}, u32[]{:S(2)}) %collective-permute-start.23) | collective-permute-done | bytes 262176 | tf_op jit(solution)/shard_map/ppermute | solution.py:71
  134.3 1.3 fusion.17
  135.6 5.3 %collective-permute-start.29 = (bf16[256,1024]{1,0:T(8,128)(2,1)S(1)}, bf16[256,1024]{1,0:T(8,128)(2,1)S(1)}, u32[]{:S(2)}, u32[]{:S(2)}) collective-permute-start(bf16[256,1024]{1,0:T(8,128)(2,1)S(1)} %bitcast.129), channel_id=1, source_target_pairs={{192,0},{128,64},{193,1},{129,65},{194,2},{130,66},{195,3},{131,67... | collective-permute-start | bytes 1572872 | tf_op jit(solution)/shard_map/ppermute | solution.py:47
  141.0 1.7 convolution_convert_fusion.4
  142.9 1.4 collective-permute-done.25
  144.9 1.0 collective-permute-start.28
  145.9 2.0 %collective-permute-start.27 = (bf16[256,512]{1,0:T(8,128)(2,1)S(1)}, bf16[256,512]{1,0:T(8,128)(2,1)S(1)}, u32[]{:S(2)}, u32[]{:S(2)}) collective-permute-start(bf16[256,512]{1,0:T(8,128)(2,1)S(1)} %get-tuple-element.66), channel_id=1, source_target_pairs={{0,6},{2,0},{4,2},{6,4},{1,7},{3,1},{5,3},{7,5},{8,14},{10,8},{12,... | collective-permute-start | bytes 786440 | tf_op jit(solution)/shard_map/ppermute | solution.py:71
  148.2 3.4 %collective-permute-done.29 = bf16[256,1024]{1,0:T(8,128)(2,1)S(1)} collective-permute-done((bf16[256,1024]{1,0:T(8,128)(2,1)S(1)}, bf16[256,1024]{1,0:T(8,128)(2,1)S(1)}, u32[]{:S(2)}, u32[]{:S(2)}) %collective-permute-start.29) | collective-permute-done | bytes 524320 | tf_op jit(solution)/shard_map/ppermute | solution.py:47
  151.8 2.0 %collective-permute-done.31 = bf16[512,1024]{1,0:T(8,128)(2,1)} collective-permute-done((bf16[512,1024]{1,0:T(8,128)(2,1)}, bf16[512,1024]{1,0:T(8,128)(2,1)}, u32[]{:S(2)}, u32[]{:S(2)}) %collective-permute-start.31) | collective-permute-done | bytes 1048608 | tf_op jit(solution)/shard_map/ppermute | solution.py:43
  153.8 2.6 %convolution_convert_fusion.1 = bf16[1024,1024]{1,0:T(8,128)(2,1)} fusion(bf16[512,1024]{1,0:T(8,128)(2,1)S(1)} %copy-done.12, bf16[512,1024]{1,0:T(8,128)(2,1)S(1)} %pad_maximum_fusion), kind=kOutput, calls=%fused_computation.3 | convolution fusion | flops 1074790400 | bytes 4194304 | tf_op jit(solution)/shard_map/dot_general | solution.py:26
  156.4 2.6 %maximum_select_fusion = bf16[1024,1024]{1,0:T(8,128)(2,1)S(1)} fusion(bf16[512,1024]{1,0:T(8,128)(2,1)} %collective-permute-done.31, bf16[512,1024]{1,0:T(8,128)(2,1)} %collective-permute-done.30, bf16[1,1024,1024]{2,1,0:T(8,128)(2,1)S(1)} %copy-done, pred[]{:T(512)S(6)} %eq.35), kind=kLoop, calls=%fused_computation | loop fusion | flops 5242880 | bytes 6291457 | tf_op jit(solution)/shard_map/jit(_where)/select_n | solution.py:146
  159.0 1.2 collective-permute-done.27
  160.8 1.1 multiply_convert_fusion
  162.0 1.3 collective-permute-start.33
  163.8 1.3 fusion.2
  165.1 8.3 %all-to-all-start.3 = ((bf16[16,16,1024]{2,1,0:T(8,128)(2,1)}), bf16[16,16,1024]{2,1,0:T(8,128)(2,1)S(1)}, u32[]{:S(2)}, u32[]{:S(2)}) async-start(bf16[16,16,1024]{2,1,0:T(8,128)(2,1)} %bitcast.37), calls=%async_computation.3 | async-start | bytes 1048576 | tf_op jit(solution)/shard_map/all_to_all | solution.py:109
  173.7 1.4 collective-permute-done.34
  175.2 2.6 %convolution_convert_fusion = bf16[1024,1024]{1,0:T(8,128)(2,1)} fusion(bf16[256,1024]{1,0:T(8,128)(2,1)S(1)} %bitcast.142, bf16[256,1024]{1,0:T(8,128)(2,1)S(1)} %bitcast.139, bf16[256,512]{1,0:T(8,128)(2,1)S(1)} %get-tuple-element.54, bf16[256,512]{1,0:T(8,128)(2,1)S(1)} %get-tuple-element.53, bf16[256,512]{1,0:T(8,128)(2,1)S(1)} %get-tuple-element.52, ...), kind=kOutput, calls=%fused_computation.2 | convolution fusion | flops 1081081856 | bytes 4194304 | tf_op jit(solution)/shard_map/dot_general | solution.py:26
  177.8 11.6 %all-to-all-done.3 = bf16[16,16,1024]{2,1,0:T(8,128)(2,1)S(1)} async-done(((bf16[16,16,1024]{2,1,0:T(8,128)(2,1)}), bf16[16,16,1024]{2,1,0:T(8,128)(2,1)S(1)}, u32[]{:S(2)}, u32[]{:S(2)}) %all-to-all-start.3) | async-done | bytes 524320 | tf_op jit(solution)/shard_map/all_to_all | solution.py:109
  189.6 5.4 %collective-permute-done.35 = bf16[16,1024]{1,0:T(8,128)(2,1)S(1)} collective-permute-done((bf16[16,1024]{1,0:T(8,128)(2,1)S(1)}, bf16[16,1024]{1,0:T(8,128)(2,1)S(1)}, u32[]{:S(2)}, u32[]{:S(2)}) %collective-permute-start.35) | collective-permute-done | bytes 32800 | tf_op jit(solution)/shard_map/ppermute | solution.py:217
  (116 shorter events, 16.7 us)
Async XLA Ops:
  2.6 10.9 %copy-start = (bf16[1,1024,1024]{2,1,0:T(8,128)(2,1)S(1)}, bf16[1,1024,1024]{2,1,0:T(8,128)(2,1)}, u32[]{:S(2)}) copy-start(bf16[1,1024,1024]{2,1,0:T(8,128)(2,1)} %param.6) | copy-start | bytes 6291460
  2.6 35.9 %all-to-all-start = ((bf16[16,32,1024]{2,1,0:T(8,128)(2,1)}), bf16[16,32,1024]{2,1,0:T(8,128)(2,1)}, u32[]{:S(2)}, u32[]{:S(2)}) async-start(bf16[16,32,1024]{2,1,0:T(8,128)(2,1)} %broadcast_in_dim.157), calls=%async_computation | async-start | bytes 2097152 | tf_op jit(solution)/shard_map/all_to_all | solution.py:120
  13.5 1.9 copy-start.6
  13.5 2.3 %copy-start.4 = (bf16[16,1,16,1024]{3,2,1,0:T(8,128)(2,1)}, bf16[16,1,16,1024]{3,2,1,0:T(8,128)(2,1)S(1)}, u32[]{:S(2)}) copy-start(bf16[16,1,16,1024]{3,2,1,0:T(8,128)(2,1)S(1)} %get-tuple-element.57) | copy-start | bytes 1572868
  15.3 2.3 %collective-permute-start = (bf16[512,512]{1,0:T(8,128)(2,1)}, bf16[512,512]{1,0:T(8,128)(2,1)}, u32[]{:S(2)}, u32[]{:S(2)}) collective-permute-start(bf16[512,512]{1,0:T(8,128)(2,1)} %pad_maximum_fusion.1), channel_id=1, source_target_pairs={{0,1},{1,0},{2,3},{3,2},{4,5},{5,4},{6,7},{7,6},{8,9},{9,8},{10,11... | collective-permute-start | bytes 1572872 | tf_op jit(solution)/shard_map/ppermute | solution.py:39
  19.5 8.1 %collective-permute-start.3 = (bf16[128,512]{1,0:T(8,128)(2,1)}, bf16[128,512]{1,0:T(8,128)(2,1)S(1)}, u32[]{:S(2)}, u32[]{:S(2)}) collective-permute-start(bf16[128,512]{1,0:T(8,128)(2,1)} %get-tuple-element.60), channel_id=1, source_target_pairs={{0,4},{2,6},{4,0},{6,2},{1,5},{3,7},{5,1},{7,3},{8,12},{10,14},{12... | collective-permute-start | bytes 393224 | tf_op jit(solution)/shard_map/ppermute | solution.py:71
  22.6 7.1 %collective-permute-start.2 = (bf16[128,512]{1,0:T(8,128)(2,1)}, bf16[128,512]{1,0:T(8,128)(2,1)S(1)}, u32[]{:S(2)}, u32[]{:S(2)}) collective-permute-start(bf16[128,512]{1,0:T(8,128)(2,1)} %get-tuple-element.61), channel_id=1, source_target_pairs={{0,6},{2,0},{4,2},{6,4},{1,7},{3,1},{5,3},{7,5},{8,14},{10,8},{12,... | collective-permute-start | bytes 393224 | tf_op jit(solution)/shard_map/ppermute | solution.py:71
  23.7 6.6 %collective-permute-start.1 = (bf16[128,512]{1,0:T(8,128)(2,1)S(1)}, bf16[128,512]{1,0:T(8,128)(2,1)}, u32[]{:S(2)}, u32[]{:S(2)}) collective-permute-start(bf16[128,512]{1,0:T(8,128)(2,1)S(1)} %get-tuple-element.59), channel_id=1, source_target_pairs={{0,2},{2,4},{4,6},{6,0},{1,3},{3,5},{5,7},{7,1},{8,10},{10,12},{12... | collective-permute-start | bytes 393224 | tf_op jit(solution)/shard_map/ppermute | solution.py:71
  29.7 0.7 copy-start.21
  31.5 10.3 %collective-permute-start.10 = (bf16[128,512]{1,0:T(8,128)(2,1)S(1)}, bf16[128,512]{1,0:T(8,128)(2,1)S(1)}, u32[]{:S(2)}, u32[]{:S(2)}) collective-permute-start(bf16[128,512]{1,0:T(8,128)(2,1)S(1)} %get-tuple-element.49), channel_id=1, source_target_pairs={{0,2},{2,4},{4,6},{6,0},{1,3},{3,5},{5,7},{7,1},{8,10},{10,12},{12... | collective-permute-start | bytes 393224 | tf_op jit(solution)/shard_map/ppermute | solution.py:71
  33.0 9.0 %collective-permute-start.9 = (bf16[128,512]{1,0:T(8,128)(2,1)S(1)}, bf16[128,512]{1,0:T(8,128)(2,1)S(1)}, u32[]{:S(2)}, u32[]{:S(2)}) collective-permute-start(bf16[128,512]{1,0:T(8,128)(2,1)S(1)} %get-tuple-element.49), channel_id=1, source_target_pairs={{0,4},{2,6},{4,0},{6,2},{1,5},{3,7},{5,1},{7,3},{8,12},{10,14},{12... | collective-permute-start | bytes 393224 | tf_op jit(solution)/shard_map/ppermute | solution.py:71
  35.7 6.3 %collective-permute-start.8 = (bf16[128,512]{1,0:T(8,128)(2,1)S(1)}, bf16[128,512]{1,0:T(8,128)(2,1)S(1)}, u32[]{:S(2)}, u32[]{:S(2)}) collective-permute-start(bf16[128,512]{1,0:T(8,128)(2,1)S(1)} %get-tuple-element.49), channel_id=1, source_target_pairs={{0,6},{2,0},{4,2},{6,4},{1,7},{3,1},{5,3},{7,5},{8,14},{10,8},{12,... | collective-permute-start | bytes 393224 | tf_op jit(solution)/shard_map/ppermute | solution.py:71
  39.8 20.8 %copy-start.2 = (bf16[16,1,16,1024]{3,2,1,0:T(8,128)(2,1)}, bf16[16,1,16,1024]{3,2,1,0:T(8,128)(2,1)S(1)}, u32[]{:S(2)}) copy-start(bf16[16,1,16,1024]{3,2,1,0:T(8,128)(2,1)S(1)} %get-tuple-element.55) | copy-start | bytes 1572868
  41.7 2.6 %collective-permute-start.11 = (bf16[256,512]{1,0:T(8,128)(2,1)S(1)}, bf16[256,512]{1,0:T(8,128)(2,1)S(1)}, u32[]{:S(2)}, u32[]{:S(2)}) collective-permute-start(bf16[256,512]{1,0:T(8,128)(2,1)S(1)} %convolution_convert_fusion.5), channel_id=1, source_target_pairs={{0,1},{1,0},{2,3},{3,2},{4,5},{5,4},{6,7},{7,6},{8,9},{9,8},{10,11... | collective-permute-start | bytes 786440 | tf_op jit(solution)/shard_map/ppermute | solution.py:39
  42.3 17.8 %copy-start.8 = (bf16[512,512]{1,0:T(8,128)(2,1)}, bf16[512,512]{1,0:T(8,128)(2,1)S(1)}, u32[]{:S(2)}) copy-start(bf16[512,512]{1,0:T(8,128)(2,1)S(1)} %fusion.52) | copy-start | bytes 1572868
  44.4 10.7 %collective-permute-start.14 = (bf16[256,512]{1,0:T(8,128)(2,1)S(1)}, bf16[256,512]{1,0:T(8,128)(2,1)S(1)}, u32[]{:S(2)}, u32[]{:S(2)}) collective-permute-start(bf16[256,512]{1,0:T(8,128)(2,1)S(1)} %fusion.54), channel_id=1, source_target_pairs={{0,4},{2,6},{4,0},{6,2},{1,5},{3,7},{5,1},{7,3},{8,12},{10,14},{12... | collective-permute-start | bytes 786440 | tf_op jit(solution)/shard_map/ppermute | solution.py:71
  47.3 12.9 %collective-permute-start.13 = (bf16[256,512]{1,0:T(8,128)(2,1)S(1)}, bf16[256,512]{1,0:T(8,128)(2,1)S(1)}, u32[]{:S(2)}, u32[]{:S(2)}) collective-permute-start(bf16[256,512]{1,0:T(8,128)(2,1)S(1)} %fusion.54), channel_id=1, source_target_pairs={{0,6},{2,0},{4,2},{6,4},{1,7},{3,1},{5,3},{7,5},{8,14},{10,8},{12,... | collective-permute-start | bytes 786440 | tf_op jit(solution)/shard_map/ppermute | solution.py:71
  48.4 11.8 %collective-permute-start.12 = (bf16[256,512]{1,0:T(8,128)(2,1)S(1)}, bf16[256,512]{1,0:T(8,128)(2,1)S(1)}, u32[]{:S(2)}, u32[]{:S(2)}) collective-permute-start(bf16[256,512]{1,0:T(8,128)(2,1)S(1)} %fusion.54), channel_id=1, source_target_pairs={{0,2},{2,4},{4,6},{6,0},{1,3},{3,5},{5,7},{7,1},{8,10},{10,12},{12... | collective-permute-start | bytes 786440 | tf_op jit(solution)/shard_map/ppermute | solution.py:71
  49.3 52.0 %collective-permute-start.18 = (bf16[1024,1024]{1,0:T(8,128)(2,1)}, bf16[1024,1024]{1,0:T(8,128)(2,1)}, u32[]{:S(2)}, u32[]{:S(2)}) collective-permute-start(bf16[1024,1024]{1,0:T(8,128)(2,1)} %bitcast.28), channel_id=1, source_target_pairs={{0,192},{64,128},{1,193},{65,129},{2,194},{66,130},{3,195},{67,131... | collective-permute-start | bytes 6291464 | tf_op jit(solution)/shard_map/ppermute | solution.py:43
  50.6 27.5 %copy-start.17 = (bf16[256,512]{1,0:T(8,128)(2,1)}, bf16[256,512]{1,0:T(8,128)(2,1)S(1)}, u32[]{:S(2)}) copy-start(bf16[256,512]{1,0:T(8,128)(2,1)S(1)} %slice.44) | copy-start | bytes 786436
  52.4 8.1 %collective-permute-start.4 = (bf16[256,512]{1,0:T(8,128)(2,1)S(1)}, bf16[256,512]{1,0:T(8,128)(2,1)S(1)}, u32[]{:S(2)}, u32[]{:S(2)}) collective-permute-start(bf16[256,512]{1,0:T(8,128)(2,1)S(1)} %convolution_convert_fusion.6), channel_id=1, source_target_pairs={{0,1},{1,0},{2,3},{3,2},{4,5},{5,4},{6,7},{7,6},{8,9},{9,8},{10,11... | collective-permute-start | bytes 786440 | tf_op jit(solution)/shard_map/ppermute | solution.py:39
  60.4 7.0 %collective-permute-start.16 = (bf16[256,512]{1,0:T(8,128)(2,1)S(1)}, bf16[256,512]{1,0:T(8,128)(2,1)S(1)}, u32[]{:S(2)}, u32[]{:S(2)}) collective-permute-start(bf16[256,512]{1,0:T(8,128)(2,1)S(1)} %multiply_convert_fusion.2), channel_id=1, source_target_pairs={{0,1},{1,0},{2,3},{3,2},{4,5},{5,4},{6,7},{7,6},{8,9},{9,8},{10,11... | collective-permute-start | bytes 786440 | tf_op jit(solution)/shard_map/ppermute | solution.py:39
  62.2 10.7 %collective-permute-start.7 = (bf16[256,512]{1,0:T(8,128)(2,1)S(1)}, bf16[256,512]{1,0:T(8,128)(2,1)S(1)}, u32[]{:S(2)}, u32[]{:S(2)}) collective-permute-start(bf16[256,512]{1,0:T(8,128)(2,1)S(1)} %get-tuple-element.64), channel_id=1, source_target_pairs={{0,4},{2,6},{4,0},{6,2},{1,5},{3,7},{5,1},{7,3},{8,12},{10,14},{12... | collective-permute-start | bytes 786440 | tf_op jit(solution)/shard_map/ppermute | solution.py:71
  65.3 12.8 %collective-permute-start.6 = (bf16[256,512]{1,0:T(8,128)(2,1)S(1)}, bf16[256,512]{1,0:T(8,128)(2,1)S(1)}, u32[]{:S(2)}, u32[]{:S(2)}) collective-permute-start(bf16[256,512]{1,0:T(8,128)(2,1)S(1)} %get-tuple-element.64), channel_id=1, source_target_pairs={{0,6},{2,0},{4,2},{6,4},{1,7},{3,1},{5,3},{7,5},{8,14},{10,8},{12,... | collective-permute-start | bytes 786440 | tf_op jit(solution)/shard_map/ppermute | solution.py:71
  66.5 11.7 %collective-permute-start.5 = (bf16[256,512]{1,0:T(8,128)(2,1)S(1)}, bf16[256,512]{1,0:T(8,128)(2,1)S(1)}, u32[]{:S(2)}, u32[]{:S(2)}) collective-permute-start(bf16[256,512]{1,0:T(8,128)(2,1)S(1)} %get-tuple-element.64), channel_id=1, source_target_pairs={{0,2},{2,4},{4,6},{6,0},{1,3},{3,5},{5,7},{7,1},{8,10},{10,12},{12... | collective-permute-start | bytes 786440 | tf_op jit(solution)/shard_map/ppermute | solution.py:71
  67.4 1.8 copy-start.13
  69.1 13.5 %collective-permute-start.17 = (bf16[256,1024]{1,0:T(8,128)(2,1)}, bf16[256,1024]{1,0:T(8,128)(2,1)}, u32[]{:S(2)}, u32[]{:S(2)}) collective-permute-start(bf16[256,1024]{1,0:T(8,128)(2,1)} %fusion.1), channel_id=1, source_target_pairs={{192,0},{128,64},{193,1},{129,65},{194,2},{130,66},{195,3},{131,67... | collective-permute-start | bytes 1572872 | tf_op jit(solution)/shard_map/ppermute | solution.py:47
  78.4 5.6 %copy-start.10 = (bf16[256,512]{1,0:T(8,128)(2,1)}, bf16[256,512]{1,0:T(8,128)(2,1)S(1)}, u32[]{:S(2)}) copy-start(bf16[256,512]{1,0:T(8,128)(2,1)S(1)} %multiply_convert_fusion.1) | copy-start | bytes 786436
  78.4 1.6 collective-permute-start.15
  80.0 3.9 %copy-start.15 = (bf16[256,512]{1,0:T(8,128)(2,1)}, bf16[256,512]{1,0:T(8,128)(2,1)S(1)}, u32[]{:S(2)}) copy-start(bf16[256,512]{1,0:T(8,128)(2,1)S(1)} %collective-permute-done.15) | copy-start | bytes 786436
  83.9 22.4 %all-to-all-start.1 = ((bf16[16,16,1024]{2,1,0:T(8,128)(2,1)}), bf16[16,16,1024]{2,1,0:T(8,128)(2,1)S(1)}, u32[]{:S(2)}, u32[]{:S(2)}) async-start(bf16[16,16,1024]{2,1,0:T(8,128)(2,1)} %bitcast.143), calls=%async_computation.1 | async-start | bytes 1048576 | tf_op jit(solution)/shard_map/all_to_all | solution.py:109
  90.4 1.5 copy-start.18
  91.9 14.4 %collective-permute-start.19 = (bf16[256,512]{1,0:T(8,128)(2,1)S(1)}, bf16[256,512]{1,0:T(8,128)(2,1)}, u32[]{:S(2)}, u32[]{:S(2)}) collective-permute-start(bf16[256,512]{1,0:T(8,128)(2,1)S(1)} %copy-done.18), channel_id=1, source_target_pairs={{0,192},{64,128},{1,193},{65,129},{2,194},{66,130},{3,195},{67,131... | collective-permute-start | bytes 786440 | tf_op jit(solution)/shard_map/ppermute | solution.py:43
  101.2 26.7 %collective-permute-start.30 = (bf16[512,1024]{1,0:T(8,128)(2,1)}, bf16[512,1024]{1,0:T(8,128)(2,1)}, u32[]{:S(2)}, u32[]{:S(2)}) collective-permute-start(bf16[512,1024]{1,0:T(8,128)(2,1)} %get-tuple-element.35), channel_id=1, source_target_pairs={{0,192},{64,128},{1,193},{65,129},{2,194},{66,130},{3,195},{67,131... | collective-permute-start | bytes 3145736 | tf_op jit(solution)/shard_map/ppermute | solution.py:43
  107.2 0.9 copy-start.19
  108.1 27.6 %all-to-all-start.2 = ((bf16[16,16,1024]{2,1,0:T(8,128)(2,1)}), bf16[16,16,1024]{2,1,0:T(8,128)(2,1)S(1)}, u32[]{:S(2)}, u32[]{:S(2)}) async-start(bf16[16,16,1024]{2,1,0:T(8,128)(2,1)} %broadcast_in_dim.175), calls=%async_computation.2 | async-start | bytes 1048576 | tf_op jit(solution)/shard_map/all_to_all | solution.py:120
  115.4 1.5 collective-permute-start.21
  117.8 11.4 %collective-permute-start.24 = (bf16[128,1024]{1,0:T(8,128)(2,1)S(1)}, bf16[128,1024]{1,0:T(8,128)(2,1)S(1)}, u32[]{:S(2)}, u32[]{:S(2)}) collective-permute-start(bf16[128,1024]{1,0:T(8,128)(2,1)S(1)} %pad_maximum_fusion.2), channel_id=1, source_target_pairs={{0,2},{2,4},{4,6},{6,0},{1,3},{3,5},{5,7},{7,1},{8,10},{10,12},{12... | collective-permute-start | bytes 786440 | tf_op jit(solution)/shard_map/ppermute | solution.py:71
  118.8 15.5 %collective-permute-start.23 = (bf16[128,1024]{1,0:T(8,128)(2,1)S(1)}, bf16[128,1024]{1,0:T(8,128)(2,1)S(1)}, u32[]{:S(2)}, u32[]{:S(2)}) collective-permute-start(bf16[128,1024]{1,0:T(8,128)(2,1)S(1)} %pad_maximum_fusion.2), channel_id=1, source_target_pairs={{0,4},{2,6},{4,0},{6,2},{1,5},{3,7},{5,1},{7,3},{8,12},{10,14},{12... | collective-permute-start | bytes 786440 | tf_op jit(solution)/shard_map/ppermute | solution.py:71
  122.4 12.0 %collective-permute-start.22 = (bf16[128,1024]{1,0:T(8,128)(2,1)S(1)}, bf16[128,1024]{1,0:T(8,128)(2,1)S(1)}, u32[]{:S(2)}, u32[]{:S(2)}) collective-permute-start(bf16[128,1024]{1,0:T(8,128)(2,1)S(1)} %pad_maximum_fusion.2), channel_id=1, source_target_pairs={{0,6},{2,0},{4,2},{6,4},{1,7},{3,1},{5,3},{7,5},{8,14},{10,8},{12,... | collective-permute-start | bytes 786440 | tf_op jit(solution)/shard_map/ppermute | solution.py:71
  128.0 25.8 %collective-permute-start.31 = (bf16[512,1024]{1,0:T(8,128)(2,1)}, bf16[512,1024]{1,0:T(8,128)(2,1)}, u32[]{:S(2)}, u32[]{:S(2)}) collective-permute-start(bf16[512,1024]{1,0:T(8,128)(2,1)} %get-tuple-element.36), channel_id=1, source_target_pairs={{0,192},{64,128},{1,193},{65,129},{2,194},{66,130},{3,195},{67,131... | collective-permute-start | bytes 3145736 | tf_op jit(solution)/shard_map/ppermute | solution.py:43
  135.6 8.7 %copy-start.1 = (bf16[1024,1024]{1,0:T(8,128)(2,1)S(1)}, bf16[1024,1024]{1,0:T(8,128)(2,1)}, u32[]{:S(2)}) copy-start(bf16[1024,1024]{1,0:T(8,128)(2,1)} %broadcast_select_fusion) | copy-start | bytes 6291460
  135.6 16.0 %collective-permute-start.29 = (bf16[256,1024]{1,0:T(8,128)(2,1)S(1)}, bf16[256,1024]{1,0:T(8,128)(2,1)S(1)}, u32[]{:S(2)}, u32[]{:S(2)}) collective-permute-start(bf16[256,1024]{1,0:T(8,128)(2,1)S(1)} %bitcast.129), channel_id=1, source_target_pairs={{192,0},{128,64},{193,1},{129,65},{194,2},{130,66},{195,3},{131,67... | collective-permute-start | bytes 1572872 | tf_op jit(solution)/shard_map/ppermute | solution.py:47
  142.7 8.9 %copy-start.3 = (bf16[16,1,16,1024]{3,2,1,0:T(8,128)(2,1)S(1)}, bf16[16,1,16,1024]{3,2,1,0:T(8,128)(2,1)}, u32[]{:S(2)}) copy-start(bf16[16,1,16,1024]{3,2,1,0:T(8,128)(2,1)} %copy-done.2) | copy-start | bytes 1572868
  142.7 1.6 collective-permute-start.25
  144.9 8.9 %copy-start.12 = (bf16[512,1024]{1,0:T(8,128)(2,1)S(1)}, bf16[512,1024]{1,0:T(8,128)(2,1)}, u32[]{:S(2)}) copy-start(bf16[512,1024]{1,0:T(8,128)(2,1)} %fusion.17) | copy-start | bytes 3145732
  144.9 14.1 %collective-permute-start.28 = (bf16[256,512]{1,0:T(8,128)(2,1)S(1)}, bf16[256,512]{1,0:T(8,128)(2,1)S(1)}, u32[]{:S(2)}, u32[]{:S(2)}) collective-permute-start(bf16[256,512]{1,0:T(8,128)(2,1)S(1)} %get-tuple-element.66), channel_id=1, source_target_pairs={{0,4},{2,6},{4,0},{6,2},{1,5},{3,7},{5,1},{7,3},{8,12},{10,14},{12... | collective-permute-start | bytes 786440 | tf_op jit(solution)/shard_map/ppermute | solution.py:71
  145.9 14.3 %collective-permute-start.27 = (bf16[256,512]{1,0:T(8,128)(2,1)S(1)}, bf16[256,512]{1,0:T(8,128)(2,1)S(1)}, u32[]{:S(2)}, u32[]{:S(2)}) collective-permute-start(bf16[256,512]{1,0:T(8,128)(2,1)S(1)} %get-tuple-element.66), channel_id=1, source_target_pairs={{0,6},{2,0},{4,2},{6,4},{1,7},{3,1},{5,3},{7,5},{8,14},{10,8},{12,... | collective-permute-start | bytes 786440 | tf_op jit(solution)/shard_map/ppermute | solution.py:71
  147.9 12.7 %collective-permute-start.26 = (bf16[256,512]{1,0:T(8,128)(2,1)S(1)}, bf16[256,512]{1,0:T(8,128)(2,1)S(1)}, u32[]{:S(2)}, u32[]{:S(2)}) collective-permute-start(bf16[256,512]{1,0:T(8,128)(2,1)S(1)} %get-tuple-element.66), channel_id=1, source_target_pairs={{0,2},{2,4},{4,6},{6,0},{1,3},{3,5},{5,7},{7,1},{8,10},{10,12},{12... | collective-permute-start | bytes 786440 | tf_op jit(solution)/shard_map/ppermute | solution.py:71
  156.4 4.4 %copy-start.9 = (bf16[512,512]{1,0:T(8,128)(2,1)S(1)}, bf16[512,512]{1,0:T(8,128)(2,1)}, u32[]{:S(2)}) copy-start(bf16[512,512]{1,0:T(8,128)(2,1)} %copy-done.8) | copy-start | bytes 1572868
  161.9 1.9 collective-permute-start.32
  162.0 11.5 %collective-permute-start.33 = (bf16[256,512]{1,0:T(8,128)(2,1)S(1)}, bf16[256,512]{1,0:T(8,128)(2,1)S(1)}, u32[]{:S(2)}, u32[]{:S(2)}) collective-permute-start(bf16[256,512]{1,0:T(8,128)(2,1)S(1)} %multiply_convert_fusion), channel_id=1, source_target_pairs={{192,0},{128,64},{193,1},{129,65},{194,2},{130,66},{195,3},{131,67... | collective-permute-start | bytes 786440 | tf_op jit(solution)/shard_map/ppermute | solution.py:47
  163.8 9.6 %copy-start.20 = (bf16[16,1024]{1,0:T(8,128)(2,1)S(1)}, bf16[16,1024]{1,0:T(8,128)(2,1)}, u32[]{:S(2)}) copy-start(bf16[16,1024]{1,0:T(8,128)(2,1)} %copy-done.19) | copy-start | bytes 98308
  163.8 9.8 %copy-start.14 = (bf16[256,512]{1,0:T(8,128)(2,1)S(1)}, bf16[256,512]{1,0:T(8,128)(2,1)}, u32[]{:S(2)}) copy-start(bf16[256,512]{1,0:T(8,128)(2,1)} %copy-done.13) | copy-start | bytes 786436
  163.8 11.3 %copy-start.11 = (bf16[256,512]{1,0:T(8,128)(2,1)S(1)}, bf16[256,512]{1,0:T(8,128)(2,1)}, u32[]{:S(2)}) copy-start(bf16[256,512]{1,0:T(8,128)(2,1)} %copy-done.10) | copy-start | bytes 786436
  163.8 11.3 %copy-start.16 = (bf16[256,512]{1,0:T(8,128)(2,1)S(1)}, bf16[256,512]{1,0:T(8,128)(2,1)}, u32[]{:S(2)}) copy-start(bf16[256,512]{1,0:T(8,128)(2,1)} %copy-done.15) | copy-start | bytes 786436
  165.1 10.1 %copy-start.5 = (bf16[16,1,16,1024]{3,2,1,0:T(8,128)(2,1)S(1)}, bf16[16,1,16,1024]{3,2,1,0:T(8,128)(2,1)}, u32[]{:S(2)}) copy-start(bf16[16,1,16,1024]{3,2,1,0:T(8,128)(2,1)} %copy-done.4) | copy-start | bytes 1572868
  165.1 10.1 %copy-start.7 = (bf16[16,1,16,1024]{3,2,1,0:T(8,128)(2,1)S(1)}, bf16[16,1,16,1024]{3,2,1,0:T(8,128)(2,1)}, u32[]{:S(2)}) copy-start(bf16[16,1,16,1024]{3,2,1,0:T(8,128)(2,1)} %copy-done.6) | copy-start | bytes 1572868
  165.1 24.3 %all-to-all-start.3 = ((bf16[16,16,1024]{2,1,0:T(8,128)(2,1)}), bf16[16,16,1024]{2,1,0:T(8,128)(2,1)S(1)}, u32[]{:S(2)}, u32[]{:S(2)}) async-start(bf16[16,16,1024]{2,1,0:T(8,128)(2,1)} %bitcast.37), calls=%async_computation.3 | async-start | bytes 1048576 | tf_op jit(solution)/shard_map/all_to_all | solution.py:109
  173.4 16.1 %collective-permute-start.20 = (bf16[16,1024]{1,0:T(8,128)(2,1)S(1)}, bf16[16,1024]{1,0:T(8,128)(2,1)S(1)}, u32[]{:S(2)}, u32[]{:S(2)}) collective-permute-start(bf16[16,1024]{1,0:T(8,128)(2,1)S(1)} %copy-done.20), channel_id=1, source_target_pairs={{0,128},{128,0},{1,129},{129,1},{2,130},{130,2},{3,131},{131,3},{4... | collective-permute-start | bytes 98312 | tf_op jit(solution)/shard_map/ppermute | solution.py:216
  173.5 1.6 collective-permute-start.34
  189.5 5.5 %collective-permute-start.35 = (bf16[16,1024]{1,0:T(8,128)(2,1)S(1)}, bf16[16,1024]{1,0:T(8,128)(2,1)S(1)}, u32[]{:S(2)}, u32[]{:S(2)}) collective-permute-start(bf16[16,1024]{1,0:T(8,128)(2,1)S(1)} %get-tuple-element.46), channel_id=1, source_target_pairs={{0,128},{128,0},{1,129},{129,1},{2,130},{130,2},{3,131},{131,3},{4... | collective-permute-start | bytes 98312 | tf_op jit(solution)/shard_map/ppermute | solution.py:217

commit v13 on v12

--- a/solution.py
+++ b/solution.py
@@ -71,8 +71,7 @@
     return lax.ppermute(block, "x", [(i, (i + distance) % X) for i in range(X)])
 
 
-def narrow_terms(mine, theirs):
-    pair = pair_sum(mine, theirs)
+def narrow_terms(pair):
     sent = pair.astype(jnp.bfloat16)
     return [pair] + [step_x(sent, distance) for distance in (1, 3, 2)]
 
@@ -89,9 +88,12 @@
     return total
 
 
-def gather_x(block):
-    rows, cols = block.shape
-    found = [block] + [step_x(block, distance) for distance in (1, 2, 3)]
+def send_x(block):
+    return [block] + [step_x(block, distance) for distance in (1, 2, 3)]
+
+
+def place_x(found):
+    rows, cols = found[0].shape
     source = lax.broadcasted_iota(jnp.int32, (X, 1, 1), 0)
     passed = lax.rem(lax.axis_index("x") - source + X, X)
     placed = found[0][None]
@@ -125,7 +127,7 @@
 def back_total(whole, down_halves):
     theirs = contract(whole, down_halves[1], 1, 1)
     mine = contract(whole, down_halves[0], 1, 1)
-    return add_terms(narrow_terms(mine, theirs))
+    return add_terms(narrow_terms(pair_sum(mine, theirs)))
 
 
 def slope_of(total, slopes):
@@ -161,14 +163,14 @@
     mine = jnp.concatenate([contract(rows, up_halves[0], 1, 0) for rows in saved], axis=0)
     act, slopes = gelu_parts(spread_x(pair_sum(mine, theirs)))
     act = act.astype(jnp.bfloat16)
-    slopes = gather_x(slopes.astype(jnp.bfloat16))
+    slopes = place_x(send_x(slopes.astype(jnp.bfloat16)))
     gathered, act = together(gather_wide(upstream), act)
 
     top = by_part(gathered)
     theirs = contract(top[0], down_halves[1], 1, 1)
     mine = contract(top[0], down_halves[0], 1, 1)
     mine, slopes = together(mine, slopes)
-    top_slope = slope_of(add_terms(narrow_terms(mine, theirs)), slopes[first])
+    top_slope = slope_of(add_terms(narrow_terms(pair_sum(mine, theirs))), slopes[first])
     moved = to_lower(back_through_up(top_slope, up_halves))
     late_slopes, _ = together(slopes[last], top_slope[0])
     top_slope_rest = slope_of(back_total(top[1], down_halves), late_slopes)
@@ -177,19 +179,24 @@
     sent_up = [to_upper(together(w_up[:half], sent_down)[0])]
     sent_up.append(to_upper(together(w_up[half:], sent_up[0])[0]))
     partial, act = together(partial, act)
-    blocks, low_down, lower_slopes = together(
-        spread_wide(partial), pick(sent_down, w_down), to_upper(slopes[last])
-    )
+    own = in_order(act, other_core(act))
+    blocks, lower_slopes, _ = together(spread_wide(partial), to_upper(slopes[last]), own)
+    low_down = pick(sent_down, w_down)
     part = upstream.shape[0] // 2
     middle = (
         pick(upstream[part:], upstream[:part]).astype(jnp.float32) + add_blocks(blocks)
     ).astype(jnp.bfloat16)
 
-    hidden = gather_x(in_order(act, other_core(act)))
-    low, hidden = together(gather_wide(middle), hidden)
+    hidden = send_x(own)
+    low = gather_wide(middle)
     lower_slopes = pick(lower_slopes, slopes[first])
     low_rest = to_lower(low)
-    low_total = back_total(low, halves(low_down, 0))
+    low_halves = halves(low_down, 0)
+    theirs = contract(low, low_halves[1], 1, 1)
+    mine = contract(low, low_halves[0], 1, 1)
+    hidden[0], theirs = together(hidden[0], theirs)
+    pair, hidden = together(pair_sum(mine, theirs), place_x(hidden))
+    low_total = add_terms(narrow_terms(pair))
     incoming = jnp.concatenate([pick(top[0], low), pick(top[1], low_rest)], axis=0)
     incoming, sent_up[1] = together(incoming, sent_up[1])
     grad_down = contract(hidden, incoming, 0, 0).astype(jnp.bfloat16)

time: 197 us -> 196 us (level)
  waiting for transfers between devices: 72.4 us -> 69.6 us
    ppermute x4, waiting for transfers between devices: 15.6 us -> 24.7 us  [to_upper(): return lax.ppermute(block, CROSS_AXES, [(0, 3), (1, 2)])]
    ppermute x18, waiting for transfers between devices: 25.4 us -> 18.7 us  [step_x(): return lax.ppermute(block, 'x', [(i, (i + distance) % X) for i in range(X)])]
    ppermute x9, waiting for transfers between devices: 7 us -> 4.12 us  [other_core(): return lax.ppermute(block, 'core', [(0, 1), (1, 0)])]
    ppermute x3, waiting for transfers between devices: 5.55 us -> 2.94 us  [to_lower(): return lax.ppermute(block, CROSS_AXES, [(3, 0), (2, 1)])]
  transfers between devices with their start and end apart: 40 -> 40, of which waited for: 23 -> 20; matrix products, arithmetic and copies ran while one was open for 21% -> 22% of each run, Pallas kernels for 0% -> 0%
where the time goes in v13:
time: 196 us; the launch traced here: 195 us
  starting transfers between devices  76.2 us (39%)
  waiting for transfers between devices  69.6 us (36%)
  matrix products  21.9 us (11%)
  other arithmetic  17 us (9%)
  local copies, waits for them, and re-layouts  8.53 us (4%)
    ppermute x18, starting transfers between devices, step_x(): return lax.ppermute(block, 'x', [(i, (i + distance) % X) for i in range(X)])  28.2 us
    ppermute x4, waiting for transfers between devices, to_upper(): return lax.ppermute(block, CROSS_AXES, [(0, 3), (1, 2)])  24.7 us
    dot_general x18, matrix products, contract(): lax.dot_general(first_op, second_op, (((first_dim,), (second_dim,)), ((),...  21.9 us
    ppermute x18, waiting for transfers between devices, step_x(): return lax.ppermute(block, 'x', [(i, (i + distance) % X) for i in range(X)])  18.7 us
    all_to_all x2, starting transfers between devices, gather_wide(): lax.all_to_all(jnp.broadcast_to(block[None], (WIDE, rows, cols)), WIDE_AX...  16 us
    all_to_all x2, starting transfers between devices, spread_wide(): lax.all_to_all(partial.reshape(WIDE, rows // WIDE, cols), WIDE_AXES, 0, 0...  15 us
    all_to_all x2, waiting for transfers between devices, spread_wide(): lax.all_to_all(partial.reshape(WIDE, rows // WIDE, cols), WIDE_AXES, 0, 0...  11.7 us
    ppermute x3, starting transfers between devices, to_lower(): return lax.ppermute(block, CROSS_AXES, [(3, 0), (2, 1)])  10.9 us
  transfers between devices with their start and end apart: 40, of which 20 were waited for; matrix products, arithmetic and copies ran while one was open for 22% of the time, Pallas kernels for 0%

profile of v13, /device:TPU:56, one launch (start us, length us, event | category | flops | bytes accessed | tf_op | source)
XLA Modules:
  0.0 194.5 jit_solution(4141475511578079346)
XLA Ops:
  0.6 1.9 broadcast_in_dim.157
  2.6 9.6 %all-to-all-start = ((bf16[16,32,1024]{2,1,0:T(8,128)(2,1)}), bf16[16,32,1024]{2,1,0:T(8,128)(2,1)}, u32[]{:S(2)}, u32[]{:S(2)}) async-start(bf16[16,32,1024]{2,1,0:T(8,128)(2,1)} %broadcast_in_dim.157), calls=%async_computation | async-start | bytes 2097152 | tf_op jit(solution)/shard_map/all_to_all | solution.py:122
  12.2 1.3 fusion.83
  16.3 1.2 collective-permute-done
  17.5 1.2 maximum_add_fusion
  19.5 3.0 %collective-permute-start.3 = (bf16[128,512]{1,0:T(8,128)(2,1)}, bf16[128,512]{1,0:T(8,128)(2,1)S(1)}, u32[]{:S(2)}, u32[]{:S(2)}) collective-permute-start(bf16[128,512]{1,0:T(8,128)(2,1)} %get-tuple-element.62), channel_id=1, source_target_pairs={{0,4},{2,6},{4,0},{6,2},{1,5},{3,7},{5,1},{7,3},{8,12},{10,14},{12... | collective-permute-start | bytes 393224 | tf_op jit(solution)/shard_map/ppermute | solution.py:71
  22.6 1.1 collective-permute-start.2
  23.7 0.9 collective-permute-start.1
  24.7 2.9 %collective-permute-done.3 = bf16[128,512]{1,0:T(8,128)(2,1)S(1)} collective-permute-done((bf16[128,512]{1,0:T(8,128)(2,1)}, bf16[128,512]{1,0:T(8,128)(2,1)S(1)}, u32[]{:S(2)}, u32[]{:S(2)}) %collective-permute-start.3) | collective-permute-done | bytes 131104 | tf_op jit(solution)/shard_map/ppermute | solution.py:71
  27.6 2.1 %collective-permute-done.2 = bf16[128,512]{1,0:T(8,128)(2,1)S(1)} collective-permute-done((bf16[128,512]{1,0:T(8,128)(2,1)}, bf16[128,512]{1,0:T(8,128)(2,1)S(1)}, u32[]{:S(2)}, u32[]{:S(2)}) %collective-permute-start.2) | collective-permute-done | bytes 131104 | tf_op jit(solution)/shard_map/ppermute | solution.py:71
  30.3 1.2 fusion.61
  31.5 1.5 collective-permute-start.10
  33.0 2.7 %collective-permute-start.9 = (bf16[128,512]{1,0:T(8,128)(2,1)S(1)}, bf16[128,512]{1,0:T(8,128)(2,1)S(1)}, u32[]{:S(2)}, u32[]{:S(2)}) collective-permute-start(bf16[128,512]{1,0:T(8,128)(2,1)S(1)} %get-tuple-element.51), channel_id=1, source_target_pairs={{0,4},{2,6},{4,0},{6,2},{1,5},{3,7},{5,1},{7,3},{8,12},{10,14},{12... | collective-permute-start | bytes 393224 | tf_op jit(solution)/shard_map/ppermute | solution.py:71
  35.7 0.9 collective-permute-start.8
  36.6 1.8 all-to-all-done
  38.5 1.3 fusion.82
  39.8 1.9 convolution_convert_fusion.4
  42.4 1.9 fusion.20
  44.3 2.9 %collective-permute-start.14 = (bf16[256,512]{1,0:T(8,128)(2,1)S(1)}, bf16[256,512]{1,0:T(8,128)(2,1)S(1)}, u32[]{:S(2)}, u32[]{:S(2)}) collective-permute-start(bf16[256,512]{1,0:T(8,128)(2,1)S(1)} %fusion.55), channel_id=1, source_target_pairs={{0,4},{2,6},{4,0},{6,2},{1,5},{3,7},{5,1},{7,3},{8,12},{10,14},{12... | collective-permute-start | bytes 786440 | tf_op jit(solution)/shard_map/ppermute | solution.py:71
  47.3 1.1 collective-permute-start.13
  48.4 0.9 collective-permute-start.12
  49.3 1.3 collective-permute-start.21
  50.6 1.8 convolution_convert_fusion.5
  52.7 2.4 %collective-permute-done.14 = bf16[256,512]{1,0:T(8,128)(2,1)S(1)} collective-permute-done((bf16[256,512]{1,0:T(8,128)(2,1)S(1)}, bf16[256,512]{1,0:T(8,128)(2,1)S(1)}, u32[]{:S(2)}, u32[]{:S(2)}) %collective-permute-start.14) | collective-permute-done | bytes 262176 | tf_op jit(solution)/shard_map/ppermute | solution.py:71
  55.1 5.1 %collective-permute-done.13 = bf16[256,512]{1,0:T(8,128)(2,1)S(1)} collective-permute-done((bf16[256,512]{1,0:T(8,128)(2,1)S(1)}, bf16[256,512]{1,0:T(8,128)(2,1)S(1)}, u32[]{:S(2)}, u32[]{:S(2)}) %collective-permute-start.13) | collective-permute-done | bytes 262176 | tf_op jit(solution)/shard_map/ppermute | solution.py:71
  60.5 1.7 fusion.54
  62.2 3.1 %collective-permute-start.7 = (bf16[256,512]{1,0:T(8,128)(2,1)S(1)}, bf16[256,512]{1,0:T(8,128)(2,1)S(1)}, u32[]{:S(2)}, u32[]{:S(2)}) collective-permute-start(bf16[256,512]{1,0:T(8,128)(2,1)S(1)} %get-tuple-element.66), channel_id=1, source_target_pairs={{0,4},{2,6},{4,0},{6,2},{1,5},{3,7},{5,1},{7,3},{8,12},{10,14},{12... | collective-permute-start | bytes 786440 | tf_op jit(solution)/shard_map/ppermute | solution.py:71
  65.3 1.1 collective-permute-start.6
  66.5 0.9 collective-permute-start.5
  67.9 1.3 fusion.1
  69.1 3.0 %collective-permute-start.17 = (bf16[256,1024]{1,0:T(8,128)(2,1)}, bf16[256,1024]{1,0:T(8,128)(2,1)}, u32[]{:S(2)}, u32[]{:S(2)}) collective-permute-start(bf16[256,1024]{1,0:T(8,128)(2,1)} %fusion.1), channel_id=1, source_target_pairs={{192,0},{128,64},{193,1},{129,65},{194,2},{130,66},{195,3},{131,67... | collective-permute-start | bytes 1572872 | tf_op jit(solution)/shard_map/ppermute | solution.py:47
  72.1 0.9 collective-permute-done.7
  73.0 5.1 %collective-permute-done.6 = bf16[256,512]{1,0:T(8,128)(2,1)S(1)} collective-permute-done((bf16[256,512]{1,0:T(8,128)(2,1)S(1)}, bf16[256,512]{1,0:T(8,128)(2,1)S(1)}, u32[]{:S(2)}, u32[]{:S(2)}) %collective-permute-start.6) | collective-permute-done | bytes 262176 | tf_op jit(solution)/shard_map/ppermute | solution.py:71
  78.6 1.4 collective-permute-done.15
  80.5 2.2 %collective-permute-done.17 = bf16[256,1024]{1,0:T(8,128)(2,1)} collective-permute-done((bf16[256,1024]{1,0:T(8,128)(2,1)}, bf16[256,1024]{1,0:T(8,128)(2,1)}, u32[]{:S(2)}, u32[]{:S(2)}) %collective-permute-start.17) | collective-permute-done | bytes 524320 | tf_op jit(solution)/shard_map/ppermute | solution.py:47
  82.6 1.3 fusion.3
  83.9 6.5 %all-to-all-start.1 = ((bf16[16,16,1024]{2,1,0:T(8,128)(2,1)}), bf16[16,16,1024]{2,1,0:T(8,128)(2,1)S(1)}, u32[]{:S(2)}, u32[]{:S(2)}) async-start(bf16[16,16,1024]{2,1,0:T(8,128)(2,1)} %bitcast.143), calls=%async_computation.1 | async-start | bytes 1048576 | tf_op jit(solution)/shard_map/all_to_all | solution.py:111
  90.4 1.5 slice_bitcast_fusion
  91.9 1.3 collective-permute-start.18
  93.2 7.8 %collective-permute-done.21 = bf16[1024,1024]{1,0:T(8,128)(2,1)} collective-permute-done((bf16[1024,1024]{1,0:T(8,128)(2,1)}, bf16[1024,1024]{1,0:T(8,128)(2,1)}, u32[]{:S(2)}, u32[]{:S(2)}) %collective-permute-start.21) | collective-permute-done | bytes 2097184 | tf_op jit(solution)/shard_map/ppermute | solution.py:43
  101.0 1.3 collective-permute-start.30
  102.3 0.9 broadcast_select_fusion.12
  104.0 2.3 %collective-permute-done.18 = bf16[256,512]{1,0:T(8,128)(2,1)} collective-permute-done((bf16[256,512]{1,0:T(8,128)(2,1)}, bf16[256,512]{1,0:T(8,128)(2,1)}, u32[]{:S(2)}, u32[]{:S(2)}) %collective-permute-start.18) | collective-permute-done | bytes 262176 | tf_op jit(solution)/shard_map/ppermute | solution.py:43
  108.0 6.4 %all-to-all-start.2 = ((bf16[16,16,1024]{2,1,0:T(8,128)(2,1)}), bf16[16,16,1024]{2,1,0:T(8,128)(2,1)S(1)}, u32[]{:S(2)}, u32[]{:S(2)}) async-start(bf16[16,16,1024]{2,1,0:T(8,128)(2,1)} %broadcast_in_dim.175), calls=%async_computation.2 | async-start | bytes 1048576 | tf_op jit(solution)/shard_map/all_to_all | solution.py:122
  115.2 3.6 %collective-permute-start.24 = (bf16[128,1024]{1,0:T(8,128)(2,1)}, bf16[128,1024]{1,0:T(8,128)(2,1)}, u32[]{:S(2)}, u32[]{:S(2)}) collective-permute-start(bf16[128,1024]{1,0:T(8,128)(2,1)} %pad_maximum_fusion.2), channel_id=1, source_target_pairs={{0,4},{2,6},{4,0},{6,2},{1,5},{3,7},{5,1},{7,3},{8,12},{10,14},{12... | collective-permute-start | bytes 786440 | tf_op jit(solution)/shard_map/ppermute | solution.py:71
  118.8 3.8 %broadcast_select_fusion = bf16[1024,1024]{1,0:T(8,128)(2,1)} fusion(bf16[1024,1024]{1,0:T(8,128)(2,1)} %collective-permute-done.21, pred[]{:T(512)S(6)} %eq.35, bf16[1,1024,1024]{2,1,0:T(8,128)(2,1)} %param.7), kind=kLoop, calls=%fused_computation.1 | loop fusion | flops 1048576 | bytes 6291457 | tf_op jit(solution)/shard_map/jit(_where)/select_n | solution.py:148
  122.6 5.4 %collective-permute-done.30 = bf16[512,1024]{1,0:T(8,128)(2,1)} collective-permute-done((bf16[512,1024]{1,0:T(8,128)(2,1)}, bf16[512,1024]{1,0:T(8,128)(2,1)}, u32[]{:S(2)}, u32[]{:S(2)}) %collective-permute-start.30) | collective-permute-done | bytes 1048608 | tf_op jit(solution)/shard_map/ppermute | solution.py:43
  128.0 1.3 collective-permute-start.31
  129.5 6.6 %collective-permute-start.29 = (bf16[256,1024]{1,0:T(8,128)(2,1)S(1)}, bf16[256,1024]{1,0:T(8,128)(2,1)S(1)}, u32[]{:S(2)}, u32[]{:S(2)}) collective-permute-start(bf16[256,1024]{1,0:T(8,128)(2,1)S(1)} %bitcast.130), channel_id=1, source_target_pairs={{192,0},{128,64},{193,1},{129,65},{194,2},{130,66},{195,3},{131,67... | collective-permute-start | bytes 1572872 | tf_op jit(solution)/shard_map/ppermute | solution.py:47
  136.1 1.7 fusion.37
  137.9 1.6 fusion.17
  140.3 1.2 collective-permute-start.28
  141.5 2.3 %collective-permute-start.27 = (bf16[256,512]{1,0:T(8,128)(2,1)S(1)}, bf16[256,512]{1,0:T(8,128)(2,1)S(1)}, u32[]{:S(2)}, u32[]{:S(2)}) collective-permute-start(bf16[256,512]{1,0:T(8,128)(2,1)S(1)} %convert_element_type.158), channel_id=1, source_target_pairs={{0,6},{2,0},{4,2},{6,4},{1,7},{3,1},{5,3},{7,5},{8,14},{10,8},{12,... | collective-permute-start | bytes 786440 | tf_op jit(solution)/shard_map/ppermute | solution.py:71
  144.8 9.2 %collective-permute-done.31 = bf16[512,1024]{1,0:T(8,128)(2,1)} collective-permute-done((bf16[512,1024]{1,0:T(8,128)(2,1)}, bf16[512,1024]{1,0:T(8,128)(2,1)}, u32[]{:S(2)}, u32[]{:S(2)}) %collective-permute-start.31) | collective-permute-done | bytes 1048608 | tf_op jit(solution)/shard_map/ppermute | solution.py:43
  154.0 2.6 %convolution_convert_fusion.1 = bf16[1024,1024]{1,0:T(8,128)(2,1)} fusion(bf16[512,1024]{1,0:T(8,128)(2,1)S(1)} %fusion.17, bf16[512,1024]{1,0:T(8,128)(2,1)S(1)} %pad_maximum_fusion), kind=kOutput, calls=%fused_computation.3 | convolution fusion | flops 1074790400 | bytes 4194304 | tf_op jit(solution)/shard_map/dot_general | solution.py:26
  156.6 2.6 %maximum_select_fusion = bf16[1024,1024]{1,0:T(8,128)(2,1)S(1)} fusion(bf16[512,1024]{1,0:T(8,128)(2,1)} %collective-permute-done.31, bf16[512,1024]{1,0:T(8,128)(2,1)} %collective-permute-done.30, bf16[1,1024,1024]{2,1,0:T(8,128)(2,1)S(1)} %copy-done, pred[]{:T(512)S(6)} %eq.35), kind=kLoop, calls=%fused_computation | loop fusion | flops 5242880 | bytes 6291457 | tf_op jit(solution)/shard_map/jit(_where)/select_n | solution.py:148
  159.4 1.1 multiply_convert_fusion
  160.6 1.3 collective-permute-start.33
  162.4 1.3 fusion.2
  163.7 8.5 %all-to-all-start.3 = ((bf16[16,16,1024]{2,1,0:T(8,128)(2,1)}), bf16[16,16,1024]{2,1,0:T(8,128)(2,1)S(1)}, u32[]{:S(2)}, u32[]{:S(2)}) async-start(bf16[16,16,1024]{2,1,0:T(8,128)(2,1)} %bitcast.37), calls=%async_computation.3 | async-start | bytes 1048576 | tf_op jit(solution)/shard_map/all_to_all | solution.py:111
  172.4 1.4 collective-permute-done.34
  174.0 2.6 %convolution_convert_fusion = bf16[1024,1024]{1,0:T(8,128)(2,1)} fusion(bf16[256,1024]{1,0:T(8,128)(2,1)S(1)} %bitcast.142, bf16[256,1024]{1,0:T(8,128)(2,1)S(1)} %bitcast.139, bf16[256,512]{1,0:T(8,128)(2,1)S(1)} %get-tuple-element.56, bf16[256,512]{1,0:T(8,128)(2,1)S(1)} %get-tuple-element.55, bf16[256,512]{1,0:T(8,128)(2,1)S(1)} %get-tuple-element.54, ...), kind=kOutput, calls=%fused_computation.2 | convolution fusion | flops 1081081856 | bytes 4194304 | tf_op jit(solution)/shard_map/dot_general | solution.py:26
  176.6 11.7 %all-to-all-done.3 = bf16[16,16,1024]{2,1,0:T(8,128)(2,1)S(1)} async-done(((bf16[16,16,1024]{2,1,0:T(8,128)(2,1)}), bf16[16,16,1024]{2,1,0:T(8,128)(2,1)S(1)}, u32[]{:S(2)}, u32[]{:S(2)}) %all-to-all-start.3) | async-done | bytes 524320 | tf_op jit(solution)/shard_map/all_to_all | solution.py:111
  188.5 5.4 %collective-permute-done.35 = bf16[16,1024]{1,0:T(8,128)(2,1)S(1)} collective-permute-done((bf16[16,1024]{1,0:T(8,128)(2,1)S(1)}, bf16[16,1024]{1,0:T(8,128)(2,1)S(1)}, u32[]{:S(2)}, u32[]{:S(2)}) %collective-permute-start.35) | collective-permute-done | bytes 32800 | tf_op jit(solution)/shard_map/ppermute | solution.py:224
  (109 shorter events, 14.1 us)
Async XLA Ops:
  2.6 10.9 %copy-start = (bf16[1,1024,1024]{2,1,0:T(8,128)(2,1)S(1)}, bf16[1,1024,1024]{2,1,0:T(8,128)(2,1)}, u32[]{:S(2)}) copy-start(bf16[1,1024,1024]{2,1,0:T(8,128)(2,1)} %param.6) | copy-start | bytes 6291460
  2.6 35.9 %all-to-all-start = ((bf16[16,32,1024]{2,1,0:T(8,128)(2,1)}), bf16[16,32,1024]{2,1,0:T(8,128)(2,1)}, u32[]{:S(2)}, u32[]{:S(2)}) async-start(bf16[16,32,1024]{2,1,0:T(8,128)(2,1)} %broadcast_in_dim.157), calls=%async_computation | async-start | bytes 2097152 | tf_op jit(solution)/shard_map/all_to_all | solution.py:122
  13.5 1.9 copy-start.6
  13.5 2.3 %copy-start.4 = (bf16[16,1,16,1024]{3,2,1,0:T(8,128)(2,1)}, bf16[16,1,16,1024]{3,2,1,0:T(8,128)(2,1)S(1)}, u32[]{:S(2)}) copy-start(bf16[16,1,16,1024]{3,2,1,0:T(8,128)(2,1)S(1)} %get-tuple-element.59) | copy-start | bytes 1572868
  15.3 2.3 %collective-permute-start = (bf16[512,512]{1,0:T(8,128)(2,1)}, bf16[512,512]{1,0:T(8,128)(2,1)}, u32[]{:S(2)}, u32[]{:S(2)}) collective-permute-start(bf16[512,512]{1,0:T(8,128)(2,1)} %pad_maximum_fusion.1), channel_id=1, source_target_pairs={{0,1},{1,0},{2,3},{3,2},{4,5},{5,4},{6,7},{7,6},{8,9},{9,8},{10,11... | collective-permute-start | bytes 1572872 | tf_op jit(solution)/shard_map/ppermute | solution.py:39
  19.5 8.1 %collective-permute-start.3 = (bf16[128,512]{1,0:T(8,128)(2,1)}, bf16[128,512]{1,0:T(8,128)(2,1)S(1)}, u32[]{:S(2)}, u32[]{:S(2)}) collective-permute-start(bf16[128,512]{1,0:T(8,128)(2,1)} %get-tuple-element.62), channel_id=1, source_target_pairs={{0,4},{2,6},{4,0},{6,2},{1,5},{3,7},{5,1},{7,3},{8,12},{10,14},{12... | collective-permute-start | bytes 393224 | tf_op jit(solution)/shard_map/ppermute | solution.py:71
  22.6 7.1 %collective-permute-start.2 = (bf16[128,512]{1,0:T(8,128)(2,1)}, bf16[128,512]{1,0:T(8,128)(2,1)S(1)}, u32[]{:S(2)}, u32[]{:S(2)}) collective-permute-start(bf16[128,512]{1,0:T(8,128)(2,1)} %get-tuple-element.63), channel_id=1, source_target_pairs={{0,6},{2,0},{4,2},{6,4},{1,7},{3,1},{5,3},{7,5},{8,14},{10,8},{12,... | collective-permute-start | bytes 393224 | tf_op jit(solution)/shard_map/ppermute | solution.py:71
  23.7 6.6 %collective-permute-start.1 = (bf16[128,512]{1,0:T(8,128)(2,1)S(1)}, bf16[128,512]{1,0:T(8,128)(2,1)}, u32[]{:S(2)}, u32[]{:S(2)}) collective-permute-start(bf16[128,512]{1,0:T(8,128)(2,1)S(1)} %get-tuple-element.61), channel_id=1, source_target_pairs={{0,2},{2,4},{4,6},{6,0},{1,3},{3,5},{5,7},{7,1},{8,10},{10,12},{12... | collective-permute-start | bytes 393224 | tf_op jit(solution)/shard_map/ppermute | solution.py:71
  29.7 0.7 copy-start.17
  31.5 10.3 %collective-permute-start.10 = (bf16[128,512]{1,0:T(8,128)(2,1)S(1)}, bf16[128,512]{1,0:T(8,128)(2,1)S(1)}, u32[]{:S(2)}, u32[]{:S(2)}) collective-permute-start(bf16[128,512]{1,0:T(8,128)(2,1)S(1)} %get-tuple-element.51), channel_id=1, source_target_pairs={{0,2},{2,4},{4,6},{6,0},{1,3},{3,5},{5,7},{7,1},{8,10},{10,12},{12... | collective-permute-start | bytes 393224 | tf_op jit(solution)/shard_map/ppermute | solution.py:71
  33.0 9.0 %collective-permute-start.9 = (bf16[128,512]{1,0:T(8,128)(2,1)S(1)}, bf16[128,512]{1,0:T(8,128)(2,1)S(1)}, u32[]{:S(2)}, u32[]{:S(2)}) collective-permute-start(bf16[128,512]{1,0:T(8,128)(2,1)S(1)} %get-tuple-element.51), channel_id=1, source_target_pairs={{0,4},{2,6},{4,0},{6,2},{1,5},{3,7},{5,1},{7,3},{8,12},{10,14},{12... | collective-permute-start | bytes 393224 | tf_op jit(solution)/shard_map/ppermute | solution.py:71
  35.7 6.3 %collective-permute-start.8 = (bf16[128,512]{1,0:T(8,128)(2,1)S(1)}, bf16[128,512]{1,0:T(8,128)(2,1)S(1)}, u32[]{:S(2)}, u32[]{:S(2)}) collective-permute-start(bf16[128,512]{1,0:T(8,128)(2,1)S(1)} %get-tuple-element.51), channel_id=1, source_target_pairs={{0,6},{2,0},{4,2},{6,4},{1,7},{3,1},{5,3},{7,5},{8,14},{10,8},{12,... | collective-permute-start | bytes 393224 | tf_op jit(solution)/shard_map/ppermute | solution.py:71
  39.8 20.8 %copy-start.2 = (bf16[16,1,16,1024]{3,2,1,0:T(8,128)(2,1)}, bf16[16,1,16,1024]{3,2,1,0:T(8,128)(2,1)S(1)}, u32[]{:S(2)}) copy-start(bf16[16,1,16,1024]{3,2,1,0:T(8,128)(2,1)S(1)} %get-tuple-element.57) | copy-start | bytes 1572868
  41.7 2.6 %collective-permute-start.11 = (bf16[256,512]{1,0:T(8,128)(2,1)S(1)}, bf16[256,512]{1,0:T(8,128)(2,1)S(1)}, u32[]{:S(2)}, u32[]{:S(2)}) collective-permute-start(bf16[256,512]{1,0:T(8,128)(2,1)S(1)} %convolution_convert_fusion.4), channel_id=1, source_target_pairs={{0,1},{1,0},{2,3},{3,2},{4,5},{5,4},{6,7},{7,6},{8,9},{9,8},{10,11... | collective-permute-start | bytes 786440 | tf_op jit(solution)/shard_map/ppermute | solution.py:39
  42.3 17.8 %copy-start.8 = (bf16[512,512]{1,0:T(8,128)(2,1)}, bf16[512,512]{1,0:T(8,128)(2,1)S(1)}, u32[]{:S(2)}) copy-start(bf16[512,512]{1,0:T(8,128)(2,1)S(1)} %fusion.53) | copy-start | bytes 1572868
  44.3 10.7 %collective-permute-start.14 = (bf16[256,512]{1,0:T(8,128)(2,1)S(1)}, bf16[256,512]{1,0:T(8,128)(2,1)S(1)}, u32[]{:S(2)}, u32[]{:S(2)}) collective-permute-start(bf16[256,512]{1,0:T(8,128)(2,1)S(1)} %fusion.55), channel_id=1, source_target_pairs={{0,4},{2,6},{4,0},{6,2},{1,5},{3,7},{5,1},{7,3},{8,12},{10,14},{12... | collective-permute-start | bytes 786440 | tf_op jit(solution)/shard_map/ppermute | solution.py:71
  47.3 12.9 %collective-permute-start.13 = (bf16[256,512]{1,0:T(8,128)(2,1)S(1)}, bf16[256,512]{1,0:T(8,128)(2,1)S(1)}, u32[]{:S(2)}, u32[]{:S(2)}) collective-permute-start(bf16[256,512]{1,0:T(8,128)(2,1)S(1)} %fusion.55), channel_id=1, source_target_pairs={{0,6},{2,0},{4,2},{6,4},{1,7},{3,1},{5,3},{7,5},{8,14},{10,8},{12,... | collective-permute-start | bytes 786440 | tf_op jit(solution)/shard_map/ppermute | solution.py:71
  48.4 11.8 %collective-permute-start.12 = (bf16[256,512]{1,0:T(8,128)(2,1)S(1)}, bf16[256,512]{1,0:T(8,128)(2,1)S(1)}, u32[]{:S(2)}, u32[]{:S(2)}) collective-permute-start(bf16[256,512]{1,0:T(8,128)(2,1)S(1)} %fusion.55), channel_id=1, source_target_pairs={{0,2},{2,4},{4,6},{6,0},{1,3},{3,5},{5,7},{7,1},{8,10},{10,12},{12... | collective-permute-start | bytes 786440 | tf_op jit(solution)/shard_map/ppermute | solution.py:71
  49.3 51.7 %collective-permute-start.21 = (bf16[1024,1024]{1,0:T(8,128)(2,1)}, bf16[1024,1024]{1,0:T(8,128)(2,1)}, u32[]{:S(2)}, u32[]{:S(2)}) collective-permute-start(bf16[1024,1024]{1,0:T(8,128)(2,1)} %bitcast.29), channel_id=1, source_target_pairs={{0,192},{64,128},{1,193},{65,129},{2,194},{66,130},{3,195},{67,131... | collective-permute-start | bytes 6291464 | tf_op jit(solution)/shard_map/ppermute | solution.py:43
  50.6 27.5 %copy-start.16 = (bf16[256,512]{1,0:T(8,128)(2,1)}, bf16[256,512]{1,0:T(8,128)(2,1)S(1)}, u32[]{:S(2)}) copy-start(bf16[256,512]{1,0:T(8,128)(2,1)S(1)} %slice.44) | copy-start | bytes 786436
  52.4 8.1 %collective-permute-start.4 = (bf16[256,512]{1,0:T(8,128)(2,1)S(1)}, bf16[256,512]{1,0:T(8,128)(2,1)S(1)}, u32[]{:S(2)}, u32[]{:S(2)}) collective-permute-start(bf16[256,512]{1,0:T(8,128)(2,1)S(1)} %convolution_convert_fusion.5), channel_id=1, source_target_pairs={{0,1},{1,0},{2,3},{3,2},{4,5},{5,4},{6,7},{7,6},{8,9},{9,8},{10,11... | collective-permute-start | bytes 786440 | tf_op jit(solution)/shard_map/ppermute | solution.py:39
  60.4 7.0 %collective-permute-start.16 = (bf16[256,512]{1,0:T(8,128)(2,1)S(1)}, bf16[256,512]{1,0:T(8,128)(2,1)S(1)}, u32[]{:S(2)}, u32[]{:S(2)}) collective-permute-start(bf16[256,512]{1,0:T(8,128)(2,1)S(1)} %multiply_convert_fusion.2), channel_id=1, source_target_pairs={{0,1},{1,0},{2,3},{3,2},{4,5},{5,4},{6,7},{7,6},{8,9},{9,8},{10,11... | collective-permute-start | bytes 786440 | tf_op jit(solution)/shard_map/ppermute | solution.py:39
  62.2 10.7 %collective-permute-start.7 = (bf16[256,512]{1,0:T(8,128)(2,1)S(1)}, bf16[256,512]{1,0:T(8,128)(2,1)S(1)}, u32[]{:S(2)}, u32[]{:S(2)}) collective-permute-start(bf16[256,512]{1,0:T(8,128)(2,1)S(1)} %get-tuple-element.66), channel_id=1, source_target_pairs={{0,4},{2,6},{4,0},{6,2},{1,5},{3,7},{5,1},{7,3},{8,12},{10,14},{12... | collective-permute-start | bytes 786440 | tf_op jit(solution)/shard_map/ppermute | solution.py:71
  65.3 12.8 %collective-permute-start.6 = (bf16[256,512]{1,0:T(8,128)(2,1)S(1)}, bf16[256,512]{1,0:T(8,128)(2,1)S(1)}, u32[]{:S(2)}, u32[]{:S(2)}) collective-permute-start(bf16[256,512]{1,0:T(8,128)(2,1)S(1)} %get-tuple-element.66), channel_id=1, source_target_pairs={{0,6},{2,0},{4,2},{6,4},{1,7},{3,1},{5,3},{7,5},{8,14},{10,8},{12,... | collective-permute-start | bytes 786440 | tf_op jit(solution)/shard_map/ppermute | solution.py:71
  66.5 11.7 %collective-permute-start.5 = (bf16[256,512]{1,0:T(8,128)(2,1)S(1)}, bf16[256,512]{1,0:T(8,128)(2,1)S(1)}, u32[]{:S(2)}, u32[]{:S(2)}) collective-permute-start(bf16[256,512]{1,0:T(8,128)(2,1)S(1)} %get-tuple-element.66), channel_id=1, source_target_pairs={{0,2},{2,4},{4,6},{6,0},{1,3},{3,5},{5,7},{7,1},{8,10},{10,12},{12... | collective-permute-start | bytes 786440 | tf_op jit(solution)/shard_map/ppermute | solution.py:71
  67.4 1.8 copy-start.12
  69.1 13.5 %collective-permute-start.17 = (bf16[256,1024]{1,0:T(8,128)(2,1)}, bf16[256,1024]{1,0:T(8,128)(2,1)}, u32[]{:S(2)}, u32[]{:S(2)}) collective-permute-start(bf16[256,1024]{1,0:T(8,128)(2,1)} %fusion.1), channel_id=1, source_target_pairs={{192,0},{128,64},{193,1},{129,65},{194,2},{130,66},{195,3},{131,67... | collective-permute-start | bytes 1572872 | tf_op jit(solution)/shard_map/ppermute | solution.py:47
  78.4 5.6 %copy-start.10 = (bf16[256,512]{1,0:T(8,128)(2,1)}, bf16[256,512]{1,0:T(8,128)(2,1)S(1)}, u32[]{:S(2)}) copy-start(bf16[256,512]{1,0:T(8,128)(2,1)S(1)} %multiply_convert_fusion.1) | copy-start | bytes 786436
  78.4 1.6 collective-permute-start.15
  80.0 3.9 %copy-start.14 = (bf16[256,512]{1,0:T(8,128)(2,1)}, bf16[256,512]{1,0:T(8,128)(2,1)S(1)}, u32[]{:S(2)}) copy-start(bf16[256,512]{1,0:T(8,128)(2,1)S(1)} %collective-permute-done.15) | copy-start | bytes 786436
  83.9 22.4 %all-to-all-start.1 = ((bf16[16,16,1024]{2,1,0:T(8,128)(2,1)}), bf16[16,16,1024]{2,1,0:T(8,128)(2,1)S(1)}, u32[]{:S(2)}, u32[]{:S(2)}) async-start(bf16[16,16,1024]{2,1,0:T(8,128)(2,1)} %bitcast.143), calls=%async_computation.1 | async-start | bytes 1048576 | tf_op jit(solution)/shard_map/all_to_all | solution.py:111
  90.4 11.8 %collective-permute-start.19 = (bf16[128,512]{1,0:T(8,128)(2,1)S(1)}, bf16[128,512]{1,0:T(8,128)(2,1)}, u32[]{:S(2)}, u32[]{:S(2)}) collective-permute-start(bf16[128,512]{1,0:T(8,128)(2,1)S(1)} %get-tuple-element.31), channel_id=1, source_target_pairs={{0,1},{1,0},{2,3},{3,2},{4,5},{5,4},{6,7},{7,6},{8,9},{9,8},{10,11... | collective-permute-start | bytes 393224 | tf_op jit(solution)/shard_map/ppermute | solution.py:39
  91.9 14.3 %collective-permute-start.18 = (bf16[256,512]{1,0:T(8,128)(2,1)}, bf16[256,512]{1,0:T(8,128)(2,1)}, u32[]{:S(2)}, u32[]{:S(2)}) collective-permute-start(bf16[256,512]{1,0:T(8,128)(2,1)} %copy-done.16), channel_id=1, source_target_pairs={{0,192},{64,128},{1,193},{65,129},{2,194},{66,130},{3,195},{67,131... | collective-permute-start | bytes 786440 | tf_op jit(solution)/shard_map/ppermute | solution.py:43
  101.0 27.0 %collective-permute-start.30 = (bf16[512,1024]{1,0:T(8,128)(2,1)}, bf16[512,1024]{1,0:T(8,128)(2,1)}, u32[]{:S(2)}, u32[]{:S(2)}) collective-permute-start(bf16[512,1024]{1,0:T(8,128)(2,1)} %get-tuple-element.37), channel_id=1, source_target_pairs={{0,192},{64,128},{1,193},{65,129},{2,194},{66,130},{3,195},{67,131... | collective-permute-start | bytes 3145736 | tf_op jit(solution)/shard_map/ppermute | solution.py:43
  108.0 21.5 %all-to-all-start.2 = ((bf16[16,16,1024]{2,1,0:T(8,128)(2,1)}), bf16[16,16,1024]{2,1,0:T(8,128)(2,1)S(1)}, u32[]{:S(2)}, u32[]{:S(2)}) async-start(bf16[16,16,1024]{2,1,0:T(8,128)(2,1)} %broadcast_in_dim.175), calls=%async_computation.2 | async-start | bytes 1048576 | tf_op jit(solution)/shard_map/all_to_all | solution.py:122
  114.4 23.4 %collective-permute-start.25 = (bf16[128,1024]{1,0:T(8,128)(2,1)}, bf16[128,1024]{1,0:T(8,128)(2,1)}, u32[]{:S(2)}, u32[]{:S(2)}) collective-permute-start(bf16[128,1024]{1,0:T(8,128)(2,1)} %pad_maximum_fusion.2), channel_id=1, source_target_pairs={{0,2},{2,4},{4,6},{6,0},{1,3},{3,5},{5,7},{7,1},{8,10},{10,12},{12... | collective-permute-start | bytes 786440 | tf_op jit(solution)/shard_map/ppermute | solution.py:71
  115.2 22.7 %collective-permute-start.24 = (bf16[128,1024]{1,0:T(8,128)(2,1)}, bf16[128,1024]{1,0:T(8,128)(2,1)}, u32[]{:S(2)}, u32[]{:S(2)}) collective-permute-start(bf16[128,1024]{1,0:T(8,128)(2,1)} %pad_maximum_fusion.2), channel_id=1, source_target_pairs={{0,4},{2,6},{4,0},{6,2},{1,5},{3,7},{5,1},{7,3},{8,12},{10,14},{12... | collective-permute-start | bytes 786440 | tf_op jit(solution)/shard_map/ppermute | solution.py:71
  118.8 19.1 %collective-permute-start.23 = (bf16[128,1024]{1,0:T(8,128)(2,1)}, bf16[128,1024]{1,0:T(8,128)(2,1)}, u32[]{:S(2)}, u32[]{:S(2)}) collective-permute-start(bf16[128,1024]{1,0:T(8,128)(2,1)} %pad_maximum_fusion.2), channel_id=1, source_target_pairs={{0,6},{2,0},{4,2},{6,4},{1,7},{3,1},{5,3},{7,5},{8,14},{10,8},{12,... | collective-permute-start | bytes 786440 | tf_op jit(solution)/shard_map/ppermute | solution.py:71
  128.0 26.1 %collective-permute-start.31 = (bf16[512,1024]{1,0:T(8,128)(2,1)}, bf16[512,1024]{1,0:T(8,128)(2,1)}, u32[]{:S(2)}, u32[]{:S(2)}) collective-permute-start(bf16[512,1024]{1,0:T(8,128)(2,1)} %get-tuple-element.38), channel_id=1, source_target_pairs={{0,192},{64,128},{1,193},{65,129},{2,194},{66,130},{3,195},{67,131... | collective-permute-start | bytes 3145736 | tf_op jit(solution)/shard_map/ppermute | solution.py:43
  129.5 15.2 %collective-permute-start.29 = (bf16[256,1024]{1,0:T(8,128)(2,1)S(1)}, bf16[256,1024]{1,0:T(8,128)(2,1)S(1)}, u32[]{:S(2)}, u32[]{:S(2)}) collective-permute-start(bf16[256,1024]{1,0:T(8,128)(2,1)S(1)} %bitcast.130), channel_id=1, source_target_pairs={{192,0},{128,64},{193,1},{129,65},{194,2},{130,66},{195,3},{131,67... | collective-permute-start | bytes 1572872 | tf_op jit(solution)/shard_map/ppermute | solution.py:47
  137.8 1.9 copy-start.1
  137.8 1.9 collective-permute-start.22
  139.5 5.1 %copy-start.3 = (bf16[16,1,16,1024]{3,2,1,0:T(8,128)(2,1)S(1)}, bf16[16,1,16,1024]{3,2,1,0:T(8,128)(2,1)}, u32[]{:S(2)}) copy-start(bf16[16,1,16,1024]{3,2,1,0:T(8,128)(2,1)} %copy-done.2) | copy-start | bytes 1572868
  140.3 18.9 %collective-permute-start.28 = (bf16[256,512]{1,0:T(8,128)(2,1)S(1)}, bf16[256,512]{1,0:T(8,128)(2,1)S(1)}, u32[]{:S(2)}, u32[]{:S(2)}) collective-permute-start(bf16[256,512]{1,0:T(8,128)(2,1)S(1)} %convert_element_type.158), channel_id=1, source_target_pairs={{0,4},{2,6},{4,0},{6,2},{1,5},{3,7},{5,1},{7,3},{8,12},{10,14},{12... | collective-permute-start | bytes 786440 | tf_op jit(solution)/shard_map/ppermute | solution.py:71
  141.5 17.7 %collective-permute-start.27 = (bf16[256,512]{1,0:T(8,128)(2,1)S(1)}, bf16[256,512]{1,0:T(8,128)(2,1)S(1)}, u32[]{:S(2)}, u32[]{:S(2)}) collective-permute-start(bf16[256,512]{1,0:T(8,128)(2,1)S(1)} %convert_element_type.158), channel_id=1, source_target_pairs={{0,6},{2,0},{4,2},{6,4},{1,7},{3,1},{5,3},{7,5},{8,14},{10,8},{12,... | collective-permute-start | bytes 786440 | tf_op jit(solution)/shard_map/ppermute | solution.py:71
  143.9 15.4 %collective-permute-start.26 = (bf16[256,512]{1,0:T(8,128)(2,1)S(1)}, bf16[256,512]{1,0:T(8,128)(2,1)S(1)}, u32[]{:S(2)}, u32[]{:S(2)}) collective-permute-start(bf16[256,512]{1,0:T(8,128)(2,1)S(1)} %convert_element_type.158), channel_id=1, source_target_pairs={{0,2},{2,4},{4,6},{6,0},{1,3},{3,5},{5,7},{7,1},{8,10},{10,12},{12... | collective-permute-start | bytes 786440 | tf_op jit(solution)/shard_map/ppermute | solution.py:71
  156.6 2.8 %copy-start.9 = (bf16[512,512]{1,0:T(8,128)(2,1)S(1)}, bf16[512,512]{1,0:T(8,128)(2,1)}, u32[]{:S(2)}) copy-start(bf16[512,512]{1,0:T(8,128)(2,1)} %copy-done.8) | copy-start | bytes 1572868
  160.5 1.9 collective-permute-start.32
  160.6 11.7 %collective-permute-start.33 = (bf16[256,512]{1,0:T(8,128)(2,1)S(1)}, bf16[256,512]{1,0:T(8,128)(2,1)S(1)}, u32[]{:S(2)}, u32[]{:S(2)}) collective-permute-start(bf16[256,512]{1,0:T(8,128)(2,1)S(1)} %multiply_convert_fusion), channel_id=1, source_target_pairs={{192,0},{128,64},{193,1},{129,65},{194,2},{130,66},{195,3},{131,67... | collective-permute-start | bytes 786440 | tf_op jit(solution)/shard_map/ppermute | solution.py:47
  162.4 10.0 %copy-start.13 = (bf16[256,512]{1,0:T(8,128)(2,1)S(1)}, bf16[256,512]{1,0:T(8,128)(2,1)}, u32[]{:S(2)}) copy-start(bf16[256,512]{1,0:T(8,128)(2,1)} %copy-done.12) | copy-start | bytes 786436
  162.4 11.5 %copy-start.11 = (bf16[256,512]{1,0:T(8,128)(2,1)S(1)}, bf16[256,512]{1,0:T(8,128)(2,1)}, u32[]{:S(2)}) copy-start(bf16[256,512]{1,0:T(8,128)(2,1)} %copy-done.10) | copy-start | bytes 786436
  162.4 11.5 %copy-start.15 = (bf16[256,512]{1,0:T(8,128)(2,1)S(1)}, bf16[256,512]{1,0:T(8,128)(2,1)}, u32[]{:S(2)}) copy-start(bf16[256,512]{1,0:T(8,128)(2,1)} %copy-done.14) | copy-start | bytes 786436
  163.7 10.2 %copy-start.5 = (bf16[16,1,16,1024]{3,2,1,0:T(8,128)(2,1)S(1)}, bf16[16,1,16,1024]{3,2,1,0:T(8,128)(2,1)}, u32[]{:S(2)}) copy-start(bf16[16,1,16,1024]{3,2,1,0:T(8,128)(2,1)} %copy-done.4) | copy-start | bytes 1572868
  163.7 10.2 %copy-start.7 = (bf16[16,1,16,1024]{3,2,1,0:T(8,128)(2,1)S(1)}, bf16[16,1,16,1024]{3,2,1,0:T(8,128)(2,1)}, u32[]{:S(2)}) copy-start(bf16[16,1,16,1024]{3,2,1,0:T(8,128)(2,1)} %copy-done.6) | copy-start | bytes 1572868
  163.7 24.5 %all-to-all-start.3 = ((bf16[16,16,1024]{2,1,0:T(8,128)(2,1)}), bf16[16,16,1024]{2,1,0:T(8,128)(2,1)S(1)}, u32[]{:S(2)}, u32[]{:S(2)}) async-start(bf16[16,16,1024]{2,1,0:T(8,128)(2,1)} %bitcast.37), calls=%async_computation.3 | async-start | bytes 1048576 | tf_op jit(solution)/shard_map/all_to_all | solution.py:111
  172.2 16.1 %collective-permute-start.20 = (bf16[16,1024]{1,0:T(8,128)(2,1)S(1)}, bf16[16,1024]{1,0:T(8,128)(2,1)S(1)}, u32[]{:S(2)}, u32[]{:S(2)}) collective-permute-start(bf16[16,1024]{1,0:T(8,128)(2,1)S(1)} %add_convert_fusion.1), channel_id=1, source_target_pairs={{0,128},{128,0},{1,129},{129,1},{2,130},{130,2},{3,131},{131,3},{4... | collective-permute-start | bytes 98312 | tf_op jit(solution)/shard_map/ppermute | solution.py:223
  172.2 1.6 collective-permute-start.34
  188.4 5.5 %collective-permute-start.35 = (bf16[16,1024]{1,0:T(8,128)(2,1)S(1)}, bf16[16,1024]{1,0:T(8,128)(2,1)S(1)}, u32[]{:S(2)}, u32[]{:S(2)}) collective-permute-start(bf16[16,1024]{1,0:T(8,128)(2,1)S(1)} %get-tuple-element.48), channel_id=1, source_target_pairs={{0,128},{128,0},{1,129},{129,1},{2,130},{130,2},{3,131},{131,3},{4... | collective-permute-start | bytes 98312 | tf_op jit(solution)/shard_map/ppermute | solution.py:224

commit v14 on v13

--- a/solution.py
+++ b/solution.py
@@ -198,10 +198,9 @@
     pair, hidden = together(pair_sum(mine, theirs), place_x(hidden))
     low_total = add_terms(narrow_terms(pair))
     incoming = jnp.concatenate([pick(top[0], low), pick(top[1], low_rest)], axis=0)
-    incoming, sent_up[1] = together(incoming, sent_up[1])
     grad_down = contract(hidden, incoming, 0, 0).astype(jnp.bfloat16)
+    low_total, grad_down, sent_up[1] = together(low_total, grad_down, sent_up[1])
     low_up = pick(jnp.concatenate(sent_up, axis=0), w_up)
-    low_total, grad_down, low_up = together(low_total, grad_down, low_up)
     low_slope = slope_of(low_total, lower_slopes)
     low_slope_rest = to_lower(low_slope[0])
     low_blocks = spread_wide(back_through_up(low_slope, halves(low_up, 1)))

time: 196 us -> 194 us (0.990)
    ppermute x4, waiting for transfers between devices: 24.7 us -> 15.5 us  [to_upper(): return lax.ppermute(block, CROSS_AXES, [(0, 3), (1, 2)])]
    ppermute x18, waiting for transfers between devices: 18.7 us -> 27.6 us  [step_x(): return lax.ppermute(block, 'x', [(i, (i + distance) % X) for i in range(X)])]
  transfers between devices with their start and end apart: 40 -> 40, of which waited for: 20 -> 22; matrix products, arithmetic and copies ran while one was open for 22% -> 22% of each run, Pallas kernels for 0% -> 0%
where the time goes in v14:
time: 194 us; the launch traced here: 193 us
  starting transfers between devices  75.1 us (39%)
  waiting for transfers between devices  69.3 us (36%)
  matrix products  21.9 us (11%)
  other arithmetic  16.9 us (9%)
  local copies, waits for them, and re-layouts  8.51 us (4%)
    ppermute x18, starting transfers between devices, step_x(): return lax.ppermute(block, 'x', [(i, (i + distance) % X) for i in range(X)])  28.2 us
    ppermute x18, waiting for transfers between devices, step_x(): return lax.ppermute(block, 'x', [(i, (i + distance) % X) for i in range(X)])  27.6 us
    dot_general x18, matrix products, contract(): lax.dot_general(first_op, second_op, (((first_dim,), (second_dim,)), ((),...  21.9 us
    all_to_all x2, starting transfers between devices, gather_wide(): lax.all_to_all(jnp.broadcast_to(block[None], (WIDE, rows, cols)), WIDE_AX...  16 us
    ppermute x4, waiting for transfers between devices, to_upper(): return lax.ppermute(block, CROSS_AXES, [(0, 3), (1, 2)])  15.5 us
    all_to_all x2, starting transfers between devices, spread_wide(): lax.all_to_all(partial.reshape(WIDE, rows // WIDE, cols), WIDE_AXES, 0, 0...  13.9 us
    all_to_all x2, waiting for transfers between devices, spread_wide(): lax.all_to_all(partial.reshape(WIDE, rows // WIDE, cols), WIDE_AXES, 0, 0...  11.7 us
    ppermute x3, starting transfers between devices, to_lower(): return lax.ppermute(block, CROSS_AXES, [(3, 0), (2, 1)])  10.9 us
  transfers between devices with their start and end apart: 40, of which 22 were waited for; matrix products, arithmetic and copies ran while one was open for 22% of the time, Pallas kernels for 0%

profile of v14, /device:TPU:56, one launch (start us, length us, event | category | flops | bytes accessed | tf_op | source)
XLA Modules:
  0.0 193.0 jit_solution(14274114936166499926)
XLA Ops:
  0.6 1.9 %broadcast_in_dim.157 = bf16[16,32,1024]{2,1,0:T(8,128)(2,1)} broadcast(bf16[32,1024]{1,0:T(8,128)(2,1)} %param.5), dimensions={1,2} | broadcast | bytes 1114112 | tf_op jit(solution)/shard_map/broadcast_in_dim | solution.py:123
  2.6 9.6 %all-to-all-start = ((bf16[16,32,1024]{2,1,0:T(8,128)(2,1)}), bf16[16,32,1024]{2,1,0:T(8,128)(2,1)}, u32[]{:S(2)}, u32[]{:S(2)}) async-start(bf16[16,32,1024]{2,1,0:T(8,128)(2,1)} %broadcast_in_dim.157), calls=%async_computation | async-start | bytes 2097152 | tf_op jit(solution)/shard_map/all_to_all | solution.py:122
  12.2 1.3 fusion.87
  16.3 1.2 collective-permute-done
  17.5 1.2 maximum_add_fusion
  19.5 3.0 %collective-permute-start.3 = (bf16[128,512]{1,0:T(8,128)(2,1)}, bf16[128,512]{1,0:T(8,128)(2,1)S(1)}, u32[]{:S(2)}, u32[]{:S(2)}) collective-permute-start(bf16[128,512]{1,0:T(8,128)(2,1)} %get-tuple-element.58), channel_id=1, source_target_pairs={{0,4},{2,6},{4,0},{6,2},{1,5},{3,7},{5,1},{7,3},{8,12},{10,14},{12... | collective-permute-start | bytes 393224 | tf_op jit(solution)/shard_map/ppermute | solution.py:71
  22.6 1.1 collective-permute-start.2
  23.7 0.9 collective-permute-start.1
  24.7 2.9 %collective-permute-done.3 = bf16[128,512]{1,0:T(8,128)(2,1)S(1)} collective-permute-done((bf16[128,512]{1,0:T(8,128)(2,1)}, bf16[128,512]{1,0:T(8,128)(2,1)S(1)}, u32[]{:S(2)}, u32[]{:S(2)}) %collective-permute-start.3) | collective-permute-done | bytes 131104 | tf_op jit(solution)/shard_map/ppermute | solution.py:71
  27.6 2.1 %collective-permute-done.2 = bf16[128,512]{1,0:T(8,128)(2,1)S(1)} collective-permute-done((bf16[128,512]{1,0:T(8,128)(2,1)}, bf16[128,512]{1,0:T(8,128)(2,1)S(1)}, u32[]{:S(2)}, u32[]{:S(2)}) %collective-permute-start.2) | collective-permute-done | bytes 131104 | tf_op jit(solution)/shard_map/ppermute | solution.py:71
  30.3 1.2 fusion.64
  31.5 1.5 collective-permute-start.10
  33.0 2.7 %collective-permute-start.9 = (bf16[128,512]{1,0:T(8,128)(2,1)S(1)}, bf16[128,512]{1,0:T(8,128)(2,1)S(1)}, u32[]{:S(2)}, u32[]{:S(2)}) collective-permute-start(bf16[128,512]{1,0:T(8,128)(2,1)S(1)} %get-tuple-element.47), channel_id=1, source_target_pairs={{0,4},{2,6},{4,0},{6,2},{1,5},{3,7},{5,1},{7,3},{8,12},{10,14},{12... | collective-permute-start | bytes 393224 | tf_op jit(solution)/shard_map/ppermute | solution.py:71
  35.7 0.9 collective-permute-start.8
  36.6 1.8 all-to-all-done
  38.5 1.3 fusion.86
  39.8 1.9 convolution_convert_fusion.4
  42.4 1.9 fusion.23
  44.3 2.9 %collective-permute-start.14 = (bf16[256,512]{1,0:T(8,128)(2,1)S(1)}, bf16[256,512]{1,0:T(8,128)(2,1)S(1)}, u32[]{:S(2)}, u32[]{:S(2)}) collective-permute-start(bf16[256,512]{1,0:T(8,128)(2,1)S(1)} %fusion.58), channel_id=1, source_target_pairs={{0,4},{2,6},{4,0},{6,2},{1,5},{3,7},{5,1},{7,3},{8,12},{10,14},{12... | collective-permute-start | bytes 786440 | tf_op jit(solution)/shard_map/ppermute | solution.py:71
  47.3 1.1 collective-permute-start.13
  48.4 0.9 collective-permute-start.12
  49.3 1.3 collective-permute-start.21
  50.6 1.8 convolution_convert_fusion.5
  52.7 2.4 %collective-permute-done.14 = bf16[256,512]{1,0:T(8,128)(2,1)S(1)} collective-permute-done((bf16[256,512]{1,0:T(8,128)(2,1)S(1)}, bf16[256,512]{1,0:T(8,128)(2,1)S(1)}, u32[]{:S(2)}, u32[]{:S(2)}) %collective-permute-start.14) | collective-permute-done | bytes 262176 | tf_op jit(solution)/shard_map/ppermute | solution.py:71
  55.1 5.1 %collective-permute-done.13 = bf16[256,512]{1,0:T(8,128)(2,1)S(1)} collective-permute-done((bf16[256,512]{1,0:T(8,128)(2,1)S(1)}, bf16[256,512]{1,0:T(8,128)(2,1)S(1)}, u32[]{:S(2)}, u32[]{:S(2)}) %collective-permute-start.13) | collective-permute-done | bytes 262176 | tf_op jit(solution)/shard_map/ppermute | solution.py:71
  60.5 1.7 fusion.57
  62.2 3.1 %collective-permute-start.7 = (bf16[256,512]{1,0:T(8,128)(2,1)S(1)}, bf16[256,512]{1,0:T(8,128)(2,1)S(1)}, u32[]{:S(2)}, u32[]{:S(2)}) collective-permute-start(bf16[256,512]{1,0:T(8,128)(2,1)S(1)} %get-tuple-element.62), channel_id=1, source_target_pairs={{0,4},{2,6},{4,0},{6,2},{1,5},{3,7},{5,1},{7,3},{8,12},{10,14},{12... | collective-permute-start | bytes 786440 | tf_op jit(solution)/shard_map/ppermute | solution.py:71
  65.3 1.1 collective-permute-start.6
  66.5 0.9 collective-permute-start.5
  67.9 1.3 fusion.1
  69.1 3.0 %collective-permute-start.17 = (bf16[256,1024]{1,0:T(8,128)(2,1)}, bf16[256,1024]{1,0:T(8,128)(2,1)}, u32[]{:S(2)}, u32[]{:S(2)}) collective-permute-start(bf16[256,1024]{1,0:T(8,128)(2,1)} %fusion.1), channel_id=1, source_target_pairs={{192,0},{128,64},{193,1},{129,65},{194,2},{130,66},{195,3},{131,67... | collective-permute-start | bytes 1572872 | tf_op jit(solution)/shard_map/ppermute | solution.py:47
  73.0 5.1 %collective-permute-done.6 = bf16[256,512]{1,0:T(8,128)(2,1)S(1)} collective-permute-done((bf16[256,512]{1,0:T(8,128)(2,1)S(1)}, bf16[256,512]{1,0:T(8,128)(2,1)S(1)}, u32[]{:S(2)}, u32[]{:S(2)}) %collective-permute-start.6) | collective-permute-done | bytes 262176 | tf_op jit(solution)/shard_map/ppermute | solution.py:71
  78.6 1.4 collective-permute-done.15
  80.5 2.2 %collective-permute-done.17 = bf16[256,1024]{1,0:T(8,128)(2,1)} collective-permute-done((bf16[256,1024]{1,0:T(8,128)(2,1)}, bf16[256,1024]{1,0:T(8,128)(2,1)}, u32[]{:S(2)}, u32[]{:S(2)}) %collective-permute-start.17) | collective-permute-done | bytes 524320 | tf_op jit(solution)/shard_map/ppermute | solution.py:47
  82.6 1.3 fusion.3
  83.9 6.5 %all-to-all-start.1 = ((bf16[16,16,1024]{2,1,0:T(8,128)(2,1)}), bf16[16,16,1024]{2,1,0:T(8,128)(2,1)S(1)}, u32[]{:S(2)}, u32[]{:S(2)}) async-start(bf16[16,16,1024]{2,1,0:T(8,128)(2,1)} %bitcast.142), calls=%async_computation.1 | async-start | bytes 1048576 | tf_op jit(solution)/shard_map/all_to_all | solution.py:111
  90.4 1.5 slice_bitcast_fusion
  91.9 1.3 collective-permute-start.18
  93.2 7.8 %collective-permute-done.21 = bf16[1024,1024]{1,0:T(8,128)(2,1)} collective-permute-done((bf16[1024,1024]{1,0:T(8,128)(2,1)}, bf16[1024,1024]{1,0:T(8,128)(2,1)}, u32[]{:S(2)}, u32[]{:S(2)}) %collective-permute-start.21) | collective-permute-done | bytes 2097184 | tf_op jit(solution)/shard_map/ppermute | solution.py:43
  101.0 1.3 collective-permute-start.30
  102.3 0.9 broadcast_select_fusion.12
  104.0 2.3 %collective-permute-done.18 = bf16[256,512]{1,0:T(8,128)(2,1)} collective-permute-done((bf16[256,512]{1,0:T(8,128)(2,1)}, bf16[256,512]{1,0:T(8,128)(2,1)}, u32[]{:S(2)}, u32[]{:S(2)}) %collective-permute-start.18) | collective-permute-done | bytes 262176 | tf_op jit(solution)/shard_map/ppermute | solution.py:43
  108.0 6.4 %all-to-all-start.2 = ((bf16[16,16,1024]{2,1,0:T(8,128)(2,1)}), bf16[16,16,1024]{2,1,0:T(8,128)(2,1)S(1)}, u32[]{:S(2)}, u32[]{:S(2)}) async-start(bf16[16,16,1024]{2,1,0:T(8,128)(2,1)} %broadcast_in_dim.175), calls=%async_computation.2 | async-start | bytes 1048576 | tf_op jit(solution)/shard_map/all_to_all | solution.py:122
  115.2 3.6 %collective-permute-start.24 = (bf16[128,1024]{1,0:T(8,128)(2,1)}, bf16[128,1024]{1,0:T(8,128)(2,1)}, u32[]{:S(2)}, u32[]{:S(2)}) collective-permute-start(bf16[128,1024]{1,0:T(8,128)(2,1)} %pad_maximum_fusion.1), channel_id=1, source_target_pairs={{0,4},{2,6},{4,0},{6,2},{1,5},{3,7},{5,1},{7,3},{8,12},{10,14},{12... | collective-permute-start | bytes 786440 | tf_op jit(solution)/shard_map/ppermute | solution.py:71
  118.8 3.8 %broadcast_select_fusion = bf16[1024,1024]{1,0:T(8,128)(2,1)} fusion(bf16[1024,1024]{1,0:T(8,128)(2,1)} %collective-permute-done.21, pred[]{:T(512)S(6)} %eq.35, bf16[1,1024,1024]{2,1,0:T(8,128)(2,1)} %param.7), kind=kLoop, calls=%fused_computation.1 | loop fusion | flops 1048576 | bytes 6291457 | tf_op jit(solution)/shard_map/jit(_where)/select_n | solution.py:148
  122.5 5.4 %collective-permute-done.30 = bf16[512,1024]{1,0:T(8,128)(2,1)} collective-permute-done((bf16[512,1024]{1,0:T(8,128)(2,1)}, bf16[512,1024]{1,0:T(8,128)(2,1)}, u32[]{:S(2)}, u32[]{:S(2)}) %collective-permute-start.30) | collective-permute-done | bytes 1048608 | tf_op jit(solution)/shard_map/ppermute | solution.py:43
  128.0 1.3 collective-permute-start.31
  129.5 6.6 %collective-permute-start.29 = (bf16[256,1024]{1,0:T(8,128)(2,1)S(1)}, bf16[256,1024]{1,0:T(8,128)(2,1)S(1)}, u32[]{:S(2)}, u32[]{:S(2)}) collective-permute-start(bf16[256,1024]{1,0:T(8,128)(2,1)S(1)} %bitcast.129), channel_id=1, source_target_pairs={{192,0},{128,64},{193,1},{129,65},{194,2},{130,66},{195,3},{131,67... | collective-permute-start | bytes 1572872 | tf_op jit(solution)/shard_map/ppermute | solution.py:47
  136.1 1.7 fusion.40
  137.9 1.6 fusion.20
  140.3 1.2 collective-permute-start.28
  141.5 2.3 %collective-permute-start.27 = (bf16[256,512]{1,0:T(8,128)(2,1)S(1)}, bf16[256,512]{1,0:T(8,128)(2,1)S(1)}, u32[]{:S(2)}, u32[]{:S(2)}) collective-permute-start(bf16[256,512]{1,0:T(8,128)(2,1)S(1)} %convert_element_type.158), channel_id=1, source_target_pairs={{0,6},{2,0},{4,2},{6,4},{1,7},{3,1},{5,3},{7,5},{8,14},{10,8},{12,... | collective-permute-start | bytes 786440 | tf_op jit(solution)/shard_map/ppermute | solution.py:71
  144.8 2.6 %convolution_convert_fusion.1 = bf16[1024,1024]{1,0:T(8,128)(2,1)} fusion(bf16[512,1024]{1,0:T(8,128)(2,1)S(1)} %fusion.20, bf16[256,1024]{1,0:T(8,128)(2,1)S(1)} %broadcast_select_fusion.1, bf16[256,1024]{1,0:T(8,128)(2,1)S(1)} %broadcast_select_fusion.2), kind=kOutput, calls=%fused_computation.3 | convolution fusion | flops 1076887552 | bytes 4194304 | tf_op jit(solution)/shard_map/dot_general | solution.py:26
  147.4 3.9 %collective-permute-done.28 = bf16[256,512]{1,0:T(8,128)(2,1)S(1)} collective-permute-done((bf16[256,512]{1,0:T(8,128)(2,1)S(1)}, bf16[256,512]{1,0:T(8,128)(2,1)S(1)}, u32[]{:S(2)}, u32[]{:S(2)}) %collective-permute-start.28) | collective-permute-done | bytes 262176 | tf_op jit(solution)/shard_map/ppermute | solution.py:71
  151.3 4.7 %collective-permute-done.27 = bf16[256,512]{1,0:T(8,128)(2,1)S(1)} collective-permute-done((bf16[256,512]{1,0:T(8,128)(2,1)S(1)}, bf16[256,512]{1,0:T(8,128)(2,1)S(1)}, u32[]{:S(2)}, u32[]{:S(2)}) %collective-permute-start.27) | collective-permute-done | bytes 262176 | tf_op jit(solution)/shard_map/ppermute | solution.py:71
  156.5 1.1 multiply_convert_fusion
  157.6 1.3 collective-permute-start.33
  158.9 2.5 %maximum_select_fusion = bf16[1024,1024]{1,0:T(8,128)(2,1)S(1)} fusion(bf16[512,1024]{1,0:T(8,128)(2,1)} %collective-permute-done.31, bf16[512,1024]{1,0:T(8,128)(2,1)} %collective-permute-done.30, bf16[1,1024,1024]{2,1,0:T(8,128)(2,1)S(1)} %copy-done, pred[]{:T(512)S(6)} %eq.35), kind=kLoop, calls=%fused_computation | loop fusion | flops 5242880 | bytes 6291457 | tf_op jit(solution)/shard_map/jit(_where)/select_n | solution.py:148
  162.0 1.3 fusion.2
  163.3 7.4 %all-to-all-start.3 = ((bf16[16,16,1024]{2,1,0:T(8,128)(2,1)}), bf16[16,16,1024]{2,1,0:T(8,128)(2,1)S(1)}, u32[]{:S(2)}, u32[]{:S(2)}) async-start(bf16[16,16,1024]{2,1,0:T(8,128)(2,1)} %bitcast.37), calls=%async_computation.3 | async-start | bytes 1048576 | tf_op jit(solution)/shard_map/all_to_all | solution.py:111
  170.9 1.4 collective-permute-done.34
  172.5 2.6 %convolution_convert_fusion = bf16[1024,1024]{1,0:T(8,128)(2,1)} fusion(bf16[256,1024]{1,0:T(8,128)(2,1)S(1)} %bitcast.141, bf16[256,1024]{1,0:T(8,128)(2,1)S(1)} %bitcast.138, bf16[256,512]{1,0:T(8,128)(2,1)S(1)} %get-tuple-element.52, bf16[256,512]{1,0:T(8,128)(2,1)S(1)} %get-tuple-element.51, bf16[256,512]{1,0:T(8,128)(2,1)S(1)} %get-tuple-element.50, ...), kind=kOutput, calls=%fused_computation.2 | convolution fusion | flops 1081081856 | bytes 4194304 | tf_op jit(solution)/shard_map/dot_general | solution.py:26
  175.1 11.7 %all-to-all-done.3 = bf16[16,16,1024]{2,1,0:T(8,128)(2,1)S(1)} async-done(((bf16[16,16,1024]{2,1,0:T(8,128)(2,1)}), bf16[16,16,1024]{2,1,0:T(8,128)(2,1)S(1)}, u32[]{:S(2)}, u32[]{:S(2)}) %all-to-all-start.3) | async-done | bytes 524320 | tf_op jit(solution)/shard_map/all_to_all | solution.py:111
  186.9 5.4 %collective-permute-done.35 = bf16[16,1024]{1,0:T(8,128)(2,1)S(1)} collective-permute-done((bf16[16,1024]{1,0:T(8,128)(2,1)S(1)}, bf16[16,1024]{1,0:T(8,128)(2,1)S(1)}, u32[]{:S(2)}, u32[]{:S(2)}) %collective-permute-start.35) | collective-permute-done | bytes 32800 | tf_op jit(solution)/shard_map/ppermute | solution.py:223
  (108 shorter events, 15.2 us)
Async XLA Ops:
  2.6 10.9 %copy-start = (bf16[1,1024,1024]{2,1,0:T(8,128)(2,1)S(1)}, bf16[1,1024,1024]{2,1,0:T(8,128)(2,1)}, u32[]{:S(2)}) copy-start(bf16[1,1024,1024]{2,1,0:T(8,128)(2,1)} %param.6) | copy-start | bytes 6291460
  2.6 35.9 %all-to-all-start = ((bf16[16,32,1024]{2,1,0:T(8,128)(2,1)}), bf16[16,32,1024]{2,1,0:T(8,128)(2,1)}, u32[]{:S(2)}, u32[]{:S(2)}) async-start(bf16[16,32,1024]{2,1,0:T(8,128)(2,1)} %broadcast_in_dim.157), calls=%async_computation | async-start | bytes 2097152 | tf_op jit(solution)/shard_map/all_to_all | solution.py:122
  13.5 1.9 copy-start.6
  13.5 2.3 %copy-start.4 = (bf16[16,1,16,1024]{3,2,1,0:T(8,128)(2,1)}, bf16[16,1,16,1024]{3,2,1,0:T(8,128)(2,1)S(1)}, u32[]{:S(2)}) copy-start(bf16[16,1,16,1024]{3,2,1,0:T(8,128)(2,1)S(1)} %get-tuple-element.55) | copy-start | bytes 1572868
  15.3 2.3 %collective-permute-start = (bf16[512,512]{1,0:T(8,128)(2,1)}, bf16[512,512]{1,0:T(8,128)(2,1)}, u32[]{:S(2)}, u32[]{:S(2)}) collective-permute-start(bf16[512,512]{1,0:T(8,128)(2,1)} %pad_maximum_fusion), channel_id=1, source_target_pairs={{0,1},{1,0},{2,3},{3,2},{4,5},{5,4},{6,7},{7,6},{8,9},{9,8},{10,11... | collective-permute-start | bytes 1572872 | tf_op jit(solution)/shard_map/ppermute | solution.py:39
  19.5 8.1 %collective-permute-start.3 = (bf16[128,512]{1,0:T(8,128)(2,1)}, bf16[128,512]{1,0:T(8,128)(2,1)S(1)}, u32[]{:S(2)}, u32[]{:S(2)}) collective-permute-start(bf16[128,512]{1,0:T(8,128)(2,1)} %get-tuple-element.58), channel_id=1, source_target_pairs={{0,4},{2,6},{4,0},{6,2},{1,5},{3,7},{5,1},{7,3},{8,12},{10,14},{12... | collective-permute-start | bytes 393224 | tf_op jit(solution)/shard_map/ppermute | solution.py:71
  22.6 7.1 %collective-permute-start.2 = (bf16[128,512]{1,0:T(8,128)(2,1)}, bf16[128,512]{1,0:T(8,128)(2,1)S(1)}, u32[]{:S(2)}, u32[]{:S(2)}) collective-permute-start(bf16[128,512]{1,0:T(8,128)(2,1)} %get-tuple-element.59), channel_id=1, source_target_pairs={{0,6},{2,0},{4,2},{6,4},{1,7},{3,1},{5,3},{7,5},{8,14},{10,8},{12,... | collective-permute-start | bytes 393224 | tf_op jit(solution)/shard_map/ppermute | solution.py:71
  23.7 6.6 %collective-permute-start.1 = (bf16[128,512]{1,0:T(8,128)(2,1)S(1)}, bf16[128,512]{1,0:T(8,128)(2,1)}, u32[]{:S(2)}, u32[]{:S(2)}) collective-permute-start(bf16[128,512]{1,0:T(8,128)(2,1)S(1)} %get-tuple-element.57), channel_id=1, source_target_pairs={{0,2},{2,4},{4,6},{6,0},{1,3},{3,5},{5,7},{7,1},{8,10},{10,12},{12... | collective-permute-start | bytes 393224 | tf_op jit(solution)/shard_map/ppermute | solution.py:71
  29.7 0.7 copy-start.17
  31.5 10.3 %collective-permute-start.10 = (bf16[128,512]{1,0:T(8,128)(2,1)S(1)}, bf16[128,512]{1,0:T(8,128)(2,1)S(1)}, u32[]{:S(2)}, u32[]{:S(2)}) collective-permute-start(bf16[128,512]{1,0:T(8,128)(2,1)S(1)} %get-tuple-element.47), channel_id=1, source_target_pairs={{0,2},{2,4},{4,6},{6,0},{1,3},{3,5},{5,7},{7,1},{8,10},{10,12},{12... | collective-permute-start | bytes 393224 | tf_op jit(solution)/shard_map/ppermute | solution.py:71
  33.0 9.0 %collective-permute-start.9 = (bf16[128,512]{1,0:T(8,128)(2,1)S(1)}, bf16[128,512]{1,0:T(8,128)(2,1)S(1)}, u32[]{:S(2)}, u32[]{:S(2)}) collective-permute-start(bf16[128,512]{1,0:T(8,128)(2,1)S(1)} %get-tuple-element.47), channel_id=1, source_target_pairs={{0,4},{2,6},{4,0},{6,2},{1,5},{3,7},{5,1},{7,3},{8,12},{10,14},{12... | collective-permute-start | bytes 393224 | tf_op jit(solution)/shard_map/ppermute | solution.py:71
  35.7 6.3 %collective-permute-start.8 = (bf16[128,512]{1,0:T(8,128)(2,1)S(1)}, bf16[128,512]{1,0:T(8,128)(2,1)S(1)}, u32[]{:S(2)}, u32[]{:S(2)}) collective-permute-start(bf16[128,512]{1,0:T(8,128)(2,1)S(1)} %get-tuple-element.47), channel_id=1, source_target_pairs={{0,6},{2,0},{4,2},{6,4},{1,7},{3,1},{5,3},{7,5},{8,14},{10,8},{12,... | collective-permute-start | bytes 393224 | tf_op jit(solution)/shard_map/ppermute | solution.py:71
  39.8 20.8 %copy-start.2 = (bf16[16,1,16,1024]{3,2,1,0:T(8,128)(2,1)}, bf16[16,1,16,1024]{3,2,1,0:T(8,128)(2,1)S(1)}, u32[]{:S(2)}) copy-start(bf16[16,1,16,1024]{3,2,1,0:T(8,128)(2,1)S(1)} %get-tuple-element.53) | copy-start | bytes 1572868
  41.7 2.6 %collective-permute-start.11 = (bf16[256,512]{1,0:T(8,128)(2,1)S(1)}, bf16[256,512]{1,0:T(8,128)(2,1)S(1)}, u32[]{:S(2)}, u32[]{:S(2)}) collective-permute-start(bf16[256,512]{1,0:T(8,128)(2,1)S(1)} %convolution_convert_fusion.4), channel_id=1, source_target_pairs={{0,1},{1,0},{2,3},{3,2},{4,5},{5,4},{6,7},{7,6},{8,9},{9,8},{10,11... | collective-permute-start | bytes 786440 | tf_op jit(solution)/shard_map/ppermute | solution.py:39
  42.3 17.8 %copy-start.8 = (bf16[512,512]{1,0:T(8,128)(2,1)}, bf16[512,512]{1,0:T(8,128)(2,1)S(1)}, u32[]{:S(2)}) copy-start(bf16[512,512]{1,0:T(8,128)(2,1)S(1)} %fusion.56) | copy-start | bytes 1572868
  44.3 10.7 %collective-permute-start.14 = (bf16[256,512]{1,0:T(8,128)(2,1)S(1)}, bf16[256,512]{1,0:T(8,128)(2,1)S(1)}, u32[]{:S(2)}, u32[]{:S(2)}) collective-permute-start(bf16[256,512]{1,0:T(8,128)(2,1)S(1)} %fusion.58), channel_id=1, source_target_pairs={{0,4},{2,6},{4,0},{6,2},{1,5},{3,7},{5,1},{7,3},{8,12},{10,14},{12... | collective-permute-start | bytes 786440 | tf_op jit(solution)/shard_map/ppermute | solution.py:71
  47.3 12.9 %collective-permute-start.13 = (bf16[256,512]{1,0:T(8,128)(2,1)S(1)}, bf16[256,512]{1,0:T(8,128)(2,1)S(1)}, u32[]{:S(2)}, u32[]{:S(2)}) collective-permute-start(bf16[256,512]{1,0:T(8,128)(2,1)S(1)} %fusion.58), channel_id=1, source_target_pairs={{0,6},{2,0},{4,2},{6,4},{1,7},{3,1},{5,3},{7,5},{8,14},{10,8},{12,... | collective-permute-start | bytes 786440 | tf_op jit(solution)/shard_map/ppermute | solution.py:71
  48.4 11.8 %collective-permute-start.12 = (bf16[256,512]{1,0:T(8,128)(2,1)S(1)}, bf16[256,512]{1,0:T(8,128)(2,1)S(1)}, u32[]{:S(2)}, u32[]{:S(2)}) collective-permute-start(bf16[256,512]{1,0:T(8,128)(2,1)S(1)} %fusion.58), channel_id=1, source_target_pairs={{0,2},{2,4},{4,6},{6,0},{1,3},{3,5},{5,7},{7,1},{8,10},{10,12},{12... | collective-permute-start | bytes 786440 | tf_op jit(solution)/shard_map/ppermute | solution.py:71
  49.3 51.7 %collective-permute-start.21 = (bf16[1024,1024]{1,0:T(8,128)(2,1)}, bf16[1024,1024]{1,0:T(8,128)(2,1)}, u32[]{:S(2)}, u32[]{:S(2)}) collective-permute-start(bf16[1024,1024]{1,0:T(8,128)(2,1)} %bitcast.29), channel_id=1, source_target_pairs={{0,192},{64,128},{1,193},{65,129},{2,194},{66,130},{3,195},{67,131... | collective-permute-start | bytes 6291464 | tf_op jit(solution)/shard_map/ppermute | solution.py:43
  50.6 27.5 %copy-start.16 = (bf16[256,512]{1,0:T(8,128)(2,1)}, bf16[256,512]{1,0:T(8,128)(2,1)S(1)}, u32[]{:S(2)}) copy-start(bf16[256,512]{1,0:T(8,128)(2,1)S(1)} %slice.44) | copy-start | bytes 786436
  52.4 8.1 %collective-permute-start.4 = (bf16[256,512]{1,0:T(8,128)(2,1)S(1)}, bf16[256,512]{1,0:T(8,128)(2,1)S(1)}, u32[]{:S(2)}, u32[]{:S(2)}) collective-permute-start(bf16[256,512]{1,0:T(8,128)(2,1)S(1)} %convolution_convert_fusion.5), channel_id=1, source_target_pairs={{0,1},{1,0},{2,3},{3,2},{4,5},{5,4},{6,7},{7,6},{8,9},{9,8},{10,11... | collective-permute-start | bytes 786440 | tf_op jit(solution)/shard_map/ppermute | solution.py:39
  60.4 7.0 %collective-permute-start.16 = (bf16[256,512]{1,0:T(8,128)(2,1)S(1)}, bf16[256,512]{1,0:T(8,128)(2,1)S(1)}, u32[]{:S(2)}, u32[]{:S(2)}) collective-permute-start(bf16[256,512]{1,0:T(8,128)(2,1)S(1)} %multiply_convert_fusion.2), channel_id=1, source_target_pairs={{0,1},{1,0},{2,3},{3,2},{4,5},{5,4},{6,7},{7,6},{8,9},{9,8},{10,11... | collective-permute-start | bytes 786440 | tf_op jit(solution)/shard_map/ppermute | solution.py:39
  62.2 10.7 %collective-permute-start.7 = (bf16[256,512]{1,0:T(8,128)(2,1)S(1)}, bf16[256,512]{1,0:T(8,128)(2,1)S(1)}, u32[]{:S(2)}, u32[]{:S(2)}) collective-permute-start(bf16[256,512]{1,0:T(8,128)(2,1)S(1)} %get-tuple-element.62), channel_id=1, source_target_pairs={{0,4},{2,6},{4,0},{6,2},{1,5},{3,7},{5,1},{7,3},{8,12},{10,14},{12... | collective-permute-start | bytes 786440 | tf_op jit(solution)/shard_map/ppermute | solution.py:71
  65.3 12.8 %collective-permute-start.6 = (bf16[256,512]{1,0:T(8,128)(2,1)S(1)}, bf16[256,512]{1,0:T(8,128)(2,1)S(1)}, u32[]{:S(2)}, u32[]{:S(2)}) collective-permute-start(bf16[256,512]{1,0:T(8,128)(2,1)S(1)} %get-tuple-element.62), channel_id=1, source_target_pairs={{0,6},{2,0},{4,2},{6,4},{1,7},{3,1},{5,3},{7,5},{8,14},{10,8},{12,... | collective-permute-start | bytes 786440 | tf_op jit(solution)/shard_map/ppermute | solution.py:71
  66.5 11.7 %collective-permute-start.5 = (bf16[256,512]{1,0:T(8,128)(2,1)S(1)}, bf16[256,512]{1,0:T(8,128)(2,1)S(1)}, u32[]{:S(2)}, u32[]{:S(2)}) collective-permute-start(bf16[256,512]{1,0:T(8,128)(2,1)S(1)} %get-tuple-element.62), channel_id=1, source_target_pairs={{0,2},{2,4},{4,6},{6,0},{1,3},{3,5},{5,7},{7,1},{8,10},{10,12},{12... | collective-permute-start | bytes 786440 | tf_op jit(solution)/shard_map/ppermute | solution.py:71
  67.4 1.8 copy-start.12
  69.1 13.5 %collective-permute-start.17 = (bf16[256,1024]{1,0:T(8,128)(2,1)}, bf16[256,1024]{1,0:T(8,128)(2,1)}, u32[]{:S(2)}, u32[]{:S(2)}) collective-permute-start(bf16[256,1024]{1,0:T(8,128)(2,1)} %fusion.1), channel_id=1, source_target_pairs={{192,0},{128,64},{193,1},{129,65},{194,2},{130,66},{195,3},{131,67... | collective-permute-start | bytes 1572872 | tf_op jit(solution)/shard_map/ppermute | solution.py:47
  78.4 5.6 %copy-start.10 = (bf16[256,512]{1,0:T(8,128)(2,1)}, bf16[256,512]{1,0:T(8,128)(2,1)S(1)}, u32[]{:S(2)}) copy-start(bf16[256,512]{1,0:T(8,128)(2,1)S(1)} %multiply_convert_fusion.1) | copy-start | bytes 786436
  78.4 1.6 collective-permute-start.15
  80.0 3.9 %copy-start.14 = (bf16[256,512]{1,0:T(8,128)(2,1)}, bf16[256,512]{1,0:T(8,128)(2,1)S(1)}, u32[]{:S(2)}) copy-start(bf16[256,512]{1,0:T(8,128)(2,1)S(1)} %collective-permute-done.15) | copy-start | bytes 786436
  83.9 22.4 %all-to-all-start.1 = ((bf16[16,16,1024]{2,1,0:T(8,128)(2,1)}), bf16[16,16,1024]{2,1,0:T(8,128)(2,1)S(1)}, u32[]{:S(2)}, u32[]{:S(2)}) async-start(bf16[16,16,1024]{2,1,0:T(8,128)(2,1)} %bitcast.142), calls=%async_computation.1 | async-start | bytes 1048576 | tf_op jit(solution)/shard_map/all_to_all | solution.py:111
  90.4 11.9 %collective-permute-start.19 = (bf16[128,512]{1,0:T(8,128)(2,1)S(1)}, bf16[128,512]{1,0:T(8,128)(2,1)}, u32[]{:S(2)}, u32[]{:S(2)}) collective-permute-start(bf16[128,512]{1,0:T(8,128)(2,1)S(1)} %get-tuple-element.29), channel_id=1, source_target_pairs={{0,1},{1,0},{2,3},{3,2},{4,5},{5,4},{6,7},{7,6},{8,9},{9,8},{10,11... | collective-permute-start | bytes 393224 | tf_op jit(solution)/shard_map/ppermute | solution.py:39
  91.9 14.4 %collective-permute-start.18 = (bf16[256,512]{1,0:T(8,128)(2,1)}, bf16[256,512]{1,0:T(8,128)(2,1)}, u32[]{:S(2)}, u32[]{:S(2)}) collective-permute-start(bf16[256,512]{1,0:T(8,128)(2,1)} %copy-done.16), channel_id=1, source_target_pairs={{0,192},{64,128},{1,193},{65,129},{2,194},{66,130},{3,195},{67,131... | collective-permute-start | bytes 786440 | tf_op jit(solution)/shard_map/ppermute | solution.py:43
  101.0 27.0 %collective-permute-start.30 = (bf16[512,1024]{1,0:T(8,128)(2,1)}, bf16[512,1024]{1,0:T(8,128)(2,1)}, u32[]{:S(2)}, u32[]{:S(2)}) collective-permute-start(bf16[512,1024]{1,0:T(8,128)(2,1)} %get-tuple-element.35), channel_id=1, source_target_pairs={{0,192},{64,128},{1,193},{65,129},{2,194},{66,130},{3,195},{67,131... | collective-permute-start | bytes 3145736 | tf_op jit(solution)/shard_map/ppermute | solution.py:43
  108.0 21.5 %all-to-all-start.2 = ((bf16[16,16,1024]{2,1,0:T(8,128)(2,1)}), bf16[16,16,1024]{2,1,0:T(8,128)(2,1)S(1)}, u32[]{:S(2)}, u32[]{:S(2)}) async-start(bf16[16,16,1024]{2,1,0:T(8,128)(2,1)} %broadcast_in_dim.175), calls=%async_computation.2 | async-start | bytes 1048576 | tf_op jit(solution)/shard_map/all_to_all | solution.py:122
  114.4 23.4 %collective-permute-start.25 = (bf16[128,1024]{1,0:T(8,128)(2,1)}, bf16[128,1024]{1,0:T(8,128)(2,1)}, u32[]{:S(2)}, u32[]{:S(2)}) collective-permute-start(bf16[128,1024]{1,0:T(8,128)(2,1)} %pad_maximum_fusion.1), channel_id=1, source_target_pairs={{0,2},{2,4},{4,6},{6,0},{1,3},{3,5},{5,7},{7,1},{8,10},{10,12},{12... | collective-permute-start | bytes 786440 | tf_op jit(solution)/shard_map/ppermute | solution.py:71
  115.2 22.7 %collective-permute-start.24 = (bf16[128,1024]{1,0:T(8,128)(2,1)}, bf16[128,1024]{1,0:T(8,128)(2,1)}, u32[]{:S(2)}, u32[]{:S(2)}) collective-permute-start(bf16[128,1024]{1,0:T(8,128)(2,1)} %pad_maximum_fusion.1), channel_id=1, source_target_pairs={{0,4},{2,6},{4,0},{6,2},{1,5},{3,7},{5,1},{7,3},{8,12},{10,14},{12... | collective-permute-start | bytes 786440 | tf_op jit(solution)/shard_map/ppermute | solution.py:71
  118.8 19.1 %collective-permute-start.23 = (bf16[128,1024]{1,0:T(8,128)(2,1)}, bf16[128,1024]{1,0:T(8,128)(2,1)}, u32[]{:S(2)}, u32[]{:S(2)}) collective-permute-start(bf16[128,1024]{1,0:T(8,128)(2,1)} %pad_maximum_fusion.1), channel_id=1, source_target_pairs={{0,6},{2,0},{4,2},{6,4},{1,7},{3,1},{5,3},{7,5},{8,14},{10,8},{12,... | collective-permute-start | bytes 786440 | tf_op jit(solution)/shard_map/ppermute | solution.py:71
  128.0 28.5 %collective-permute-start.31 = (bf16[512,1024]{1,0:T(8,128)(2,1)}, bf16[512,1024]{1,0:T(8,128)(2,1)}, u32[]{:S(2)}, u32[]{:S(2)}) collective-permute-start(bf16[512,1024]{1,0:T(8,128)(2,1)} %get-tuple-element.36), channel_id=1, source_target_pairs={{0,192},{64,128},{1,193},{65,129},{2,194},{66,130},{3,195},{67,131... | collective-permute-start | bytes 3145736 | tf_op jit(solution)/shard_map/ppermute | solution.py:43
  129.5 15.2 %collective-permute-start.29 = (bf16[256,1024]{1,0:T(8,128)(2,1)S(1)}, bf16[256,1024]{1,0:T(8,128)(2,1)S(1)}, u32[]{:S(2)}, u32[]{:S(2)}) collective-permute-start(bf16[256,1024]{1,0:T(8,128)(2,1)S(1)} %bitcast.129), channel_id=1, source_target_pairs={{192,0},{128,64},{193,1},{129,65},{194,2},{130,66},{195,3},{131,67... | collective-permute-start | bytes 1572872 | tf_op jit(solution)/shard_map/ppermute | solution.py:47
  137.8 1.9 copy-start.1
  137.8 1.9 collective-permute-start.22
  139.5 5.1 %copy-start.3 = (bf16[16,1,16,1024]{3,2,1,0:T(8,128)(2,1)S(1)}, bf16[16,1,16,1024]{3,2,1,0:T(8,128)(2,1)}, u32[]{:S(2)}) copy-start(bf16[16,1,16,1024]{3,2,1,0:T(8,128)(2,1)} %copy-done.2) | copy-start | bytes 1572868
  140.3 11.0 %collective-permute-start.28 = (bf16[256,512]{1,0:T(8,128)(2,1)S(1)}, bf16[256,512]{1,0:T(8,128)(2,1)S(1)}, u32[]{:S(2)}, u32[]{:S(2)}) collective-permute-start(bf16[256,512]{1,0:T(8,128)(2,1)S(1)} %convert_element_type.158), channel_id=1, source_target_pairs={{0,4},{2,6},{4,0},{6,2},{1,5},{3,7},{5,1},{7,3},{8,12},{10,14},{12... | collective-permute-start | bytes 786440 | tf_op jit(solution)/shard_map/ppermute | solution.py:71
  141.5 14.5 %collective-permute-start.27 = (bf16[256,512]{1,0:T(8,128)(2,1)S(1)}, bf16[256,512]{1,0:T(8,128)(2,1)S(1)}, u32[]{:S(2)}, u32[]{:S(2)}) collective-permute-start(bf16[256,512]{1,0:T(8,128)(2,1)S(1)} %convert_element_type.158), channel_id=1, source_target_pairs={{0,6},{2,0},{4,2},{6,4},{1,7},{3,1},{5,3},{7,5},{8,14},{10,8},{12,... | collective-permute-start | bytes 786440 | tf_op jit(solution)/shard_map/ppermute | solution.py:71
  143.9 12.4 %collective-permute-start.26 = (bf16[256,512]{1,0:T(8,128)(2,1)S(1)}, bf16[256,512]{1,0:T(8,128)(2,1)S(1)}, u32[]{:S(2)}, u32[]{:S(2)}) collective-permute-start(bf16[256,512]{1,0:T(8,128)(2,1)S(1)} %convert_element_type.158), channel_id=1, source_target_pairs={{0,2},{2,4},{4,6},{6,0},{1,3},{3,5},{5,7},{7,1},{8,10},{10,12},{12... | collective-permute-start | bytes 786440 | tf_op jit(solution)/shard_map/ppermute | solution.py:71
  144.8 11.7 %copy-start.9 = (bf16[512,512]{1,0:T(8,128)(2,1)S(1)}, bf16[512,512]{1,0:T(8,128)(2,1)}, u32[]{:S(2)}) copy-start(bf16[512,512]{1,0:T(8,128)(2,1)} %copy-done.8) | copy-start | bytes 1572868
  157.5 4.0 %collective-permute-start.32 = (bf16[256,512]{1,0:T(8,128)(2,1)S(1)}, bf16[256,512]{1,0:T(8,128)(2,1)S(1)}, u32[]{:S(2)}, u32[]{:S(2)}) collective-permute-start(bf16[256,512]{1,0:T(8,128)(2,1)S(1)} %multiply_convert_fusion), channel_id=1, source_target_pairs={{0,1},{1,0},{2,3},{3,2},{4,5},{5,4},{6,7},{7,6},{8,9},{9,8},{10,11... | collective-permute-start | bytes 786440 | tf_op jit(solution)/shard_map/ppermute | solution.py:39
  157.6 13.1 %collective-permute-start.33 = (bf16[256,512]{1,0:T(8,128)(2,1)S(1)}, bf16[256,512]{1,0:T(8,128)(2,1)S(1)}, u32[]{:S(2)}, u32[]{:S(2)}) collective-permute-start(bf16[256,512]{1,0:T(8,128)(2,1)S(1)} %multiply_convert_fusion), channel_id=1, source_target_pairs={{192,0},{128,64},{193,1},{129,65},{194,2},{130,66},{195,3},{131,67... | collective-permute-start | bytes 786440 | tf_op jit(solution)/shard_map/ppermute | solution.py:47
  162.0 8.8 %copy-start.13 = (bf16[256,512]{1,0:T(8,128)(2,1)S(1)}, bf16[256,512]{1,0:T(8,128)(2,1)}, u32[]{:S(2)}) copy-start(bf16[256,512]{1,0:T(8,128)(2,1)} %copy-done.12) | copy-start | bytes 786436
  162.0 10.4 %copy-start.11 = (bf16[256,512]{1,0:T(8,128)(2,1)S(1)}, bf16[256,512]{1,0:T(8,128)(2,1)}, u32[]{:S(2)}) copy-start(bf16[256,512]{1,0:T(8,128)(2,1)} %copy-done.10) | copy-start | bytes 786436
  162.0 10.3 %copy-start.15 = (bf16[256,512]{1,0:T(8,128)(2,1)S(1)}, bf16[256,512]{1,0:T(8,128)(2,1)}, u32[]{:S(2)}) copy-start(bf16[256,512]{1,0:T(8,128)(2,1)} %copy-done.14) | copy-start | bytes 786436
  163.3 9.1 %copy-start.5 = (bf16[16,1,16,1024]{3,2,1,0:T(8,128)(2,1)S(1)}, bf16[16,1,16,1024]{3,2,1,0:T(8,128)(2,1)}, u32[]{:S(2)}) copy-start(bf16[16,1,16,1024]{3,2,1,0:T(8,128)(2,1)} %copy-done.4) | copy-start | bytes 1572868
  163.3 9.1 %copy-start.7 = (bf16[16,1,16,1024]{3,2,1,0:T(8,128)(2,1)S(1)}, bf16[16,1,16,1024]{3,2,1,0:T(8,128)(2,1)}, u32[]{:S(2)}) copy-start(bf16[16,1,16,1024]{3,2,1,0:T(8,128)(2,1)} %copy-done.6) | copy-start | bytes 1572868
  163.3 23.4 %all-to-all-start.3 = ((bf16[16,16,1024]{2,1,0:T(8,128)(2,1)}), bf16[16,16,1024]{2,1,0:T(8,128)(2,1)S(1)}, u32[]{:S(2)}, u32[]{:S(2)}) async-start(bf16[16,16,1024]{2,1,0:T(8,128)(2,1)} %bitcast.37), calls=%async_computation.3 | async-start | bytes 1048576 | tf_op jit(solution)/shard_map/all_to_all | solution.py:111
  170.7 16.1 %collective-permute-start.20 = (bf16[16,1024]{1,0:T(8,128)(2,1)S(1)}, bf16[16,1024]{1,0:T(8,128)(2,1)S(1)}, u32[]{:S(2)}, u32[]{:S(2)}) collective-permute-start(bf16[16,1024]{1,0:T(8,128)(2,1)S(1)} %add_convert_fusion.1), channel_id=1, source_target_pairs={{0,128},{128,0},{1,129},{129,1},{2,130},{130,2},{3,131},{131,3},{4... | collective-permute-start | bytes 98312 | tf_op jit(solution)/shard_map/ppermute | solution.py:222
  170.7 1.6 collective-permute-start.34
  186.8 5.5 %collective-permute-start.35 = (bf16[16,1024]{1,0:T(8,128)(2,1)S(1)}, bf16[16,1024]{1,0:T(8,128)(2,1)S(1)}, u32[]{:S(2)}, u32[]{:S(2)}) collective-permute-start(bf16[16,1024]{1,0:T(8,128)(2,1)S(1)} %get-tuple-element.44), channel_id=1, source_target_pairs={{0,128},{128,0},{1,129},{129,1},{2,130},{130,2},{3,131},{131,3},{4... | collective-permute-start | bytes 98312 | tf_op jit(solution)/shard_map/ppermute | solution.py:223

commit v15 on v14

--- a/solution.py
+++ b/solution.py
@@ -199,11 +199,16 @@
     low_total = add_terms(narrow_terms(pair))
     incoming = jnp.concatenate([pick(top[0], low), pick(top[1], low_rest)], axis=0)
     grad_down = contract(hidden, incoming, 0, 0).astype(jnp.bfloat16)
-    low_total, grad_down, sent_up[1] = together(low_total, grad_down, sent_up[1])
-    low_up = pick(jnp.concatenate(sent_up, axis=0), w_up)
+    low_up = [pick(sent_up[0], w_up[:half])]
+    low_total, grad_down, sent_up[1], low_up[0] = together(
+        low_total, grad_down, sent_up[1], low_up[0]
+    )
+    low_up.append(pick(sent_up[1], w_up[half:]))
     low_slope = slope_of(low_total, lower_slopes)
     low_slope_rest = to_lower(low_slope[0])
-    low_blocks = spread_wide(back_through_up(low_slope, halves(low_up, 1)))
+    low_blocks = spread_wide(
+        jnp.concatenate([back_through_up(low_slope, halves(piece, 1)) for piece in low_up], axis=1)
+    )
     slope_grad = jnp.concatenate(
         [
             in_order(*[pick(u, l) for u, l in zip(top_slope, low_slope)]),

time: 194 us -> 203 us (1.046)
  starting transfers between devices: 75.1 us -> 79.3 us
  waiting for transfers between devices: 69.3 us -> 72.3 us
    ppermute x4, waiting for transfers between devices: 15.5 us -> 19.9 us  [to_upper(): return lax.ppermute(block, CROSS_AXES, [(0, 3), (1, 2)])]
    all_to_all x2, starting transfers between devices: 13.9 us -> 16.1 us  [spread_wide(): lax.all_to_all(partial.reshape(WIDE, rows // WIDE, cols), WIDE_AXES, 0, 0...]
    select_n x6 -> x7, other arithmetic: 6.56 us -> 7.66 us  [pick(): return jnp.where(is_upper, upper, lower)]
    dot_general x18 -> x20, matrix products: 21.9 us -> 21.5 us  [contract(): lax.dot_general(first_op, second_op, (((first_dim,), (second_dim,)), ((),...]
  transfers between devices with their start and end apart: 40 -> 40, of which waited for: 22 -> 21; matrix products, arithmetic and copies ran while one was open for 22% -> 22% of each run, Pallas kernels for 0% -> 0%
where the time goes in v15:
time: 203 us; the launch traced here: 202 us
  starting transfers between devices  79.3 us (39%)
  waiting for transfers between devices  72.3 us (36%)
  matrix products  21.5 us (11%)
  other arithmetic  18.8 us (9%)
  local copies, waits for them, and re-layouts  8.53 us (4%)
    ppermute x18, starting transfers between devices, step_x(): return lax.ppermute(block, 'x', [(i, (i + distance) % X) for i in range(X)])  28.6 us
    ppermute x18, waiting for transfers between devices, step_x(): return lax.ppermute(block, 'x', [(i, (i + distance) % X) for i in range(X)])  27.6 us
    dot_general x20, matrix products, contract(): lax.dot_general(first_op, second_op, (((first_dim,), (second_dim,)), ((),...  21.5 us
    ppermute x4, waiting for transfers between devices, to_upper(): return lax.ppermute(block, CROSS_AXES, [(0, 3), (1, 2)])  19.9 us
    all_to_all x2, starting transfers between devices, spread_wide(): lax.all_to_all(partial.reshape(WIDE, rows // WIDE, cols), WIDE_AXES, 0, 0...  16.1 us
    all_to_all x2, starting transfers between devices, gather_wide(): lax.all_to_all(jnp.broadcast_to(block[None], (WIDE, rows, cols)), WIDE_AX...  16 us
    ppermute x3, starting transfers between devices, to_lower(): return lax.ppermute(block, CROSS_AXES, [(3, 0), (2, 1)])  12.4 us
    all_to_all x2, waiting for transfers between devices, spread_wide(): lax.all_to_all(partial.reshape(WIDE, rows // WIDE, cols), WIDE_AXES, 0, 0...  11.2 us
  transfers between devices with their start and end apart: 40, of which 21 were waited for; matrix products, arithmetic and copies ran while one was open for 22% of the time, Pallas kernels for 0%

profile of v15, /device:TPU:56, one launch (start us, length us, event | category | flops | bytes accessed | tf_op | source)
XLA Modules:
  0.0 201.7 jit_solution(7135356969213652703)
XLA Ops:
  0.6 1.9 broadcast_in_dim.157
  2.6 9.6 %all-to-all-start = ((bf16[16,32,1024]{2,1,0:T(8,128)(2,1)}), bf16[16,32,1024]{2,1,0:T(8,128)(2,1)}, u32[]{:S(2)}, u32[]{:S(2)}) async-start(bf16[16,32,1024]{2,1,0:T(8,128)(2,1)} %broadcast_in_dim.157), calls=%async_computation | async-start | bytes 2097152 | tf_op jit(solution)/shard_map/all_to_all | solution.py:122
  12.2 1.3 fusion.93
  16.3 1.2 collective-permute-done
  17.5 1.2 maximum_add_fusion
  19.5 3.0 %collective-permute-start.3 = (bf16[128,512]{1,0:T(8,128)(2,1)}, bf16[128,512]{1,0:T(8,128)(2,1)S(1)}, u32[]{:S(2)}, u32[]{:S(2)}) collective-permute-start(bf16[128,512]{1,0:T(8,128)(2,1)} %get-tuple-element.60), channel_id=1, source_target_pairs={{0,4},{2,6},{4,0},{6,2},{1,5},{3,7},{5,1},{7,3},{8,12},{10,14},{12... | collective-permute-start | bytes 393224 | tf_op jit(solution)/shard_map/ppermute | solution.py:71
  22.6 1.1 collective-permute-start.2
  23.7 0.9 collective-permute-start.1
  24.7 2.9 %collective-permute-done.3 = bf16[128,512]{1,0:T(8,128)(2,1)S(1)} collective-permute-done((bf16[128,512]{1,0:T(8,128)(2,1)}, bf16[128,512]{1,0:T(8,128)(2,1)S(1)}, u32[]{:S(2)}, u32[]{:S(2)}) %collective-permute-start.3) | collective-permute-done | bytes 131104 | tf_op jit(solution)/shard_map/ppermute | solution.py:71
  27.6 2.1 %collective-permute-done.2 = bf16[128,512]{1,0:T(8,128)(2,1)S(1)} collective-permute-done((bf16[128,512]{1,0:T(8,128)(2,1)}, bf16[128,512]{1,0:T(8,128)(2,1)S(1)}, u32[]{:S(2)}, u32[]{:S(2)}) %collective-permute-start.2) | collective-permute-done | bytes 131104 | tf_op jit(solution)/shard_map/ppermute | solution.py:71
  30.3 1.2 fusion.68
  31.5 1.5 collective-permute-start.10
  33.0 2.7 %collective-permute-start.9 = (bf16[128,512]{1,0:T(8,128)(2,1)S(1)}, bf16[128,512]{1,0:T(8,128)(2,1)S(1)}, u32[]{:S(2)}, u32[]{:S(2)}) collective-permute-start(bf16[128,512]{1,0:T(8,128)(2,1)S(1)} %get-tuple-element.49), channel_id=1, source_target_pairs={{0,4},{2,6},{4,0},{6,2},{1,5},{3,7},{5,1},{7,3},{8,12},{10,14},{12... | collective-permute-start | bytes 393224 | tf_op jit(solution)/shard_map/ppermute | solution.py:71
  35.7 0.9 collective-permute-start.8
  36.6 1.8 all-to-all-done
  38.5 1.3 fusion.92
  39.8 1.9 convolution_convert_fusion.4
  42.4 1.9 fusion.24
  44.4 2.9 %collective-permute-start.14 = (bf16[256,512]{1,0:T(8,128)(2,1)S(1)}, bf16[256,512]{1,0:T(8,128)(2,1)S(1)}, u32[]{:S(2)}, u32[]{:S(2)}) collective-permute-start(bf16[256,512]{1,0:T(8,128)(2,1)S(1)} %fusion.62), channel_id=1, source_target_pairs={{0,4},{2,6},{4,0},{6,2},{1,5},{3,7},{5,1},{7,3},{8,12},{10,14},{12... | collective-permute-start | bytes 786440 | tf_op jit(solution)/shard_map/ppermute | solution.py:71
  47.3 1.1 collective-permute-start.13
  48.4 0.9 collective-permute-start.12
  49.3 1.3 collective-permute-start.21
  50.6 1.8 convolution_convert_fusion.5
  52.7 2.4 %collective-permute-done.14 = bf16[256,512]{1,0:T(8,128)(2,1)S(1)} collective-permute-done((bf16[256,512]{1,0:T(8,128)(2,1)S(1)}, bf16[256,512]{1,0:T(8,128)(2,1)S(1)}, u32[]{:S(2)}, u32[]{:S(2)}) %collective-permute-start.14) | collective-permute-done | bytes 262176 | tf_op jit(solution)/shard_map/ppermute | solution.py:71
  55.1 5.1 %collective-permute-done.13 = bf16[256,512]{1,0:T(8,128)(2,1)S(1)} collective-permute-done((bf16[256,512]{1,0:T(8,128)(2,1)S(1)}, bf16[256,512]{1,0:T(8,128)(2,1)S(1)}, u32[]{:S(2)}, u32[]{:S(2)}) %collective-permute-start.13) | collective-permute-done | bytes 262176 | tf_op jit(solution)/shard_map/ppermute | solution.py:71
  60.5 1.7 fusion.61
  62.2 3.1 %collective-permute-start.7 = (bf16[256,512]{1,0:T(8,128)(2,1)S(1)}, bf16[256,512]{1,0:T(8,128)(2,1)S(1)}, u32[]{:S(2)}, u32[]{:S(2)}) collective-permute-start(bf16[256,512]{1,0:T(8,128)(2,1)S(1)} %get-tuple-element.64), channel_id=1, source_target_pairs={{0,4},{2,6},{4,0},{6,2},{1,5},{3,7},{5,1},{7,3},{8,12},{10,14},{12... | collective-permute-start | bytes 786440 | tf_op jit(solution)/shard_map/ppermute | solution.py:71
  65.3 1.1 collective-permute-start.6
  67.9 1.3 fusion.1
  69.1 3.0 %collective-permute-start.17 = (bf16[256,1024]{1,0:T(8,128)(2,1)}, bf16[256,1024]{1,0:T(8,128)(2,1)}, u32[]{:S(2)}, u32[]{:S(2)}) collective-permute-start(bf16[256,1024]{1,0:T(8,128)(2,1)} %fusion.1), channel_id=1, source_target_pairs={{192,0},{128,64},{193,1},{129,65},{194,2},{130,66},{195,3},{131,67... | collective-permute-start | bytes 1572872 | tf_op jit(solution)/shard_map/ppermute | solution.py:47
  73.0 5.1 %collective-permute-done.6 = bf16[256,512]{1,0:T(8,128)(2,1)S(1)} collective-permute-done((bf16[256,512]{1,0:T(8,128)(2,1)S(1)}, bf16[256,512]{1,0:T(8,128)(2,1)S(1)}, u32[]{:S(2)}, u32[]{:S(2)}) %collective-permute-start.6) | collective-permute-done | bytes 262176 | tf_op jit(solution)/shard_map/ppermute | solution.py:71
  78.6 1.4 collective-permute-done.15
  80.5 2.2 %collective-permute-done.17 = bf16[256,1024]{1,0:T(8,128)(2,1)} collective-permute-done((bf16[256,1024]{1,0:T(8,128)(2,1)}, bf16[256,1024]{1,0:T(8,128)(2,1)}, u32[]{:S(2)}, u32[]{:S(2)}) %collective-permute-start.17) | collective-permute-done | bytes 524320 | tf_op jit(solution)/shard_map/ppermute | solution.py:47
  82.6 1.3 fusion.2
  83.9 6.5 %all-to-all-start.1 = ((bf16[16,16,1024]{2,1,0:T(8,128)(2,1)}), bf16[16,16,1024]{2,1,0:T(8,128)(2,1)S(1)}, u32[]{:S(2)}, u32[]{:S(2)}) async-start(bf16[16,16,1024]{2,1,0:T(8,128)(2,1)} %bitcast.146), calls=%async_computation.1 | async-start | bytes 1048576 | tf_op jit(solution)/shard_map/all_to_all | solution.py:111
  90.5 1.5 slice_bitcast_fusion
  92.0 1.3 collective-permute-start.18
  93.3 7.7 %collective-permute-done.21 = bf16[1024,1024]{1,0:T(8,128)(2,1)} collective-permute-done((bf16[1024,1024]{1,0:T(8,128)(2,1)}, bf16[1024,1024]{1,0:T(8,128)(2,1)}, u32[]{:S(2)}, u32[]{:S(2)}) %collective-permute-start.21) | collective-permute-done | bytes 2097184 | tf_op jit(solution)/shard_map/ppermute | solution.py:43
  101.0 1.3 collective-permute-start.30
  102.3 0.9 broadcast_select_fusion.14
  104.0 2.3 %collective-permute-done.18 = bf16[256,512]{1,0:T(8,128)(2,1)} collective-permute-done((bf16[256,512]{1,0:T(8,128)(2,1)}, bf16[256,512]{1,0:T(8,128)(2,1)}, u32[]{:S(2)}, u32[]{:S(2)}) %collective-permute-start.18) | collective-permute-done | bytes 262176 | tf_op jit(solution)/shard_map/ppermute | solution.py:43
  108.0 6.4 %all-to-all-start.2 = ((bf16[16,16,1024]{2,1,0:T(8,128)(2,1)}), bf16[16,16,1024]{2,1,0:T(8,128)(2,1)S(1)}, u32[]{:S(2)}, u32[]{:S(2)}) async-start(bf16[16,16,1024]{2,1,0:T(8,128)(2,1)} %broadcast_in_dim.175), calls=%async_computation.2 | async-start | bytes 1048576 | tf_op jit(solution)/shard_map/all_to_all | solution.py:122
  114.4 3.8 %broadcast_select_fusion = bf16[1024,1024]{1,0:T(8,128)(2,1)} fusion(bf16[1024,1024]{1,0:T(8,128)(2,1)} %collective-permute-done.21, pred[]{:T(512)S(6)} %eq.35, bf16[1,1024,1024]{2,1,0:T(8,128)(2,1)} %param.7), kind=kLoop, calls=%fused_computation | loop fusion | flops 1048576 | bytes 6291457 | tf_op jit(solution)/shard_map/jit(_where)/select_n | solution.py:148
  118.2 9.8 %collective-permute-done.30 = bf16[512,1024]{1,0:T(8,128)(2,1)} collective-permute-done((bf16[512,1024]{1,0:T(8,128)(2,1)}, bf16[512,1024]{1,0:T(8,128)(2,1)}, u32[]{:S(2)}, u32[]{:S(2)}) %collective-permute-start.30) | collective-permute-done | bytes 1048608 | tf_op jit(solution)/shard_map/ppermute | solution.py:43
  128.0 1.3 collective-permute-start.31
  129.9 3.2 %collective-permute-start.24 = (bf16[128,1024]{1,0:T(8,128)(2,1)}, bf16[128,1024]{1,0:T(8,128)(2,1)}, u32[]{:S(2)}, u32[]{:S(2)}) collective-permute-start(bf16[128,1024]{1,0:T(8,128)(2,1)} %pad_maximum_fusion.2), channel_id=1, source_target_pairs={{0,4},{2,6},{4,0},{6,2},{1,5},{3,7},{5,1},{7,3},{8,12},{10,14},{12... | collective-permute-start | bytes 786440 | tf_op jit(solution)/shard_map/ppermute | solution.py:71
  133.2 2.3 %broadcast_select_fusion.2 = bf16[512,1024]{1,0:T(8,128)(2,1)} fusion(bf16[512,1024]{1,0:T(8,128)(2,1)} %collective-permute-done.30, pred[]{:T(512)S(6)} %eq.35, bf16[1,1024,1024]{2,1,0:T(8,128)(2,1)S(1)} %copy-done), kind=kLoop, calls=%fused_computation.62 | loop fusion | flops 524288 | bytes 3145729 | tf_op jit(solution)/shard_map/jit(_where)/select_n | solution.py:148
  135.5 5.5 %collective-permute-start.29 = (bf16[256,1024]{1,0:T(8,128)(2,1)S(1)}, bf16[256,1024]{1,0:T(8,128)(2,1)S(1)}, u32[]{:S(2)}, u32[]{:S(2)}) collective-permute-start(bf16[256,1024]{1,0:T(8,128)(2,1)S(1)} %bitcast.133), channel_id=1, source_target_pairs={{192,0},{128,64},{193,1},{129,65},{194,2},{130,66},{195,3},{131,67... | collective-permute-start | bytes 1572872 | tf_op jit(solution)/shard_map/ppermute | solution.py:47
  141.0 1.7 fusion.38
  143.5 1.5 fusion.21
  145.7 2.1 %collective-permute-start.28 = (bf16[256,512]{1,0:T(8,128)(2,1)S(1)}, bf16[256,512]{1,0:T(8,128)(2,1)S(1)}, u32[]{:S(2)}, u32[]{:S(2)}) collective-permute-start(bf16[256,512]{1,0:T(8,128)(2,1)S(1)} %convert_element_type.161), channel_id=1, source_target_pairs={{0,4},{2,6},{4,0},{6,2},{1,5},{3,7},{5,1},{7,3},{8,12},{10,14},{12... | collective-permute-start | bytes 786440 | tf_op jit(solution)/shard_map/ppermute | solution.py:71
  147.9 2.4 %collective-permute-start.27 = (bf16[256,512]{1,0:T(8,128)(2,1)S(1)}, bf16[256,512]{1,0:T(8,128)(2,1)S(1)}, u32[]{:S(2)}, u32[]{:S(2)}) collective-permute-start(bf16[256,512]{1,0:T(8,128)(2,1)S(1)} %convert_element_type.161), channel_id=1, source_target_pairs={{0,6},{2,0},{4,2},{6,4},{1,7},{3,1},{5,3},{7,5},{8,14},{10,8},{12,... | collective-permute-start | bytes 786440 | tf_op jit(solution)/shard_map/ppermute | solution.py:71
  150.3 2.6 %convolution_convert_fusion.1 = bf16[1024,1024]{1,0:T(8,128)(2,1)} fusion(bf16[512,1024]{1,0:T(8,128)(2,1)S(1)} %fusion.21, bf16[256,1024]{1,0:T(8,128)(2,1)S(1)} %broadcast_select_fusion.3, bf16[256,1024]{1,0:T(8,128)(2,1)S(1)} %broadcast_select_fusion.4), kind=kOutput, calls=%fused_computation.2 | convolution fusion | flops 1076887552 | bytes 4194304 | tf_op jit(solution)/shard_map/dot_general | solution.py:26
  153.0 3.8 %collective-permute-done.28 = bf16[256,512]{1,0:T(8,128)(2,1)S(1)} collective-permute-done((bf16[256,512]{1,0:T(8,128)(2,1)S(1)}, bf16[256,512]{1,0:T(8,128)(2,1)S(1)}, u32[]{:S(2)}, u32[]{:S(2)}) %collective-permute-start.28) | collective-permute-done | bytes 262176 | tf_op jit(solution)/shard_map/ppermute | solution.py:71
  156.7 3.3 %collective-permute-done.27 = bf16[256,512]{1,0:T(8,128)(2,1)S(1)} collective-permute-done((bf16[256,512]{1,0:T(8,128)(2,1)S(1)}, bf16[256,512]{1,0:T(8,128)(2,1)S(1)}, u32[]{:S(2)}, u32[]{:S(2)}) %collective-permute-start.27) | collective-permute-done | bytes 262176 | tf_op jit(solution)/shard_map/ppermute | solution.py:71
  160.0 1.2 collective-permute-done.26
  161.3 1.1 multiply_convert_fusion
  162.5 4.0 %collective-permute-start.33 = (bf16[256,512]{1,0:T(8,128)(2,1)S(1)}, bf16[256,512]{1,0:T(8,128)(2,1)S(1)}, u32[]{:S(2)}, u32[]{:S(2)}) collective-permute-start(bf16[256,512]{1,0:T(8,128)(2,1)S(1)} %multiply_convert_fusion), channel_id=1, source_target_pairs={{192,0},{128,64},{193,1},{129,65},{194,2},{130,66},{195,3},{131,67... | collective-permute-start | bytes 786440 | tf_op jit(solution)/shard_map/ppermute | solution.py:47
  166.5 1.3 broadcast_select_fusion.1
  170.2 9.6 %all-to-all-start.3 = ((bf16[16,16,1024]{2,1,0:T(8,128)(2,1)}), bf16[16,16,1024]{2,1,0:T(8,128)(2,1)S(1)}, u32[]{:S(2)}, u32[]{:S(2)}) async-start(bf16[16,16,1024]{2,1,0:T(8,128)(2,1)} %bitcast.36), calls=%async_computation.3 | async-start | bytes 1048576 | tf_op jit(solution)/shard_map/all_to_all | solution.py:111
  180.0 1.4 collective-permute-done.34
  181.6 2.6 %convolution_convert_fusion = bf16[1024,1024]{1,0:T(8,128)(2,1)} fusion(bf16[256,1024]{1,0:T(8,128)(2,1)S(1)} %bitcast.145, bf16[256,1024]{1,0:T(8,128)(2,1)S(1)} %bitcast.142, bf16[256,512]{1,0:T(8,128)(2,1)S(1)} %get-tuple-element.54, bf16[256,512]{1,0:T(8,128)(2,1)S(1)} %get-tuple-element.53, bf16[256,512]{1,0:T(8,128)(2,1)S(1)} %get-tuple-element.52, ...), kind=kOutput, calls=%fused_computation.1 | convolution fusion | flops 1081081856 | bytes 4194304 | tf_op jit(solution)/shard_map/dot_general | solution.py:26
  184.2 11.2 %all-to-all-done.3 = bf16[16,16,1024]{2,1,0:T(8,128)(2,1)S(1)} async-done(((bf16[16,16,1024]{2,1,0:T(8,128)(2,1)}), bf16[16,16,1024]{2,1,0:T(8,128)(2,1)S(1)}, u32[]{:S(2)}, u32[]{:S(2)}) %all-to-all-start.3) | async-done | bytes 524320 | tf_op jit(solution)/shard_map/all_to_all | solution.py:111
  195.6 5.4 %collective-permute-done.35 = bf16[16,1024]{1,0:T(8,128)(2,1)S(1)} collective-permute-done((bf16[16,1024]{1,0:T(8,128)(2,1)S(1)}, bf16[16,1024]{1,0:T(8,128)(2,1)S(1)}, u32[]{:S(2)}, u32[]{:S(2)}) %collective-permute-start.35) | collective-permute-done | bytes 32800 | tf_op jit(solution)/shard_map/ppermute | solution.py:228
  (114 shorter events, 17.1 us)
Async XLA Ops:
  2.6 10.9 %copy-start = (bf16[1,1024,1024]{2,1,0:T(8,128)(2,1)S(1)}, bf16[1,1024,1024]{2,1,0:T(8,128)(2,1)}, u32[]{:S(2)}) copy-start(bf16[1,1024,1024]{2,1,0:T(8,128)(2,1)} %param.6) | copy-start | bytes 6291460
  2.6 35.9 %all-to-all-start = ((bf16[16,32,1024]{2,1,0:T(8,128)(2,1)}), bf16[16,32,1024]{2,1,0:T(8,128)(2,1)}, u32[]{:S(2)}, u32[]{:S(2)}) async-start(bf16[16,32,1024]{2,1,0:T(8,128)(2,1)} %broadcast_in_dim.157), calls=%async_computation | async-start | bytes 2097152 | tf_op jit(solution)/shard_map/all_to_all | solution.py:122
  13.5 1.9 copy-start.6
  13.5 2.3 %copy-start.4 = (bf16[16,1,16,1024]{3,2,1,0:T(8,128)(2,1)}, bf16[16,1,16,1024]{3,2,1,0:T(8,128)(2,1)S(1)}, u32[]{:S(2)}) copy-start(bf16[16,1,16,1024]{3,2,1,0:T(8,128)(2,1)S(1)} %get-tuple-element.57) | copy-start | bytes 1572868
  15.3 2.3 %collective-permute-start = (bf16[512,512]{1,0:T(8,128)(2,1)}, bf16[512,512]{1,0:T(8,128)(2,1)}, u32[]{:S(2)}, u32[]{:S(2)}) collective-permute-start(bf16[512,512]{1,0:T(8,128)(2,1)} %pad_maximum_fusion), channel_id=1, source_target_pairs={{0,1},{1,0},{2,3},{3,2},{4,5},{5,4},{6,7},{7,6},{8,9},{9,8},{10,11... | collective-permute-start | bytes 1572872 | tf_op jit(solution)/shard_map/ppermute | solution.py:39
  19.5 8.1 %collective-permute-start.3 = (bf16[128,512]{1,0:T(8,128)(2,1)}, bf16[128,512]{1,0:T(8,128)(2,1)S(1)}, u32[]{:S(2)}, u32[]{:S(2)}) collective-permute-start(bf16[128,512]{1,0:T(8,128)(2,1)} %get-tuple-element.60), channel_id=1, source_target_pairs={{0,4},{2,6},{4,0},{6,2},{1,5},{3,7},{5,1},{7,3},{8,12},{10,14},{12... | collective-permute-start | bytes 393224 | tf_op jit(solution)/shard_map/ppermute | solution.py:71
  22.6 7.1 %collective-permute-start.2 = (bf16[128,512]{1,0:T(8,128)(2,1)}, bf16[128,512]{1,0:T(8,128)(2,1)S(1)}, u32[]{:S(2)}, u32[]{:S(2)}) collective-permute-start(bf16[128,512]{1,0:T(8,128)(2,1)} %get-tuple-element.61), channel_id=1, source_target_pairs={{0,6},{2,0},{4,2},{6,4},{1,7},{3,1},{5,3},{7,5},{8,14},{10,8},{12,... | collective-permute-start | bytes 393224 | tf_op jit(solution)/shard_map/ppermute | solution.py:71
  23.7 6.6 %collective-permute-start.1 = (bf16[128,512]{1,0:T(8,128)(2,1)S(1)}, bf16[128,512]{1,0:T(8,128)(2,1)}, u32[]{:S(2)}, u32[]{:S(2)}) collective-permute-start(bf16[128,512]{1,0:T(8,128)(2,1)S(1)} %get-tuple-element.59), channel_id=1, source_target_pairs={{0,2},{2,4},{4,6},{6,0},{1,3},{3,5},{5,7},{7,1},{8,10},{10,12},{12... | collective-permute-start | bytes 393224 | tf_op jit(solution)/shard_map/ppermute | solution.py:71
  29.7 0.7 copy-start.18
  31.5 10.3 %collective-permute-start.10 = (bf16[128,512]{1,0:T(8,128)(2,1)S(1)}, bf16[128,512]{1,0:T(8,128)(2,1)S(1)}, u32[]{:S(2)}, u32[]{:S(2)}) collective-permute-start(bf16[128,512]{1,0:T(8,128)(2,1)S(1)} %get-tuple-element.49), channel_id=1, source_target_pairs={{0,2},{2,4},{4,6},{6,0},{1,3},{3,5},{5,7},{7,1},{8,10},{10,12},{12... | collective-permute-start | bytes 393224 | tf_op jit(solution)/shard_map/ppermute | solution.py:71
  33.0 9.0 %collective-permute-start.9 = (bf16[128,512]{1,0:T(8,128)(2,1)S(1)}, bf16[128,512]{1,0:T(8,128)(2,1)S(1)}, u32[]{:S(2)}, u32[]{:S(2)}) collective-permute-start(bf16[128,512]{1,0:T(8,128)(2,1)S(1)} %get-tuple-element.49), channel_id=1, source_target_pairs={{0,4},{2,6},{4,0},{6,2},{1,5},{3,7},{5,1},{7,3},{8,12},{10,14},{12... | collective-permute-start | bytes 393224 | tf_op jit(solution)/shard_map/ppermute | solution.py:71
  35.7 6.3 %collective-permute-start.8 = (bf16[128,512]{1,0:T(8,128)(2,1)S(1)}, bf16[128,512]{1,0:T(8,128)(2,1)S(1)}, u32[]{:S(2)}, u32[]{:S(2)}) collective-permute-start(bf16[128,512]{1,0:T(8,128)(2,1)S(1)} %get-tuple-element.49), channel_id=1, source_target_pairs={{0,6},{2,0},{4,2},{6,4},{1,7},{3,1},{5,3},{7,5},{8,14},{10,8},{12,... | collective-permute-start | bytes 393224 | tf_op jit(solution)/shard_map/ppermute | solution.py:71
  39.8 20.8 %copy-start.2 = (bf16[16,1,16,1024]{3,2,1,0:T(8,128)(2,1)}, bf16[16,1,16,1024]{3,2,1,0:T(8,128)(2,1)S(1)}, u32[]{:S(2)}) copy-start(bf16[16,1,16,1024]{3,2,1,0:T(8,128)(2,1)S(1)} %get-tuple-element.55) | copy-start | bytes 1572868
  41.7 2.6 %collective-permute-start.11 = (bf16[256,512]{1,0:T(8,128)(2,1)S(1)}, bf16[256,512]{1,0:T(8,128)(2,1)S(1)}, u32[]{:S(2)}, u32[]{:S(2)}) collective-permute-start(bf16[256,512]{1,0:T(8,128)(2,1)S(1)} %convolution_convert_fusion.4), channel_id=1, source_target_pairs={{0,1},{1,0},{2,3},{3,2},{4,5},{5,4},{6,7},{7,6},{8,9},{9,8},{10,11... | collective-permute-start | bytes 786440 | tf_op jit(solution)/shard_map/ppermute | solution.py:39
  42.3 17.8 %copy-start.9 = (bf16[512,512]{1,0:T(8,128)(2,1)}, bf16[512,512]{1,0:T(8,128)(2,1)S(1)}, u32[]{:S(2)}) copy-start(bf16[512,512]{1,0:T(8,128)(2,1)S(1)} %fusion.54) | copy-start | bytes 1572868
  44.4 10.7 %collective-permute-start.14 = (bf16[256,512]{1,0:T(8,128)(2,1)S(1)}, bf16[256,512]{1,0:T(8,128)(2,1)S(1)}, u32[]{:S(2)}, u32[]{:S(2)}) collective-permute-start(bf16[256,512]{1,0:T(8,128)(2,1)S(1)} %fusion.62), channel_id=1, source_target_pairs={{0,4},{2,6},{4,0},{6,2},{1,5},{3,7},{5,1},{7,3},{8,12},{10,14},{12... | collective-permute-start | bytes 786440 | tf_op jit(solution)/shard_map/ppermute | solution.py:71
  47.3 12.9 %collective-permute-start.13 = (bf16[256,512]{1,0:T(8,128)(2,1)S(1)}, bf16[256,512]{1,0:T(8,128)(2,1)S(1)}, u32[]{:S(2)}, u32[]{:S(2)}) collective-permute-start(bf16[256,512]{1,0:T(8,128)(2,1)S(1)} %fusion.62), channel_id=1, source_target_pairs={{0,6},{2,0},{4,2},{6,4},{1,7},{3,1},{5,3},{7,5},{8,14},{10,8},{12,... | collective-permute-start | bytes 786440 | tf_op jit(solution)/shard_map/ppermute | solution.py:71
  48.4 11.8 %collective-permute-start.12 = (bf16[256,512]{1,0:T(8,128)(2,1)S(1)}, bf16[256,512]{1,0:T(8,128)(2,1)S(1)}, u32[]{:S(2)}, u32[]{:S(2)}) collective-permute-start(bf16[256,512]{1,0:T(8,128)(2,1)S(1)} %fusion.62), channel_id=1, source_target_pairs={{0,2},{2,4},{4,6},{6,0},{1,3},{3,5},{5,7},{7,1},{8,10},{10,12},{12... | collective-permute-start | bytes 786440 | tf_op jit(solution)/shard_map/ppermute | solution.py:71
  49.3 51.7 %collective-permute-start.21 = (bf16[1024,1024]{1,0:T(8,128)(2,1)}, bf16[1024,1024]{1,0:T(8,128)(2,1)}, u32[]{:S(2)}, u32[]{:S(2)}) collective-permute-start(bf16[1024,1024]{1,0:T(8,128)(2,1)} %bitcast.29), channel_id=1, source_target_pairs={{0,192},{64,128},{1,193},{65,129},{2,194},{66,130},{3,195},{67,131... | collective-permute-start | bytes 6291464 | tf_op jit(solution)/shard_map/ppermute | solution.py:43
  50.6 27.5 %copy-start.17 = (bf16[256,512]{1,0:T(8,128)(2,1)}, bf16[256,512]{1,0:T(8,128)(2,1)S(1)}, u32[]{:S(2)}) copy-start(bf16[256,512]{1,0:T(8,128)(2,1)S(1)} %slice.46) | copy-start | bytes 786436
  52.4 8.1 %collective-permute-start.4 = (bf16[256,512]{1,0:T(8,128)(2,1)S(1)}, bf16[256,512]{1,0:T(8,128)(2,1)S(1)}, u32[]{:S(2)}, u32[]{:S(2)}) collective-permute-start(bf16[256,512]{1,0:T(8,128)(2,1)S(1)} %convolution_convert_fusion.5), channel_id=1, source_target_pairs={{0,1},{1,0},{2,3},{3,2},{4,5},{5,4},{6,7},{7,6},{8,9},{9,8},{10,11... | collective-permute-start | bytes 786440 | tf_op jit(solution)/shard_map/ppermute | solution.py:39
  60.4 7.0 %collective-permute-start.16 = (bf16[256,512]{1,0:T(8,128)(2,1)S(1)}, bf16[256,512]{1,0:T(8,128)(2,1)S(1)}, u32[]{:S(2)}, u32[]{:S(2)}) collective-permute-start(bf16[256,512]{1,0:T(8,128)(2,1)S(1)} %multiply_convert_fusion.2), channel_id=1, source_target_pairs={{0,1},{1,0},{2,3},{3,2},{4,5},{5,4},{6,7},{7,6},{8,9},{9,8},{10,11... | collective-permute-start | bytes 786440 | tf_op jit(solution)/shard_map/ppermute | solution.py:39
  62.2 10.7 %collective-permute-start.7 = (bf16[256,512]{1,0:T(8,128)(2,1)S(1)}, bf16[256,512]{1,0:T(8,128)(2,1)S(1)}, u32[]{:S(2)}, u32[]{:S(2)}) collective-permute-start(bf16[256,512]{1,0:T(8,128)(2,1)S(1)} %get-tuple-element.64), channel_id=1, source_target_pairs={{0,4},{2,6},{4,0},{6,2},{1,5},{3,7},{5,1},{7,3},{8,12},{10,14},{12... | collective-permute-start | bytes 786440 | tf_op jit(solution)/shard_map/ppermute | solution.py:71
  65.3 12.8 %collective-permute-start.6 = (bf16[256,512]{1,0:T(8,128)(2,1)S(1)}, bf16[256,512]{1,0:T(8,128)(2,1)S(1)}, u32[]{:S(2)}, u32[]{:S(2)}) collective-permute-start(bf16[256,512]{1,0:T(8,128)(2,1)S(1)} %get-tuple-element.64), channel_id=1, source_target_pairs={{0,6},{2,0},{4,2},{6,4},{1,7},{3,1},{5,3},{7,5},{8,14},{10,8},{12,... | collective-permute-start | bytes 786440 | tf_op jit(solution)/shard_map/ppermute | solution.py:71
  66.5 11.7 %collective-permute-start.5 = (bf16[256,512]{1,0:T(8,128)(2,1)S(1)}, bf16[256,512]{1,0:T(8,128)(2,1)S(1)}, u32[]{:S(2)}, u32[]{:S(2)}) collective-permute-start(bf16[256,512]{1,0:T(8,128)(2,1)S(1)} %get-tuple-element.64), channel_id=1, source_target_pairs={{0,2},{2,4},{4,6},{6,0},{1,3},{3,5},{5,7},{7,1},{8,10},{10,12},{12... | collective-permute-start | bytes 786440 | tf_op jit(solution)/shard_map/ppermute | solution.py:71
  67.4 1.8 copy-start.13
  69.1 13.5 %collective-permute-start.17 = (bf16[256,1024]{1,0:T(8,128)(2,1)}, bf16[256,1024]{1,0:T(8,128)(2,1)}, u32[]{:S(2)}, u32[]{:S(2)}) collective-permute-start(bf16[256,1024]{1,0:T(8,128)(2,1)} %fusion.1), channel_id=1, source_target_pairs={{192,0},{128,64},{193,1},{129,65},{194,2},{130,66},{195,3},{131,67... | collective-permute-start | bytes 1572872 | tf_op jit(solution)/shard_map/ppermute | solution.py:47
  78.4 5.6 %copy-start.11 = (bf16[256,512]{1,0:T(8,128)(2,1)}, bf16[256,512]{1,0:T(8,128)(2,1)S(1)}, u32[]{:S(2)}) copy-start(bf16[256,512]{1,0:T(8,128)(2,1)S(1)} %multiply_convert_fusion.1) | copy-start | bytes 786436
  78.4 1.6 collective-permute-start.15
  80.0 3.9 %copy-start.15 = (bf16[256,512]{1,0:T(8,128)(2,1)}, bf16[256,512]{1,0:T(8,128)(2,1)S(1)}, u32[]{:S(2)}) copy-start(bf16[256,512]{1,0:T(8,128)(2,1)S(1)} %collective-permute-done.15) | copy-start | bytes 786436
  83.9 22.4 %all-to-all-start.1 = ((bf16[16,16,1024]{2,1,0:T(8,128)(2,1)}), bf16[16,16,1024]{2,1,0:T(8,128)(2,1)S(1)}, u32[]{:S(2)}, u32[]{:S(2)}) async-start(bf16[16,16,1024]{2,1,0:T(8,128)(2,1)} %bitcast.146), calls=%async_computation.1 | async-start | bytes 1048576 | tf_op jit(solution)/shard_map/all_to_all | solution.py:111
  90.5 11.8 %collective-permute-start.19 = (bf16[128,512]{1,0:T(8,128)(2,1)S(1)}, bf16[128,512]{1,0:T(8,128)(2,1)}, u32[]{:S(2)}, u32[]{:S(2)}) collective-permute-start(bf16[128,512]{1,0:T(8,128)(2,1)S(1)} %get-tuple-element.30), channel_id=1, source_target_pairs={{0,1},{1,0},{2,3},{3,2},{4,5},{5,4},{6,7},{7,6},{8,9},{9,8},{10,11... | collective-permute-start | bytes 393224 | tf_op jit(solution)/shard_map/ppermute | solution.py:39
  92.0 14.3 %collective-permute-start.18 = (bf16[256,512]{1,0:T(8,128)(2,1)}, bf16[256,512]{1,0:T(8,128)(2,1)}, u32[]{:S(2)}, u32[]{:S(2)}) collective-permute-start(bf16[256,512]{1,0:T(8,128)(2,1)} %copy-done.17), channel_id=1, source_target_pairs={{0,192},{64,128},{1,193},{65,129},{2,194},{66,130},{3,195},{67,131... | collective-permute-start | bytes 786440 | tf_op jit(solution)/shard_map/ppermute | solution.py:43
  101.0 27.0 %collective-permute-start.30 = (bf16[512,1024]{1,0:T(8,128)(2,1)}, bf16[512,1024]{1,0:T(8,128)(2,1)}, u32[]{:S(2)}, u32[]{:S(2)}) collective-permute-start(bf16[512,1024]{1,0:T(8,128)(2,1)} %get-tuple-element.36), channel_id=1, source_target_pairs={{0,192},{64,128},{1,193},{65,129},{2,194},{66,130},{3,195},{67,131... | collective-permute-start | bytes 3145736 | tf_op jit(solution)/shard_map/ppermute | solution.py:43
  108.0 27.5 %all-to-all-start.2 = ((bf16[16,16,1024]{2,1,0:T(8,128)(2,1)}), bf16[16,16,1024]{2,1,0:T(8,128)(2,1)S(1)}, u32[]{:S(2)}, u32[]{:S(2)}) async-start(bf16[16,16,1024]{2,1,0:T(8,128)(2,1)} %broadcast_in_dim.175), calls=%async_computation.2 | async-start | bytes 1048576 | tf_op jit(solution)/shard_map/all_to_all | solution.py:122
  128.0 33.4 %collective-permute-start.31 = (bf16[512,1024]{1,0:T(8,128)(2,1)}, bf16[512,1024]{1,0:T(8,128)(2,1)}, u32[]{:S(2)}, u32[]{:S(2)}) collective-permute-start(bf16[512,1024]{1,0:T(8,128)(2,1)} %get-tuple-element.37), channel_id=1, source_target_pairs={{0,192},{64,128},{1,193},{65,129},{2,194},{66,130},{3,195},{67,131... | collective-permute-start | bytes 3145736 | tf_op jit(solution)/shard_map/ppermute | solution.py:43
  129.3 13.4 %collective-permute-start.25 = (bf16[128,1024]{1,0:T(8,128)(2,1)}, bf16[128,1024]{1,0:T(8,128)(2,1)}, u32[]{:S(2)}, u32[]{:S(2)}) collective-permute-start(bf16[128,1024]{1,0:T(8,128)(2,1)} %pad_maximum_fusion.2), channel_id=1, source_target_pairs={{0,2},{2,4},{4,6},{6,0},{1,3},{3,5},{5,7},{7,1},{8,10},{10,12},{12... | collective-permute-start | bytes 786440 | tf_op jit(solution)/shard_map/ppermute | solution.py:71
  129.9 13.5 %collective-permute-start.24 = (bf16[128,1024]{1,0:T(8,128)(2,1)}, bf16[128,1024]{1,0:T(8,128)(2,1)}, u32[]{:S(2)}, u32[]{:S(2)}) collective-permute-start(bf16[128,1024]{1,0:T(8,128)(2,1)} %pad_maximum_fusion.2), channel_id=1, source_target_pairs={{0,4},{2,6},{4,0},{6,2},{1,5},{3,7},{5,1},{7,3},{8,12},{10,14},{12... | collective-permute-start | bytes 786440 | tf_op jit(solution)/shard_map/ppermute | solution.py:71
  133.2 10.3 %collective-permute-start.23 = (bf16[128,1024]{1,0:T(8,128)(2,1)}, bf16[128,1024]{1,0:T(8,128)(2,1)}, u32[]{:S(2)}, u32[]{:S(2)}) collective-permute-start(bf16[128,1024]{1,0:T(8,128)(2,1)} %pad_maximum_fusion.2), channel_id=1, source_target_pairs={{0,6},{2,0},{4,2},{6,4},{1,7},{3,1},{5,3},{7,5},{8,14},{10,8},{12,... | collective-permute-start | bytes 786440 | tf_op jit(solution)/shard_map/ppermute | solution.py:71
  135.5 14.8 %collective-permute-start.29 = (bf16[256,1024]{1,0:T(8,128)(2,1)S(1)}, bf16[256,1024]{1,0:T(8,128)(2,1)S(1)}, u32[]{:S(2)}, u32[]{:S(2)}) collective-permute-start(bf16[256,1024]{1,0:T(8,128)(2,1)S(1)} %bitcast.133), channel_id=1, source_target_pairs={{192,0},{128,64},{193,1},{129,65},{194,2},{130,66},{195,3},{131,67... | collective-permute-start | bytes 1572872 | tf_op jit(solution)/shard_map/ppermute | solution.py:47
  142.7 2.5 %copy-start.1 = (bf16[1024,1024]{1,0:T(8,128)(2,1)S(1)}, bf16[1024,1024]{1,0:T(8,128)(2,1)}, u32[]{:S(2)}) copy-start(bf16[1024,1024]{1,0:T(8,128)(2,1)} %broadcast_select_fusion) | copy-start | bytes 6291460
  142.7 2.4 %collective-permute-start.22 = (bf16[256,512]{1,0:T(8,128)(2,1)S(1)}, bf16[256,512]{1,0:T(8,128)(2,1)S(1)}, u32[]{:S(2)}, u32[]{:S(2)}) collective-permute-start(bf16[256,512]{1,0:T(8,128)(2,1)S(1)} %fusion.38), channel_id=1, source_target_pairs={{0,1},{1,0},{2,3},{3,2},{4,5},{5,4},{6,7},{7,6},{8,9},{9,8},{10,11... | collective-permute-start | bytes 786440 | tf_op jit(solution)/shard_map/ppermute | solution.py:39
  145.0 5.3 %copy-start.3 = (bf16[16,1,16,1024]{3,2,1,0:T(8,128)(2,1)S(1)}, bf16[16,1,16,1024]{3,2,1,0:T(8,128)(2,1)}, u32[]{:S(2)}) copy-start(bf16[16,1,16,1024]{3,2,1,0:T(8,128)(2,1)} %copy-done.2) | copy-start | bytes 1572868
  145.7 11.0 %collective-permute-start.28 = (bf16[256,512]{1,0:T(8,128)(2,1)S(1)}, bf16[256,512]{1,0:T(8,128)(2,1)S(1)}, u32[]{:S(2)}, u32[]{:S(2)}) collective-permute-start(bf16[256,512]{1,0:T(8,128)(2,1)S(1)} %convert_element_type.161), channel_id=1, source_target_pairs={{0,4},{2,6},{4,0},{6,2},{1,5},{3,7},{5,1},{7,3},{8,12},{10,14},{12... | collective-permute-start | bytes 786440 | tf_op jit(solution)/shard_map/ppermute | solution.py:71
  147.9 12.1 %collective-permute-start.27 = (bf16[256,512]{1,0:T(8,128)(2,1)S(1)}, bf16[256,512]{1,0:T(8,128)(2,1)S(1)}, u32[]{:S(2)}, u32[]{:S(2)}) collective-permute-start(bf16[256,512]{1,0:T(8,128)(2,1)S(1)} %convert_element_type.161), channel_id=1, source_target_pairs={{0,6},{2,0},{4,2},{6,4},{1,7},{3,1},{5,3},{7,5},{8,14},{10,8},{12,... | collective-permute-start | bytes 786440 | tf_op jit(solution)/shard_map/ppermute | solution.py:71
  150.2 11.0 %collective-permute-start.26 = (bf16[256,512]{1,0:T(8,128)(2,1)S(1)}, bf16[256,512]{1,0:T(8,128)(2,1)S(1)}, u32[]{:S(2)}, u32[]{:S(2)}) collective-permute-start(bf16[256,512]{1,0:T(8,128)(2,1)S(1)} %convert_element_type.161), channel_id=1, source_target_pairs={{0,2},{2,4},{4,6},{6,0},{1,3},{3,5},{5,7},{7,1},{8,10},{10,12},{12... | collective-permute-start | bytes 786440 | tf_op jit(solution)/shard_map/ppermute | solution.py:71
  150.3 11.0 %copy-start.10 = (bf16[512,512]{1,0:T(8,128)(2,1)S(1)}, bf16[512,512]{1,0:T(8,128)(2,1)}, u32[]{:S(2)}) copy-start(bf16[512,512]{1,0:T(8,128)(2,1)} %copy-done.9) | copy-start | bytes 1572868
  162.4 5.8 %copy-start.8 = (bf16[512,1024]{1,0:T(8,128)(2,1)S(1)}, bf16[512,1024]{1,0:T(8,128)(2,1)}, u32[]{:S(2)}) copy-start(bf16[512,1024]{1,0:T(8,128)(2,1)} %broadcast_select_fusion.2) | copy-start | bytes 3145732
  162.4 5.8 %collective-permute-start.32 = (bf16[256,512]{1,0:T(8,128)(2,1)S(1)}, bf16[256,512]{1,0:T(8,128)(2,1)S(1)}, u32[]{:S(2)}, u32[]{:S(2)}) collective-permute-start(bf16[256,512]{1,0:T(8,128)(2,1)S(1)} %multiply_convert_fusion), channel_id=1, source_target_pairs={{0,1},{1,0},{2,3},{3,2},{4,5},{5,4},{6,7},{7,6},{8,9},{9,8},{10,11... | collective-permute-start | bytes 786440 | tf_op jit(solution)/shard_map/ppermute | solution.py:39
  162.5 17.3 %collective-permute-start.33 = (bf16[256,512]{1,0:T(8,128)(2,1)S(1)}, bf16[256,512]{1,0:T(8,128)(2,1)S(1)}, u32[]{:S(2)}, u32[]{:S(2)}) collective-permute-start(bf16[256,512]{1,0:T(8,128)(2,1)S(1)} %multiply_convert_fusion), channel_id=1, source_target_pairs={{192,0},{128,64},{193,1},{129,65},{194,2},{130,66},{195,3},{131,67... | collective-permute-start | bytes 786440 | tf_op jit(solution)/shard_map/ppermute | solution.py:47
  168.9 11.0 %copy-start.14 = (bf16[256,512]{1,0:T(8,128)(2,1)S(1)}, bf16[256,512]{1,0:T(8,128)(2,1)}, u32[]{:S(2)}) copy-start(bf16[256,512]{1,0:T(8,128)(2,1)} %copy-done.13) | copy-start | bytes 786436
  169.3 12.2 %copy-start.12 = (bf16[256,512]{1,0:T(8,128)(2,1)S(1)}, bf16[256,512]{1,0:T(8,128)(2,1)}, u32[]{:S(2)}) copy-start(bf16[256,512]{1,0:T(8,128)(2,1)} %copy-done.11) | copy-start | bytes 786436
  169.3 12.2 %copy-start.16 = (bf16[256,512]{1,0:T(8,128)(2,1)S(1)}, bf16[256,512]{1,0:T(8,128)(2,1)}, u32[]{:S(2)}) copy-start(bf16[256,512]{1,0:T(8,128)(2,1)} %copy-done.15) | copy-start | bytes 786436
  170.2 11.3 %copy-start.5 = (bf16[16,1,16,1024]{3,2,1,0:T(8,128)(2,1)S(1)}, bf16[16,1,16,1024]{3,2,1,0:T(8,128)(2,1)}, u32[]{:S(2)}) copy-start(bf16[16,1,16,1024]{3,2,1,0:T(8,128)(2,1)} %copy-done.4) | copy-start | bytes 1572868
  170.2 11.3 %copy-start.7 = (bf16[16,1,16,1024]{3,2,1,0:T(8,128)(2,1)S(1)}, bf16[16,1,16,1024]{3,2,1,0:T(8,128)(2,1)}, u32[]{:S(2)}) copy-start(bf16[16,1,16,1024]{3,2,1,0:T(8,128)(2,1)} %copy-done.6) | copy-start | bytes 1572868
  170.2 25.2 %all-to-all-start.3 = ((bf16[16,16,1024]{2,1,0:T(8,128)(2,1)}), bf16[16,16,1024]{2,1,0:T(8,128)(2,1)S(1)}, u32[]{:S(2)}, u32[]{:S(2)}) async-start(bf16[16,16,1024]{2,1,0:T(8,128)(2,1)} %bitcast.36), calls=%async_computation.3 | async-start | bytes 1048576 | tf_op jit(solution)/shard_map/all_to_all | solution.py:111
  179.8 15.7 %collective-permute-start.20 = (bf16[16,1024]{1,0:T(8,128)(2,1)S(1)}, bf16[16,1024]{1,0:T(8,128)(2,1)S(1)}, u32[]{:S(2)}, u32[]{:S(2)}) collective-permute-start(bf16[16,1024]{1,0:T(8,128)(2,1)S(1)} %add_convert_fusion.1), channel_id=1, source_target_pairs={{0,128},{128,0},{1,129},{129,1},{2,130},{130,2},{3,131},{131,3},{4... | collective-permute-start | bytes 98312 | tf_op jit(solution)/shard_map/ppermute | solution.py:227
  179.8 1.6 collective-permute-start.34
  195.5 5.5 %collective-permute-start.35 = (bf16[16,1024]{1,0:T(8,128)(2,1)S(1)}, bf16[16,1024]{1,0:T(8,128)(2,1)S(1)}, u32[]{:S(2)}, u32[]{:S(2)}) collective-permute-start(bf16[16,1024]{1,0:T(8,128)(2,1)S(1)} %get-tuple-element.46), channel_id=1, source_target_pairs={{0,128},{128,0},{1,129},{129,1},{2,130},{130,2},{3,131},{131,3},{4... | collective-permute-start | bytes 98312 | tf_op jit(solution)/shard_map/ppermute | solution.py:228
